TPU v7x, 32 devices: a whole 2x2x4 slice. The times are simulated.
32 devices in a mesh: gx: 2 (over y), gy: 4 (over z), gz: 4 (over x, core).
Axes of the slice: x: 2, y: 2, z: 4, core: 2. Of those that a mesh axis runs over, the one named last changes fastest.
Arguments:
- residual_q2: bfloat16 [64, 64, 1024], P('gx', 'gy', 'gz'), may hold values from -6 to 6
- viscosity: float32 [32, 32, 512], P('gx', 'gy', 'gz'), may hold values from 0.001 to 1000
- pinned: int32 [32, 32, 512], P('gx', 'gy', 'gz'), may hold values 0 or 1
Outputs:
- scaled_correction: float32 [32, 32, 512], P('gx', 'gy', 'gz')
All inputs are finite; a program needn't handle non-finite values. No bound on the sum of `pinned` on one device may be relied on, other than what follows from the above.
Results may differ from a plain program's by a relative error of at most 0.0003.
Values sent between devices are 32-bit elements; how exact they have to be, the bound alone decides.
No kernel may reach another device: no remote copies, remote signals or barrier semaphores. Data moves between devices by JAX's collectives and lax.ppermute only.
A program may use at most 192 MiB of HBM per device.

v0:
```python
import jax
import jax.numpy as jnp
from jax import lax
from jax.sharding import PartitionSpec as P

NU = 3


OMEGA = 0.6


def with_halo(block, sides, width):
    for axis, dim in sides:
        count = lax.axis_size(axis)
        forward = [(i, i + 1) for i in range(count - 1)]
        backward = [(target, source) for source, target in forward]
        low = lax.ppermute(
            lax.slice_in_dim(block, block.shape[dim] - width, None, axis=dim), axis, forward
        )
        high = lax.ppermute(lax.slice_in_dim(block, 0, width, axis=dim), axis, backward)
        block = jnp.concatenate([low, block, high], axis=dim)
    return block


def coarsen(x):
    a, b, c = x.shape
    return x.reshape(a // 2, 2, b // 2, 2, c // 2, 2).sum(axis=(1, 3, 5))


def refine(x):
    return jnp.repeat(jnp.repeat(jnp.repeat(x, 2, 0), 2, 1), 2, 2)


def extended(field):
    return with_halo(field, (("gx", 0), ("gy", 1), ("gz", 2)), 1)


def shifted(padded):
    return [
        padded[2:, 1:-1, 1:-1],
        padded[:-2, 1:-1, 1:-1],
        padded[1:-1, 2:, 1:-1],
        padded[1:-1, :-2, 1:-1],
        padded[1:-1, 1:-1, 2:],
        padded[1:-1, 1:-1, :-2],
    ]


def neighbours(field):
    return shifted(extended(field))


def harmonic(fluid, near, factor):
    total = fluid + near
    return jnp.where(total > 0, factor * 2.0 * fluid * near / jnp.where(total > 0, total, 1.0), 0.0)


def couplings(fluid, factor):
    return [harmonic(fluid, near, factor) for near in neighbours(fluid)]


def apply_op(field, weights, diag):
    total = diag * field
    for weight, near in zip(weights, neighbours(field)):
        total = total - weight * near
    return total


def presmooth(rhs, weights, diag):
    corr = OMEGA * rhs / diag
    for sweep in range(NU - 1):
        corr = corr + OMEGA * (rhs - apply_op(corr, weights, diag)) / diag
    return corr


def postsmooth(corr, rhs, weights, diag):
    for sweep in range(NU):
        corr = corr + OMEGA * (rhs - apply_op(corr, weights, diag)) / diag
    return corr


def tridiag(coeffs, rhs):
    solved = lax.linalg.tridiagonal_solve(coeffs[0], coeffs[1], coeffs[2], rhs[..., None])[..., 0]
    last = rhs.ndim - 1
    shift_col = jnp.sum(rhs, axis=last, keepdims=True) / jnp.sum(
        coeffs[3], axis=last, keepdims=True
    )
    return solved + shift_col


def prepare_columns(weights, diag):
    lower = -weights[5]
    upper = -weights[4]
    across = diag + lower + upper
    return (
        lax.all_gather(lower, "gz", axis=2, tiled=True),
        lax.all_gather(diag, "gz", axis=2, tiled=True),
        lax.all_gather(upper, "gz", axis=2, tiled=True),
        lax.all_gather(across, "gz", axis=2, tiled=True),
    )


def column_solve(rhs, coeffs):
    depth = rhs.shape[2]
    whole = lax.all_gather(rhs, "gz", axis=2, tiled=True)
    solved = tridiag(coeffs, whole)
    return lax.dynamic_slice_in_dim(solved, lax.axis_index("gz") * depth, depth, 2)


def per_device(residual_q2, viscosity, pinned):
    fluid1 = 1.0 / viscosity
    pin1 = 4.0 * pinned.astype(jnp.float32) * fluid1
    rhs1 = coarsen(residual_q2.astype(jnp.float32))
    fluid2 = coarsen(fluid1) / 8.0
    pin2 = coarsen(pin1) / 4.0
    fluid3 = coarsen(fluid2) / 8.0
    pin3 = coarsen(pin2) / 4.0
    weights1 = couplings(fluid1, 1.0)
    weights2 = couplings(fluid2, 2.0)
    weights3 = couplings(fluid3, 4.0)
    diag1 = sum(weights1) + pin1
    diag2 = sum(weights2) + pin2
    diag3 = sum(weights3) + pin3
    coeffs = prepare_columns(weights3, diag3)
    corr1 = presmooth(rhs1, weights1, diag1)
    rhs2 = coarsen(rhs1 - apply_op(corr1, weights1, diag1))
    corr2 = presmooth(rhs2, weights2, diag2)
    rhs3 = coarsen(rhs2 - apply_op(corr2, weights2, diag2))
    corr3 = column_solve(rhs3, coeffs)
    corr3 = corr3 + column_solve(rhs3 - apply_op(corr3, weights3, diag3), coeffs)
    corr2 = postsmooth(corr2 + refine(corr3), rhs2, weights2, diag2)
    corr1 = postsmooth(corr1 + refine(corr2), rhs1, weights1, diag1)
    return diag1 * corr1


def solution(mesh):
    placed = (P("gx", "gy", "gz"), P("gx", "gy", "gz"), P("gx", "gy", "gz"))
    return jax.shard_map(
        per_device, mesh=mesh, in_specs=placed, out_specs=P("gx", "gy", "gz"), check_vma=False
    )
```

profile of v0, /device:TPU:0, one launch (start us, length us, event | category | flops | bytes accessed | tf_op | source)
XLA Modules:
  0.0 539.0 jit_solution(3002629062792760114)
XLA Ops:
  2.2 4.9 collective-permute-start.1
  7.0 5.6 %reshape.940 = f32[8,2,4,2,64,2]{5,4,3,2,1,0:T(8,128)} reshape(f32[16,8,128]{2,1,0:T(8,128)S(1)} %broadcast_divide_fusion) | data formatting | bytes 131072 | tf_op jit(solution)/shard_map/reshape | solution.py:27
  15.3 4.6 collective-permute-start.3
  24.5 4.2 collective-permute-done.2
  31.5 34.5 %reshape.965 = f32[16,2,8,2,128,2]{5,4,3,2,1,0:T(8,128)} reshape(bf16[32,16,256]{2,1,0:T(8,128)(2,1)S(1)} %copy-done) | data formatting | bytes 786432 | tf_op jit(solution)/shard_map/reshape | solution.py:27
  66.0 12.2 %reduce_sum.94 = f32[16,8,128]{2,1,0:T(8,128)S(1)} reduce(f32[16,2,8,2,128,2]{5,4,3,2,1,0:T(8,128)} %reshape.965, f32[]{:T(128)} %constant.127.clone.1), dimensions={1,3,5}, to_apply=%region_0.0 | reduce | flops 114688 | bytes 589828 | tf_op jit(solution)/shard_map/reduce_sum | solution.py:27
  79.9 4.5 collective-permute-start.7
  85.8 4.5 collective-permute-start.42
  95.2 4.2 collective-permute-done.8
  110.4 4.5 collective-permute-start.13
  116.3 5.2 collective-permute-start.27
  126.9 4.2 collective-permute-done.14
  137.3 6.1 %collective-permute-start.47 = (f32[6,4,1]{2,1,0:T(4,128)S(1)}, f32[6,4,1]{2,1,0:T(4,128)S(1)}, u32[]{:S(2)}, u32[]{:S(2)}) collective-permute-start(f32[6,4,1]{2,1,0:T(4,128)S(1)} %get-tuple-element.985), channel_id=1, source_target_pairs={{0,1},{1,2},{2,3},{4,5},{5,6},{6,7},{8,9},{9,10},{10,11},{12,13},{... | collective-permute-start | bytes 296 | tf_op jit(solution)/shard_map/ppermute | solution.py:17
  145.1 4.5 collective-permute-start.19
  154.3 4.2 collective-permute-done.20
  168.1 5.6 %reshape.941 = f32[8,2,4,2,64,2]{5,4,3,2,1,0:T(8,128)} reshape(f32[16,8,128]{2,1,0:T(8,128)S(1)} %get-tuple-element.877) | data formatting | bytes 131072 | tf_op jit(solution)/shard_map/reshape | solution.py:27
  176.6 5.6 %reshape.939 = f32[8,2,4,2,64,2]{5,4,3,2,1,0:T(8,128)} reshape(f32[16,8,128]{2,1,0:T(8,128)S(1)} %fusion.757) | data formatting | bytes 131072 | tf_op jit(solution)/shard_map/reshape | solution.py:27
  186.2 4.5 collective-permute-start.31
  193.4 4.5 collective-permute-start.33
  198.1 5.6 %all_gather.18 = f32[4,2,128]{0,1,2:T(2,128)S(1)} all-gather(f32[4,2,32]{0,1,2:T(2,128)S(1)} %copy.1978), channel_id=1, replica_groups=mesh['gx'=2,'gy'=4,'gz'=4] {'gz'}, dimensions={2}, use_global_device_ids=true | all-gather | bytes 5120 | tf_op jit(solution)/shard_map/all_gather | solution.py:98
  211.5 4.5 collective-permute-start.37
  216.1 6.3 %all_gather.19 = f32[4,2,128]{0,1,2:T(2,128)S(1)} all-gather(f32[4,2,32]{0,1,2:T(2,128)S(1)} %copy.1981), channel_id=1, replica_groups=mesh['gx'=2,'gy'=4,'gz'=4] {'gz'}, dimensions={2}, use_global_device_ids=true | all-gather | bytes 5120 | tf_op jit(solution)/shard_map/all_gather | solution.py:97
  223.6 4.5 collective-permute-start.39
  237.5 4.5 collective-permute-start.49
  242.0 6.3 %all_gather.21 = f32[4,2,128]{0,1,2:T(2,128)S(1)} all-gather(f32[4,2,32]{0,1,2:T(2,128)S(1)} %copy.1984), channel_id=1, replica_groups=mesh['gx'=2,'gy'=4,'gz'=4] {'gz'}, dimensions={2}, use_global_device_ids=true | all-gather | bytes 5120 | tf_op jit(solution)/shard_map/all_gather | solution.py:96
  249.6 4.8 collective-permute-start.51
  254.5 5.4 %all_gather.22 = f32[4,2,128]{0,1,2:T(2,128)S(1)} all-gather(f32[4,2,32]{0,1,2:T(2,128)S(1)} %copy.2152), channel_id=1, replica_groups=mesh['gx'=2,'gy'=4,'gz'=4] {'gz'}, dimensions={2}, use_global_device_ids=true | all-gather | bytes 5120 | tf_op jit(solution)/shard_map/all_gather | solution.py:99
  267.4 6.8 %all_gather.20 = f32[4,2,128]{0,1,2:T(2,128)S(1)} all-gather(f32[4,2,32]{0,1,2:T(2,128)S(1)} %copy.1983), channel_id=1, replica_groups=mesh['gx'=2,'gy'=4,'gz'=4] {'gz'}, dimensions={2}, use_global_device_ids=true | all-gather | bytes 5120 | tf_op jit(solution)/shard_map/all_gather | solution.py:105
  274.3 21.7 %while.64 = (s32[]{:T(128)}, f32[4,2]{0,1:T(2,128)S(1)}, f32[4,2,1]{0,1,2:T(2,128)S(1)}, f32[3,32,4,2]{1,0,3,2:T(4,128)S(1)}, f32[3,32,4,2,1]{1,0,3,2,4:T(4,128)...) while((s32[]{:T(128)}, f32[4,2]{0,1:T(2,128)S(1)}, ...), condition=%wide.region_8.9_spmd, body=%wide.region_7.8_spmd.sunk | while | flops 1585 | bytes 23697 | solution.py:83
  309.9 10.8 %while.65 = (s32[]{:T(128)}, f32[4,2,1]{0,1,2:T(2,128)S(1)}, f32[3,32,4,2,1]{1,0,2,3,4:T(4,128)S(1)}, f32[3,32,4,2,1]{2,3,4,1,0:T(2,128)S(1)}, f32[3,32,4,2]{2,3...) while((s32[]{:T(128)}, f32[4,2,1]{0,1,2:T(2,128)S(1)}, ...), condition=%wide.region_10.11_spmd, body=%wide.region_9.10_spmd.sunk | while | flops 546 | bytes 10169 | solution.py:83
  326.0 4.5 collective-permute-start.55
  333.1 4.6 collective-permute-start.57
  344.5 6.8 %all_gather.23 = f32[4,2,128]{0,1,2:T(2,128)S(1)} all-gather(f32[4,2,32]{0,1,2:T(2,128)S(1)} %copy.2158), channel_id=1, replica_groups=mesh['gx'=2,'gy'=4,'gz'=4] {'gz'}, dimensions={2}, use_global_device_ids=true | all-gather | bytes 5120 | tf_op jit(solution)/shard_map/all_gather | solution.py:105
  351.4 21.7 %while.66 = (s32[]{:T(128)}, f32[4,2]{0,1:T(2,128)S(1)}, f32[4,2,1]{0,1,2:T(2,128)S(1)}, f32[3,32,4,2]{1,0,3,2:T(4,128)S(1)}, f32[3,32,4,2,1]{1,0,3,2,4:T(4,128)...) while((s32[]{:T(128)}, f32[4,2]{0,1:T(2,128)S(1)}, ...), condition=%wide.region_14.15_spmd, body=%wide.region_13.14_spmd.sunk | while | flops 1585 | bytes 23697 | solution.py:83
  387.0 10.8 %while.67 = (s32[]{:T(128)}, f32[4,2,1]{0,1,2:T(2,128)S(1)}, f32[3,32,4,2,1]{1,0,2,3,4:T(4,128)S(1)}, f32[3,32,4,2,1]{2,3,4,1,0:T(2,128)S(1)}, f32[3,32,4,2]{2,3...) while((s32[]{:T(128)}, f32[4,2,1]{0,1,2:T(2,128)S(1)}, ...), condition=%wide.region_16.17_spmd, body=%wide.region_15.16_spmd.sunk | while | flops 546 | bytes 10169 | solution.py:83
  403.4 4.5 collective-permute-start.61
  410.6 4.8 collective-permute-start.63
  424.8 4.5 collective-permute-start.67
  431.9 4.8 collective-permute-start.69
  446.9 4.5 collective-permute-start.73
  454.0 4.8 collective-permute-start.75
  469.4 4.5 collective-permute-start.79
  475.3 4.2 collective-permute-start.81
  480.9 4.2 collective-permute-done.80
  492.1 4.5 collective-permute-start.85
  503.3 4.2 collective-permute-done.86
  514.8 4.5 collective-permute-start.91
  531.3 5.9 %collective-permute-start.95 = (f32[18,10,1]{2,0,1:T(8,128)S(1)}, f32[18,10,1]{2,0,1:T(8,128)S(1)}, u32[]{:S(2)}, u32[]{:S(2)}) collective-permute-start(f32[18,10,1]{2,0,1:T(8,128)S(1)} %get-tuple-element.883), channel_id=1, source_target_pairs={{0,1},{1,2},{2,3},{4,5},{5,6},{6,7},{8,9},{9,10},{10,11},{12,13},{... | collective-permute-start | bytes 2168 | tf_op jit(solution)/shard_map/ppermute | solution.py:17
  (1379 shorter events, 282.7 us)
Async XLA Ops:
  0.9 14.4 %collective-permute-start = (f32[1,8,128]{2,1,0:T(8,128)S(1)}, f32[1,8,128]{2,1,0:T(8,128)S(1)}, u32[]{:S(2)}, u32[]{:S(2)}) collective-permute-start(f32[1,8,128]{2,1,0:T(8,128)S(1)} %get-tuple-element.935), channel_id=1, source_target_pairs={{16,0},{17,1},{18,2},{19,3},{20,4},{21,5},{22,6},{23,7},{24,8},{25... | collective-permute-start | bytes 12296 | tf_op jit(solution)/shard_map/ppermute | solution.py:20
  2.2 13.1 %collective-permute-start.1 = (f32[1,8,128]{2,1,0:T(8,128)S(1)}, f32[1,8,128]{2,1,0:T(8,128)S(1)}, u32[]{:S(2)}, u32[]{:S(2)}) collective-permute-start(f32[1,8,128]{2,1,0:T(8,128)S(1)} %get-tuple-element.934), channel_id=1, source_target_pairs={{0,16},{1,17},{2,18},{3,19},{4,20},{5,21},{6,22},{7,23},{8,24},{9,... | collective-permute-start | bytes 12296 | tf_op jit(solution)/shard_map/ppermute | solution.py:17
  15.3 9.2 %collective-permute-start.3 = (f32[18,1,128]{2,1,0:T(1,128)S(1)}, f32[18,1,128]{2,1,0:T(1,128)S(1)}, u32[]{:S(2)}, u32[]{:S(2)}) collective-permute-start(f32[18,1,128]{2,1,0:T(1,128)S(1)} %get-tuple-element.920), channel_id=1, source_target_pairs={{0,4},{4,8},{8,12},{1,5},{5,9},{9,13},{2,6},{6,10},{10,14},{3,7},{... | collective-permute-start | bytes 27656 | tf_op jit(solution)/shard_map/ppermute | solution.py:17
  19.9 90.5 %collective-permute-start.25 = (f32[1,4,64]{2,1,0:T(4,128)S(1)}, f32[1,4,64]{2,1,0:T(4,128)S(1)}, u32[]{:S(2)}, u32[]{:S(2)}) collective-permute-start(f32[1,4,64]{2,1,0:T(4,128)S(1)} %get-tuple-element.977), channel_id=1, source_target_pairs={{0,16},{1,17},{2,18},{3,19},{4,20},{5,21},{6,22},{7,23},{8,24},{9,... | collective-permute-start | bytes 3080 | tf_op jit(solution)/shard_map/ppermute | solution.py:17
  21.2 93.8 %collective-permute-start.24 = (f32[1,4,64]{2,1,0:T(4,128)S(1)}, f32[1,4,64]{2,1,0:T(4,128)S(1)}, u32[]{:S(2)}, u32[]{:S(2)}) collective-permute-start(f32[1,4,64]{2,1,0:T(4,128)S(1)} %get-tuple-element.976), channel_id=1, source_target_pairs={{16,0},{17,1},{18,2},{19,3},{20,4},{21,5},{22,6},{23,7},{24,8},{25... | collective-permute-start | bytes 3080 | tf_op jit(solution)/shard_map/ppermute | solution.py:20
  28.8 49.4 %collective-permute-start.5 = (f32[18,10,1]{2,0,1:T(8,128)S(1)}, f32[18,10,1]{2,0,1:T(8,128)S(1)}, u32[]{:S(2)}, u32[]{:S(2)}) collective-permute-start(f32[18,10,1]{2,0,1:T(8,128)S(1)} %get-tuple-element.906), channel_id=1, source_target_pairs={{0,1},{1,2},{2,3},{4,5},{5,6},{6,7},{8,9},{9,10},{10,11},{12,13},{... | collective-permute-start | bytes 2168 | tf_op jit(solution)/shard_map/ppermute | solution.py:17
  30.1 48.1 %collective-permute-start.4 = (f32[18,10,1]{2,0,1:T(8,128)S(1)}, f32[18,10,1]{2,0,1:T(8,128)S(1)}, u32[]{:S(2)}, u32[]{:S(2)}) collective-permute-start(f32[18,10,1]{2,0,1:T(8,128)S(1)} %get-tuple-element.907), channel_id=1, source_target_pairs={{1,0},{2,1},{3,2},{5,4},{6,5},{7,6},{9,8},{10,9},{11,10},{13,12},{... | collective-permute-start | bytes 2168 | tf_op jit(solution)/shard_map/ppermute | solution.py:20
  78.6 7.2 %collective-permute-start.6 = (f32[1,8,128]{2,1,0:T(8,128)S(1)}, f32[1,8,128]{2,1,0:T(8,128)S(1)}, u32[]{:S(2)}, u32[]{:S(2)}) collective-permute-start(f32[1,8,128]{2,1,0:T(8,128)S(1)} %get-tuple-element.933), channel_id=1, source_target_pairs={{16,0},{17,1},{18,2},{19,3},{20,4},{21,5},{22,6},{23,7},{24,8},{25... | collective-permute-start | bytes 12296 | tf_op jit(solution)/shard_map/ppermute | solution.py:20
  79.9 10.4 %collective-permute-start.7 = (f32[1,8,128]{2,1,0:T(8,128)S(1)}, f32[1,8,128]{2,1,0:T(8,128)S(1)}, u32[]{:S(2)}, u32[]{:S(2)}) collective-permute-start(f32[1,8,128]{2,1,0:T(8,128)S(1)} %get-tuple-element.932), channel_id=1, source_target_pairs={{0,16},{1,17},{2,18},{3,19},{4,20},{5,21},{6,22},{7,23},{8,24},{9,... | collective-permute-start | bytes 12296 | tf_op jit(solution)/shard_map/ppermute | solution.py:17
  84.4 9.4 %collective-permute-start.43 = (f32[1,2,32]{2,0,1:T(1,128)S(1)}, f32[1,2,32]{2,0,1:T(1,128)S(1)}, u32[]{:S(2)}, u32[]{:S(2)}) collective-permute-start(f32[1,2,32]{2,0,1:T(1,128)S(1)} %get-tuple-element.1117), channel_id=1, source_target_pairs={{16,0},{17,1},{18,2},{19,3},{20,4},{21,5},{22,6},{23,7},{24,8},{25... | collective-permute-start | bytes 776 | tf_op jit(solution)/shard_map/ppermute | solution.py:20
  85.8 8.1 %collective-permute-start.42 = (f32[1,2,32]{2,0,1:T(1,128)S(1)}, f32[1,2,32]{2,0,1:T(1,128)S(1)}, u32[]{:S(2)}, u32[]{:S(2)}) collective-permute-start(f32[1,2,32]{2,0,1:T(1,128)S(1)} %get-tuple-element.1116), channel_id=1, source_target_pairs={{0,16},{1,17},{2,18},{3,19},{4,20},{5,21},{6,22},{7,23},{8,24},{9,... | collective-permute-start | bytes 776 | tf_op jit(solution)/shard_map/ppermute | solution.py:17
  99.5 7.9 %collective-permute-start.10 = (f32[18,10,1]{2,0,1:T(8,128)S(1)}, f32[18,10,1]{2,0,1:T(8,128)S(1)}, u32[]{:S(2)}, u32[]{:S(2)}) collective-permute-start(f32[18,10,1]{2,0,1:T(8,128)S(1)} %get-tuple-element.902), channel_id=1, source_target_pairs={{1,0},{2,1},{3,2},{5,4},{6,5},{7,6},{9,8},{10,9},{11,10},{13,12},{... | collective-permute-start | bytes 2168 | tf_op jit(solution)/shard_map/ppermute | solution.py:20
  100.8 8.0 %collective-permute-start.11 = (f32[18,10,1]{2,0,1:T(8,128)S(1)}, f32[18,10,1]{2,0,1:T(8,128)S(1)}, u32[]{:S(2)}, u32[]{:S(2)}) collective-permute-start(f32[18,10,1]{2,0,1:T(8,128)S(1)} %get-tuple-element.903), channel_id=1, source_target_pairs={{0,1},{1,2},{2,3},{4,5},{5,6},{6,7},{8,9},{9,10},{10,11},{12,13},{... | collective-permute-start | bytes 2168 | tf_op jit(solution)/shard_map/ppermute | solution.py:17
  104.0 17.5 %collective-permute-start.44 = (f32[6,1,32]{2,0,1:T(8,128)S(1)}, f32[6,1,32]{2,0,1:T(8,128)S(1)}, u32[]{:S(2)}, u32[]{:S(2)}) collective-permute-start(f32[6,1,32]{2,0,1:T(8,128)S(1)} %get-tuple-element.989), channel_id=1, source_target_pairs={{0,4},{4,8},{8,12},{1,5},{5,9},{9,13},{2,6},{6,10},{10,14},{3,7},{... | collective-permute-start | bytes 2312 | tf_op jit(solution)/shard_map/ppermute | solution.py:17
  107.5 8.8 %collective-permute-start.45 = (f32[6,1,32]{2,0,1:T(8,128)S(1)}, f32[6,1,32]{2,0,1:T(8,128)S(1)}, u32[]{:S(2)}, u32[]{:S(2)}) collective-permute-start(f32[6,1,32]{2,0,1:T(8,128)S(1)} %get-tuple-element.988), channel_id=1, source_target_pairs={{4,0},{8,4},{12,8},{5,1},{9,5},{13,9},{6,2},{10,6},{14,10},{7,3},{... | collective-permute-start | bytes 2312 | tf_op jit(solution)/shard_map/ppermute | solution.py:20
  109.1 12.4 %collective-permute-start.12 = (f32[1,8,128]{2,1,0:T(8,128)S(1)}, f32[1,8,128]{2,1,0:T(8,128)S(1)}, u32[]{:S(2)}, u32[]{:S(2)}) collective-permute-start(f32[1,8,128]{2,1,0:T(8,128)S(1)} %get-tuple-element.931), channel_id=1, source_target_pairs={{16,0},{17,1},{18,2},{19,3},{20,4},{21,5},{22,6},{23,7},{24,8},{25... | collective-permute-start | bytes 12296 | tf_op jit(solution)/shard_map/ppermute | solution.py:20
  110.4 11.1 %collective-permute-start.13 = (f32[1,8,128]{2,1,0:T(8,128)S(1)}, f32[1,8,128]{2,1,0:T(8,128)S(1)}, u32[]{:S(2)}, u32[]{:S(2)}) collective-permute-start(f32[1,8,128]{2,1,0:T(8,128)S(1)} %get-tuple-element.930), channel_id=1, source_target_pairs={{0,16},{1,17},{2,18},{3,19},{4,20},{5,21},{6,22},{7,23},{8,24},{9,... | collective-permute-start | bytes 12296 | tf_op jit(solution)/shard_map/ppermute | solution.py:17
  115.0 37.9 %collective-permute-start.26 = (f32[10,1,64]{2,1,0:T(1,128)S(1)}, f32[10,1,64]{2,1,0:T(1,128)S(1)}, u32[]{:S(2)}, u32[]{:S(2)}) collective-permute-start(f32[10,1,64]{2,1,0:T(1,128)S(1)} %get-tuple-element.963), channel_id=1, source_target_pairs={{4,0},{8,4},{12,8},{5,1},{9,5},{13,9},{6,2},{10,6},{14,10},{7,3},{... | collective-permute-start | bytes 7688 | tf_op jit(solution)/shard_map/ppermute | solution.py:20
  116.3 36.6 %collective-permute-start.27 = (f32[10,1,64]{2,1,0:T(1,128)S(1)}, f32[10,1,64]{2,1,0:T(1,128)S(1)}, u32[]{:S(2)}, u32[]{:S(2)}) collective-permute-start(f32[10,1,64]{2,1,0:T(1,128)S(1)} %get-tuple-element.962), channel_id=1, source_target_pairs={{0,4},{4,8},{8,12},{1,5},{5,9},{9,13},{2,6},{6,10},{10,14},{3,7},{... | collective-permute-start | bytes 7688 | tf_op jit(solution)/shard_map/ppermute | solution.py:17
  131.2 6.1 %collective-permute-start.16 = (f32[18,10,1]{2,0,1:T(8,128)S(1)}, f32[18,10,1]{2,0,1:T(8,128)S(1)}, u32[]{:S(2)}, u32[]{:S(2)}) collective-permute-start(f32[18,10,1]{2,0,1:T(8,128)S(1)} %get-tuple-element.898), channel_id=1, source_target_pairs={{1,0},{2,1},{3,2},{5,4},{6,5},{7,6},{9,8},{10,9},{11,10},{13,12},{... | collective-permute-start | bytes 2168 | tf_op jit(solution)/shard_map/ppermute | solution.py:20
  132.5 11.0 %collective-permute-start.17 = (f32[18,10,1]{2,0,1:T(8,128)S(1)}, f32[18,10,1]{2,0,1:T(8,128)S(1)}, u32[]{:S(2)}, u32[]{:S(2)}) collective-permute-start(f32[18,10,1]{2,0,1:T(8,128)S(1)} %get-tuple-element.899), channel_id=1, source_target_pairs={{0,1},{1,2},{2,3},{4,5},{5,6},{6,7},{8,9},{9,10},{10,11},{12,13},{... | collective-permute-start | bytes 2168 | tf_op jit(solution)/shard_map/ppermute | solution.py:17
  136.0 9.1 %collective-permute-start.46 = (f32[6,4,1]{2,1,0:T(4,128)S(1)}, f32[6,4,1]{2,1,0:T(4,128)S(1)}, u32[]{:S(2)}, u32[]{:S(2)}) collective-permute-start(f32[6,4,1]{2,1,0:T(4,128)S(1)} %get-tuple-element.984), channel_id=1, source_target_pairs={{1,0},{2,1},{3,2},{5,4},{6,5},{7,6},{9,8},{10,9},{11,10},{13,12},{... | collective-permute-start | bytes 296 | tf_op jit(solution)/shard_map/ppermute | solution.py:20
  137.3 12.3 %collective-permute-start.47 = (f32[6,4,1]{2,1,0:T(4,128)S(1)}, f32[6,4,1]{2,1,0:T(4,128)S(1)}, u32[]{:S(2)}, u32[]{:S(2)}) collective-permute-start(f32[6,4,1]{2,1,0:T(4,128)S(1)} %get-tuple-element.985), channel_id=1, source_target_pairs={{0,1},{1,2},{2,3},{4,5},{5,6},{6,7},{8,9},{9,10},{10,11},{12,13},{... | collective-permute-start | bytes 296 | tf_op jit(solution)/shard_map/ppermute | solution.py:17
  143.8 6.0 %collective-permute-start.18 = (f32[1,8,128]{2,1,0:T(8,128)S(1)}, f32[1,8,128]{2,1,0:T(8,128)S(1)}, u32[]{:S(2)}, u32[]{:S(2)}) collective-permute-start(f32[1,8,128]{2,1,0:T(8,128)S(1)} %get-tuple-element.929), channel_id=1, source_target_pairs={{16,0},{17,1},{18,2},{19,3},{20,4},{21,5},{22,6},{23,7},{24,8},{25... | collective-permute-start | bytes 12296 | tf_op jit(solution)/shard_map/ppermute | solution.py:20
  158.6 17.6 %collective-permute-start.22 = (f32[18,10,1]{2,0,1:T(8,128)S(1)}, f32[18,10,1]{2,0,1:T(8,128)S(1)}, u32[]{:S(2)}, u32[]{:S(2)}) collective-permute-start(f32[18,10,1]{2,0,1:T(8,128)S(1)} %get-tuple-element.894), channel_id=1, source_target_pairs={{1,0},{2,1},{3,2},{5,4},{6,5},{7,6},{9,8},{10,9},{11,10},{13,12},{... | collective-permute-start | bytes 2168 | tf_op jit(solution)/shard_map/ppermute | solution.py:20
  159.9 16.3 %collective-permute-start.23 = (f32[18,10,1]{2,0,1:T(8,128)S(1)}, f32[18,10,1]{2,0,1:T(8,128)S(1)}, u32[]{:S(2)}, u32[]{:S(2)}) collective-permute-start(f32[18,10,1]{2,0,1:T(8,128)S(1)} %get-tuple-element.895), channel_id=1, source_target_pairs={{0,1},{1,2},{2,3},{4,5},{5,6},{6,7},{8,9},{9,10},{10,11},{12,13},{... | collective-permute-start | bytes 2168 | tf_op jit(solution)/shard_map/ppermute | solution.py:17
  163.1 21.7 %collective-permute-start.28 = (f32[10,6,1]{2,1,0:T(8,128)S(1)}, f32[10,6,1]{2,1,0:T(8,128)S(1)}, u32[]{:S(2)}, u32[]{:S(2)}) collective-permute-start(f32[10,6,1]{2,1,0:T(8,128)S(1)} %get-tuple-element.949), channel_id=1, source_target_pairs={{1,0},{2,1},{3,2},{5,4},{6,5},{7,6},{9,8},{10,9},{11,10},{13,12},{... | collective-permute-start | bytes 728 | tf_op jit(solution)/shard_map/ppermute | solution.py:20
  164.3 20.4 %collective-permute-start.29 = (f32[10,6,1]{2,1,0:T(8,128)S(1)}, f32[10,6,1]{2,1,0:T(8,128)S(1)}, u32[]{:S(2)}, u32[]{:S(2)}) collective-permute-start(f32[10,6,1]{2,1,0:T(8,128)S(1)} %get-tuple-element.948), channel_id=1, source_target_pairs={{0,1},{1,2},{2,3},{4,5},{5,6},{6,7},{8,9},{9,10},{10,11},{12,13},{... | collective-permute-start | bytes 728 | tf_op jit(solution)/shard_map/ppermute | solution.py:17
  184.9 6.5 %collective-permute-start.30 = (f32[1,4,64]{2,1,0:T(4,128)S(1)}, f32[1,4,64]{2,1,0:T(4,128)S(1)}, u32[]{:S(2)}, u32[]{:S(2)}) collective-permute-start(f32[1,4,64]{2,1,0:T(4,128)S(1)} %get-tuple-element.975), channel_id=1, source_target_pairs={{16,0},{17,1},{18,2},{19,3},{20,4},{21,5},{22,6},{23,7},{24,8},{25... | collective-permute-start | bytes 3080 | tf_op jit(solution)/shard_map/ppermute | solution.py:20
  192.1 11.6 %collective-permute-start.32 = (f32[10,1,64]{2,1,0:T(1,128)S(1)}, f32[10,1,64]{2,1,0:T(1,128)S(1)}, u32[]{:S(2)}, u32[]{:S(2)}) collective-permute-start(f32[10,1,64]{2,1,0:T(1,128)S(1)} %get-tuple-element.961), channel_id=1, source_target_pairs={{4,0},{8,4},{12,8},{5,1},{9,5},{13,9},{6,2},{10,6},{14,10},{7,3},{... | collective-permute-start | bytes 7688 | tf_op jit(solution)/shard_map/ppermute | solution.py:20
  193.4 10.3 %collective-permute-start.33 = (f32[10,1,64]{2,1,0:T(1,128)S(1)}, f32[10,1,64]{2,1,0:T(1,128)S(1)}, u32[]{:S(2)}, u32[]{:S(2)}) collective-permute-start(f32[10,1,64]{2,1,0:T(1,128)S(1)} %get-tuple-element.960), channel_id=1, source_target_pairs={{0,4},{4,8},{8,12},{1,5},{5,9},{9,13},{2,6},{6,10},{10,14},{3,7},{... | collective-permute-start | bytes 7688 | tf_op jit(solution)/shard_map/ppermute | solution.py:17
  210.2 12.1 %collective-permute-start.36 = (f32[1,4,64]{2,1,0:T(4,128)S(1)}, f32[1,4,64]{2,1,0:T(4,128)S(1)}, u32[]{:S(2)}, u32[]{:S(2)}) collective-permute-start(f32[1,4,64]{2,1,0:T(4,128)S(1)} %get-tuple-element.973), channel_id=1, source_target_pairs={{16,0},{17,1},{18,2},{19,3},{20,4},{21,5},{22,6},{23,7},{24,8},{25... | collective-permute-start | bytes 3080 | tf_op jit(solution)/shard_map/ppermute | solution.py:20
  211.5 10.8 %collective-permute-start.37 = (f32[1,4,64]{2,1,0:T(4,128)S(1)}, f32[1,4,64]{2,1,0:T(4,128)S(1)}, u32[]{:S(2)}, u32[]{:S(2)}) collective-permute-start(f32[1,4,64]{2,1,0:T(4,128)S(1)} %get-tuple-element.972), channel_id=1, source_target_pairs={{0,16},{1,17},{2,18},{3,19},{4,20},{5,21},{6,22},{7,23},{8,24},{9,... | collective-permute-start | bytes 3080 | tf_op jit(solution)/shard_map/ppermute | solution.py:17
  222.3 5.9 %collective-permute-start.38 = (f32[10,1,64]{2,1,0:T(1,128)S(1)}, f32[10,1,64]{2,1,0:T(1,128)S(1)}, u32[]{:S(2)}, u32[]{:S(2)}) collective-permute-start(f32[10,1,64]{2,1,0:T(1,128)S(1)} %get-tuple-element.959), channel_id=1, source_target_pairs={{4,0},{8,4},{12,8},{5,1},{9,5},{13,9},{6,2},{10,6},{14,10},{7,3},{... | collective-permute-start | bytes 7688 | tf_op jit(solution)/shard_map/ppermute | solution.py:20
  223.6 5.9 %collective-permute-start.39 = (f32[10,1,64]{2,1,0:T(1,128)S(1)}, f32[10,1,64]{2,1,0:T(1,128)S(1)}, u32[]{:S(2)}, u32[]{:S(2)}) collective-permute-start(f32[10,1,64]{2,1,0:T(1,128)S(1)} %get-tuple-element.958), channel_id=1, source_target_pairs={{0,4},{4,8},{8,12},{1,5},{5,9},{9,13},{2,6},{6,10},{10,14},{3,7},{... | collective-permute-start | bytes 7688 | tf_op jit(solution)/shard_map/ppermute | solution.py:17
  236.2 12.1 %collective-permute-start.48 = (f32[1,4,64]{2,1,0:T(4,128)S(1)}, f32[1,4,64]{2,1,0:T(4,128)S(1)}, u32[]{:S(2)}, u32[]{:S(2)}) collective-permute-start(f32[1,4,64]{2,1,0:T(4,128)S(1)} %get-tuple-element.971), channel_id=1, source_target_pairs={{16,0},{17,1},{18,2},{19,3},{20,4},{21,5},{22,6},{23,7},{24,8},{25... | collective-permute-start | bytes 3080 | tf_op jit(solution)/shard_map/ppermute | solution.py:20
  237.5 10.8 %collective-permute-start.49 = (f32[1,4,64]{2,1,0:T(4,128)S(1)}, f32[1,4,64]{2,1,0:T(4,128)S(1)}, u32[]{:S(2)}, u32[]{:S(2)}) collective-permute-start(f32[1,4,64]{2,1,0:T(4,128)S(1)} %get-tuple-element.970), channel_id=1, source_target_pairs={{0,16},{1,17},{2,18},{3,19},{4,20},{5,21},{6,22},{7,23},{8,24},{9,... | collective-permute-start | bytes 3080 | tf_op jit(solution)/shard_map/ppermute | solution.py:17
  248.3 11.7 %collective-permute-start.50 = (f32[10,1,64]{2,1,0:T(1,128)S(1)}, f32[10,1,64]{2,1,0:T(1,128)S(1)}, u32[]{:S(2)}, u32[]{:S(2)}) collective-permute-start(f32[10,1,64]{2,1,0:T(1,128)S(1)} %get-tuple-element.957), channel_id=1, source_target_pairs={{4,0},{8,4},{12,8},{5,1},{9,5},{13,9},{6,2},{10,6},{14,10},{7,3},{... | collective-permute-start | bytes 7688 | tf_op jit(solution)/shard_map/ppermute | solution.py:20
  249.6 10.4 %collective-permute-start.51 = (f32[10,1,64]{2,1,0:T(1,128)S(1)}, f32[10,1,64]{2,1,0:T(1,128)S(1)}, u32[]{:S(2)}, u32[]{:S(2)}) collective-permute-start(f32[10,1,64]{2,1,0:T(1,128)S(1)} %get-tuple-element.956), channel_id=1, source_target_pairs={{0,4},{4,8},{8,12},{1,5},{5,9},{9,13},{2,6},{6,10},{10,14},{3,7},{... | collective-permute-start | bytes 7688 | tf_op jit(solution)/shard_map/ppermute | solution.py:17
  331.8 5.9 %collective-permute-start.56 = (f32[6,1,32]{2,0,1:T(8,128)S(1)}, f32[6,1,32]{2,0,1:T(8,128)S(1)}, u32[]{:S(2)}, u32[]{:S(2)}) collective-permute-start(f32[6,1,32]{2,0,1:T(8,128)S(1)} %get-tuple-element.986), channel_id=1, source_target_pairs={{4,0},{8,4},{12,8},{5,1},{9,5},{13,9},{6,2},{10,6},{14,10},{7,3},{... | collective-permute-start | bytes 2312 | tf_op jit(solution)/shard_map/ppermute | solution.py:20
  409.3 6.1 %collective-permute-start.62 = (f32[10,1,64]{2,1,0:T(1,128)S(1)}, f32[10,1,64]{2,1,0:T(1,128)S(1)}, u32[]{:S(2)}, u32[]{:S(2)}) collective-permute-start(f32[10,1,64]{2,1,0:T(1,128)S(1)} %get-tuple-element.955), channel_id=1, source_target_pairs={{4,0},{8,4},{12,8},{5,1},{9,5},{13,9},{6,2},{10,6},{14,10},{7,3},{... | collective-permute-start | bytes 7688 | tf_op jit(solution)/shard_map/ppermute | solution.py:20
  410.6 6.1 %collective-permute-start.63 = (f32[10,1,64]{2,1,0:T(1,128)S(1)}, f32[10,1,64]{2,1,0:T(1,128)S(1)}, u32[]{:S(2)}, u32[]{:S(2)}) collective-permute-start(f32[10,1,64]{2,1,0:T(1,128)S(1)} %get-tuple-element.954), channel_id=1, source_target_pairs={{0,4},{4,8},{8,12},{1,5},{5,9},{9,13},{2,6},{6,10},{10,14},{3,7},{... | collective-permute-start | bytes 7688 | tf_op jit(solution)/shard_map/ppermute | solution.py:17
  430.6 6.1 %collective-permute-start.68 = (f32[10,1,64]{2,1,0:T(1,128)S(1)}, f32[10,1,64]{2,1,0:T(1,128)S(1)}, u32[]{:S(2)}, u32[]{:S(2)}) collective-permute-start(f32[10,1,64]{2,1,0:T(1,128)S(1)} %get-tuple-element.953), channel_id=1, source_target_pairs={{4,0},{8,4},{12,8},{5,1},{9,5},{13,9},{6,2},{10,6},{14,10},{7,3},{... | collective-permute-start | bytes 7688 | tf_op jit(solution)/shard_map/ppermute | solution.py:20
  431.9 6.1 %collective-permute-start.69 = (f32[10,1,64]{2,1,0:T(1,128)S(1)}, f32[10,1,64]{2,1,0:T(1,128)S(1)}, u32[]{:S(2)}, u32[]{:S(2)}) collective-permute-start(f32[10,1,64]{2,1,0:T(1,128)S(1)} %get-tuple-element.952), channel_id=1, source_target_pairs={{0,4},{4,8},{8,12},{1,5},{5,9},{9,13},{2,6},{6,10},{10,14},{3,7},{... | collective-permute-start | bytes 7688 | tf_op jit(solution)/shard_map/ppermute | solution.py:17
  452.7 6.1 %collective-permute-start.74 = (f32[10,1,64]{2,1,0:T(1,128)S(1)}, f32[10,1,64]{2,1,0:T(1,128)S(1)}, u32[]{:S(2)}, u32[]{:S(2)}) collective-permute-start(f32[10,1,64]{2,1,0:T(1,128)S(1)} %get-tuple-element.951), channel_id=1, source_target_pairs={{4,0},{8,4},{12,8},{5,1},{9,5},{13,9},{6,2},{10,6},{14,10},{7,3},{... | collective-permute-start | bytes 7688 | tf_op jit(solution)/shard_map/ppermute | solution.py:20
  454.0 6.1 %collective-permute-start.75 = (f32[10,1,64]{2,1,0:T(1,128)S(1)}, f32[10,1,64]{2,1,0:T(1,128)S(1)}, u32[]{:S(2)}, u32[]{:S(2)}) collective-permute-start(f32[10,1,64]{2,1,0:T(1,128)S(1)} %get-tuple-element.950), channel_id=1, source_target_pairs={{0,4},{4,8},{8,12},{1,5},{5,9},{9,13},{2,6},{6,10},{10,14},{3,7},{... | collective-permute-start | bytes 7688 | tf_op jit(solution)/shard_map/ppermute | solution.py:17
  530.0 7.2 %collective-permute-start.94 = (f32[18,10,1]{2,0,1:T(8,128)S(1)}, f32[18,10,1]{2,0,1:T(8,128)S(1)}, u32[]{:S(2)}, u32[]{:S(2)}) collective-permute-start(f32[18,10,1]{2,0,1:T(8,128)S(1)} %get-tuple-element.882), channel_id=1, source_target_pairs={{1,0},{2,1},{3,2},{5,4},{6,5},{7,6},{9,8},{10,9},{11,10},{13,12},{... | collective-permute-start | bytes 2168 | tf_op jit(solution)/shard_map/ppermute | solution.py:20
  531.3 6.8 %collective-permute-start.95 = (f32[18,10,1]{2,0,1:T(8,128)S(1)}, f32[18,10,1]{2,0,1:T(8,128)S(1)}, u32[]{:S(2)}, u32[]{:S(2)}) collective-permute-start(f32[18,10,1]{2,0,1:T(8,128)S(1)} %get-tuple-element.883), channel_id=1, source_target_pairs={{0,1},{1,2},{2,3},{4,5},{5,6},{6,7},{8,9},{9,10},{10,11},{12,13},{... | collective-permute-start | bytes 2168 | tf_op jit(solution)/shard_map/ppermute | solution.py:17
  (51 other events, 285.0 us)
where the time goes:
time: 548 us; the launch traced here: 539 us
  starting transfers between devices  247 us (45%)
  local copies, waits for them, and re-layouts  150 us (27%)
  waiting for transfers between devices  70.1 us (13%)
  blocking collectives  37.2 us (7%)
  other arithmetic  30.8 us (6%)
    ppermute x48, starting transfers between devices, with_halo(): lax.ppermute(lax.slice_in_dim(block, block.shape[dim] - width, None, axis...  185 us
    broadcast_in_dim x764, local copies, waits for them, and re-layouts, tridiag(): lax.linalg.tridiagonal_solve(coeffs[0], coeffs[1], coeffs[2], rhs[..., No...  74.9 us
    ppermute x48, starting transfers between devices, with_halo(): lax.ppermute(lax.slice_in_dim(block, 0, width, axis=dim), axis, backward)  62 us
    reshape x5, local copies, waits for them, and re-layouts, coarsen(): return x.reshape(a // 2, 2, b // 2, 2, c // 2, 2).sum(axis=(1, 3, 5))  51.8 us
    ppermute x48, waiting for transfers between devices, with_halo(): lax.ppermute(lax.slice_in_dim(block, 0, width, axis=dim), axis, backward)  48.9 us
    ppermute x48, waiting for transfers between devices, with_halo(): lax.ppermute(lax.slice_in_dim(block, block.shape[dim] - width, None, axis...  21.2 us
    reduce_sum x7, other arithmetic, coarsen(): return x.reshape(a // 2, 2, b // 2, 2, c // 2, 2).sum(axis=(1, 3, 5))  20.3 us
    all_gather x2, blocking collectives, column_solve(): whole = lax.all_gather(rhs, 'gz', axis=2, tiled=True)  13.6 us
  transfers between devices with their start and end apart: 96, of which 34 were waited for; matrix products, arithmetic and copies ran while one was open for 14% of the time, Pallas kernels for 0%

commit v1 on v0

--- a/solution.py
+++ b/solution.py
@@ -1,6 +1,10 @@
+import functools
+
 import jax
 import jax.numpy as jnp
 from jax import lax
+from jax.experimental import pallas as pl
+from jax.experimental.pallas import tpu as pltpu
 from jax.sharding import PartitionSpec as P
 
 NU = 3
@@ -133,8 +137,455 @@
     return diag1 * corr1
 
 
+PLANE = (32, 32)
+SPLIT = (2, 4)
+ROWS = 8
+LANES = 128
+HALO = 18
+SLAB = 56
+NEAR = 8
+F32 = jnp.float32
+
+
+def iota(shape, dim):
+    return lax.broadcasted_iota(jnp.int32, shape, dim)
+
+
+def dot01(field, chosen, dims=(((1,), (0,)), ((), ()))):
+    total = None
+    rest = field
+    for part in range(3):
+        piece = rest.astype(jnp.bfloat16)
+        term = lax.dot_general(piece, chosen, dims, preferred_element_type=F32)
+        total = term if total is None else total + term
+        if part < 2:
+            rest = rest - piece.astype(F32)
+    return total
+
+
+def where01(condition):
+    return jnp.where(condition, 1.0, 0.0).astype(jnp.bfloat16)
+
+
+def loop(low, high, size, body):
+    size = min(size, high - low)
+    steps = -(-(high - low) // size)
+
+    def step(index, carry):
+        body(jnp.minimum(low + index * size, high - size), size)
+        return carry
+
+    lax.fori_loop(0, steps, step, 0)
+
+
+class Level:
+    def __init__(self, level):
+        self.ny = PLANE[1] >> level
+        self.xs = 4 >> level
+        self.factor = float(2**level)
+
+    def masks(self, shape):
+        lane = iota(shape, 2)
+        row = iota(shape, 1)
+        within = (lane // self.ny) % self.xs
+        y = lane % self.ny
+        last_x = (row == ROWS - 1) & (within == self.xs - 1)
+        return within, y == self.ny - 1, last_x
+
+    def next_x(self, field):
+        within = (iota(field.shape, 2) // self.ny) % self.xs
+        moved = pltpu.roll(field, LANES - self.ny, 2)
+        return jnp.where(within == self.xs - 1, pltpu.roll(moved, ROWS - 1, 1), moved)
+
+    def last_x(self, field):
+        within = (iota(field.shape, 2) // self.ny) % self.xs
+        moved = pltpu.roll(field, self.ny, 2)
+        return jnp.where(within == 0, pltpu.roll(moved, 1, 1), moved)
+
+    def next_y(self, field):
+        return pltpu.roll(field, LANES - 1, 2)
+
+    def last_y(self, field):
+        return pltpu.roll(field, 1, 2)
+
+    def balance(self, field, wx, wy, wz):
+        mid = field[1:-1]
+        flow_x = wx * (self.next_x(mid) - mid)
+        flow_y = wy * (self.next_y(mid) - mid)
+        flow_z = wz * (field[1:] - field[:-1])
+        return (
+            (flow_x - self.last_x(flow_x))
+            + (flow_y - self.last_y(flow_y))
+            + (flow_z[1:] - flow_z[:-1])
+        )
+
+
+def mean_of(fluid, near, factor):
+    total = fluid + near
+    safe = jnp.where(total > 0, total, 1.0)
+    return jnp.where(total > 0, (factor * 2.0) * fluid * near / safe, 0.0)
+
+
+def set_level(level, low, high, size, fluid, pin, rhs, wx, wy, wz, gain, corr):
+    def body(plane, count):
+        wide = fluid[pl.ds(plane - 1, count + 2)]
+        mid = wide[1:-1]
+        within, end_y, end_x = level.masks(mid.shape)
+        to_x = jnp.where(end_x, 0.0, mean_of(mid, level.next_x(mid), level.factor))
+        to_y = jnp.where(end_y, 0.0, mean_of(mid, level.next_y(mid), level.factor))
+        to_z = mean_of(wide[:-1], wide[1:], level.factor)
+        diag = (
+            (to_x + level.last_x(to_x))
+            + (to_y + level.last_y(to_y))
+            + (to_z[1:] + to_z[:-1])
+            + pin[pl.ds(plane, count)]
+        )
+        some = diag > 0
+        scale = jnp.where(some, OMEGA / jnp.where(some, diag, 1.0), 0.0)
+        wx[pl.ds(plane, count)] = to_x
+        wy[pl.ds(plane, count)] = to_y
+        wz[pl.ds(plane, count)] = to_z[1:]
+        gain[pl.ds(plane, count)] = scale
+        if corr is not None:
+            corr[pl.ds(plane, count)] = scale * rhs[pl.ds(plane, count)]
+
+    loop(low, high, size, body)
+
+
+def residual_of(level, plane, count, fields, corr):
+    rhs, pin, wx, wy, wz = fields
+    field = corr[pl.ds(plane - 1, count + 2)]
+    spread = level.balance(
+        field, wx[pl.ds(plane, count)], wy[pl.ds(plane, count)], wz[pl.ds(plane - 1, count + 1)]
+    )
+    mid = field[1:-1]
+    return mid, (rhs[pl.ds(plane, count)] - pin[pl.ds(plane, count)] * mid) + spread
+
+
+def sweep(level, low, high, size, fields, gain, source, target):
+    def body(plane, count):
+        mid, rest = residual_of(level, plane, count, fields, source)
+        target[pl.ds(plane, count)] = mid + gain[pl.ds(plane, count)] * rest
+
+    loop(low, high, size, body)
+
+
+def pair_sum(field):
+    half = field.reshape((field.shape[0] // 2, 2) + field.shape[1:])
+    return half[:, 0] + half[:, 1]
+
+
+def coarse_residual(level, low, high, size, fields, corr, target):
+    assert (high - low) % size == 0 and size % 2 == 0
+
+    def body(plane, count):
+        _, rest = residual_of(level, plane, count, fields, corr)
+        target[pl.ds((plane - low) // 2, count // 2)] = pair_sum(rest)
+
+    loop(low, high, size, body)
+
+
+def lanes_down(level):
+    fine = iota((LANES, LANES), 0)
+    coarse = iota((LANES, LANES), 1)
+    ny, xs = PLANE[1] >> level, 4 >> level
+    half = xs // 2
+    same_x = ((fine // ny) % xs) // 2 == (coarse // (ny // 2)) % half
+    same_y = (fine % ny) // 2 == coarse % (ny // 2)
+    return where01((fine < ny * xs) & same_x & same_y)
+
+
+def in_lanes(field, chosen):
+    flat = field.reshape(field.shape[0] * ROWS, LANES)
+    return dot01(flat, chosen).reshape(field.shape)
+
+
+def prepare_kernel(res_ref, visc_ref, pin_ref, own_ref, top_ref, bottom_ref):
+    bx, by, depth = visc_ref.shape
+    cells = bx * by
+    groups = bx // 4
+    pick = where01(iota((depth, 2 * depth), 1) // 2 == iota((depth, 2 * depth), 0))
+    deep = lax.dot_general(
+        pick, res_ref[...], (((1,), (1,)), ((), ())), preferred_element_type=F32
+    )
+
+    def lane_of(x, y):
+        return (x % 4) * (groups * by) + (x // 4) * by + y
+
+    fine = iota((4 * cells, cells), 0)
+    lane = iota((4 * cells, cells), 1)
+    chosen = where01(lane_of(fine // (4 * by), (fine % (2 * by)) // 2) == lane)
+    rhs = dot01(deep, chosen)
+    fluid = 1.0 / visc_ref[...].reshape(cells, depth)
+    pin = 4.0 * pin_ref[...].reshape(cells, depth).astype(F32) * fluid
+    cell = iota((cells, cells), 0)
+    lane = iota((cells, cells), 1)
+    chosen = where01(lane_of(cell // by, cell % by) == lane)
+    fluid = dot01(fluid.T, chosen)
+    pin = dot01(pin.T, chosen)
+    for index, field in enumerate((fluid, rhs, pin)):
+        own_ref[index * depth : (index + 1) * depth] = field
+        top_ref[index * HALO : (index + 1) * HALO] = field[depth - HALO :]
+        bottom_ref[index * HALO : (index + 1) * HALO] = field[:HALO]
+    empty = jnp.zeros((SLAB - 3 * HALO, LANES), F32)
+    top_ref[3 * HALO :] = empty
+    bottom_ref[3 * HALO :] = empty
+
+
+def place(gathered, row, target, plane, groups, by):
+    group = (iota((ROWS, LANES), 1) // by) % groups
+    nx, ny = SPLIT
+    for ix in range(nx):
+        found = [gathered[ix * ny + iy, pl.ds(row, ROWS), :] for iy in range(ny)]
+        for part in range(groups):
+            total = found[part]
+            for iy in range(ny):
+                if iy != part:
+                    moved = pltpu.roll(found[iy], (by * (iy - part)) % LANES, 1)
+                    total = jnp.where(group == iy, moved, total)
+            target[pl.ds(plane, ROWS), ix * groups + part, :] = total
+
+
+def down_kernel(
+    groups, by, depth, sizes,
+    gathered,
+    rhs1, pin1, wx1, wy1, wz1, gain1, corr1,
+    rhs2, pin2, wx2, wy2, wz2, gain2, corr2,
+    packed,
+    fluid1, other1, fluid2, other2, sums,
+):
+    for index, target in enumerate((fluid1, rhs1, pin1)):
+        def body(step, carry, index=index, target=target):
+            row = pl.multiple_of(index * depth + step * ROWS, ROWS)
+            place(gathered, row, target, HALO + step * ROWS, groups, by)
+            return carry
+
+        lax.fori_loop(0, depth // ROWS, body, 0)
+        for side, plane in enumerate((0, HALO + depth)):
+            for start in (0, ROWS, HALO - ROWS):
+                row = 3 * depth + side * SLAB + index * HALO + start
+                place(gathered, row, target, plane + start, groups, by)
+
+    fine, coarse = Level(0), Level(1)
+    down1, down2 = lanes_down(0), lanes_down(1)
+    planes = depth + 2 * HALO
+    fields1 = (rhs1, pin1, wx1, wy1, wz1)
+    fields2 = (rhs2, pin2, wx2, wy2, wz2)
+    set_level(fine, 1, planes - 1, sizes[0], fluid1, pin1, rhs1, wx1, wy1, wz1, gain1, other1)
+    sweep(fine, 2, planes - 2, sizes[1], fields1, gain1, other1, corr1)
+    sweep(fine, 3, planes - 3, sizes[1], fields1, gain1, corr1, other1)
+    corr1[...] = other1[...]
+    count2 = depth // 2 + 2 * NEAR
+    begin = HALO - 2 * NEAR
+    for source, target, share in ((fluid1, fluid2, 8.0), (pin1, pin2, 4.0)):
+        whole = pair_sum(source[begin : begin + 2 * count2])
+        target[...] = in_lanes(whole, down1) * (1.0 / share)
+    inner = count2 - 2
+    coarse_residual(fine, begin + 2, begin + 2 + 2 * inner, sizes[2], fields1, corr1, sums)
+    rhs2[1 : 1 + inner] = in_lanes(sums[0:inner], down1)
+    set_level(coarse, 1, 1 + inner, sizes[3], fluid2, pin2, rhs2, wx2, wy2, wz2, gain2, other2)
+    sweep(coarse, 2, inner, sizes[4], fields2, gain2, other2, corr2)
+    sweep(coarse, 3, inner - 1, sizes[4], fields2, gain2, corr2, other2)
+    corr2[...] = other2[...]
+    coarse_residual(coarse, NEAR, NEAR + depth // 2, sizes[5], fields2, corr2, sums)
+    count3 = depth // 4
+    rhs3 = in_lanes(sums[0:count3], down2)
+    fluid3 = in_lanes(pair_sum(fluid2[NEAR : NEAR + 2 * count3]), down2) * 0.125
+    pin3 = in_lanes(pair_sum(pin2[NEAR : NEAR + 2 * count3]), down2) * 0.25
+    lane = iota((count3, LANES), 1) // ROWS
+    first = jnp.zeros((count3, LANES), F32)
+    second = jnp.zeros((count3, LANES), F32)
+    for row in range(ROWS):
+        first = jnp.where(lane == row, rhs3[:, row, :], first)
+        first = jnp.where(lane == ROWS + row, fluid3[:, row, :], first)
+        second = jnp.where(lane == row, pin3[:, row, :], second)
+    packed[0:count3] = first
+    packed[count3 : 2 * count3] = second
+
+
+def columns(rhs, fluid, pin):
+    shape = fluid.shape
+    depth = shape[2]
+    lane, y = iota(shape, 2), iota(shape, 1)
+    edge = jnp.zeros((1,) + shape[1:], F32)
+    wz = jnp.where(lane == depth - 1, 0.0, mean_of(fluid, pltpu.roll(fluid, depth - 1, 2), 4.0))
+    wy = jnp.where(y == ROWS - 1, 0.0, mean_of(fluid, pltpu.roll(fluid, ROWS - 1, 1), 4.0))
+    wx = jnp.concatenate([mean_of(fluid[:-1], fluid[1:], 4.0), edge], axis=0)
+    back_x = jnp.concatenate([edge, wx[:-1]], axis=0)
+    across = (wx + back_x) + (wy + pltpu.roll(wy, 1, 1)) + pin
+    share = 1.0 / jnp.sum(across, axis=2, keepdims=True)
+
+    above, below, own = pltpu.roll(wz, 1, 2), wz, across
+    steps = []
+    stride = 1
+    while stride < depth:
+        inverse = 1.0 / (above + below + own)
+        up = above * pltpu.roll(inverse, stride, 2)
+        down = below * pltpu.roll(inverse, depth - stride, 2)
+        own = own + up * pltpu.roll(own, stride, 2) + down * pltpu.roll(own, depth - stride, 2)
+        above = up * pltpu.roll(above, stride, 2)
+        below = down * pltpu.roll(below, depth - stride, 2)
+        steps.append((stride, up, down))
+        stride *= 2
+    inverse = 1.0 / (above + below + own)
+
+    def solve(right):
+        mean = jnp.sum(right, axis=2, keepdims=True) * share
+        for stride, up, down in steps:
+            right = (
+                right
+                + up * pltpu.roll(right, stride, 2)
+                + down * pltpu.roll(right, depth - stride, 2)
+            )
+        return right * inverse + mean
+
+    corr = solve(rhs)
+    flow_x = wx[:-1] * (corr[1:] - corr[:-1])
+    flow_x = jnp.concatenate([flow_x, edge], 0) - jnp.concatenate([edge, flow_x], 0)
+    flow_y = wy * (pltpu.roll(corr, ROWS - 1, 1) - corr)
+    flow_z = wz * (pltpu.roll(corr, depth - 1, 2) - corr)
+    rest = (
+        (rhs - pin * corr)
+        + flow_x
+        + (flow_y - pltpu.roll(flow_y, 1, 1))
+        + (flow_z - pltpu.roll(flow_z, 1, 2))
+    )
+    return corr + solve(rest)
+
+
+def up_kernel(
+    groups, by, depth, sizes,
+    packed,
+    rhs1, pin1, wx1, wy1, wz1, gain1, corr1,
+    rhs2, pin2, wx2, wy2, wz2, gain2, corr2,
+    out_ref,
+    one1, two1, one2, two2, lifted,
+):
+    count3 = depth // 4
+    shares = packed.shape[0]
+    first = jnp.concatenate([packed[i, 0:count3] for i in range(shares)], axis=0).T
+    second = jnp.concatenate([packed[i, count3 : 2 * count3] for i in range(shares)], axis=0).T
+    cells = ROWS * ROWS
+    total3 = shares * count3
+    shape3 = (ROWS, ROWS, total3)
+    corr3 = columns(
+        first[:cells].reshape(shape3), first[cells:].reshape(shape3), second[:cells].reshape(shape3)
+    ).reshape(cells, total3)
+
+    part = lax.axis_index("gz")
+    mine = pltpu.roll(corr3, lax.rem(NEAR - part * count3 + total3, total3), 1)
+    tall = jnp.concatenate([mine, mine], axis=0).T
+    count = count3 + 2 * NEAR
+    fine, coarse = Level(0), Level(1)
+    cell = iota((LANES, ROWS * LANES), 0)
+    lane = iota((LANES, ROWS * LANES), 1)
+    same_y = cell % ROWS == (lane % coarse.ny) // 2
+    spread = where01((cell // ROWS == lane // LANES) & same_y)
+    wide = dot01(tall[0:count], spread)
+    for row in range(ROWS):
+        lifted[0:count, row, :] = wide[:, row * LANES : (row + 1) * LANES]
+
+    fields1 = (rhs1, pin1, wx1, wy1, wz1)
+    fields2 = (rhs2, pin2, wx2, wy2, wz2)
+    low, high = NEAR - 6, NEAR + depth // 2 + 6
+    parents = lifted[low // 2 + NEAR // 2 : high // 2 + NEAR // 2]
+    twice = jnp.broadcast_to(parents[:, None], (parents.shape[0], 2, ROWS, LANES))
+    one2[low:high] = corr2[low:high] + twice.reshape(high - low, ROWS, LANES)
+    reach = depth // 2 + NEAR
+    sweep(coarse, NEAR - 4, reach + 4, sizes[4], fields2, gain2, one2, two2)
+    sweep(coarse, NEAR - 3, reach + 3, sizes[4], fields2, gain2, two2, one2)
+    sweep(coarse, NEAR - 2, reach + 2, sizes[4], fields2, gain2, one2, two2)
+
+    fine_lane, coarse_lane = iota((LANES, LANES), 1), iota((LANES, LANES), 0)
+    x_of = (fine_lane // fine.ny) // 2
+    y_of = (fine_lane % fine.ny) // 2
+    up = where01(coarse_lane == x_of * coarse.ny + y_of)
+    lifted[0 : depth // 2 + 4] = in_lanes(two2[NEAR - 2 : reach + 2], up)
+    parents = lifted[0 : depth // 2 + 4]
+    twice = jnp.broadcast_to(parents[:, None], (parents.shape[0], 2, ROWS, LANES))
+    low, high = HALO - 4, HALO + depth + 4
+    one1[low:high] = corr1[low:high] + twice.reshape(high - low, ROWS, LANES)
+    reach = depth + HALO
+    sweep(fine, HALO - 2, reach + 2, sizes[1], fields1, gain1, one1, two1)
+    sweep(fine, HALO - 1, reach + 1, sizes[1], fields1, gain1, two1, one1)
+    sweep(fine, HALO, reach, sizes[1], fields1, gain1, one1, two1)
+
+    ix, iy = lax.axis_index("gx"), lax.axis_index("gy")
+    cells = 4 * groups * by
+    cell = iota((cells, LANES), 0)
+    lane = iota((cells, LANES), 1)
+    total = None
+    for part in range(groups):
+        scaled = two1[pl.ds(HALO, depth), ix * groups + part, :] * (
+            OMEGA / gain1[pl.ds(HALO, depth), ix * groups + part, :]
+        )
+        x, y = cell // by, cell % by
+        chosen = where01((x // 4 == part) & (lane == (x % 4) * fine.ny + iy * by + y))
+        term = dot01(scaled, chosen, (((1,), (1,)), ((), ())))
+        total = term if total is None else total + term
+    out_ref[...] = total.T.reshape(out_ref.shape)
+
+
+def whole_planes(residual_q2, viscosity, pinned):
+    bx, by, depth = viscosity.shape
+    groups = bx // 4
+    sizes = (9, 16, 12, 13, 16, 16)
+    planes = depth + 2 * HALO
+    count2 = depth // 2 + 2 * NEAR
+    limit = pltpu.CompilerParams(vmem_limit_bytes=32 * 2**20)
+
+    def flat(rows):
+        return jax.ShapeDtypeStruct((rows, LANES), F32)
+
+    def field(count):
+        return jax.ShapeDtypeStruct((count, ROWS, LANES), F32)
+
+    def room(count):
+        return pltpu.VMEM((count, ROWS, LANES), F32)
+
+    own, top, bottom = pl.pallas_call(
+        prepare_kernel,
+        out_shape=(flat(3 * depth), flat(SLAB), flat(SLAB)),
+        compiler_params=limit,
+        name="prepare",
+    )(residual_q2.reshape(4 * bx * by, 2 * depth), viscosity, pinned)
+    length = lax.axis_size("gz")
+    forward = [(i, i + 1) for i in range(length - 1)]
+    low = lax.ppermute(top, "gz", forward)
+    high = lax.ppermute(bottom, "gz", [(target, source) for source, target in forward])
+    whole = lax.all_gather(jnp.concatenate([own, low, high], axis=0), ("gx", "gy"))
+    saved = (field(planes),) * 7 + (field(count2),) * 7
+    results = pl.pallas_call(
+        functools.partial(down_kernel, groups, by, depth, sizes),
+        out_shape=saved + (flat(depth // 2),),
+        scratch_shapes=[room(planes), room(planes), room(count2), room(count2), room(count2)],
+        compiler_params=limit,
+        name="down",
+    )(whole)
+    packed = lax.all_gather(results[-1], "gz")
+    return pl.pallas_call(
+        functools.partial(up_kernel, groups, by, depth, sizes),
+        out_shape=jax.ShapeDtypeStruct((bx, by, depth), F32),
+        scratch_shapes=[room(planes), room(planes), room(count2), room(count2), room(count2)],
+        compiler_params=limit,
+        name="up",
+    )(packed, *results[:-1])
+
+
+def one_tile_planes(mesh, viscosity):
+    split = (mesh.shape["gx"], mesh.shape["gy"])
+    depth = viscosity.shape[2]
+    fits = viscosity.shape[:2] == PLANE and split == SPLIT
+    return fits and depth == 4 * LANES and depth // mesh.shape["gz"] == LANES
+
+
 def solution(mesh):
     placed = (P("gx", "gy", "gz"), P("gx", "gy", "gz"), P("gx", "gy", "gz"))
-    return jax.shard_map(
-        per_device, mesh=mesh, in_specs=placed, out_specs=P("gx", "gy", "gz"), check_vma=False
-    )
+
+    def cycle(residual_q2, viscosity, pinned):
+        chosen = whole_planes if one_tile_planes(mesh, viscosity) else per_device
+        return jax.shard_map(
+            chosen, mesh=mesh, in_specs=placed, out_specs=P("gx", "gy", "gz"), check_vma=False
+        )(residual_q2, viscosity, pinned)
+
+    return cycle

time: 548 us -> 118 us (0.22); the launches traced: 539 us -> 118 us
  starting transfers between devices: 247 us -> 3.65 us
  local copies, waits for them, and re-layouts: 150 us -> 4.19 us
  Pallas kernels: 0 us -> 34.9 us
  blocking collectives: 37.2 us -> 5.43 us
  other arithmetic: 30.8 us -> 0.72 us
  waiting for transfers between devices: 70.1 us -> 55.3 us
  between operations: 2.38 us -> 13.4 us
    ppermute x96 -> x2, starting transfers between devices: 247 us -> 3.65 us  [the longest x1 2.36 us: whole_planes(): low = lax.ppermute(top, 'gz', forward)]
    broadcast_in_dim x770 -> x0, local copies, waits for them, and re-layouts: 75.1 us -> none  [the longest x764 74.9 us: tridiag(): lax.linalg.tridiagonal_solve(coeffs[0], coeffs[1], coeffs[2], rhs[..., No...]
    ppermute x96 -> x2, waiting for transfers between devices: 70.1 us -> 3.89 us  [the longest x1 3.89 us: whole_planes(): lax.ppermute(bottom, 'gz', [(target, source) for source, target in forward])]
    reshape x19 -> x0, local copies, waits for them, and re-layouts: 52.8 us -> none  [the longest x5 51.8 us: coarsen(): return x.reshape(a // 2, 2, b // 2, 2, c // 2, 2).sum(axis=(1, 3, 5))]
    all_gather x0 -> x1, waiting for transfers between devices: none -> 51.4 us  [whole_planes(): lax.all_gather(jnp.concatenate([own, low, high], axis=0), ('gx', 'gy'))]
    pallas_call x0 -> x3, Pallas kernels: none -> 34.9 us  [the longest x1 21.4 us: whole_planes(): pl.pallas_call(functools.partial(down_kernel, groups, by, depth, sizes),...]
    all_gather x6 -> x1, blocking collectives: 37.2 us -> 5.43 us  [whole_planes(): packed = lax.all_gather(results[-1], 'gz')]
    reduce_sum x10 -> x0, other arithmetic: 20.7 us -> none  [the longest x7 20.3 us: coarsen(): return x.reshape(a // 2, 2, b // 2, 2, c // 2, 2).sum(axis=(1, 3, 5))]
  transfers between devices with their start and end apart: 96 -> 3, of which waited for: 34 -> 2; matrix products, arithmetic and copies ran while one was open for 14% -> 0% of each run, Pallas kernels for 0% -> 0%
where the time goes in v1:
time: 118 us
  waiting for transfers between devices  55.3 us (47%)
  Pallas kernels  34.9 us (30%)
  between operations  13.4 us (11%)
  blocking collectives  5.43 us (5%)
  local copies, waits for them, and re-layouts  4.19 us (4%)
  starting transfers between devices  3.65 us (3%)
    all_gather x1, waiting for transfers between devices, whole_planes(): lax.all_gather(jnp.concatenate([own, low, high], axis=0), ('gx', 'gy'))  51.4 us
    pallas_call x1, Pallas kernels, whole_planes(): pl.pallas_call(functools.partial(down_kernel, groups, by, depth, sizes),...  21.4 us
    pallas_call x1, Pallas kernels, whole_planes(): pl.pallas_call(functools.partial(up_kernel, groups, by, depth, sizes), ou...  13 us
    all_gather x1, blocking collectives, whole_planes(): packed = lax.all_gather(results[-1], 'gz')  5.43 us
    unnamed x8, local copies, waits for them, and re-layouts  4.19 us
    ppermute x1, waiting for transfers between devices, whole_planes(): lax.ppermute(bottom, 'gz', [(target, source) for source, target in forward])  3.89 us
    ppermute x1, starting transfers between devices, whole_planes(): low = lax.ppermute(top, 'gz', forward)  2.36 us
  transfers between devices with their start and end apart: 3, of which 2 were waited for; matrix products, arithmetic and copies ran while one was open for 0% of the time, Pallas kernels for 0%

profile of v1, /device:TPU:0, one launch (start us, length us, event | category | flops | bytes accessed | tf_op | source)
XLA Modules:
  0.0 117.7 jit_solution(11655392042788855862)
XLA Ops:
  6.5 0.0 all-gather.4.cloned.1.call-start
  6.5 0.0 copy-start.1
  6.5 0.9 copy-done.1
  7.5 0.0 copy-start.2
  7.5 0.8 copy-done.2
  8.3 0.0 copy-start.3
  8.3 0.8 copy-done.3
  9.2 0.5 prepare.1
  9.7 2.4 %collective-permute-start = (f32[56,128]{1,0:T(8,128)S(1)}, f32[56,128]{1,0:T(8,128)S(1)}, u32[]{:S(2)}, u32[]{:S(2)}) collective-permute-start(f32[56,128]{1,0:T(8,128)S(1)} %get-tuple-element.24), channel_id=1, source_target_pairs={{0,1},{1,2},{2,3},{4,5},{5,6},{6,7},{8,9},{9,10},{10,11},{12,13},{... | collective-permute-start | bytes 86024 | tf_op jit(solution)/shard_map/ppermute | solution.py:554
  12.0 1.3 %collective-permute-start.1 = (f32[56,128]{1,0:T(8,128)S(1)}, f32[56,128]{1,0:T(8,128)S(1)}, u32[]{:S(2)}, u32[]{:S(2)}) collective-permute-start(f32[56,128]{1,0:T(8,128)S(1)} %get-tuple-element.25), channel_id=1, source_target_pairs={{1,0},{2,1},{3,2},{5,4},{6,5},{7,6},{9,8},{10,9},{11,10},{13,12},{... | collective-permute-start | bytes 86024 | tf_op jit(solution)/shard_map/ppermute | solution.py:555
  13.3 0.0 collective-permute-done
  13.3 3.9 %collective-permute-done.1 = f32[56,128]{1,0:T(8,128)S(1)} collective-permute-done((f32[56,128]{1,0:T(8,128)S(1)}, f32[56,128]{1,0:T(8,128)S(1)}, u32[]{:S(2)}, u32[]{:S(2)}) %collective-permute-start.1) | collective-permute-done | bytes 28704 | tf_op jit(solution)/shard_map/ppermute | solution.py:555
  17.2 0.7 pad_maximum_fusion
  18.0 0.0 all-gather.4.cloned.1.call-update
  18.0 51.4 %all-gather.4.cloned.1.call-done = f32[3968,128]{1,0:T(8,128)} async-done(((f32[496,128]{1,0:T(8,128)}), f32[3968,128]{1,0:T(8,128)}) %all-gather.4.cloned.1.call-update) | async-done | bytes 2031632 | tf_op jit(solution)/shard_map/all_gather | solution.py:556
  69.4 0.0 copy-start
  69.4 1.6 %copy-done = f32[3968,128]{1,0:T(8,128)S(1)} copy-done((f32[3968,128]{1,0:T(8,128)S(1)}, f32[3968,128]{1,0:T(8,128)}, u32[]{:S(2)}) %copy-start) | copy-done | bytes 2031640
  71.0 21.4 %down.1 = (f32[164,8,128]{2,1,0:T(8,128)S(1)}, f32[164,8,128]{2,1,0:T(8,128)S(1)}, f32[164,8,128]{2,1,0:T(8,128)S(1)}, f32[164,8,128]{2,1,0:T(8,128)S(1)}, f32[1...) custom-call(f32[8,496,128]{2,1,0:T(8,128)S(1)} %bitcast.3), custom_call_target="tpu_custom_call" | custom-call | tf_op jit(solution)/shard_map/down/pallas_call | solution.py:558
  92.4 5.4 %all-gather.1 = f32[256,128]{1,0:T(8,128)S(1)} all-gather(f32[64,128]{1,0:T(8,128)S(1)} %get-tuple-element.26), channel_id=3, replica_groups=mesh['gx'=2,'gy'=4,'gz'=4] {'gz'}, dimensions={0}, use_global_device_ids=true | all-gather | bytes 163840 | tf_op jit(solution)/shard_map/all_gather | solution.py:565
  97.8 13.0 %up.1 = f32[16,8,128]{2,1,0:T(8,128)} custom-call(f32[4,64,128]{2,1,0:T(8,128)S(1)} %bitcast.4, f32[164,8,128]{2,1,0:T(8,128)S(1)} %get-tuple-element.27.rhs1, f32[164,8,128]{2,1,0:T(8,128)S(1)} %get-tuple-element.28.pin1, f32[164,8,128]{2,1,0:T(8,128)S(1)} %get-tuple-element.29.wx1, f32[164,8,128]{2,1,0:T(8,128)S(1)} %get-tuple-element.30.wy1, ...), custom_call_target="tpu_custom_call" | custom-call | tf_op jit(solution)/shard_map/up/pallas_call | solution.py:566
Async XLA Ops:
  6.5 62.9 %all-gather.4.cloned.1.call-start = ((), (), s32[]{:S(2)}) async-start(), calls=%async_computation | async-start | bytes 2285568 | tf_op jit(solution)/shard_map/all_gather | solution.py:556
  6.5 0.9 copy-start.1
  7.5 0.8 copy-start.2
  8.3 0.8 copy-start.3
  9.7 3.7 %collective-permute-start = (f32[56,128]{1,0:T(8,128)S(1)}, f32[56,128]{1,0:T(8,128)S(1)}, u32[]{:S(2)}, u32[]{:S(2)}) collective-permute-start(f32[56,128]{1,0:T(8,128)S(1)} %get-tuple-element.24), channel_id=1, source_target_pairs={{0,1},{1,2},{2,3},{4,5},{5,6},{6,7},{8,9},{9,10},{10,11},{12,13},{... | collective-permute-start | bytes 86024 | tf_op jit(solution)/shard_map/ppermute | solution.py:554
  12.0 5.2 %collective-permute-start.1 = (f32[56,128]{1,0:T(8,128)S(1)}, f32[56,128]{1,0:T(8,128)S(1)}, u32[]{:S(2)}, u32[]{:S(2)}) collective-permute-start(f32[56,128]{1,0:T(8,128)S(1)} %get-tuple-element.25), channel_id=1, source_target_pairs={{1,0},{2,1},{3,2},{5,4},{6,5},{7,6},{9,8},{10,9},{11,10},{13,12},{... | collective-permute-start | bytes 86024 | tf_op jit(solution)/shard_map/ppermute | solution.py:555
  69.4 1.6 %copy-start = (f32[3968,128]{1,0:T(8,128)S(1)}, f32[3968,128]{1,0:T(8,128)}, u32[]{:S(2)}) copy-start(f32[3968,128]{1,0:T(8,128)} %all-gather.4.cloned.1.call-done) | copy-start | bytes 6094852
Sparse Core Ops, SparseCore 0:
  18.1 51.2 all-gather.3

commit v2 on v1

--- a/solution.py
+++ b/solution.py
@@ -175,7 +175,10 @@
         body(jnp.minimum(low + index * size, high - size), size)
         return carry
 
-    lax.fori_loop(0, steps, step, 0)
+    if steps == 1:
+        body(low, size)
+    else:
+        lax.fori_loop(0, steps, step, 0)
 
 
 class Level:
@@ -276,6 +279,7 @@
 
 
 def coarse_residual(level, low, high, size, fields, corr, target):
+    size = min(size, high - low)
     assert (high - low) % size == 0 and size % 2 == 0
 
     def body(plane, count):
@@ -300,7 +304,19 @@
     return dot01(flat, chosen).reshape(field.shape)
 
 
-def prepare_kernel(res_ref, visc_ref, pin_ref, own_ref, top_ref, bottom_ref):
+def prepare_kernel(
+    res_in, visc_in, pin_in, own_ref, top_ref, bottom_ref, res_ref, visc_ref, pin_ref, arrived
+):
+    copies = [
+        pltpu.make_async_copy(source, target, arrived.at[index])
+        for index, (source, target) in enumerate(
+            ((visc_in, visc_ref), (pin_in, pin_ref), (res_in, res_ref))
+        )
+    ]
+    for copy in copies:
+        copy.start()
+    for copy in copies:
+        copy.wait()
     bx, by, depth = visc_ref.shape
     cells = bx * by
     groups = bx // 4
@@ -332,6 +348,25 @@
     bottom_ref[3 * HALO :] = empty
 
 
+def pack_kernel(depth, span, own, low, high, out_ref):
+    share = span - 2 * HALO
+    for index in range(3):
+        for peer in range(depth // share):
+            begin, end = peer * share - HALO, peer * share + share + HALO
+            row = index * span
+            ahead, behind = max(0, -begin), max(0, end - depth)
+            if ahead:
+                first = (index + 1) * HALO
+                out_ref[peer, row : row + ahead] = low[first - ahead : first]
+            inner = own[index * depth + max(begin, 0) : index * depth + min(end, depth)]
+            out_ref[peer, row + ahead : row + span - behind] = inner
+            if behind:
+                first = index * HALO
+                out_ref[peer, row + span - behind : row + span] = high[first : first + behind]
+    spare = out_ref.shape[1] - 3 * span
+    out_ref[:, 3 * span :] = jnp.zeros((depth // share, spare, LANES), F32)
+
+
 def place(gathered, row, target, plane, groups, by):
     group = (iota((ROWS, LANES), 1) // by) % groups
     nx, ny = SPLIT
@@ -354,21 +389,13 @@
     packed,
     fluid1, other1, fluid2, other2, sums,
 ):
+    planes = depth + 2 * HALO
     for index, target in enumerate((fluid1, rhs1, pin1)):
-        def body(step, carry, index=index, target=target):
-            row = pl.multiple_of(index * depth + step * ROWS, ROWS)
-            place(gathered, row, target, HALO + step * ROWS, groups, by)
-            return carry
-
-        lax.fori_loop(0, depth // ROWS, body, 0)
-        for side, plane in enumerate((0, HALO + depth)):
-            for start in (0, ROWS, HALO - ROWS):
-                row = 3 * depth + side * SLAB + index * HALO + start
-                place(gathered, row, target, plane + start, groups, by)
+        for start in [*range(0, planes - ROWS, ROWS), planes - ROWS]:
+            place(gathered, index * planes + start, target, start, groups, by)
 
     fine, coarse = Level(0), Level(1)
     down1, down2 = lanes_down(0), lanes_down(1)
-    planes = depth + 2 * HALO
     fields1 = (rhs1, pin1, wx1, wy1, wz1)
     fields2 = (rhs2, pin2, wx2, wy2, wz2)
     set_level(fine, 1, planes - 1, sizes[0], fluid1, pin1, rhs1, wx1, wy1, wz1, gain1, other1)
@@ -472,7 +499,9 @@
         first[:cells].reshape(shape3), first[cells:].reshape(shape3), second[:cells].reshape(shape3)
     ).reshape(cells, total3)
 
-    part = lax.axis_index("gz")
+    nx, ny = SPLIT
+    ix, iy = lax.axis_index("gx"), lax.axis_index("gy")
+    part = (lax.axis_index("gz") * nx + ix) * ny + iy
     mine = pltpu.roll(corr3, lax.rem(NEAR - part * count3 + total3, total3), 1)
     tall = jnp.concatenate([mine, mine], axis=0).T
     count = count3 + 2 * NEAR
@@ -510,66 +539,101 @@
     sweep(fine, HALO - 1, reach + 1, sizes[1], fields1, gain1, two1, one1)
     sweep(fine, HALO, reach, sizes[1], fields1, gain1, one1, two1)
 
-    ix, iy = lax.axis_index("gx"), lax.axis_index("gy")
-    cells = 4 * groups * by
-    cell = iota((cells, LANES), 0)
-    lane = iota((cells, LANES), 1)
-    total = None
-    for part in range(groups):
-        scaled = two1[pl.ds(HALO, depth), ix * groups + part, :] * (
-            OMEGA / gain1[pl.ds(HALO, depth), ix * groups + part, :]
-        )
-        x, y = cell // by, cell % by
-        chosen = where01((x // 4 == part) & (lane == (x % 4) * fine.ny + iy * by + y))
-        term = dot01(scaled, chosen, (((1,), (1,)), ((), ())))
-        total = term if total is None else total + term
-    out_ref[...] = total.T.reshape(out_ref.shape)
+    group = (iota((depth, LANES), 1) // by) % groups
+    for ix in range(nx):
+        scaled = [
+            two1[HALO:reach, ix * groups + part, :]
+            * (OMEGA / gain1[HALO:reach, ix * groups + part, :])
+            for part in range(groups)
+        ]
+        for iy in range(ny):
+            total = scaled[iy]
+            for part in range(groups):
+                if part != iy:
+                    moved = pltpu.roll(scaled[part], (by * (part - iy)) % LANES, 1)
+                    total = jnp.where(group == part, moved, total)
+            out_ref[ix * ny + iy] = total
+
+
+def finish_kernel(blocks, out_ref):
+    bx, by, depth = out_ref.shape
+    cells = bx * by
+    cell = iota((cells, cells), 0)
+    lane = iota((cells, cells), 1)
+    x, y = cell // by, cell % by
+    chosen = where01((x % 4) * (bx // 4 * by) + (x // 4) * by + y == lane)
+    turned = dot01(blocks[...].reshape(depth, cells), chosen, (((1,), (1,)), ((), ())))
+    out_ref[...] = turned.T.reshape(out_ref.shape)
 
 
 def whole_planes(residual_q2, viscosity, pinned):
     bx, by, depth = viscosity.shape
     groups = bx // 4
-    sizes = (9, 16, 12, 13, 16, 16)
-    planes = depth + 2 * HALO
-    count2 = depth // 2 + 2 * NEAR
+    peers = SPLIT[0] * SPLIT[1]
+    share = depth // peers
+    planes = share + 2 * HALO
+    count2 = share // 2 + 2 * NEAR
+    sizes = (10, 24, 22, 11, 24, 24)
     limit = pltpu.CompilerParams(vmem_limit_bytes=32 * 2**20)
 
     def flat(rows):
         return jax.ShapeDtypeStruct((rows, LANES), F32)
 
-    def field(count):
-        return jax.ShapeDtypeStruct((count, ROWS, LANES), F32)
+    def blocks(count, rows):
+        return jax.ShapeDtypeStruct((count, rows, LANES), F32)
 
     def room(count):
         return pltpu.VMEM((count, ROWS, LANES), F32)
 
+    residual = residual_q2.reshape(4 * bx * by, 2 * depth)
     own, top, bottom = pl.pallas_call(
         prepare_kernel,
+        in_specs=[pl.BlockSpec(memory_space=pltpu.HBM)] * 3,
         out_shape=(flat(3 * depth), flat(SLAB), flat(SLAB)),
+        scratch_shapes=[
+            pltpu.VMEM(residual.shape, residual.dtype),
+            pltpu.VMEM(viscosity.shape, viscosity.dtype),
+            pltpu.VMEM(pinned.shape, pinned.dtype),
+            pltpu.SemaphoreType.DMA((3,)),
+        ],
         compiler_params=limit,
         name="prepare",
-    )(residual_q2.reshape(4 * bx * by, 2 * depth), viscosity, pinned)
+    )(residual, viscosity, pinned)
     length = lax.axis_size("gz")
     forward = [(i, i + 1) for i in range(length - 1)]
     low = lax.ppermute(top, "gz", forward)
     high = lax.ppermute(bottom, "gz", [(target, source) for source, target in forward])
-    whole = lax.all_gather(jnp.concatenate([own, low, high], axis=0), ("gx", "gy"))
-    saved = (field(planes),) * 7 + (field(count2),) * 7
+    rows = -(-3 * planes // ROWS) * ROWS
+    parcels = pl.pallas_call(
+        functools.partial(pack_kernel, depth, planes),
+        out_shape=blocks(peers, rows),
+        compiler_params=limit,
+        name="pack",
+    )(own, low, high)
+    gathered = lax.all_to_all(parcels, ("gx", "gy"), 0, 0, tiled=True)
+    saved = (blocks(planes, ROWS),) * 7 + (blocks(count2, ROWS),) * 7
     results = pl.pallas_call(
-        functools.partial(down_kernel, groups, by, depth, sizes),
-        out_shape=saved + (flat(depth // 2),),
+        functools.partial(down_kernel, groups, by, share, sizes),
+        out_shape=saved + (flat(share // 2),),
         scratch_shapes=[room(planes), room(planes), room(count2), room(count2), room(count2)],
         compiler_params=limit,
         name="down",
-    )(whole)
-    packed = lax.all_gather(results[-1], "gz")
-    return pl.pallas_call(
-        functools.partial(up_kernel, groups, by, depth, sizes),
-        out_shape=jax.ShapeDtypeStruct((bx, by, depth), F32),
+    )(gathered)
+    copies = jnp.broadcast_to(results[-1], (length * peers, share // 2, LANES))
+    packed = lax.all_to_all(copies, ("gz", "gx", "gy"), 0, 0, tiled=True)
+    mine = pl.pallas_call(
+        functools.partial(up_kernel, groups, by, share, sizes),
+        out_shape=blocks(peers, share),
         scratch_shapes=[room(planes), room(planes), room(count2), room(count2), room(count2)],
         compiler_params=limit,
         name="up",
     )(packed, *results[:-1])
+    return pl.pallas_call(
+        finish_kernel,
+        out_shape=jax.ShapeDtypeStruct((bx, by, depth), F32),
+        compiler_params=limit,
+        name="finish",
+    )(lax.all_to_all(mine, ("gx", "gy"), 0, 0, tiled=True))
 
 
 def one_tile_planes(mesh, viscosity):

time: 118 us -> 64.2 us (0.54)
  waiting for transfers between devices: 55.3 us -> 3.89 us
  blocking collectives: 5.43 us -> 43.9 us
  Pallas kernels: 34.9 us -> 9.74 us
  between operations: 13.4 us -> 0.07 us
  local copies, waits for them, and re-layouts: 4.19 us -> 2.64 us
    all_gather x1 -> x0, waiting for transfers between devices: 51.4 us -> none  [whole_planes(): lax.all_gather(jnp.concatenate([own, low, high], axis=0), ('gx', 'gy'))]
    all_to_all x0 -> x3, blocking collectives: none -> 43.9 us  [the longest x1 23.9 us: whole_planes(): gathered = lax.all_to_all(parcels, ('gx', 'gy'), 0, 0, tiled=True)]
    pallas_call x3 -> x5, Pallas kernels: 34.9 us -> 9.74 us  [the longest x1 4.61 us: whole_planes(): pl.pallas_call(functools.partial(down_kernel, groups, by, share, sizes),...]
    all_gather x1 -> x0, blocking collectives: 5.43 us -> none  [whole_planes(): packed = lax.all_gather(results[-1], 'gz')]
    unnamed x8 -> x6, local copies, waits for them, and re-layouts: 4.19 us -> 2.63 us
  transfers between devices with their start and end apart: 3 -> 2, of which waited for: 2 -> 1; matrix products, arithmetic and copies ran while one was open for 0% -> 0% of each run, Pallas kernels for 0% -> 0%
where the time goes in v2:
time: 64.2 us; the launch traced here: 63.9 us
  blocking collectives  43.9 us (68%)
  Pallas kernels  9.74 us (15%)
  waiting for transfers between devices  3.89 us (6%)
  starting transfers between devices  3.65 us (6%)
  local copies, waits for them, and re-layouts  2.64 us (4%)
    all_to_all x1, blocking collectives, whole_planes(): gathered = lax.all_to_all(parcels, ('gx', 'gy'), 0, 0, tiled=True)  23.9 us
    all_to_all x1, blocking collectives, whole_planes(): lax.all_to_all(mine, ('gx', 'gy'), 0, 0, tiled=True)  10 us
    all_to_all x1, blocking collectives, whole_planes(): packed = lax.all_to_all(copies, ('gz', 'gx', 'gy'), 0, 0, tiled=True)  10 us
    pallas_call x1, Pallas kernels, whole_planes(): pl.pallas_call(functools.partial(down_kernel, groups, by, share, sizes),...  4.61 us
    ppermute x1, waiting for transfers between devices, whole_planes(): lax.ppermute(bottom, 'gz', [(target, source) for source, target in forward])  3.89 us
    pallas_call x1, Pallas kernels, whole_planes(): pl.pallas_call(functools.partial(up_kernel, groups, by, share, sizes), ou...  3.45 us
    unnamed x6, local copies, waits for them, and re-layouts  2.63 us
    ppermute x1, starting transfers between devices, whole_planes(): low = lax.ppermute(top, 'gz', forward)  2.36 us
  transfers between devices with their start and end apart: 2, of which 1 were waited for; matrix products, arithmetic and copies ran while one was open for 0% of the time, Pallas kernels for 0%

profile of v2, /device:TPU:0, one launch (start us, length us, event | category | flops | bytes accessed | tf_op | source)
XLA Modules:
  0.0 63.9 jit_solution(9860085582287074713)
XLA Ops:
  0.0 0.0 copy-start
  0.0 0.9 %copy-done = bf16[32,16,256]{2,1,0:T(8,128)(2,1)S(1)} copy-done((bf16[32,16,256]{2,1,0:T(8,128)(2,1)S(1)}, bf16[32,16,256]{2,1,0:T(8,128)(2,1)}, u32[]{:S(2)}) %copy-start) | copy-done | bytes 262168
  1.0 0.0 copy-start.1
  1.0 0.8 %copy-done.1 = f32[16,8,128]{2,1,0:T(8,128)S(1)} copy-done((f32[16,8,128]{2,1,0:T(8,128)S(1)}, f32[16,8,128]{2,1,0:T(8,128)}, u32[]{:S(2)}) %copy-start.1) | copy-done | bytes 65560
  1.8 0.0 copy-start.2
  1.8 0.8 %copy-done.2 = s32[16,8,128]{2,1,0:T(8,128)S(1)} copy-done((s32[16,8,128]{2,1,0:T(8,128)S(1)}, s32[16,8,128]{2,1,0:T(8,128)}, u32[]{:S(2)}) %copy-start.2) | copy-done | bytes 65560
  2.6 0.7 %prepare.1 = (f32[384,128]{1,0:T(8,128)S(1)}, f32[56,128]{1,0:T(8,128)S(1)}, f32[56,128]{1,0:T(8,128)S(1)}) custom-call(bf16[512,256]{1,0:T(8,128)(2,1)S(1)} %bitcast.1, f32[16,8,128]{2,1,0:T(8,128)S(1)} %copy-done.1, s32[16,8,128]{2,1,0:T(8,128)S(1)} %copy-done.2), custom_call_target="tpu_custom_call" | custom-call | tf_op jit(solution)/shard_map/prepare/pallas_call | solution.py:589
  3.3 2.4 %collective-permute-start = (f32[56,128]{1,0:T(8,128)S(1)}, f32[56,128]{1,0:T(8,128)S(1)}, u32[]{:S(2)}, u32[]{:S(2)}) collective-permute-start(f32[56,128]{1,0:T(8,128)S(1)} %get-tuple-element.24), channel_id=1, source_target_pairs={{0,1},{1,2},{2,3},{4,5},{5,6},{6,7},{8,9},{9,10},{10,11},{12,13},{... | collective-permute-start | bytes 86024 | tf_op jit(solution)/shard_map/ppermute | solution.py:604
  5.7 1.3 %collective-permute-start.1 = (f32[56,128]{1,0:T(8,128)S(1)}, f32[56,128]{1,0:T(8,128)S(1)}, u32[]{:S(2)}, u32[]{:S(2)}) collective-permute-start(f32[56,128]{1,0:T(8,128)S(1)} %get-tuple-element.25), channel_id=1, source_target_pairs={{1,0},{2,1},{3,2},{5,4},{6,5},{7,6},{9,8},{10,9},{11,10},{13,12},{... | collective-permute-start | bytes 86024 | tf_op jit(solution)/shard_map/ppermute | solution.py:605
  7.0 0.0 collective-permute-done.low
  7.0 3.9 %collective-permute-done.1.high = f32[56,128]{1,0:T(8,128)S(1)} collective-permute-done((f32[56,128]{1,0:T(8,128)S(1)}, f32[56,128]{1,0:T(8,128)S(1)}, u32[]{:S(2)}, u32[]{:S(2)}) %collective-permute-start.1) | collective-permute-done | bytes 28704 | tf_op jit(solution)/shard_map/ppermute | solution.py:605
  10.9 0.1 pack.1
  10.9 23.9 %all_to_all.15.gathered = f32[8,160,128]{2,1,0:T(8,128)S(1)} all-to-all(f32[8,160,128]{2,1,0:T(8,128)S(1)} %pack.1), channel_id=1, replica_groups=mesh['gx'=2,'gy'=4,'gz'=4] {'gx','gy'}, dimensions={0} | all-to-all | bytes 1310720 | tf_op jit(solution)/shard_map/all_to_all | solution.py:613
  34.8 4.6 %down.1 = (f32[52,8,128]{2,1,0:T(8,128)S(1)}, f32[52,8,128]{2,1,0:T(8,128)S(1)}, f32[52,8,128]{2,1,0:T(8,128)S(1)}, f32[52,8,128]{2,1,0:T(8,128)S(1)}, f32[52,8,...) custom-call(f32[8,160,128]{2,1,0:T(8,128)S(1)} %all_to_all.15.gathered), custom_call_target="tpu_custom_call" | custom-call | tf_op jit(solution)/shard_map/down/pallas_call | solution.py:615
  39.4 10.0 %all_to_all.16.packed = f32[32,8,128]{2,1,0:T(8,128)S(1)} all-to-all(f32[32,8,128]{2,1,0:T(8,128)S(1)} %broadcast_in_dim.3), channel_id=1, replica_groups=mesh['gx'=2,'gy'=4,'gz'=4] {'gz','gx','gy'}, dimensions={0} | all-to-all | bytes 262144 | tf_op jit(solution)/shard_map/all_to_all | solution.py:623
  49.4 3.5 %up.1 = f32[8,16,128]{2,1,0:T(8,128)S(1)} custom-call(f32[32,8,128]{2,1,0:T(8,128)S(1)} %all_to_all.16.packed, f32[52,8,128]{2,1,0:T(8,128)S(1)} %get-tuple-element.27.rhs1, f32[52,8,128]{2,1,0:T(8,128)S(1)} %get-tuple-element.28.pin1, f32[52,8,128]{2,1,0:T(8,128)S(1)} %get-tuple-element.29.wx1, f32[52,8,128]{2,1,0:T(8,128)S(1)} %get-tuple-element.30.wy1, ...), custom_call_target="tpu_custom_call" | custom-call | tf_op jit(solution)/shard_map/up/pallas_call | solution.py:624
  52.9 10.0 %all_to_all.17.blocks = f32[8,16,128]{2,1,0:T(8,128)S(1)} all-to-all(f32[8,16,128]{2,1,0:T(8,128)S(1)} %up.1), channel_id=1, replica_groups=mesh['gx'=2,'gy'=4,'gz'=4] {'gx','gy'}, dimensions={0} | all-to-all | bytes 131072 | tf_op jit(solution)/shard_map/all_to_all | solution.py:636
  62.9 0.9 %finish.1 = f32[16,8,128]{2,1,0:T(8,128)} custom-call(f32[8,16,128]{2,1,0:T(8,128)S(1)} %all_to_all.17.blocks), custom_call_target="tpu_custom_call" | custom-call | tf_op jit(solution)/shard_map/finish/pallas_call | solution.py:631
  (1 shorter events, 0.0 us)
Async XLA Ops:
  0.0 0.9 %copy-start = (bf16[32,16,256]{2,1,0:T(8,128)(2,1)S(1)}, bf16[32,16,256]{2,1,0:T(8,128)(2,1)}, u32[]{:S(2)}) copy-start(bf16[32,16,256]{2,1,0:T(8,128)(2,1)} %param.3) | copy-start | bytes 786436
  1.0 0.8 %copy-start.1 = (f32[16,8,128]{2,1,0:T(8,128)S(1)}, f32[16,8,128]{2,1,0:T(8,128)}, u32[]{:S(2)}) copy-start(f32[16,8,128]{2,1,0:T(8,128)} %visc_in.1) | copy-start | bytes 196612
  1.8 0.8 %copy-start.2 = (s32[16,8,128]{2,1,0:T(8,128)S(1)}, s32[16,8,128]{2,1,0:T(8,128)}, u32[]{:S(2)}) copy-start(s32[16,8,128]{2,1,0:T(8,128)} %pin_in.1) | copy-start | bytes 196612
  3.3 3.7 %collective-permute-start = (f32[56,128]{1,0:T(8,128)S(1)}, f32[56,128]{1,0:T(8,128)S(1)}, u32[]{:S(2)}, u32[]{:S(2)}) collective-permute-start(f32[56,128]{1,0:T(8,128)S(1)} %get-tuple-element.24), channel_id=1, source_target_pairs={{0,1},{1,2},{2,3},{4,5},{5,6},{6,7},{8,9},{9,10},{10,11},{12,13},{... | collective-permute-start | bytes 86024 | tf_op jit(solution)/shard_map/ppermute | solution.py:604
  5.7 5.2 %collective-permute-start.1 = (f32[56,128]{1,0:T(8,128)S(1)}, f32[56,128]{1,0:T(8,128)S(1)}, u32[]{:S(2)}, u32[]{:S(2)}) collective-permute-start(f32[56,128]{1,0:T(8,128)S(1)} %get-tuple-element.25), channel_id=1, source_target_pairs={{1,0},{2,1},{3,2},{5,4},{6,5},{7,6},{9,8},{10,9},{11,10},{13,12},{... | collective-permute-start | bytes 86024 | tf_op jit(solution)/shard_map/ppermute | solution.py:605

commit v3 on v2

--- a/solution.py
+++ b/solution.py
@@ -142,7 +142,6 @@
 ROWS = 8
 LANES = 128
 HALO = 18
-SLAB = 56
 NEAR = 8
 F32 = jnp.float32
 
@@ -304,20 +303,14 @@
     return dot01(flat, chosen).reshape(field.shape)
 
 
-def prepare_kernel(
-    res_in, visc_in, pin_in, own_ref, top_ref, bottom_ref, res_ref, visc_ref, pin_ref, arrived
-):
-    copies = [
-        pltpu.make_async_copy(source, target, arrived.at[index])
-        for index, (source, target) in enumerate(
-            ((visc_in, visc_ref), (pin_in, pin_ref), (res_in, res_ref))
-        )
-    ]
-    for copy in copies:
-        copy.start()
-    for copy in copies:
-        copy.wait()
-    bx, by, depth = visc_ref.shape
+def rank_of(peer):
+    ny = SPLIT[1]
+    ix, iy = peer // ny, peer % ny
+    return ix * ny + (ny - 1 - iy if ix % 2 else iy)
+
+
+def prepare_kernel(share, res_ref, fluid_ref, pin_ref, out_ref):
+    bx, by, depth = fluid_ref.shape
     cells = bx * by
     groups = bx // 4
     pick = where01(iota((depth, 2 * depth), 1) // 2 == iota((depth, 2 * depth), 0))
@@ -332,39 +325,26 @@
     lane = iota((4 * cells, cells), 1)
     chosen = where01(lane_of(fine // (4 * by), (fine % (2 * by)) // 2) == lane)
     rhs = dot01(deep, chosen)
-    fluid = 1.0 / visc_ref[...].reshape(cells, depth)
-    pin = 4.0 * pin_ref[...].reshape(cells, depth).astype(F32) * fluid
     cell = iota((cells, cells), 0)
     lane = iota((cells, cells), 1)
     chosen = where01(lane_of(cell // by, cell % by) == lane)
-    fluid = dot01(fluid.T, chosen)
-    pin = dot01(pin.T, chosen)
+    fluid = dot01(fluid_ref[...].reshape(cells, depth).T, chosen)
+    pin = dot01(pin_ref[...].reshape(cells, depth).T, chosen)
     for index, field in enumerate((fluid, rhs, pin)):
-        own_ref[index * depth : (index + 1) * depth] = field
-        top_ref[index * HALO : (index + 1) * HALO] = field[depth - HALO :]
-        bottom_ref[index * HALO : (index + 1) * HALO] = field[:HALO]
-    empty = jnp.zeros((SLAB - 3 * HALO, LANES), F32)
-    top_ref[3 * HALO :] = empty
-    bottom_ref[3 * HALO :] = empty
-
-
-def pack_kernel(depth, span, own, low, high, out_ref):
-    share = span - 2 * HALO
+        for peer in range(depth // share):
+            begin = rank_of(peer) * share
+            out_ref[peer, index * share : (index + 1) * share] = field[begin : begin + share]
+
+
+def spread_kernel(groups, by, edge, gathered, own, top, bottom):
+    rows = own.shape[0]
+    for start in range(0, rows, ROWS):
+        place(gathered, start, own, start, groups, by)
+    share = rows // 3
     for index in range(3):
-        for peer in range(depth // share):
-            begin, end = peer * share - HALO, peer * share + share + HALO
-            row = index * span
-            ahead, behind = max(0, -begin), max(0, end - depth)
-            if ahead:
-                first = (index + 1) * HALO
-                out_ref[peer, row : row + ahead] = low[first - ahead : first]
-            inner = own[index * depth + max(begin, 0) : index * depth + min(end, depth)]
-            out_ref[peer, row + ahead : row + span - behind] = inner
-            if behind:
-                first = index * HALO
-                out_ref[peer, row + span - behind : row + span] = high[first : first + behind]
-    spare = out_ref.shape[1] - 3 * span
-    out_ref[:, 3 * span :] = jnp.zeros((depth // share, spare, LANES), F32)
+        first, last = index * share, (index + 1) * share
+        top[index * edge : (index + 1) * edge] = own[last - edge : last]
+        bottom[index * edge : (index + 1) * edge] = own[first : first + edge]
 
 
 def place(gathered, row, target, plane, groups, by):
@@ -383,7 +363,7 @@
 
 def down_kernel(
     groups, by, depth, sizes,
-    gathered,
+    low2, low1, own, high1, high2,
     rhs1, pin1, wx1, wy1, wz1, gain1, corr1,
     rhs2, pin2, wx2, wy2, wz2, gain2, corr2,
     packed,
@@ -391,8 +371,11 @@
 ):
     planes = depth + 2 * HALO
     for index, target in enumerate((fluid1, rhs1, pin1)):
-        for start in [*range(0, planes - ROWS, ROWS), planes - ROWS]:
-            place(gathered, index * planes + start, target, start, groups, by)
+        start = 0
+        for piece in (low2, low1, own, high1, high2):
+            count = piece.shape[0] // 3
+            target[start : start + count] = piece[index * count : (index + 1) * count]
+            start += count
 
     fine, coarse = Level(0), Level(1)
     down1, down2 = lanes_down(0), lanes_down(1)
@@ -490,8 +473,10 @@
 ):
     count3 = depth // 4
     shares = packed.shape[0]
-    first = jnp.concatenate([packed[i, 0:count3] for i in range(shares)], axis=0).T
-    second = jnp.concatenate([packed[i, count3 : 2 * count3] for i in range(shares)], axis=0).T
+    peers = SPLIT[0] * SPLIT[1]
+    slabs = sorted(range(shares), key=lambda i: (i // peers, rank_of(i % peers)))
+    first = jnp.concatenate([packed[i, 0:count3] for i in slabs], axis=0).T
+    second = jnp.concatenate([packed[i, count3 : 2 * count3] for i in slabs], axis=0).T
     cells = ROWS * ROWS
     total3 = shares * count3
     shape3 = (ROWS, ROWS, total3)
@@ -501,7 +486,8 @@
 
     nx, ny = SPLIT
     ix, iy = lax.axis_index("gx"), lax.axis_index("gy")
-    part = (lax.axis_index("gz") * nx + ix) * ny + iy
+    along = jnp.where(lax.rem(ix, 2) == 1, ny - 1 - iy, iy)
+    part = (lax.axis_index("gz") * nx + ix) * ny + along
     mine = pltpu.roll(corr3, lax.rem(NEAR - part * count3 + total3, total3), 1)
     tall = jnp.concatenate([mine, mine], axis=0).T
     count = count3 + 2 * NEAR
@@ -562,7 +548,9 @@
     lane = iota((cells, cells), 1)
     x, y = cell // by, cell % by
     chosen = where01((x % 4) * (bx // 4 * by) + (x // 4) * by + y == lane)
-    turned = dot01(blocks[...].reshape(depth, cells), chosen, (((1,), (1,)), ((), ())))
+    peers = blocks.shape[0]
+    ordered = jnp.concatenate([blocks[i] for i in sorted(range(peers), key=rank_of)], axis=0)
+    turned = dot01(ordered, chosen, (((1,), (1,)), ((), ())))
     out_ref[...] = turned.T.reshape(out_ref.shape)
 
 
@@ -585,32 +573,32 @@
     def room(count):
         return pltpu.VMEM((count, ROWS, LANES), F32)
 
-    residual = residual_q2.reshape(4 * bx * by, 2 * depth)
-    own, top, bottom = pl.pallas_call(
-        prepare_kernel,
-        in_specs=[pl.BlockSpec(memory_space=pltpu.HBM)] * 3,
-        out_shape=(flat(3 * depth), flat(SLAB), flat(SLAB)),
-        scratch_shapes=[
-            pltpu.VMEM(residual.shape, residual.dtype),
-            pltpu.VMEM(viscosity.shape, viscosity.dtype),
-            pltpu.VMEM(pinned.shape, pinned.dtype),
-            pltpu.SemaphoreType.DMA((3,)),
-        ],
+    fluid = 1.0 / viscosity
+    pin = 4.0 * pinned.astype(F32) * fluid
+    parcels = pl.pallas_call(
+        functools.partial(prepare_kernel, share),
+        out_shape=blocks(peers, 3 * share),
         compiler_params=limit,
         name="prepare",
-    )(residual, viscosity, pinned)
+    )(residual_q2.reshape(4 * bx * by, 2 * depth), fluid, pin)
+    edge = HALO - share
+    own, top, bottom = pl.pallas_call(
+        functools.partial(spread_kernel, groups, by, edge),
+        out_shape=(blocks(3 * share, ROWS), blocks(3 * edge, ROWS), blocks(3 * edge, ROWS)),
+        compiler_params=limit,
+        name="spread",
+    )(lax.all_to_all(parcels, ("gx", "gy"), 0, 0, tiled=True))
     length = lax.axis_size("gz")
-    forward = [(i, i + 1) for i in range(length - 1)]
-    low = lax.ppermute(top, "gz", forward)
-    high = lax.ppermute(bottom, "gz", [(target, source) for source, target in forward])
-    rows = -(-3 * planes // ROWS) * ROWS
-    parcels = pl.pallas_call(
-        functools.partial(pack_kernel, depth, planes),
-        out_shape=blocks(peers, rows),
-        compiler_params=limit,
-        name="pack",
-    )(own, low, high)
-    gathered = lax.all_to_all(parcels, ("gx", "gy"), 0, 0, tiled=True)
+    slabs = sorted(range(peers), key=rank_of)
+    parts = length * peers
+
+    def step(field, ahead):
+        device = [slabs[i % peers] * length + i // peers for i in range(parts)]
+        pairs = [(device[i], device[i + ahead]) for i in range(parts) if 0 <= i + ahead < parts]
+        return lax.ppermute(field, ("gx", "gy", "gz"), pairs)
+
+    low1, high1 = step(own, 1), step(own, -1)
+    low2, high2 = step(top, 2), step(bottom, -2)
     saved = (blocks(planes, ROWS),) * 7 + (blocks(count2, ROWS),) * 7
     results = pl.pallas_call(
         functools.partial(down_kernel, groups, by, share, sizes),
@@ -618,8 +606,8 @@
         scratch_shapes=[room(planes), room(planes), room(count2), room(count2), room(count2)],
         compiler_params=limit,
         name="down",
-    )(gathered)
-    copies = jnp.broadcast_to(results[-1], (length * peers, share // 2, LANES))
+    )(low2, low1, own, high1, high2)
+    copies = jnp.broadcast_to(results[-1], (parts, share // 2, LANES))
     packed = lax.all_to_all(copies, ("gz", "gx", "gy"), 0, 0, tiled=True)
     mine = pl.pallas_call(
         functools.partial(up_kernel, groups, by, share, sizes),

time: 64.2 us -> 62.6 us (0.975)
  blocking collectives: 43.9 us -> 37.4 us
  starting transfers between devices: 3.65 us -> 8.97 us
  local copies, waits for them, and re-layouts: 2.64 us -> 0.09 us
  waiting for transfers between devices: 3.89 us -> 5.59 us
  other arithmetic: 0 us -> 0.93 us
    all_to_all x1, blocking collectives: 23.9 us -> 15.8 us  [whole_planes(): lax.all_to_all(parcels, ('gx', 'gy'), 0, 0, tiled=True)]
    ppermute x2 -> x4, starting transfers between devices: 3.65 us -> 8.97 us  [step(): return lax.ppermute(field, ('gx', 'gy', 'gz'), pairs)]
    unnamed x6 -> x2, local copies, waits for them, and re-layouts: 2.63 us -> 0.08 us
    ppermute x2 -> x4, waiting for transfers between devices: 3.89 us -> 5.59 us  [step(): return lax.ppermute(field, ('gx', 'gy', 'gz'), pairs)]
    all_to_all x1, blocking collectives: 10 us -> 11.6 us  [whole_planes(): packed = lax.all_to_all(copies, ('gz', 'gx', 'gy'), 0, 0, tiled=True)]
    mul x0 -> x1, other arithmetic: none -> 0.93 us  [whole_planes(): pin = 4.0 * pinned.astype(F32) * fluid]
  transfers between devices with their start and end apart: 2 -> 4, of which waited for: 1 -> 2; matrix products, arithmetic and copies ran while one was open for 0% -> 0% of each run, Pallas kernels for 0% -> 0%
where the time goes in v3:
time: 62.6 us; the launch traced here: 62.3 us
  blocking collectives  37.4 us (60%)
  Pallas kernels  9.17 us (15%)
  starting transfers between devices  8.97 us (14%)
  waiting for transfers between devices  5.59 us (9%)
  other arithmetic  0.93 us (1%)
    all_to_all x1, blocking collectives, whole_planes(): lax.all_to_all(parcels, ('gx', 'gy'), 0, 0, tiled=True)  15.8 us
    all_to_all x1, blocking collectives, whole_planes(): packed = lax.all_to_all(copies, ('gz', 'gx', 'gy'), 0, 0, tiled=True)  11.6 us
    all_to_all x1, blocking collectives, whole_planes(): lax.all_to_all(mine, ('gx', 'gy'), 0, 0, tiled=True)  10 us
    ppermute x4, starting transfers between devices, step(): return lax.ppermute(field, ('gx', 'gy', 'gz'), pairs)  8.97 us
    ppermute x4, waiting for transfers between devices, step(): return lax.ppermute(field, ('gx', 'gy', 'gz'), pairs)  5.59 us
    pallas_call x1, Pallas kernels, whole_planes(): pl.pallas_call(functools.partial(down_kernel, groups, by, share, sizes),...  4.06 us
    pallas_call x1, Pallas kernels, whole_planes(): pl.pallas_call(functools.partial(up_kernel, groups, by, share, sizes), ou...  3.46 us
  transfers between devices with their start and end apart: 4, of which 2 were waited for; matrix products, arithmetic and copies ran while one was open for 0% of the time, Pallas kernels for 0%

profile of v3, /device:TPU:0, one launch (start us, length us, event | category | flops | bytes accessed | tf_op | source)
XLA Modules:
  0.0 62.3 jit_solution(8229578732653454489)
XLA Ops:
  0.0 0.0 copy-start
  0.0 0.9 %multiply_multiply_fusion = (f32[16,8,128]{2,1,0:T(8,128)S(1)}, f32[16,8,128]{2,1,0:T(8,128)S(1)}) fusion(s32[16,8,128]{2,1,0:T(8,128)} %param.5, f32[16,8,128]{2,1,0:T(8,128)} %param.4), kind=kLoop, calls=%fused_computation | loop fusion | flops 65536 | bytes 262144 | tf_op jit(solution)/shard_map/mul | solution.py:577
  0.9 0.1 copy-done
  1.0 0.5 prepare.1
  1.5 15.8 %all_to_all.15.gathered = f32[8,48,128]{2,1,0:T(8,128)S(1)} all-to-all(f32[8,48,128]{2,1,0:T(8,128)S(1)} %prepare.1), channel_id=1, replica_groups=mesh['gx'=2,'gy'=4,'gz'=4] {'gx','gy'}, dimensions={0} | all-to-all | bytes 393216 | tf_op jit(solution)/shard_map/all_to_all | solution.py:590
  17.3 0.2 spread.1
  17.6 1.3 %collective-permute-start.2 = (f32[48,8,128]{2,1,0:T(8,128)S(1)}, f32[48,8,128]{2,1,0:T(8,128)S(1)}, u32[]{:S(2)}, u32[]{:S(2)}) collective-permute-start(f32[48,8,128]{2,1,0:T(8,128)S(1)} %get-tuple-element.24.own), channel_id=1, source_target_pairs={{4,0},{8,4},{12,8},{28,12},{24,28},{20,24},{16,20},{1,16},{5,1},{9... | collective-permute-start | bytes 589832 | tf_op jit(solution)/shard_map/ppermute | solution.py:598
  18.9 4.6 %collective-permute-start.1 = (f32[48,8,128]{2,1,0:T(8,128)S(1)}, f32[48,8,128]{2,1,0:T(8,128)S(1)}, u32[]{:S(2)}, u32[]{:S(2)}) collective-permute-start(f32[48,8,128]{2,1,0:T(8,128)S(1)} %get-tuple-element.24.own), channel_id=1, source_target_pairs={{0,4},{4,8},{8,12},{12,28},{28,24},{24,20},{20,16},{16,1},{1,5},{5... | collective-permute-start | bytes 589832 | tf_op jit(solution)/shard_map/ppermute | solution.py:598
  23.4 1.8 %collective-permute-start = (f32[6,8,128]{2,1,0:T(8,128)S(1)}, f32[6,8,128]{2,1,0:T(8,128)S(1)}, u32[]{:S(2)}, u32[]{:S(2)}) collective-permute-start(f32[6,8,128]{2,1,0:T(8,128)S(1)} %get-tuple-element.23), channel_id=1, source_target_pairs={{0,8},{4,12},{8,28},{12,24},{28,20},{24,16},{20,1},{16,5},{1,9},{5... | collective-permute-start | bytes 73736 | tf_op jit(solution)/shard_map/ppermute | solution.py:598
  25.3 1.3 %collective-permute-start.3 = (f32[6,8,128]{2,1,0:T(8,128)S(1)}, f32[6,8,128]{2,1,0:T(8,128)S(1)}, u32[]{:S(2)}, u32[]{:S(2)}) collective-permute-start(f32[6,8,128]{2,1,0:T(8,128)S(1)} %get-tuple-element.25), channel_id=1, source_target_pairs={{8,0},{12,4},{28,8},{24,12},{20,28},{16,24},{1,20},{5,16},{9,1},{1... | collective-permute-start | bytes 73736 | tf_op jit(solution)/shard_map/ppermute | solution.py:598
  26.6 0.6 %collective-permute-done.low2 = f32[6,8,128]{2,1,0:T(8,128)S(1)} collective-permute-done((f32[6,8,128]{2,1,0:T(8,128)S(1)}, f32[6,8,128]{2,1,0:T(8,128)S(1)}, u32[]{:S(2)}, u32[]{:S(2)}) %collective-permute-start) | collective-permute-done | bytes 24608 | tf_op jit(solution)/shard_map/ppermute | solution.py:598
  27.2 5.0 %collective-permute-done.3.high2 = f32[6,8,128]{2,1,0:T(8,128)S(1)} collective-permute-done((f32[6,8,128]{2,1,0:T(8,128)S(1)}, f32[6,8,128]{2,1,0:T(8,128)S(1)}, u32[]{:S(2)}, u32[]{:S(2)}) %collective-permute-start.3) | collective-permute-done | bytes 24608 | tf_op jit(solution)/shard_map/ppermute | solution.py:598
  32.1 0.0 collective-permute-done.2.high1
  32.1 0.0 collective-permute-done.1.low1
  32.1 4.1 %down.1 = (f32[52,8,128]{2,1,0:T(8,128)S(1)}, f32[52,8,128]{2,1,0:T(8,128)S(1)}, f32[52,8,128]{2,1,0:T(8,128)S(1)}, f32[52,8,128]{2,1,0:T(8,128)S(1)}, f32[52,8,...) custom-call(f32[6,8,128]{2,1,0:T(8,128)S(1)} %collective-permute-don, ...), custom_call_target="tpu_custom_call" | custom-call | tf_op jit(solution)/shard_map/down/pallas_call | solution.py:603
  36.2 11.6 %all_to_all.16.packed = f32[32,8,128]{2,1,0:T(8,128)S(1)} all-to-all(f32[32,8,128]{2,1,0:T(8,128)S(1)} %broadcast_in_dim.3), channel_id=1, replica_groups=mesh['gx'=2,'gy'=4,'gz'=4] {'gz','gx','gy'}, dimensions={0} | all-to-all | bytes 262144 | tf_op jit(solution)/shard_map/all_to_all | solution.py:611
  47.8 3.5 %up.1 = f32[8,16,128]{2,1,0:T(8,128)S(1)} custom-call(f32[32,8,128]{2,1,0:T(8,128)S(1)} %all_to_all.16.packed, f32[52,8,128]{2,1,0:T(8,128)S(1)} %get-tuple-element.27.rhs1, f32[52,8,128]{2,1,0:T(8,128)S(1)} %get-tuple-element.28.pin1, f32[52,8,128]{2,1,0:T(8,128)S(1)} %get-tuple-element.29.wx1, f32[52,8,128]{2,1,0:T(8,128)S(1)} %get-tuple-element.30.wy1, ...), custom_call_target="tpu_custom_call" | custom-call | tf_op jit(solution)/shard_map/up/pallas_call | solution.py:612
  51.3 10.0 %all_to_all.17.blocks = f32[8,16,128]{2,1,0:T(8,128)S(1)} all-to-all(f32[8,16,128]{2,1,0:T(8,128)S(1)} %up.1), channel_id=1, replica_groups=mesh['gx'=2,'gy'=4,'gz'=4] {'gx','gy'}, dimensions={0} | all-to-all | bytes 131072 | tf_op jit(solution)/shard_map/all_to_all | solution.py:624
  61.3 0.9 %finish.1 = f32[16,8,128]{2,1,0:T(8,128)} custom-call(f32[8,16,128]{2,1,0:T(8,128)S(1)} %all_to_all.17.blocks), custom_call_target="tpu_custom_call" | custom-call | tf_op jit(solution)/shard_map/finish/pallas_call | solution.py:619
  (1 shorter events, 0.0 us)
Async XLA Ops:
  0.0 1.0 %copy-start = (bf16[32,16,256]{2,1,0:T(8,128)(2,1)S(1)}, bf16[32,16,256]{2,1,0:T(8,128)(2,1)}, u32[]{:S(2)}) copy-start(bf16[32,16,256]{2,1,0:T(8,128)(2,1)} %param.3) | copy-start | bytes 786436
  17.6 14.6 %collective-permute-start.2 = (f32[48,8,128]{2,1,0:T(8,128)S(1)}, f32[48,8,128]{2,1,0:T(8,128)S(1)}, u32[]{:S(2)}, u32[]{:S(2)}) collective-permute-start(f32[48,8,128]{2,1,0:T(8,128)S(1)} %get-tuple-element.24.own), channel_id=1, source_target_pairs={{4,0},{8,4},{12,8},{28,12},{24,28},{20,24},{16,20},{1,16},{5,1},{9... | collective-permute-start | bytes 589832 | tf_op jit(solution)/shard_map/ppermute | solution.py:598
  18.9 13.3 %collective-permute-start.1 = (f32[48,8,128]{2,1,0:T(8,128)S(1)}, f32[48,8,128]{2,1,0:T(8,128)S(1)}, u32[]{:S(2)}, u32[]{:S(2)}) collective-permute-start(f32[48,8,128]{2,1,0:T(8,128)S(1)} %get-tuple-element.24.own), channel_id=1, source_target_pairs={{0,4},{4,8},{8,12},{12,28},{28,24},{24,20},{20,16},{16,1},{1,5},{5... | collective-permute-start | bytes 589832 | tf_op jit(solution)/shard_map/ppermute | solution.py:598
  23.4 3.8 %collective-permute-start = (f32[6,8,128]{2,1,0:T(8,128)S(1)}, f32[6,8,128]{2,1,0:T(8,128)S(1)}, u32[]{:S(2)}, u32[]{:S(2)}) collective-permute-start(f32[6,8,128]{2,1,0:T(8,128)S(1)} %get-tuple-element.23), channel_id=1, source_target_pairs={{0,8},{4,12},{8,28},{12,24},{28,20},{24,16},{20,1},{16,5},{1,9},{5... | collective-permute-start | bytes 73736 | tf_op jit(solution)/shard_map/ppermute | solution.py:598
  25.3 6.9 %collective-permute-start.3 = (f32[6,8,128]{2,1,0:T(8,128)S(1)}, f32[6,8,128]{2,1,0:T(8,128)S(1)}, u32[]{:S(2)}, u32[]{:S(2)}) collective-permute-start(f32[6,8,128]{2,1,0:T(8,128)S(1)} %get-tuple-element.25), channel_id=1, source_target_pairs={{8,0},{12,4},{28,8},{24,12},{20,28},{16,24},{1,20},{5,16},{9,1},{1... | collective-permute-start | bytes 73736 | tf_op jit(solution)/shard_map/ppermute | solution.py:598

commit v4 on v3

--- a/solution.py
+++ b/solution.py
@@ -141,7 +141,7 @@
 SPLIT = (2, 4)
 ROWS = 8
 LANES = 128
-HALO = 18
+HALO = 16
 NEAR = 8
 F32 = jnp.float32
 
@@ -336,15 +336,9 @@
             out_ref[peer, index * share : (index + 1) * share] = field[begin : begin + share]
 
 
-def spread_kernel(groups, by, edge, gathered, own, top, bottom):
-    rows = own.shape[0]
-    for start in range(0, rows, ROWS):
+def spread_kernel(groups, by, gathered, own):
+    for start in range(0, own.shape[0], ROWS):
         place(gathered, start, own, start, groups, by)
-    share = rows // 3
-    for index in range(3):
-        first, last = index * share, (index + 1) * share
-        top[index * edge : (index + 1) * edge] = own[last - edge : last]
-        bottom[index * edge : (index + 1) * edge] = own[first : first + edge]
 
 
 def place(gathered, row, target, plane, groups, by):
@@ -363,7 +357,7 @@
 
 def down_kernel(
     groups, by, depth, sizes,
-    low2, low1, own, high1, high2,
+    low, own, high,
     rhs1, pin1, wx1, wy1, wz1, gain1, corr1,
     rhs2, pin2, wx2, wy2, wz2, gain2, corr2,
     packed,
@@ -372,7 +366,7 @@
     planes = depth + 2 * HALO
     for index, target in enumerate((fluid1, rhs1, pin1)):
         start = 0
-        for piece in (low2, low1, own, high1, high2):
+        for piece in (low, own, high):
             count = piece.shape[0] // 3
             target[start : start + count] = piece[index * count : (index + 1) * count]
             start += count
@@ -390,12 +384,15 @@
     for source, target, share in ((fluid1, fluid2, 8.0), (pin1, pin2, 4.0)):
         whole = pair_sum(source[begin : begin + 2 * count2])
         target[...] = in_lanes(whole, down1) * (1.0 / share)
-    inner = count2 - 2
-    coarse_residual(fine, begin + 2, begin + 2 + 2 * inner, sizes[2], fields1, corr1, sums)
-    rhs2[1 : 1 + inner] = in_lanes(sums[0:inner], down1)
-    set_level(coarse, 1, 1 + inner, sizes[3], fluid2, pin2, rhs2, wx2, wy2, wz2, gain2, other2)
-    sweep(coarse, 2, inner, sizes[4], fields2, gain2, other2, corr2)
-    sweep(coarse, 3, inner - 1, sizes[4], fields2, gain2, corr2, other2)
+    low2, high2 = (begin + 4) // 2, count2 - (begin + 4) // 2
+    inner = high2 - low2
+    coarse_residual(
+        fine, begin + 2 * low2, begin + 2 * high2, sizes[2], fields1, corr1, sums
+    )
+    rhs2[low2:high2] = in_lanes(sums[0:inner], down1)
+    set_level(coarse, low2, high2, sizes[3], fluid2, pin2, rhs2, wx2, wy2, wz2, gain2, other2)
+    sweep(coarse, low2 + 1, high2 - 1, sizes[4], fields2, gain2, other2, corr2)
+    sweep(coarse, low2 + 2, high2 - 2, sizes[4], fields2, gain2, corr2, other2)
     corr2[...] = other2[...]
     coarse_residual(coarse, NEAR, NEAR + depth // 2, sizes[5], fields2, corr2, sums)
     count3 = depth // 4
@@ -411,6 +408,10 @@
         second = jnp.where(lane == row, pin3[:, row, :], second)
     packed[0:count3] = first
     packed[count3 : 2 * count3] = second
+    lane = iota((ROWS, LANES), 1)
+    packed[2 * count3 :] = jnp.where(
+        lane < LANES // 2, corr2[NEAR + depth // 2 - 5], corr2[NEAR + 4]
+    )
 
 
 def columns(rhs, fluid, pin):
@@ -484,6 +485,13 @@
         first[:cells].reshape(shape3), first[cells:].reshape(shape3), second[:cells].reshape(shape3)
     ).reshape(cells, total3)
 
+    def slab_of(index):
+        index = jnp.clip(index, 0, shares - 1)
+        row = lax.rem(index, peers) // ny
+        column = lax.rem(index, ny)
+        column = jnp.where(lax.rem(row, 2) == 1, ny - 1 - column, column)
+        return (index // peers) * peers + row * ny + column
+
     nx, ny = SPLIT
     ix, iy = lax.axis_index("gx"), lax.axis_index("gy")
     along = jnp.where(lax.rem(ix, 2) == 1, ny - 1 - iy, iy)
@@ -502,11 +510,18 @@
 
     fields1 = (rhs1, pin1, wx1, wy1, wz1)
     fields2 = (rhs2, pin2, wx2, wy2, wz2)
-    low, high = NEAR - 6, NEAR + depth // 2 + 6
+    low, high = NEAR - 4, NEAR + depth // 2 + 4
     parents = lifted[low // 2 + NEAR // 2 : high // 2 + NEAR // 2]
     twice = jnp.broadcast_to(parents[:, None], (parents.shape[0], 2, ROWS, LANES))
+    reach = depth // 2 + NEAR
+    half = iota((ROWS, LANES), 1) < LANES // 2
+    before = packed[slab_of(part - 1), 2 * count3 :]
+    after = packed[slab_of(part + 1), 2 * count3 :]
+    before = jnp.where(half, before, pltpu.roll(before, LANES // 2, 1))
+    after = jnp.where(half, pltpu.roll(after, LANES // 2, 1), after)
+    one2[low - 1] = before + lifted[(low - 1) // 2 + NEAR // 2]
     one2[low:high] = corr2[low:high] + twice.reshape(high - low, ROWS, LANES)
-    reach = depth // 2 + NEAR
+    one2[high] = after + lifted[high // 2 + NEAR // 2]
     sweep(coarse, NEAR - 4, reach + 4, sizes[4], fields2, gain2, one2, two2)
     sweep(coarse, NEAR - 3, reach + 3, sizes[4], fields2, gain2, two2, one2)
     sweep(coarse, NEAR - 2, reach + 2, sizes[4], fields2, gain2, one2, two2)
@@ -561,7 +576,7 @@
     share = depth // peers
     planes = share + 2 * HALO
     count2 = share // 2 + 2 * NEAR
-    sizes = (10, 24, 22, 11, 24, 24)
+    sizes = (23, 22, 20, 10, 24, 24)
     limit = pltpu.CompilerParams(vmem_limit_bytes=32 * 2**20)
 
     def flat(rows):
@@ -581,10 +596,9 @@
         compiler_params=limit,
         name="prepare",
     )(residual_q2.reshape(4 * bx * by, 2 * depth), fluid, pin)
-    edge = HALO - share
-    own, top, bottom = pl.pallas_call(
-        functools.partial(spread_kernel, groups, by, edge),
-        out_shape=(blocks(3 * share, ROWS), blocks(3 * edge, ROWS), blocks(3 * edge, ROWS)),
+    own = pl.pallas_call(
+        functools.partial(spread_kernel, groups, by),
+        out_shape=blocks(3 * share, ROWS),
         compiler_params=limit,
         name="spread",
     )(lax.all_to_all(parcels, ("gx", "gy"), 0, 0, tiled=True))
@@ -597,18 +611,16 @@
         pairs = [(device[i], device[i + ahead]) for i in range(parts) if 0 <= i + ahead < parts]
         return lax.ppermute(field, ("gx", "gy", "gz"), pairs)
 
-    low1, high1 = step(own, 1), step(own, -1)
-    low2, high2 = step(top, 2), step(bottom, -2)
+    low, high = step(own, 1), step(own, -1)
     saved = (blocks(planes, ROWS),) * 7 + (blocks(count2, ROWS),) * 7
     results = pl.pallas_call(
         functools.partial(down_kernel, groups, by, share, sizes),
-        out_shape=saved + (flat(share // 2),),
+        out_shape=saved + (flat(share // 2 + ROWS),),
         scratch_shapes=[room(planes), room(planes), room(count2), room(count2), room(count2)],
         compiler_params=limit,
         name="down",
-    )(low2, low1, own, high1, high2)
-    copies = jnp.broadcast_to(results[-1], (parts, share // 2, LANES))
-    packed = lax.all_to_all(copies, ("gz", "gx", "gy"), 0, 0, tiled=True)
+    )(low, own, high)
+    packed = lax.all_gather(results[-1], ("gz", "gx", "gy"))
     mine = pl.pallas_call(
         functools.partial(up_kernel, groups, by, share, sizes),
         out_shape=blocks(peers, share),

time: 62.6 us -> 112 us (1.79)
  blocking collectives: 37.4 us -> 93.1 us
  starting transfers between devices: 8.97 us -> 5.85 us
  waiting for transfers between devices: 5.59 us -> 3.24 us
    all_gather x0 -> x1, blocking collectives: none -> 67.9 us  [whole_planes(): packed = lax.all_gather(results[-1], ('gz', 'gx', 'gy'))]
    all_to_all x1 -> x0, blocking collectives: 11.6 us -> none  [whole_planes(): packed = lax.all_to_all(copies, ('gz', 'gx', 'gy'), 0, 0, tiled=True)]
    ppermute x4 -> x2, starting transfers between devices: 8.97 us -> 5.85 us  [step(): return lax.ppermute(field, ('gx', 'gy', 'gz'), pairs)]
    ppermute x4 -> x2, waiting for transfers between devices: 5.59 us -> 3.24 us  [step(): return lax.ppermute(field, ('gx', 'gy', 'gz'), pairs)]
  transfers between devices with their start and end apart: 4 -> 2, of which waited for: 2 -> 2; matrix products, arithmetic and copies ran while one was open for 0% -> 0% of each run, Pallas kernels for 0% -> 0%
where the time goes in v4:
time: 112 us
  blocking collectives  93.1 us (83%)
  Pallas kernels  8.51 us (8%)
  starting transfers between devices  5.85 us (5%)
  waiting for transfers between devices  3.24 us (3%)
    all_gather x1, blocking collectives, whole_planes(): packed = lax.all_gather(results[-1], ('gz', 'gx', 'gy'))  67.9 us
    all_to_all x1, blocking collectives, whole_planes(): lax.all_to_all(parcels, ('gx', 'gy'), 0, 0, tiled=True)  15.8 us
    all_to_all x1, blocking collectives, whole_planes(): lax.all_to_all(mine, ('gx', 'gy'), 0, 0, tiled=True)  9.37 us
    ppermute x2, starting transfers between devices, step(): return lax.ppermute(field, ('gx', 'gy', 'gz'), pairs)  5.85 us
    pallas_call x1, Pallas kernels, whole_planes(): pl.pallas_call(functools.partial(up_kernel, groups, by, share, sizes), ou...  3.44 us
    pallas_call x1, Pallas kernels, whole_planes(): pl.pallas_call(functools.partial(down_kernel, groups, by, share, sizes),...  3.41 us
    ppermute x2, waiting for transfers between devices, step(): return lax.ppermute(field, ('gx', 'gy', 'gz'), pairs)  3.24 us
  transfers between devices with their start and end apart: 2, of which 2 were waited for; matrix products, arithmetic and copies ran while one was open for 0% of the time, Pallas kernels for 0%

profile of v4, /device:TPU:0, one launch (start us, length us, event | category | flops | bytes accessed | tf_op | source)
XLA Modules:
  0.0 111.7 jit_solution(12143929229238754241)
XLA Ops:
  0.0 0.0 copy-start
  0.0 0.9 multiply_multiply_fusion
  0.9 0.1 copy-done
  1.0 0.5 prepare.1
  1.5 15.8 %all_to_all.10.gathered = f32[8,48,128]{2,1,0:T(8,128)S(1)} all-to-all(f32[8,48,128]{2,1,0:T(8,128)S(1)} %prepare.1), channel_id=1, replica_groups=mesh['gx'=2,'gy'=4,'gz'=4] {'gx','gy'}, dimensions={0} | all-to-all | bytes 393216 | tf_op jit(solution)/shard_map/all_to_all | solution.py:604
  17.3 0.2 spread.1.own
  17.6 1.3 %collective-permute-start.1 = (f32[48,8,128]{2,1,0:T(8,128)S(1)}, f32[48,8,128]{2,1,0:T(8,128)S(1)}, u32[]{:S(2)}, u32[]{:S(2)}) collective-permute-start(f32[48,8,128]{2,1,0:T(8,128)S(1)} %spread.1.own), channel_id=1, source_target_pairs={{4,0},{8,4},{12,8},{28,12},{24,28},{20,24},{16,20},{1,16},{5,1},{9... | collective-permute-start | bytes 589832 | tf_op jit(solution)/shard_map/ppermute | solution.py:612
  18.9 4.6 %collective-permute-start = (f32[48,8,128]{2,1,0:T(8,128)S(1)}, f32[48,8,128]{2,1,0:T(8,128)S(1)}, u32[]{:S(2)}, u32[]{:S(2)}) collective-permute-start(f32[48,8,128]{2,1,0:T(8,128)S(1)} %spread.1.own), channel_id=1, source_target_pairs={{0,4},{4,8},{8,12},{12,28},{28,24},{24,20},{20,16},{16,1},{1,5},{5... | collective-permute-start | bytes 589832 | tf_op jit(solution)/shard_map/ppermute | solution.py:612
  23.4 1.7 %collective-permute-done.1.high = f32[48,8,128]{2,1,0:T(8,128)S(1)} collective-permute-done((f32[48,8,128]{2,1,0:T(8,128)S(1)}, f32[48,8,128]{2,1,0:T(8,128)S(1)}, u32[]{:S(2)}, u32[]{:S(2)}) %collective-permute-start.1) | collective-permute-done | bytes 196640 | tf_op jit(solution)/shard_map/ppermute | solution.py:612
  25.1 1.5 %collective-permute-done.low = f32[48,8,128]{2,1,0:T(8,128)S(1)} collective-permute-done((f32[48,8,128]{2,1,0:T(8,128)S(1)}, f32[48,8,128]{2,1,0:T(8,128)S(1)}, u32[]{:S(2)}, u32[]{:S(2)}) %collective-permute-start) | collective-permute-done | bytes 196640 | tf_op jit(solution)/shard_map/ppermute | solution.py:612
  26.7 3.4 %down.1 = (f32[48,8,128]{2,1,0:T(8,128)S(1)}, f32[48,8,128]{2,1,0:T(8,128)S(1)}, f32[48,8,128]{2,1,0:T(8,128)S(1)}, f32[48,8,128]{2,1,0:T(8,128)S(1)}, f32[48,8,...) custom-call(f32[48,8,128]{2,1,0:T(8,128)S(1)} %collective-permute-do, ...), custom_call_target="tpu_custom_call" | custom-call | tf_op jit(solution)/shard_map/down/pallas_call | solution.py:616
  30.1 67.9 %all-gather = f32[512,128]{1,0:T(8,128)S(1)} all-gather(f32[16,128]{1,0:T(8,128)S(1)} %get-tuple-element.20), channel_id=2, replica_groups=mesh['gx'=2,'gy'=4,'gz'=4] {'gz','gx','gy'}, dimensions={0}, use_global_device_ids=true | all-gather | bytes 270336 | tf_op jit(solution)/shard_map/all_gather | solution.py:623
  98.0 3.4 %up.1 = f32[8,16,128]{2,1,0:T(8,128)S(1)} custom-call(f32[32,16,128]{2,1,0:T(8,128)S(1)} %bitcast.2, f32[48,8,128]{2,1,0:T(8,128)S(1)} %get-tuple-element.21.rhs1, f32[48,8,128]{2,1,0:T(8,128)S(1)} %get-tuple-element.22.pin1, f32[48,8,128]{2,1,0:T(8,128)S(1)} %get-tuple-element.23.wx1, f32[48,8,128]{2,1,0:T(8,128)S(1)} %get-tuple-element.24.wy1, ...), custom_call_target="tpu_custom_call" | custom-call | tf_op jit(solution)/shard_map/up/pallas_call | solution.py:624
  101.4 9.4 %all_to_all.11.blocks = f32[8,16,128]{2,1,0:T(8,128)S(1)} all-to-all(f32[8,16,128]{2,1,0:T(8,128)S(1)} %up.1), channel_id=1, replica_groups=mesh['gx'=2,'gy'=4,'gz'=4] {'gx','gy'}, dimensions={0} | all-to-all | bytes 131072 | tf_op jit(solution)/shard_map/all_to_all | solution.py:636
  110.8 0.9 finish.1
Async XLA Ops:
  0.0 1.0 copy-start
  17.6 7.6 %collective-permute-start.1 = (f32[48,8,128]{2,1,0:T(8,128)S(1)}, f32[48,8,128]{2,1,0:T(8,128)S(1)}, u32[]{:S(2)}, u32[]{:S(2)}) collective-permute-start(f32[48,8,128]{2,1,0:T(8,128)S(1)} %spread.1.own), channel_id=1, source_target_pairs={{4,0},{8,4},{12,8},{28,12},{24,28},{20,24},{16,20},{1,16},{5,1},{9... | collective-permute-start | bytes 589832 | tf_op jit(solution)/shard_map/ppermute | solution.py:612
  18.9 7.8 %collective-permute-start = (f32[48,8,128]{2,1,0:T(8,128)S(1)}, f32[48,8,128]{2,1,0:T(8,128)S(1)}, u32[]{:S(2)}, u32[]{:S(2)}) collective-permute-start(f32[48,8,128]{2,1,0:T(8,128)S(1)} %spread.1.own), channel_id=1, source_target_pairs={{0,4},{4,8},{8,12},{12,28},{28,24},{24,20},{20,16},{16,1},{1,5},{5... | collective-permute-start | bytes 589832 | tf_op jit(solution)/shard_map/ppermute | solution.py:612

commit v5 on v4

--- a/solution.py
+++ b/solution.py
@@ -620,7 +620,8 @@
         compiler_params=limit,
         name="down",
     )(low, own, high)
-    packed = lax.all_gather(results[-1], ("gz", "gx", "gy"))
+    copies = jnp.broadcast_to(results[-1], (parts,) + results[-1].shape)
+    packed = lax.all_to_all(copies, ("gz", "gx", "gy"), 0, 0, tiled=True)
     mine = pl.pallas_call(
         functools.partial(up_kernel, groups, by, share, sizes),
         out_shape=blocks(peers, share),

time: 112 us -> 59 us (0.53)
  blocking collectives: 93.1 us -> 40 us
    all_gather x1 -> x0, blocking collectives: 67.9 us -> none  [whole_planes(): packed = lax.all_gather(results[-1], ('gz', 'gx', 'gy'))]
    all_to_all x0 -> x1, blocking collectives: none -> 14.6 us  [whole_planes(): packed = lax.all_to_all(copies, ('gz', 'gx', 'gy'), 0, 0, tiled=True)]
where the time goes in v5:
time: 59 us; the launch traced here: 58.7 us
  blocking collectives  40 us (68%)
  Pallas kernels  8.51 us (14%)
  starting transfers between devices  5.85 us (10%)
  waiting for transfers between devices  3.24 us (5%)
  other arithmetic  0.93 us (2%)
    all_to_all x1, blocking collectives, whole_planes(): lax.all_to_all(parcels, ('gx', 'gy'), 0, 0, tiled=True)  15.8 us
    all_to_all x1, blocking collectives, whole_planes(): packed = lax.all_to_all(copies, ('gz', 'gx', 'gy'), 0, 0, tiled=True)  14.6 us
    all_to_all x1, blocking collectives, whole_planes(): lax.all_to_all(mine, ('gx', 'gy'), 0, 0, tiled=True)  9.6 us
    ppermute x2, starting transfers between devices, step(): return lax.ppermute(field, ('gx', 'gy', 'gz'), pairs)  5.85 us
    pallas_call x1, Pallas kernels, whole_planes(): pl.pallas_call(functools.partial(up_kernel, groups, by, share, sizes), ou...  3.44 us
    pallas_call x1, Pallas kernels, whole_planes(): pl.pallas_call(functools.partial(down_kernel, groups, by, share, sizes),...  3.41 us
    ppermute x2, waiting for transfers between devices, step(): return lax.ppermute(field, ('gx', 'gy', 'gz'), pairs)  3.24 us
  transfers between devices with their start and end apart: 2, of which 2 were waited for; matrix products, arithmetic and copies ran while one was open for 0% of the time, Pallas kernels for 0%

profile of v5, /device:TPU:0, one launch (start us, length us, event | category | flops | bytes accessed | tf_op | source)
XLA Modules:
  0.0 58.7 jit_solution(2173859382250477826)
XLA Ops:
  0.0 0.0 copy-start
  0.0 0.9 %multiply_multiply_fusion = (f32[16,8,128]{2,1,0:T(8,128)S(1)}, f32[16,8,128]{2,1,0:T(8,128)S(1)}) fusion(s32[16,8,128]{2,1,0:T(8,128)} %param.5, f32[16,8,128]{2,1,0:T(8,128)} %param.4), kind=kLoop, calls=%fused_computation | loop fusion | flops 65536 | bytes 262144 | tf_op jit(solution)/shard_map/mul | solution.py:592
  0.9 0.1 copy-done
  1.0 0.5 prepare.1
  1.5 15.8 %all_to_all.15.gathered = f32[8,48,128]{2,1,0:T(8,128)S(1)} all-to-all(f32[8,48,128]{2,1,0:T(8,128)S(1)} %prepare.1), channel_id=1, replica_groups=mesh['gx'=2,'gy'=4,'gz'=4] {'gx','gy'}, dimensions={0} | all-to-all | bytes 393216 | tf_op jit(solution)/shard_map/all_to_all | solution.py:604
  17.3 0.2 spread.1.own
  17.6 1.3 %collective-permute-start.1 = (f32[48,8,128]{2,1,0:T(8,128)S(1)}, f32[48,8,128]{2,1,0:T(8,128)S(1)}, u32[]{:S(2)}, u32[]{:S(2)}) collective-permute-start(f32[48,8,128]{2,1,0:T(8,128)S(1)} %spread.1.own), channel_id=1, source_target_pairs={{4,0},{8,4},{12,8},{28,12},{24,28},{20,24},{16,20},{1,16},{5,1},{9... | collective-permute-start | bytes 589832 | tf_op jit(solution)/shard_map/ppermute | solution.py:612
  18.9 4.6 %collective-permute-start = (f32[48,8,128]{2,1,0:T(8,128)S(1)}, f32[48,8,128]{2,1,0:T(8,128)S(1)}, u32[]{:S(2)}, u32[]{:S(2)}) collective-permute-start(f32[48,8,128]{2,1,0:T(8,128)S(1)} %spread.1.own), channel_id=1, source_target_pairs={{0,4},{4,8},{8,12},{12,28},{28,24},{24,20},{20,16},{16,1},{1,5},{5... | collective-permute-start | bytes 589832 | tf_op jit(solution)/shard_map/ppermute | solution.py:612
  23.4 1.7 %collective-permute-done.1.high = f32[48,8,128]{2,1,0:T(8,128)S(1)} collective-permute-done((f32[48,8,128]{2,1,0:T(8,128)S(1)}, f32[48,8,128]{2,1,0:T(8,128)S(1)}, u32[]{:S(2)}, u32[]{:S(2)}) %collective-permute-start.1) | collective-permute-done | bytes 196640 | tf_op jit(solution)/shard_map/ppermute | solution.py:612
  25.1 1.5 %collective-permute-done.low = f32[48,8,128]{2,1,0:T(8,128)S(1)} collective-permute-done((f32[48,8,128]{2,1,0:T(8,128)S(1)}, f32[48,8,128]{2,1,0:T(8,128)S(1)}, u32[]{:S(2)}, u32[]{:S(2)}) %collective-permute-start) | collective-permute-done | bytes 196640 | tf_op jit(solution)/shard_map/ppermute | solution.py:612
  26.7 3.4 %down.1 = (f32[48,8,128]{2,1,0:T(8,128)S(1)}, f32[48,8,128]{2,1,0:T(8,128)S(1)}, f32[48,8,128]{2,1,0:T(8,128)S(1)}, f32[48,8,128]{2,1,0:T(8,128)S(1)}, f32[48,8,...) custom-call(f32[48,8,128]{2,1,0:T(8,128)S(1)} %collective-permute-do, ...), custom_call_target="tpu_custom_call" | custom-call | tf_op jit(solution)/shard_map/down/pallas_call | solution.py:616
  30.1 14.6 %all_to_all.16.packed = f32[32,16,128]{2,1,0:T(8,128)S(1)} all-to-all(f32[32,16,128]{2,1,0:T(8,128)S(1)} %broadcast_in_dim.3), channel_id=1, replica_groups=mesh['gx'=2,'gy'=4,'gz'=4] {'gz','gx','gy'}, dimensions={0} | all-to-all | bytes 524288 | tf_op jit(solution)/shard_map/all_to_all | solution.py:624
  44.7 3.4 %up.1 = f32[8,16,128]{2,1,0:T(8,128)S(1)} custom-call(f32[32,16,128]{2,1,0:T(8,128)S(1)} %all_to_all.16.packed, f32[48,8,128]{2,1,0:T(8,128)S(1)} %get-tuple-element.21.rhs1, f32[48,8,128]{2,1,0:T(8,128)S(1)} %get-tuple-element.22.pin1, f32[48,8,128]{2,1,0:T(8,128)S(1)} %get-tuple-element.23.wx1, f32[48,8,128]{2,1,0:T(8,128)S(1)} %get-tuple-element.24.wy1, ...), custom_call_target="tpu_custom_call" | custom-call | tf_op jit(solution)/shard_map/up/pallas_call | solution.py:625
  48.2 9.6 %all_to_all.17.blocks = f32[8,16,128]{2,1,0:T(8,128)S(1)} all-to-all(f32[8,16,128]{2,1,0:T(8,128)S(1)} %up.1), channel_id=1, replica_groups=mesh['gx'=2,'gy'=4,'gz'=4] {'gx','gy'}, dimensions={0} | all-to-all | bytes 131072 | tf_op jit(solution)/shard_map/all_to_all | solution.py:637
  57.8 0.9 %finish.1 = f32[16,8,128]{2,1,0:T(8,128)} custom-call(f32[8,16,128]{2,1,0:T(8,128)S(1)} %all_to_all.17.blocks), custom_call_target="tpu_custom_call" | custom-call | tf_op jit(solution)/shard_map/finish/pallas_call | solution.py:632
  (1 shorter events, 0.0 us)
Async XLA Ops:
  0.0 1.0 %copy-start = (bf16[32,16,256]{2,1,0:T(8,128)(2,1)S(1)}, bf16[32,16,256]{2,1,0:T(8,128)(2,1)}, u32[]{:S(2)}) copy-start(bf16[32,16,256]{2,1,0:T(8,128)(2,1)} %param.3) | copy-start | bytes 786436
  17.6 7.6 %collective-permute-start.1 = (f32[48,8,128]{2,1,0:T(8,128)S(1)}, f32[48,8,128]{2,1,0:T(8,128)S(1)}, u32[]{:S(2)}, u32[]{:S(2)}) collective-permute-start(f32[48,8,128]{2,1,0:T(8,128)S(1)} %spread.1.own), channel_id=1, source_target_pairs={{4,0},{8,4},{12,8},{28,12},{24,28},{20,24},{16,20},{1,16},{5,1},{9... | collective-permute-start | bytes 589832 | tf_op jit(solution)/shard_map/ppermute | solution.py:612
  18.9 7.8 %collective-permute-start = (f32[48,8,128]{2,1,0:T(8,128)S(1)}, f32[48,8,128]{2,1,0:T(8,128)S(1)}, u32[]{:S(2)}, u32[]{:S(2)}) collective-permute-start(f32[48,8,128]{2,1,0:T(8,128)S(1)} %spread.1.own), channel_id=1, source_target_pairs={{0,4},{4,8},{8,12},{12,28},{28,24},{24,20},{20,16},{16,1},{1,5},{5... | collective-permute-start | bytes 589832 | tf_op jit(solution)/shard_map/ppermute | solution.py:612

commit v6 on v5

--- a/solution.py
+++ b/solution.py
@@ -375,10 +375,9 @@
     down1, down2 = lanes_down(0), lanes_down(1)
     fields1 = (rhs1, pin1, wx1, wy1, wz1)
     fields2 = (rhs2, pin2, wx2, wy2, wz2)
-    set_level(fine, 1, planes - 1, sizes[0], fluid1, pin1, rhs1, wx1, wy1, wz1, gain1, other1)
-    sweep(fine, 2, planes - 2, sizes[1], fields1, gain1, other1, corr1)
-    sweep(fine, 3, planes - 3, sizes[1], fields1, gain1, corr1, other1)
-    corr1[...] = other1[...]
+    set_level(fine, 1, planes - 1, sizes[0], fluid1, pin1, rhs1, wx1, wy1, wz1, gain1, corr1)
+    sweep(fine, 2, planes - 2, sizes[1], fields1, gain1, corr1, other1)
+    sweep(fine, 3, planes - 3, sizes[1], fields1, gain1, other1, corr1)
     count2 = depth // 2 + 2 * NEAR
     begin = HALO - 2 * NEAR
     for source, target, share in ((fluid1, fluid2, 8.0), (pin1, pin2, 4.0)):
@@ -390,10 +389,9 @@
         fine, begin + 2 * low2, begin + 2 * high2, sizes[2], fields1, corr1, sums
     )
     rhs2[low2:high2] = in_lanes(sums[0:inner], down1)
-    set_level(coarse, low2, high2, sizes[3], fluid2, pin2, rhs2, wx2, wy2, wz2, gain2, other2)
-    sweep(coarse, low2 + 1, high2 - 1, sizes[4], fields2, gain2, other2, corr2)
-    sweep(coarse, low2 + 2, high2 - 2, sizes[4], fields2, gain2, corr2, other2)
-    corr2[...] = other2[...]
+    set_level(coarse, low2, high2, sizes[3], fluid2, pin2, rhs2, wx2, wy2, wz2, gain2, corr2)
+    sweep(coarse, low2 + 1, high2 - 1, sizes[4], fields2, gain2, corr2, other2)
+    sweep(coarse, low2 + 2, high2 - 2, sizes[4], fields2, gain2, other2, corr2)
     coarse_residual(coarse, NEAR, NEAR + depth // 2, sizes[5], fields2, corr2, sums)
     count3 = depth // 4
     rhs3 = in_lanes(sums[0:count3], down2)
@@ -405,61 +403,74 @@
     for row in range(ROWS):
         first = jnp.where(lane == row, rhs3[:, row, :], first)
         first = jnp.where(lane == ROWS + row, fluid3[:, row, :], first)
-        second = jnp.where(lane == row, pin3[:, row, :], second)
-    packed[0:count3] = first
-    packed[count3 : 2 * count3] = second
-    lane = iota((ROWS, LANES), 1)
-    packed[2 * count3 :] = jnp.where(
-        lane < LANES // 2, corr2[NEAR + depth // 2 - 5], corr2[NEAR + 4]
-    )
+        second = jnp.where(lane % ROWS == row, pin3[:, row, :], second)
+    packed[0] = first[0:2]
+    packed[1] = first[2:4]
+    packed[2] = jnp.where(lane[0:2] < ROWS, second[0:2], second[2:4])
+    lane = iota((1, LANES), 1) // (LANES // 4)
+    for index, plane in enumerate((NEAR + depth // 2 - 5, NEAR + 4)):
+        for half in range(2):
+            row = jnp.zeros((1, LANES), F32)
+            for quarter in range(4):
+                at = half * 4 + quarter
+                row = jnp.where(lane == quarter, corr2[plane, at : at + 1, :], row)
+            packed[3 + index, half : half + 1, :] = row
+
+
+def rolled(field, shift):
+    count = field.shape[0]
+    shift %= count
+    if shift % ROWS:
+        return pltpu.roll(field, shift, 0)
+    return jnp.concatenate([field[count - shift :], field[: count - shift]], axis=0)
 
 
 def columns(rhs, fluid, pin):
-    shape = fluid.shape
-    depth = shape[2]
-    lane, y = iota(shape, 2), iota(shape, 1)
-    edge = jnp.zeros((1,) + shape[1:], F32)
-    wz = jnp.where(lane == depth - 1, 0.0, mean_of(fluid, pltpu.roll(fluid, depth - 1, 2), 4.0))
-    wy = jnp.where(y == ROWS - 1, 0.0, mean_of(fluid, pltpu.roll(fluid, ROWS - 1, 1), 4.0))
-    wx = jnp.concatenate([mean_of(fluid[:-1], fluid[1:], 4.0), edge], axis=0)
-    back_x = jnp.concatenate([edge, wx[:-1]], axis=0)
-    across = (wx + back_x) + (wy + pltpu.roll(wy, 1, 1)) + pin
-    share = 1.0 / jnp.sum(across, axis=2, keepdims=True)
-
-    above, below, own = pltpu.roll(wz, 1, 2), wz, across
+    depth = fluid.shape[0]
+    z, lane = iota(fluid.shape, 0), iota(fluid.shape, 1)
+    y, x = lane % ROWS, (lane // ROWS) % ROWS
+
+    def next_x(field):
+        return pltpu.roll(field, LANES - ROWS, 1)
+
+    def next_y(field):
+        return pltpu.roll(field, LANES - 1, 1)
+
+    wz = jnp.where(z == depth - 1, 0.0, mean_of(fluid, rolled(fluid, -1), 4.0))
+    wy = jnp.where(y == ROWS - 1, 0.0, mean_of(fluid, next_y(fluid), 4.0))
+    wx = jnp.where(x == ROWS - 1, 0.0, mean_of(fluid, next_x(fluid), 4.0))
+    across = (wx + pltpu.roll(wx, ROWS, 1)) + (wy + pltpu.roll(wy, 1, 1)) + pin
+    share = 1.0 / jnp.sum(across, axis=0, keepdims=True)
+
+    above, below, own = rolled(wz, 1), wz, across
     steps = []
     stride = 1
     while stride < depth:
         inverse = 1.0 / (above + below + own)
-        up = above * pltpu.roll(inverse, stride, 2)
-        down = below * pltpu.roll(inverse, depth - stride, 2)
-        own = own + up * pltpu.roll(own, stride, 2) + down * pltpu.roll(own, depth - stride, 2)
-        above = up * pltpu.roll(above, stride, 2)
-        below = down * pltpu.roll(below, depth - stride, 2)
+        up = above * rolled(inverse, stride)
+        down = below * rolled(inverse, -stride)
+        own = own + up * rolled(own, stride) + down * rolled(own, -stride)
+        above = up * rolled(above, stride)
+        below = down * rolled(below, -stride)
         steps.append((stride, up, down))
         stride *= 2
     inverse = 1.0 / (above + below + own)
 
     def solve(right):
-        mean = jnp.sum(right, axis=2, keepdims=True) * share
+        mean = jnp.sum(right, axis=0, keepdims=True) * share
         for stride, up, down in steps:
-            right = (
-                right
-                + up * pltpu.roll(right, stride, 2)
-                + down * pltpu.roll(right, depth - stride, 2)
-            )
+            right = right + up * rolled(right, stride) + down * rolled(right, -stride)
         return right * inverse + mean
 
     corr = solve(rhs)
-    flow_x = wx[:-1] * (corr[1:] - corr[:-1])
-    flow_x = jnp.concatenate([flow_x, edge], 0) - jnp.concatenate([edge, flow_x], 0)
-    flow_y = wy * (pltpu.roll(corr, ROWS - 1, 1) - corr)
-    flow_z = wz * (pltpu.roll(corr, depth - 1, 2) - corr)
+    flow_x = wx * (next_x(corr) - corr)
+    flow_y = wy * (next_y(corr) - corr)
+    flow_z = wz * (rolled(corr, -1) - corr)
     rest = (
         (rhs - pin * corr)
-        + flow_x
+        + (flow_x - pltpu.roll(flow_x, ROWS, 1))
         + (flow_y - pltpu.roll(flow_y, 1, 1))
-        + (flow_z - pltpu.roll(flow_z, 1, 2))
+        + (flow_z - rolled(flow_z, 1))
     )
     return corr + solve(rest)
 
@@ -470,20 +481,32 @@
     rhs1, pin1, wx1, wy1, wz1, gain1, corr1,
     rhs2, pin2, wx2, wy2, wz2, gain2, corr2,
     out_ref,
-    one1, two1, one2, two2, lifted,
+    one1, two1, one2, two2, lifted, first, second, solved,
 ):
     count3 = depth // 4
     shares = packed.shape[0]
     peers = SPLIT[0] * SPLIT[1]
     slabs = sorted(range(shares), key=lambda i: (i // peers, rank_of(i % peers)))
-    first = jnp.concatenate([packed[i, 0:count3] for i in slabs], axis=0).T
-    second = jnp.concatenate([packed[i, count3 : 2 * count3] for i in slabs], axis=0).T
-    cells = ROWS * ROWS
-    total3 = shares * count3
-    shape3 = (ROWS, ROWS, total3)
-    corr3 = columns(
-        first[:cells].reshape(shape3), first[cells:].reshape(shape3), second[:cells].reshape(shape3)
-    ).reshape(cells, total3)
+    for slab, index in enumerate(slabs):
+        row = slab * count3
+        first[row : row + 2] = packed[index, 0]
+        first[row + 2 : row + 4] = packed[index, 1]
+        both = packed[index, 2]
+        second[row : row + 2] = both
+        second[row + 2 : row + 4] = pltpu.roll(both, LANES // 2, 1)
+    half = iota((shares * count3, LANES), 1) < LANES // 2
+
+    def low_half(field):
+        return jnp.where(half, field, pltpu.roll(field, LANES // 2, 1))
+
+    def high_half(field):
+        return jnp.where(half, pltpu.roll(field, LANES // 2, 1), field)
+
+    solved[NEAR : NEAR + shares * count3] = columns(
+        low_half(first[...]), high_half(first[...]), low_half(second[...])
+    )
+    solved[0:NEAR] = jnp.zeros((NEAR, LANES), F32)
+    solved[NEAR + shares * count3 :] = jnp.zeros((2 * NEAR, LANES), F32)
 
     def slab_of(index):
         index = jnp.clip(index, 0, shares - 1)
@@ -496,17 +519,16 @@
     ix, iy = lax.axis_index("gx"), lax.axis_index("gy")
     along = jnp.where(lax.rem(ix, 2) == 1, ny - 1 - iy, iy)
     part = (lax.axis_index("gz") * nx + ix) * ny + along
-    mine = pltpu.roll(corr3, lax.rem(NEAR - part * count3 + total3, total3), 1)
-    tall = jnp.concatenate([mine, mine], axis=0).T
     count = count3 + 2 * NEAR
+    tall = solved[pl.ds(part * count3, count + count3), :]
     fine, coarse = Level(0), Level(1)
     cell = iota((LANES, ROWS * LANES), 0)
     lane = iota((LANES, ROWS * LANES), 1)
     same_y = cell % ROWS == (lane % coarse.ny) // 2
     spread = where01((cell // ROWS == lane // LANES) & same_y)
-    wide = dot01(tall[0:count], spread)
+    wide = dot01(tall, spread)
     for row in range(ROWS):
-        lifted[0:count, row, :] = wide[:, row * LANES : (row + 1) * LANES]
+        lifted[0:count, row, :] = wide[:count, row * LANES : (row + 1) * LANES]
 
     fields1 = (rhs1, pin1, wx1, wy1, wz1)
     fields2 = (rhs2, pin2, wx2, wy2, wz2)
@@ -514,11 +536,20 @@
     parents = lifted[low // 2 + NEAR // 2 : high // 2 + NEAR // 2]
     twice = jnp.broadcast_to(parents[:, None], (parents.shape[0], 2, ROWS, LANES))
     reach = depth // 2 + NEAR
-    half = iota((ROWS, LANES), 1) < LANES // 2
-    before = packed[slab_of(part - 1), 2 * count3 :]
-    after = packed[slab_of(part + 1), 2 * count3 :]
-    before = jnp.where(half, before, pltpu.roll(before, LANES // 2, 1))
-    after = jnp.where(half, pltpu.roll(after, LANES // 2, 1), after)
+    quarter = iota((ROWS, LANES), 1) // (LANES // 4)
+    row = iota((ROWS, LANES), 0)
+
+    def unpacked(index, which):
+        pair = packed[slab_of(index), which]
+        total = None
+        for shift in range(4):
+            moved = pltpu.roll(pair, shift * (LANES // 4), 1)
+            wide = jnp.where(row < 4, moved[0:1, :], moved[1:2, :])
+            kept = jnp.where((quarter - shift) % 4 == row % 4, wide, 0.0)
+            total = kept if total is None else total + kept
+        return total
+
+    before, after = unpacked(part - 1, 3), unpacked(part + 1, 4)
     one2[low - 1] = before + lifted[(low - 1) // 2 + NEAR // 2]
     one2[low:high] = corr2[low:high] + twice.reshape(high - low, ROWS, LANES)
     one2[high] = after + lifted[high // 2 + NEAR // 2]
@@ -615,17 +646,19 @@
     saved = (blocks(planes, ROWS),) * 7 + (blocks(count2, ROWS),) * 7
     results = pl.pallas_call(
         functools.partial(down_kernel, groups, by, share, sizes),
-        out_shape=saved + (flat(share // 2 + ROWS),),
+        out_shape=saved + (blocks(5, 2),),
         scratch_shapes=[room(planes), room(planes), room(count2), room(count2), room(count2)],
         compiler_params=limit,
         name="down",
     )(low, own, high)
     copies = jnp.broadcast_to(results[-1], (parts,) + results[-1].shape)
     packed = lax.all_to_all(copies, ("gz", "gx", "gy"), 0, 0, tiled=True)
+    depth3 = parts * share // 4
     mine = pl.pallas_call(
         functools.partial(up_kernel, groups, by, share, sizes),
         out_shape=blocks(peers, share),
-        scratch_shapes=[room(planes), room(planes), room(count2), room(count2), room(count2)],
+        scratch_shapes=[room(planes), room(planes), room(count2), room(count2), room(count2)]
+        + [pltpu.VMEM((rows, LANES), F32) for rows in (depth3, depth3, depth3 + 3 * NEAR)],
         compiler_params=limit,
         name="up",
     )(packed, *results[:-1])

time: 59 us -> 56.1 us (0.951)
  blocking collectives: 40 us -> 38.1 us
  Pallas kernels: 8.51 us -> 7.52 us
    all_to_all x1, blocking collectives: 14.6 us -> 12.1 us  [whole_planes(): packed = lax.all_to_all(copies, ('gz', 'gx', 'gy'), 0, 0, tiled=True)]
    pallas_call x1, Pallas kernels: 3.44 us -> 2.48 us  [whole_planes(): pl.pallas_call(functools.partial(up_kernel, groups, by, share, sizes), ou...]
    all_to_all x1, blocking collectives: 9.6 us -> 10.2 us  [whole_planes(): lax.all_to_all(mine, ('gx', 'gy'), 0, 0, tiled=True)]
where the time goes in v6:
time: 56.1 us; the launch traced here: 55.8 us
  blocking collectives  38.1 us (68%)
  Pallas kernels  7.52 us (13%)
  starting transfers between devices  5.85 us (10%)
  waiting for transfers between devices  3.24 us (6%)
  other arithmetic  0.93 us (2%)
    all_to_all x1, blocking collectives, whole_planes(): lax.all_to_all(parcels, ('gx', 'gy'), 0, 0, tiled=True)  15.8 us
    all_to_all x1, blocking collectives, whole_planes(): packed = lax.all_to_all(copies, ('gz', 'gx', 'gy'), 0, 0, tiled=True)  12.1 us
    all_to_all x1, blocking collectives, whole_planes(): lax.all_to_all(mine, ('gx', 'gy'), 0, 0, tiled=True)  10.2 us
    ppermute x2, starting transfers between devices, step(): return lax.ppermute(field, ('gx', 'gy', 'gz'), pairs)  5.85 us
    pallas_call x1, Pallas kernels, whole_planes(): pl.pallas_call(functools.partial(down_kernel, groups, by, share, sizes),...  3.39 us
    ppermute x2, waiting for transfers between devices, step(): return lax.ppermute(field, ('gx', 'gy', 'gz'), pairs)  3.24 us
    pallas_call x1, Pallas kernels, whole_planes(): pl.pallas_call(functools.partial(up_kernel, groups, by, share, sizes), ou...  2.48 us
  transfers between devices with their start and end apart: 2, of which 2 were waited for; matrix products, arithmetic and copies ran while one was open for 0% of the time, Pallas kernels for 0%

profile of v6, /device:TPU:0, one launch (start us, length us, event | category | flops | bytes accessed | tf_op | source)
XLA Modules:
  0.0 55.8 jit_solution(13259010105974791115)
XLA Ops:
  0.0 0.0 copy-start
  0.0 0.9 %multiply_multiply_fusion = (f32[16,8,128]{2,1,0:T(8,128)S(1)}, f32[16,8,128]{2,1,0:T(8,128)S(1)}) fusion(s32[16,8,128]{2,1,0:T(8,128)} %param.5, f32[16,8,128]{2,1,0:T(8,128)} %param.4), kind=kLoop, calls=%fused_computation | loop fusion | flops 65536 | bytes 262144 | tf_op jit(solution)/shard_map/mul | solution.py:623
  0.9 0.1 copy-done
  1.0 0.5 prepare.1
  1.5 15.8 %all_to_all.15.gathered = f32[8,48,128]{2,1,0:T(8,128)S(1)} all-to-all(f32[8,48,128]{2,1,0:T(8,128)S(1)} %prepare.1), channel_id=1, replica_groups=mesh['gx'=2,'gy'=4,'gz'=4] {'gx','gy'}, dimensions={0} | all-to-all | bytes 393216 | tf_op jit(solution)/shard_map/all_to_all | solution.py:635
  17.3 0.2 spread.1.own
  17.6 1.3 %collective-permute-start.1 = (f32[48,8,128]{2,1,0:T(8,128)S(1)}, f32[48,8,128]{2,1,0:T(8,128)S(1)}, u32[]{:S(2)}, u32[]{:S(2)}) collective-permute-start(f32[48,8,128]{2,1,0:T(8,128)S(1)} %spread.1.own), channel_id=1, source_target_pairs={{4,0},{8,4},{12,8},{28,12},{24,28},{20,24},{16,20},{1,16},{5,1},{9... | collective-permute-start | bytes 589832 | tf_op jit(solution)/shard_map/ppermute | solution.py:643
  18.9 4.6 %collective-permute-start = (f32[48,8,128]{2,1,0:T(8,128)S(1)}, f32[48,8,128]{2,1,0:T(8,128)S(1)}, u32[]{:S(2)}, u32[]{:S(2)}) collective-permute-start(f32[48,8,128]{2,1,0:T(8,128)S(1)} %spread.1.own), channel_id=1, source_target_pairs={{0,4},{4,8},{8,12},{12,28},{28,24},{24,20},{20,16},{16,1},{1,5},{5... | collective-permute-start | bytes 589832 | tf_op jit(solution)/shard_map/ppermute | solution.py:643
  23.4 1.7 %collective-permute-done.1.high = f32[48,8,128]{2,1,0:T(8,128)S(1)} collective-permute-done((f32[48,8,128]{2,1,0:T(8,128)S(1)}, f32[48,8,128]{2,1,0:T(8,128)S(1)}, u32[]{:S(2)}, u32[]{:S(2)}) %collective-permute-start.1) | collective-permute-done | bytes 196640 | tf_op jit(solution)/shard_map/ppermute | solution.py:643
  25.1 1.5 %collective-permute-done.low = f32[48,8,128]{2,1,0:T(8,128)S(1)} collective-permute-done((f32[48,8,128]{2,1,0:T(8,128)S(1)}, f32[48,8,128]{2,1,0:T(8,128)S(1)}, u32[]{:S(2)}, u32[]{:S(2)}) %collective-permute-start) | collective-permute-done | bytes 196640 | tf_op jit(solution)/shard_map/ppermute | solution.py:643
  26.7 3.4 %down.1 = (f32[48,8,128]{2,1,0:T(8,128)S(1)}, f32[48,8,128]{2,1,0:T(8,128)S(1)}, f32[48,8,128]{2,1,0:T(8,128)S(1)}, f32[48,8,128]{2,1,0:T(8,128)S(1)}, f32[48,8,...) custom-call(f32[48,8,128]{2,1,0:T(8,128)S(1)} %collective-permute-do, ...), custom_call_target="tpu_custom_call" | custom-call | tf_op jit(solution)/shard_map/down/pallas_call | solution.py:647
  30.1 12.1 %all_to_all.16.packed = f32[32,5,2,128]{3,2,1,0:T(2,128)S(1)} all-to-all(f32[32,5,2,128]{3,2,1,0:T(2,128)S(1)} %broadcast_in_dim.3), channel_id=1, replica_groups=mesh['gx'=2,'gy'=4,'gz'=4] {'gz','gx','gy'}, dimensions={0} | all-to-all | bytes 327680 | tf_op jit(solution)/shard_map/all_to_all | solution.py:655
  42.2 2.5 %up.1 = f32[8,16,128]{2,1,0:T(8,128)S(1)} custom-call(f32[32,5,2,128]{3,2,1,0:T(2,128)S(1)} %all_to_all.16.packed, f32[48,8,128]{2,1,0:T(8,128)S(1)} %get-tuple-element.21.rhs1, f32[48,8,128]{2,1,0:T(8,128)S(1)} %get-tuple-element.22.pin1, f32[48,8,128]{2,1,0:T(8,128)S(1)} %get-tuple-element.23.wx1, f32[48,8,128]{2,1,0:T(8,128)S(1)} %get-tuple-element.24.wy1, ...), custom_call_target="tpu_custom_call" | custom-call | tf_op jit(solution)/shard_map/up/pallas_call | solution.py:657
  44.7 10.2 %all_to_all.17.blocks = f32[8,16,128]{2,1,0:T(8,128)S(1)} all-to-all(f32[8,16,128]{2,1,0:T(8,128)S(1)} %up.1), channel_id=1, replica_groups=mesh['gx'=2,'gy'=4,'gz'=4] {'gx','gy'}, dimensions={0} | all-to-all | bytes 131072 | tf_op jit(solution)/shard_map/all_to_all | solution.py:670
  54.9 0.9 %finish.1 = f32[16,8,128]{2,1,0:T(8,128)} custom-call(f32[8,16,128]{2,1,0:T(8,128)S(1)} %all_to_all.17.blocks), custom_call_target="tpu_custom_call" | custom-call | tf_op jit(solution)/shard_map/finish/pallas_call | solution.py:665
  (1 shorter events, 0.0 us)
Async XLA Ops:
  0.0 1.0 %copy-start = (bf16[32,16,256]{2,1,0:T(8,128)(2,1)S(1)}, bf16[32,16,256]{2,1,0:T(8,128)(2,1)}, u32[]{:S(2)}) copy-start(bf16[32,16,256]{2,1,0:T(8,128)(2,1)} %param.3) | copy-start | bytes 786436
  17.6 7.6 %collective-permute-start.1 = (f32[48,8,128]{2,1,0:T(8,128)S(1)}, f32[48,8,128]{2,1,0:T(8,128)S(1)}, u32[]{:S(2)}, u32[]{:S(2)}) collective-permute-start(f32[48,8,128]{2,1,0:T(8,128)S(1)} %spread.1.own), channel_id=1, source_target_pairs={{4,0},{8,4},{12,8},{28,12},{24,28},{20,24},{16,20},{1,16},{5,1},{9... | collective-permute-start | bytes 589832 | tf_op jit(solution)/shard_map/ppermute | solution.py:643
  18.9 7.8 %collective-permute-start = (f32[48,8,128]{2,1,0:T(8,128)S(1)}, f32[48,8,128]{2,1,0:T(8,128)S(1)}, u32[]{:S(2)}, u32[]{:S(2)}) collective-permute-start(f32[48,8,128]{2,1,0:T(8,128)S(1)} %spread.1.own), channel_id=1, source_target_pairs={{0,4},{4,8},{8,12},{12,28},{28,24},{24,20},{20,16},{16,1},{1,5},{5... | collective-permute-start | bytes 589832 | tf_op jit(solution)/shard_map/ppermute | solution.py:643

commit v7 on v6

--- a/solution.py
+++ b/solution.py
@@ -143,6 +143,8 @@
 LANES = 128
 HALO = 16
 NEAR = 8
+PIECE = 8
+TINY = 1e-30
 F32 = jnp.float32
 
 
@@ -162,22 +164,32 @@
     return total
 
 
+def dot10(chosen, field):
+    total = None
+    rest = field
+    for part in range(3):
+        piece = rest.astype(jnp.bfloat16)
+        term = lax.dot_general(
+            chosen, piece, (((1,), (1,)), ((), ())), preferred_element_type=F32
+        )
+        total = term if total is None else total + term
+        if part < 2:
+            rest = rest - piece.astype(F32)
+    return total
+
+
 def where01(condition):
     return jnp.where(condition, 1.0, 0.0).astype(jnp.bfloat16)
 
 
 def loop(low, high, size, body):
-    size = min(size, high - low)
-    steps = -(-(high - low) // size)
-
-    def step(index, carry):
-        body(jnp.minimum(low + index * size, high - size), size)
-        return carry
-
-    if steps == 1:
-        body(low, size)
-    else:
-        lax.fori_loop(0, steps, step, 0)
+    for plane in range(low, high, size):
+        body(plane, min(size, high - plane))
+
+
+def inverse_of(field):
+    first = pl.reciprocal(field, approx=True)
+    return first * (2.0 - field * first)
 
 
 class Level:
@@ -210,25 +222,23 @@
     def last_y(self, field):
         return pltpu.roll(field, 1, 2)
 
-    def balance(self, field, wx, wy, wz):
+    def spread(self, field, scaled, plane, count):
         mid = field[1:-1]
-        flow_x = wx * (self.next_x(mid) - mid)
-        flow_y = wy * (self.next_y(mid) - mid)
-        flow_z = wz * (field[1:] - field[:-1])
-        return (
-            (flow_x - self.last_x(flow_x))
-            + (flow_y - self.last_y(flow_y))
-            + (flow_z[1:] - flow_z[:-1])
+        near = (
+            self.next_x(mid), self.last_x(mid), self.next_y(mid), self.last_y(mid),
+            field[2:], field[:-2],
         )
+        terms = [weight[pl.ds(plane, count)] * value for weight, value in zip(scaled, near)]
+        return mid, ((terms[0] + terms[1]) + (terms[2] + terms[3])) + (terms[4] + terms[5])
 
 
 def mean_of(fluid, near, factor):
-    total = fluid + near
-    safe = jnp.where(total > 0, total, 1.0)
-    return jnp.where(total > 0, (factor * 2.0) * fluid * near / safe, 0.0)
-
-
-def set_level(level, low, high, size, fluid, pin, rhs, wx, wy, wz, gain, corr):
+    return ((factor * 2.0) * fluid * near) * inverse_of(jnp.maximum(fluid + near, TINY))
+
+
+def set_level(level, low, high, fluid, pin, rhs, fields):
+    scaled, start, diag = fields
+
     def body(plane, count):
         wide = fluid[pl.ds(plane - 1, count + 2)]
         mid = wide[1:-1]
@@ -236,40 +246,30 @@
         to_x = jnp.where(end_x, 0.0, mean_of(mid, level.next_x(mid), level.factor))
         to_y = jnp.where(end_y, 0.0, mean_of(mid, level.next_y(mid), level.factor))
         to_z = mean_of(wide[:-1], wide[1:], level.factor)
-        diag = (
-            (to_x + level.last_x(to_x))
-            + (to_y + level.last_y(to_y))
-            + (to_z[1:] + to_z[:-1])
+        weights = (to_x, level.last_x(to_x), to_y, level.last_y(to_y), to_z[1:], to_z[:-1])
+        total = (
+            (weights[0] + weights[1])
+            + (weights[2] + weights[3])
+            + (weights[4] + weights[5])
             + pin[pl.ds(plane, count)]
         )
-        some = diag > 0
-        scale = jnp.where(some, OMEGA / jnp.where(some, diag, 1.0), 0.0)
-        wx[pl.ds(plane, count)] = to_x
-        wy[pl.ds(plane, count)] = to_y
-        wz[pl.ds(plane, count)] = to_z[1:]
-        gain[pl.ds(plane, count)] = scale
-        if corr is not None:
-            corr[pl.ds(plane, count)] = scale * rhs[pl.ds(plane, count)]
-
-    loop(low, high, size, body)
-
-
-def residual_of(level, plane, count, fields, corr):
-    rhs, pin, wx, wy, wz = fields
-    field = corr[pl.ds(plane - 1, count + 2)]
-    spread = level.balance(
-        field, wx[pl.ds(plane, count)], wy[pl.ds(plane, count)], wz[pl.ds(plane - 1, count + 1)]
-    )
-    mid = field[1:-1]
-    return mid, (rhs[pl.ds(plane, count)] - pin[pl.ds(plane, count)] * mid) + spread
-
-
-def sweep(level, low, high, size, fields, gain, source, target):
+        gain = OMEGA * inverse_of(jnp.maximum(total, TINY))
+        for target, weight in zip(scaled, weights):
+            target[pl.ds(plane, count)] = gain * weight
+        start[pl.ds(plane, count)] = gain * rhs[pl.ds(plane, count)]
+        diag[pl.ds(plane, count)] = total
+
+    loop(low, high, PIECE, body)
+
+
+def sweep(level, low, high, fields, source, target):
+    scaled, start, _ = fields
+
     def body(plane, count):
-        mid, rest = residual_of(level, plane, count, fields, source)
-        target[pl.ds(plane, count)] = mid + gain[pl.ds(plane, count)] * rest
-
-    loop(low, high, size, body)
+        mid, total = level.spread(source[pl.ds(plane - 1, count + 2)], scaled, plane, count)
+        target[pl.ds(plane, count)] = (1.0 - OMEGA) * mid + (start[pl.ds(plane, count)] + total)
+
+    loop(low, high, PIECE, body)
 
 
 def pair_sum(field):
@@ -277,15 +277,16 @@
     return half[:, 0] + half[:, 1]
 
 
-def coarse_residual(level, low, high, size, fields, corr, target):
-    size = min(size, high - low)
-    assert (high - low) % size == 0 and size % 2 == 0
+def coarse_residual(level, low, high, fields, corr, target):
+    scaled, start, diag = fields
 
     def body(plane, count):
-        _, rest = residual_of(level, plane, count, fields, corr)
+        mid, total = level.spread(corr[pl.ds(plane - 1, count + 2)], scaled, plane, count)
+        rest = (start[pl.ds(plane, count)] + total) - OMEGA * mid
+        rest = rest * (diag[pl.ds(plane, count)] * (1.0 / OMEGA))
         target[pl.ds((plane - low) // 2, count // 2)] = pair_sum(rest)
 
-    loop(low, high, size, body)
+    loop(low, high, PIECE, body)
 
 
 def lanes_down(level):
@@ -356,12 +357,12 @@
 
 
 def down_kernel(
-    groups, by, depth, sizes,
+    groups, by, depth,
     low, own, high,
-    rhs1, pin1, wx1, wy1, wz1, gain1, corr1,
-    rhs2, pin2, wx2, wy2, wz2, gain2, corr2,
+    xn1, xl1, yn1, yl1, zn1, zl1, start1, diag1, corr1,
+    xn2, xl2, yn2, yl2, zn2, zl2, start2, diag2, corr2,
     packed,
-    fluid1, other1, fluid2, other2, sums,
+    fluid1, rhs1, pin1, other1, fluid2, rhs2, pin2, other2, sums,
 ):
     planes = depth + 2 * HALO
     for index, target in enumerate((fluid1, rhs1, pin1)):
@@ -373,11 +374,11 @@
 
     fine, coarse = Level(0), Level(1)
     down1, down2 = lanes_down(0), lanes_down(1)
-    fields1 = (rhs1, pin1, wx1, wy1, wz1)
-    fields2 = (rhs2, pin2, wx2, wy2, wz2)
-    set_level(fine, 1, planes - 1, sizes[0], fluid1, pin1, rhs1, wx1, wy1, wz1, gain1, corr1)
-    sweep(fine, 2, planes - 2, sizes[1], fields1, gain1, corr1, other1)
-    sweep(fine, 3, planes - 3, sizes[1], fields1, gain1, other1, corr1)
+    fields1 = ((xn1, xl1, yn1, yl1, zn1, zl1), start1, diag1)
+    fields2 = ((xn2, xl2, yn2, yl2, zn2, zl2), start2, diag2)
+    set_level(fine, 1, planes - 1, fluid1, pin1, rhs1, fields1)
+    sweep(fine, 2, planes - 2, fields1, start1, other1)
+    sweep(fine, 3, planes - 3, fields1, other1, corr1)
     count2 = depth // 2 + 2 * NEAR
     begin = HALO - 2 * NEAR
     for source, target, share in ((fluid1, fluid2, 8.0), (pin1, pin2, 4.0)):
@@ -385,14 +386,12 @@
         target[...] = in_lanes(whole, down1) * (1.0 / share)
     low2, high2 = (begin + 4) // 2, count2 - (begin + 4) // 2
     inner = high2 - low2
-    coarse_residual(
-        fine, begin + 2 * low2, begin + 2 * high2, sizes[2], fields1, corr1, sums
-    )
+    coarse_residual(fine, begin + 2 * low2, begin + 2 * high2, fields1, corr1, sums)
     rhs2[low2:high2] = in_lanes(sums[0:inner], down1)
-    set_level(coarse, low2, high2, sizes[3], fluid2, pin2, rhs2, wx2, wy2, wz2, gain2, corr2)
-    sweep(coarse, low2 + 1, high2 - 1, sizes[4], fields2, gain2, corr2, other2)
-    sweep(coarse, low2 + 2, high2 - 2, sizes[4], fields2, gain2, other2, corr2)
-    coarse_residual(coarse, NEAR, NEAR + depth // 2, sizes[5], fields2, corr2, sums)
+    set_level(coarse, low2, high2, fluid2, pin2, rhs2, fields2)
+    sweep(coarse, low2 + 1, high2 - 1, fields2, start2, other2)
+    sweep(coarse, low2 + 2, high2 - 2, fields2, other2, corr2)
+    coarse_residual(coarse, NEAR, NEAR + depth // 2, fields2, corr2, sums)
     count3 = depth // 4
     rhs3 = in_lanes(sums[0:count3], down2)
     fluid3 = in_lanes(pair_sum(fluid2[NEAR : NEAR + 2 * count3]), down2) * 0.125
@@ -446,7 +445,7 @@
     steps = []
     stride = 1
     while stride < depth:
-        inverse = 1.0 / (above + below + own)
+        inverse = inverse_of(above + below + own)
         up = above * rolled(inverse, stride)
         down = below * rolled(inverse, -stride)
         own = own + up * rolled(own, stride) + down * rolled(own, -stride)
@@ -454,7 +453,7 @@
         below = down * rolled(below, -stride)
         steps.append((stride, up, down))
         stride *= 2
-    inverse = 1.0 / (above + below + own)
+    inverse = inverse_of(above + below + own)
 
     def solve(right):
         mean = jnp.sum(right, axis=0, keepdims=True) * share
@@ -476,10 +475,10 @@
 
 
 def up_kernel(
-    groups, by, depth, sizes,
+    groups, by, depth,
     packed,
-    rhs1, pin1, wx1, wy1, wz1, gain1, corr1,
-    rhs2, pin2, wx2, wy2, wz2, gain2, corr2,
+    xn1, xl1, yn1, yl1, zn1, zl1, start1, diag1, corr1,
+    xn2, xl2, yn2, yl2, zn2, zl2, start2, diag2, corr2,
     out_ref,
     one1, two1, one2, two2, lifted, first, second, solved,
 ):
@@ -530,8 +529,8 @@
     for row in range(ROWS):
         lifted[0:count, row, :] = wide[:count, row * LANES : (row + 1) * LANES]
 
-    fields1 = (rhs1, pin1, wx1, wy1, wz1)
-    fields2 = (rhs2, pin2, wx2, wy2, wz2)
+    fields1 = ((xn1, xl1, yn1, yl1, zn1, zl1), start1, diag1)
+    fields2 = ((xn2, xl2, yn2, yl2, zn2, zl2), start2, diag2)
     low, high = NEAR - 4, NEAR + depth // 2 + 4
     parents = lifted[low // 2 + NEAR // 2 : high // 2 + NEAR // 2]
     twice = jnp.broadcast_to(parents[:, None], (parents.shape[0], 2, ROWS, LANES))
@@ -553,9 +552,9 @@
     one2[low - 1] = before + lifted[(low - 1) // 2 + NEAR // 2]
     one2[low:high] = corr2[low:high] + twice.reshape(high - low, ROWS, LANES)
     one2[high] = after + lifted[high // 2 + NEAR // 2]
-    sweep(coarse, NEAR - 4, reach + 4, sizes[4], fields2, gain2, one2, two2)
-    sweep(coarse, NEAR - 3, reach + 3, sizes[4], fields2, gain2, two2, one2)
-    sweep(coarse, NEAR - 2, reach + 2, sizes[4], fields2, gain2, one2, two2)
+    sweep(coarse, NEAR - 4, reach + 4, fields2, one2, two2)
+    sweep(coarse, NEAR - 3, reach + 3, fields2, two2, one2)
+    sweep(coarse, NEAR - 2, reach + 2, fields2, one2, two2)
 
     fine_lane, coarse_lane = iota((LANES, LANES), 1), iota((LANES, LANES), 0)
     x_of = (fine_lane // fine.ny) // 2
@@ -567,15 +566,14 @@
     low, high = HALO - 4, HALO + depth + 4
     one1[low:high] = corr1[low:high] + twice.reshape(high - low, ROWS, LANES)
     reach = depth + HALO
-    sweep(fine, HALO - 2, reach + 2, sizes[1], fields1, gain1, one1, two1)
-    sweep(fine, HALO - 1, reach + 1, sizes[1], fields1, gain1, two1, one1)
-    sweep(fine, HALO, reach, sizes[1], fields1, gain1, one1, two1)
+    sweep(fine, HALO - 2, reach + 2, fields1, one1, two1)
+    sweep(fine, HALO - 1, reach + 1, fields1, two1, one1)
+    sweep(fine, HALO, reach, fields1, one1, two1)
 
     group = (iota((depth, LANES), 1) // by) % groups
     for ix in range(nx):
         scaled = [
-            two1[HALO:reach, ix * groups + part, :]
-            * (OMEGA / gain1[HALO:reach, ix * groups + part, :])
+            two1[HALO:reach, ix * groups + part, :] * diag1[HALO:reach, ix * groups + part, :]
             for part in range(groups)
         ]
         for iy in range(ny):
@@ -596,8 +594,7 @@
     chosen = where01((x % 4) * (bx // 4 * by) + (x // 4) * by + y == lane)
     peers = blocks.shape[0]
     ordered = jnp.concatenate([blocks[i] for i in sorted(range(peers), key=rank_of)], axis=0)
-    turned = dot01(ordered, chosen, (((1,), (1,)), ((), ())))
-    out_ref[...] = turned.T.reshape(out_ref.shape)
+    out_ref[...] = dot10(chosen, ordered).reshape(out_ref.shape)
 
 
 def whole_planes(residual_q2, viscosity, pinned):
@@ -607,7 +604,6 @@
     share = depth // peers
     planes = share + 2 * HALO
     count2 = share // 2 + 2 * NEAR
-    sizes = (23, 22, 20, 10, 24, 24)
     limit = pltpu.CompilerParams(vmem_limit_bytes=32 * 2**20)
 
     def flat(rows):
@@ -643,11 +639,11 @@
         return lax.ppermute(field, ("gx", "gy", "gz"), pairs)
 
     low, high = step(own, 1), step(own, -1)
-    saved = (blocks(planes, ROWS),) * 7 + (blocks(count2, ROWS),) * 7
+    saved = (blocks(planes, ROWS),) * 9 + (blocks(count2, ROWS),) * 9
     results = pl.pallas_call(
-        functools.partial(down_kernel, groups, by, share, sizes),
+        functools.partial(down_kernel, groups, by, share),
         out_shape=saved + (blocks(5, 2),),
-        scratch_shapes=[room(planes), room(planes), room(count2), room(count2), room(count2)],
+        scratch_shapes=[room(planes)] * 4 + [room(count2)] * 5,
         compiler_params=limit,
         name="down",
     )(low, own, high)
@@ -655,7 +651,7 @@
     packed = lax.all_to_all(copies, ("gz", "gx", "gy"), 0, 0, tiled=True)
     depth3 = parts * share // 4
     mine = pl.pallas_call(
-        functools.partial(up_kernel, groups, by, share, sizes),
+        functools.partial(up_kernel, groups, by, share),
         out_shape=blocks(peers, share),
         scratch_shapes=[room(planes), room(planes), room(count2), room(count2), room(count2)]
         + [pltpu.VMEM((rows, LANES), F32) for rows in (depth3, depth3, depth3 + 3 * NEAR)],

time: 56.1 us -> 54.1 us (0.964)
  Pallas kernels: 7.52 us -> 5.58 us
    pallas_call x2, Pallas kernels: 5.86 us -> 4.03 us  [the longest x1 2.09 us: whole_planes(): pl.pallas_call(functools.partial(up_kernel, groups, by, share), out_shape...]
where the time goes in v7:
time: 54.1 us; the launch traced here: 53.9 us
  blocking collectives  38.1 us (70%)
  starting transfers between devices  5.85 us (11%)
  Pallas kernels  5.58 us (10%)
  waiting for transfers between devices  3.24 us (6%)
  other arithmetic  0.93 us (2%)
    all_to_all x1, blocking collectives, whole_planes(): lax.all_to_all(parcels, ('gx', 'gy'), 0, 0, tiled=True)  15.8 us
    all_to_all x1, blocking collectives, whole_planes(): packed = lax.all_to_all(copies, ('gz', 'gx', 'gy'), 0, 0, tiled=True)  12.1 us
    all_to_all x1, blocking collectives, whole_planes(): lax.all_to_all(mine, ('gx', 'gy'), 0, 0, tiled=True)  10.2 us
    ppermute x2, starting transfers between devices, step(): return lax.ppermute(field, ('gx', 'gy', 'gz'), pairs)  5.85 us
    ppermute x2, waiting for transfers between devices, step(): return lax.ppermute(field, ('gx', 'gy', 'gz'), pairs)  3.24 us
    pallas_call x1, Pallas kernels, whole_planes(): pl.pallas_call(functools.partial(up_kernel, groups, by, share), out_shape...  2.09 us
    pallas_call x1, Pallas kernels, whole_planes(): pl.pallas_call(functools.partial(down_kernel, groups, by, share), out_sha...  1.94 us
  transfers between devices with their start and end apart: 2, of which 2 were waited for; matrix products, arithmetic and copies ran while one was open for 0% of the time, Pallas kernels for 0%

profile of v7, /device:TPU:0, one launch (start us, length us, event | category | flops | bytes accessed | tf_op | source)
XLA Modules:
  0.0 53.9 jit_solution(8478225799685351957)
XLA Ops:
  0.0 0.0 copy-start
  0.0 0.9 %multiply_multiply_fusion = (f32[16,8,128]{2,1,0:T(8,128)S(1)}, f32[16,8,128]{2,1,0:T(8,128)S(1)}) fusion(s32[16,8,128]{2,1,0:T(8,128)} %param.5, f32[16,8,128]{2,1,0:T(8,128)} %param.4), kind=kLoop, calls=%fused_computation | loop fusion | flops 65536 | bytes 262144 | tf_op jit(solution)/shard_map/mul | solution.py:619
  0.9 0.1 copy-done
  1.0 0.5 prepare.1
  1.5 15.8 %all_to_all.15.gathered = f32[8,48,128]{2,1,0:T(8,128)S(1)} all-to-all(f32[8,48,128]{2,1,0:T(8,128)S(1)} %prepare.1), channel_id=1, replica_groups=mesh['gx'=2,'gy'=4,'gz'=4] {'gx','gy'}, dimensions={0} | all-to-all | bytes 393216 | tf_op jit(solution)/shard_map/all_to_all | solution.py:631
  17.3 0.2 spread.1.own
  17.6 1.3 %collective-permute-start.1 = (f32[48,8,128]{2,1,0:T(8,128)S(1)}, f32[48,8,128]{2,1,0:T(8,128)S(1)}, u32[]{:S(2)}, u32[]{:S(2)}) collective-permute-start(f32[48,8,128]{2,1,0:T(8,128)S(1)} %spread.1.own), channel_id=1, source_target_pairs={{4,0},{8,4},{12,8},{28,12},{24,28},{20,24},{16,20},{1,16},{5,1},{9... | collective-permute-start | bytes 589832 | tf_op jit(solution)/shard_map/ppermute | solution.py:639
  18.9 4.6 %collective-permute-start = (f32[48,8,128]{2,1,0:T(8,128)S(1)}, f32[48,8,128]{2,1,0:T(8,128)S(1)}, u32[]{:S(2)}, u32[]{:S(2)}) collective-permute-start(f32[48,8,128]{2,1,0:T(8,128)S(1)} %spread.1.own), channel_id=1, source_target_pairs={{0,4},{4,8},{8,12},{12,28},{28,24},{24,20},{20,16},{16,1},{1,5},{5... | collective-permute-start | bytes 589832 | tf_op jit(solution)/shard_map/ppermute | solution.py:639
  23.4 1.7 %collective-permute-done.1.high = f32[48,8,128]{2,1,0:T(8,128)S(1)} collective-permute-done((f32[48,8,128]{2,1,0:T(8,128)S(1)}, f32[48,8,128]{2,1,0:T(8,128)S(1)}, u32[]{:S(2)}, u32[]{:S(2)}) %collective-permute-start.1) | collective-permute-done | bytes 196640 | tf_op jit(solution)/shard_map/ppermute | solution.py:639
  25.1 1.5 %collective-permute-done.low = f32[48,8,128]{2,1,0:T(8,128)S(1)} collective-permute-done((f32[48,8,128]{2,1,0:T(8,128)S(1)}, f32[48,8,128]{2,1,0:T(8,128)S(1)}, u32[]{:S(2)}, u32[]{:S(2)}) %collective-permute-start) | collective-permute-done | bytes 196640 | tf_op jit(solution)/shard_map/ppermute | solution.py:639
  26.7 1.9 %down.1 = (f32[48,8,128]{2,1,0:T(8,128)S(1)}, f32[48,8,128]{2,1,0:T(8,128)S(1)}, f32[48,8,128]{2,1,0:T(8,128)S(1)}, f32[48,8,128]{2,1,0:T(8,128)S(1)}, f32[48,8,...) custom-call(f32[48,8,128]{2,1,0:T(8,128)S(1)} %collective-permute-do, ...), custom_call_target="tpu_custom_call" | custom-call | tf_op jit(solution)/shard_map/down/pallas_call | solution.py:643
  28.6 12.1 %all_to_all.16.packed = f32[32,5,2,128]{3,2,1,0:T(2,128)S(1)} all-to-all(f32[32,5,2,128]{3,2,1,0:T(2,128)S(1)} %broadcast_in_dim.3), channel_id=1, replica_groups=mesh['gx'=2,'gy'=4,'gz'=4] {'gz','gx','gy'}, dimensions={0} | all-to-all | bytes 327680 | tf_op jit(solution)/shard_map/all_to_all | solution.py:651
  40.7 2.1 %up.1 = f32[8,16,128]{2,1,0:T(8,128)S(1)} custom-call(f32[32,5,2,128]{3,2,1,0:T(2,128)S(1)} %all_to_all.16.packed, f32[48,8,128]{2,1,0:T(8,128)S(1)} %get-tuple-element.25.xn1, f32[48,8,128]{2,1,0:T(8,128)S(1)} %get-tuple-element.26.xl1, f32[48,8,128]{2,1,0:T(8,128)S(1)} %get-tuple-element.27.yn1, f32[48,8,128]{2,1,0:T(8,128)S(1)} %get-tuple-element.28.yl1, ...), custom_call_target="tpu_custom_call" | custom-call | tf_op jit(solution)/shard_map/up/pallas_call | solution.py:653
  42.8 10.2 %all_to_all.17.blocks = f32[8,16,128]{2,1,0:T(8,128)S(1)} all-to-all(f32[8,16,128]{2,1,0:T(8,128)S(1)} %up.1), channel_id=1, replica_groups=mesh['gx'=2,'gy'=4,'gz'=4] {'gx','gy'}, dimensions={0} | all-to-all | bytes 131072 | tf_op jit(solution)/shard_map/all_to_all | solution.py:666
  53.0 0.8 %finish.1 = f32[16,8,128]{2,1,0:T(8,128)} custom-call(f32[8,16,128]{2,1,0:T(8,128)S(1)} %all_to_all.17.blocks), custom_call_target="tpu_custom_call" | custom-call | tf_op jit(solution)/shard_map/finish/pallas_call | solution.py:661
  (1 shorter events, 0.0 us)
Async XLA Ops:
  0.0 1.0 %copy-start = (bf16[32,16,256]{2,1,0:T(8,128)(2,1)S(1)}, bf16[32,16,256]{2,1,0:T(8,128)(2,1)}, u32[]{:S(2)}) copy-start(bf16[32,16,256]{2,1,0:T(8,128)(2,1)} %param.3) | copy-start | bytes 786436
  17.6 7.6 %collective-permute-start.1 = (f32[48,8,128]{2,1,0:T(8,128)S(1)}, f32[48,8,128]{2,1,0:T(8,128)S(1)}, u32[]{:S(2)}, u32[]{:S(2)}) collective-permute-start(f32[48,8,128]{2,1,0:T(8,128)S(1)} %spread.1.own), channel_id=1, source_target_pairs={{4,0},{8,4},{12,8},{28,12},{24,28},{20,24},{16,20},{1,16},{5,1},{9... | collective-permute-start | bytes 589832 | tf_op jit(solution)/shard_map/ppermute | solution.py:639
  18.9 7.8 %collective-permute-start = (f32[48,8,128]{2,1,0:T(8,128)S(1)}, f32[48,8,128]{2,1,0:T(8,128)S(1)}, u32[]{:S(2)}, u32[]{:S(2)}) collective-permute-start(f32[48,8,128]{2,1,0:T(8,128)S(1)} %spread.1.own), channel_id=1, source_target_pairs={{0,4},{4,8},{8,12},{12,28},{28,24},{24,20},{20,16},{16,1},{1,5},{5... | collective-permute-start | bytes 589832 | tf_op jit(solution)/shard_map/ppermute | solution.py:639

commit v8 on v7

--- a/solution.py
+++ b/solution.py
@@ -304,10 +304,32 @@
     return dot01(flat, chosen).reshape(field.shape)
 
 
-def rank_of(peer):
+def peer_at(rank):
     ny = SPLIT[1]
-    ix, iy = peer // ny, peer % ny
-    return ix * ny + (ny - 1 - iy if ix % 2 else iy)
+    ix, place_on_row = rank // ny, rank % ny
+    return ix * ny + (ny - 1 - place_on_row if ix % 2 else place_on_row)
+
+
+def peer_of(group, rank):
+    return peer_at(SPLIT[0] * SPLIT[1] - 1 - rank if group % 2 else rank)
+
+
+def own_peer_of(rank):
+    return jnp.where(lax.axis_index("gz") % 2 == 1, peer_of(1, rank), peer_of(0, rank))
+
+
+def slab_of(ix, iy, group):
+    nx, ny = SPLIT
+    rank = ix * ny + jnp.where(ix % 2 == 1, ny - 1 - iy, iy)
+    return group * nx * ny + jnp.where(group % 2 == 1, nx * ny - 1 - rank, rank)
+
+
+def device_of(slab):
+    nx, ny = SPLIT
+    group, rank = slab // (nx * ny), slab % (nx * ny)
+    rank = jnp.where(group % 2 == 1, nx * ny - 1 - rank, rank)
+    row, column = rank // ny, rank % ny
+    return group * nx * ny + row * ny + jnp.where(row % 2 == 1, ny - 1 - column, column)
 
 
 def prepare_kernel(share, res_ref, fluid_ref, pin_ref, out_ref):
@@ -331,9 +353,9 @@
     chosen = where01(lane_of(cell // by, cell % by) == lane)
     fluid = dot01(fluid_ref[...].reshape(cells, depth).T, chosen)
     pin = dot01(pin_ref[...].reshape(cells, depth).T, chosen)
-    for index, field in enumerate((fluid, rhs, pin)):
-        for peer in range(depth // share):
-            begin = rank_of(peer) * share
+    for rank in range(depth // share):
+        peer, begin = own_peer_of(rank), rank * share
+        for index, field in enumerate((fluid, rhs, pin)):
             out_ref[peer, index * share : (index + 1) * share] = field[begin : begin + share]
 
 
@@ -485,8 +507,8 @@
     count3 = depth // 4
     shares = packed.shape[0]
     peers = SPLIT[0] * SPLIT[1]
-    slabs = sorted(range(shares), key=lambda i: (i // peers, rank_of(i % peers)))
-    for slab, index in enumerate(slabs):
+    for slab in range(shares):
+        index = slab // peers * peers + peer_of(slab // peers, slab % peers)
         row = slab * count3
         first[row : row + 2] = packed[index, 0]
         first[row + 2 : row + 4] = packed[index, 1]
@@ -507,17 +529,8 @@
     solved[0:NEAR] = jnp.zeros((NEAR, LANES), F32)
     solved[NEAR + shares * count3 :] = jnp.zeros((2 * NEAR, LANES), F32)
 
-    def slab_of(index):
-        index = jnp.clip(index, 0, shares - 1)
-        row = lax.rem(index, peers) // ny
-        column = lax.rem(index, ny)
-        column = jnp.where(lax.rem(row, 2) == 1, ny - 1 - column, column)
-        return (index // peers) * peers + row * ny + column
-
     nx, ny = SPLIT
-    ix, iy = lax.axis_index("gx"), lax.axis_index("gy")
-    along = jnp.where(lax.rem(ix, 2) == 1, ny - 1 - iy, iy)
-    part = (lax.axis_index("gz") * nx + ix) * ny + along
+    part = slab_of(lax.axis_index("gx"), lax.axis_index("gy"), lax.axis_index("gz"))
     count = count3 + 2 * NEAR
     tall = solved[pl.ds(part * count3, count + count3), :]
     fine, coarse = Level(0), Level(1)
@@ -539,7 +552,7 @@
     row = iota((ROWS, LANES), 0)
 
     def unpacked(index, which):
-        pair = packed[slab_of(index), which]
+        pair = packed[device_of(jnp.clip(index, 0, shares - 1)), which]
         total = None
         for shift in range(4):
             moved = pltpu.roll(pair, shift * (LANES // 4), 1)
@@ -593,7 +606,7 @@
     x, y = cell // by, cell % by
     chosen = where01((x % 4) * (bx // 4 * by) + (x // 4) * by + y == lane)
     peers = blocks.shape[0]
-    ordered = jnp.concatenate([blocks[i] for i in sorted(range(peers), key=rank_of)], axis=0)
+    ordered = jnp.concatenate([blocks[own_peer_of(rank)] for rank in range(peers)], axis=0)
     out_ref[...] = dot10(chosen, ordered).reshape(out_ref.shape)
 
 
@@ -630,11 +643,10 @@
         name="spread",
     )(lax.all_to_all(parcels, ("gx", "gy"), 0, 0, tiled=True))
     length = lax.axis_size("gz")
-    slabs = sorted(range(peers), key=rank_of)
     parts = length * peers
 
     def step(field, ahead):
-        device = [slabs[i % peers] * length + i // peers for i in range(parts)]
+        device = [peer_of(i // peers, i % peers) * length + i // peers for i in range(parts)]
         pairs = [(device[i], device[i + ahead]) for i in range(parts) if 0 <= i + ahead < parts]
         return lax.ppermute(field, ("gx", "gy", "gz"), pairs)
 

time: 54.1 us -> 53.8 us (level)
  no operation moved by 1% of the time
where the time goes in v8:
time: 53.8 us; the launch traced here: 53.5 us
  blocking collectives  37.8 us (70%)
  starting transfers between devices  5.85 us (11%)
  Pallas kernels  5.6 us (10%)
  waiting for transfers between devices  3.16 us (6%)
  other arithmetic  0.93 us (2%)
    all_to_all x1, blocking collectives, whole_planes(): lax.all_to_all(parcels, ('gx', 'gy'), 0, 0, tiled=True)  15.8 us
    all_to_all x1, blocking collectives, whole_planes(): packed = lax.all_to_all(copies, ('gz', 'gx', 'gy'), 0, 0, tiled=True)  11.8 us
    all_to_all x1, blocking collectives, whole_planes(): lax.all_to_all(mine, ('gx', 'gy'), 0, 0, tiled=True)  10.2 us
    ppermute x2, starting transfers between devices, step(): return lax.ppermute(field, ('gx', 'gy', 'gz'), pairs)  5.85 us
    ppermute x2, waiting for transfers between devices, step(): return lax.ppermute(field, ('gx', 'gy', 'gz'), pairs)  3.16 us
    pallas_call x1, Pallas kernels, whole_planes(): pl.pallas_call(functools.partial(up_kernel, groups, by, share), out_shape...  2.09 us
    pallas_call x1, Pallas kernels, whole_planes(): pl.pallas_call(functools.partial(down_kernel, groups, by, share), out_sha...  1.94 us
  transfers between devices with their start and end apart: 2, of which 2 were waited for; matrix products, arithmetic and copies ran while one was open for 0% of the time, Pallas kernels for 0%

profile of v8, /device:TPU:0, one launch (start us, length us, event | category | flops | bytes accessed | tf_op | source)
XLA Modules:
  0.0 53.5 jit_solution(14804374676403121071)
XLA Ops:
  0.0 0.0 copy-start
  0.0 0.9 %multiply_multiply_fusion = (f32[16,8,128]{2,1,0:T(8,128)S(1)}, f32[16,8,128]{2,1,0:T(8,128)S(1)}) fusion(s32[16,8,128]{2,1,0:T(8,128)} %param.5, f32[16,8,128]{2,1,0:T(8,128)} %param.4), kind=kLoop, calls=%fused_computation | loop fusion | flops 65536 | bytes 262144 | tf_op jit(solution)/shard_map/mul | solution.py:632
  0.9 0.1 copy-done
  1.0 0.5 prepare.1
  1.5 15.8 %all_to_all.15.gathered = f32[8,48,128]{2,1,0:T(8,128)S(1)} all-to-all(f32[8,48,128]{2,1,0:T(8,128)S(1)} %prepare.1), channel_id=1, replica_groups=mesh['gx'=2,'gy'=4,'gz'=4] {'gx','gy'}, dimensions={0} | all-to-all | bytes 393216 | tf_op jit(solution)/shard_map/all_to_all | solution.py:644
  17.3 0.2 spread.1.own
  17.6 1.3 %collective-permute-start.1 = (f32[48,8,128]{2,1,0:T(8,128)S(1)}, f32[48,8,128]{2,1,0:T(8,128)S(1)}, u32[]{:S(2)}, u32[]{:S(2)}) collective-permute-start(f32[48,8,128]{2,1,0:T(8,128)S(1)} %spread.1.own), channel_id=1, source_target_pairs={{4,0},{8,4},{12,8},{28,12},{24,28},{20,24},{16,20},{17,16},{21,17}... | collective-permute-start | bytes 589832 | tf_op jit(solution)/shard_map/ppermute | solution.py:651
  18.9 4.6 %collective-permute-start = (f32[48,8,128]{2,1,0:T(8,128)S(1)}, f32[48,8,128]{2,1,0:T(8,128)S(1)}, u32[]{:S(2)}, u32[]{:S(2)}) collective-permute-start(f32[48,8,128]{2,1,0:T(8,128)S(1)} %spread.1.own), channel_id=1, source_target_pairs={{0,4},{4,8},{8,12},{12,28},{28,24},{24,20},{20,16},{16,17},{17,21}... | collective-permute-start | bytes 589832 | tf_op jit(solution)/shard_map/ppermute | solution.py:651
  23.4 2.6 %collective-permute-done.1.high = f32[48,8,128]{2,1,0:T(8,128)S(1)} collective-permute-done((f32[48,8,128]{2,1,0:T(8,128)S(1)}, f32[48,8,128]{2,1,0:T(8,128)S(1)}, u32[]{:S(2)}, u32[]{:S(2)}) %collective-permute-start.1) | collective-permute-done | bytes 196640 | tf_op jit(solution)/shard_map/ppermute | solution.py:651
  26.0 0.5 %collective-permute-done.low = f32[48,8,128]{2,1,0:T(8,128)S(1)} collective-permute-done((f32[48,8,128]{2,1,0:T(8,128)S(1)}, f32[48,8,128]{2,1,0:T(8,128)S(1)}, u32[]{:S(2)}, u32[]{:S(2)}) %collective-permute-start) | collective-permute-done | bytes 196640 | tf_op jit(solution)/shard_map/ppermute | solution.py:651
  26.6 1.9 %down.1 = (f32[48,8,128]{2,1,0:T(8,128)S(1)}, f32[48,8,128]{2,1,0:T(8,128)S(1)}, f32[48,8,128]{2,1,0:T(8,128)S(1)}, f32[48,8,128]{2,1,0:T(8,128)S(1)}, f32[48,8,...) custom-call(f32[48,8,128]{2,1,0:T(8,128)S(1)} %collective-permute-do, ...), custom_call_target="tpu_custom_call" | custom-call | tf_op jit(solution)/shard_map/down/pallas_call | solution.py:655
  28.6 11.8 %all_to_all.16.packed = f32[32,5,2,128]{3,2,1,0:T(2,128)S(1)} all-to-all(f32[32,5,2,128]{3,2,1,0:T(2,128)S(1)} %broadcast_in_dim.3), channel_id=1, replica_groups=mesh['gx'=2,'gy'=4,'gz'=4] {'gz','gx','gy'}, dimensions={0} | all-to-all | bytes 327680 | tf_op jit(solution)/shard_map/all_to_all | solution.py:663
  40.4 2.1 %up.1 = f32[8,16,128]{2,1,0:T(8,128)S(1)} custom-call(f32[32,5,2,128]{3,2,1,0:T(2,128)S(1)} %all_to_all.16.packed, f32[48,8,128]{2,1,0:T(8,128)S(1)} %get-tuple-element.25.xn1, f32[48,8,128]{2,1,0:T(8,128)S(1)} %get-tuple-element.26.xl1, f32[48,8,128]{2,1,0:T(8,128)S(1)} %get-tuple-element.27.yn1, f32[48,8,128]{2,1,0:T(8,128)S(1)} %get-tuple-element.28.yl1, ...), custom_call_target="tpu_custom_call" | custom-call | tf_op jit(solution)/shard_map/up/pallas_call | solution.py:665
  42.5 10.2 %all_to_all.17.blocks = f32[8,16,128]{2,1,0:T(8,128)S(1)} all-to-all(f32[8,16,128]{2,1,0:T(8,128)S(1)} %up.1), channel_id=1, replica_groups=mesh['gx'=2,'gy'=4,'gz'=4] {'gx','gy'}, dimensions={0} | all-to-all | bytes 131072 | tf_op jit(solution)/shard_map/all_to_all | solution.py:678
  52.7 0.8 %finish.1 = f32[16,8,128]{2,1,0:T(8,128)} custom-call(f32[8,16,128]{2,1,0:T(8,128)S(1)} %all_to_all.17.blocks), custom_call_target="tpu_custom_call" | custom-call | tf_op jit(solution)/shard_map/finish/pallas_call | solution.py:673
  (1 shorter events, 0.0 us)
Async XLA Ops:
  0.0 1.0 %copy-start = (bf16[32,16,256]{2,1,0:T(8,128)(2,1)S(1)}, bf16[32,16,256]{2,1,0:T(8,128)(2,1)}, u32[]{:S(2)}) copy-start(bf16[32,16,256]{2,1,0:T(8,128)(2,1)} %param.3) | copy-start | bytes 786436
  17.6 8.5 %collective-permute-start.1 = (f32[48,8,128]{2,1,0:T(8,128)S(1)}, f32[48,8,128]{2,1,0:T(8,128)S(1)}, u32[]{:S(2)}, u32[]{:S(2)}) collective-permute-start(f32[48,8,128]{2,1,0:T(8,128)S(1)} %spread.1.own), channel_id=1, source_target_pairs={{4,0},{8,4},{12,8},{28,12},{24,28},{20,24},{16,20},{17,16},{21,17}... | collective-permute-start | bytes 589832 | tf_op jit(solution)/shard_map/ppermute | solution.py:651
  18.9 7.7 %collective-permute-start = (f32[48,8,128]{2,1,0:T(8,128)S(1)}, f32[48,8,128]{2,1,0:T(8,128)S(1)}, u32[]{:S(2)}, u32[]{:S(2)}) collective-permute-start(f32[48,8,128]{2,1,0:T(8,128)S(1)} %spread.1.own), channel_id=1, source_target_pairs={{0,4},{4,8},{8,12},{12,28},{28,24},{24,20},{20,16},{16,17},{17,21}... | collective-permute-start | bytes 589832 | tf_op jit(solution)/shard_map/ppermute | solution.py:651

commit v9 on v8

--- a/solution.py
+++ b/solution.py
@@ -380,19 +380,20 @@
 
 def down_kernel(
     groups, by, depth,
-    low, own, high,
+    own, inner, outer,
     xn1, xl1, yn1, yl1, zn1, zl1, start1, diag1, corr1,
     xn2, xl2, yn2, yl2, zn2, zl2, start2, diag2, corr2,
     packed,
     fluid1, rhs1, pin1, other1, fluid2, rhs2, pin2, other2, sums,
 ):
     planes = depth + 2 * HALO
+    part = slab_of(lax.axis_index("gx"), lax.axis_index("gy"), lax.axis_index("gz"))
+    odd = part % 2 == 1
     for index, target in enumerate((fluid1, rhs1, pin1)):
-        start = 0
-        for piece in (low, own, high):
-            count = piece.shape[0] // 3
-            target[start : start + count] = piece[index * count : (index + 1) * count]
-            start += count
+        rows = slice(index * depth, (index + 1) * depth)
+        target[0:HALO] = jnp.where(odd, inner[rows], outer[rows])
+        target[HALO : HALO + depth] = own[rows]
+        target[HALO + depth :] = jnp.where(odd, outer[rows], inner[rows])
 
     fine, coarse = Level(0), Level(1)
     down1, down2 = lanes_down(0), lanes_down(1)
@@ -645,12 +646,13 @@
     length = lax.axis_size("gz")
     parts = length * peers
 
-    def step(field, ahead):
-        device = [peer_of(i // peers, i % peers) * length + i // peers for i in range(parts)]
-        pairs = [(device[i], device[i + ahead]) for i in range(parts) if 0 <= i + ahead < parts]
-        return lax.ppermute(field, ("gx", "gy", "gz"), pairs)
-
-    low, high = step(own, 1), step(own, -1)
+    device = [peer_of(i // peers, i % peers) * length + i // peers for i in range(parts)]
+
+    def swap(field, first):
+        pairs = [(device[i], device[i + 1]) for i in range(first, parts - 1, 2)]
+        return lax.ppermute(field, ("gx", "gy", "gz"), pairs + [pair[::-1] for pair in pairs])
+
+    inner, outer = swap(own, 0), swap(own, 1)
     saved = (blocks(planes, ROWS),) * 9 + (blocks(count2, ROWS),) * 9
     results = pl.pallas_call(
         functools.partial(down_kernel, groups, by, share),
@@ -658,7 +660,7 @@
         scratch_shapes=[room(planes)] * 4 + [room(count2)] * 5,
         compiler_params=limit,
         name="down",
-    )(low, own, high)
+    )(own, inner, outer)
     copies = jnp.broadcast_to(results[-1], (parts,) + results[-1].shape)
     packed = lax.all_to_all(copies, ("gz", "gx", "gy"), 0, 0, tiled=True)
     depth3 = parts * share // 4

time: 53.8 us -> 52.1 us (0.968)
  starting transfers between devices: 5.85 us -> 2.47 us
  waiting for transfers between devices: 3.16 us -> 4.95 us
    ppermute x2, starting transfers between devices: 5.85 us -> 2.47 us  [swap(): lax.ppermute(field, ('gx', 'gy', 'gz'), pairs + [pair[::-1] for pair in p...]
    ppermute x2, waiting for transfers between devices: 3.16 us -> 4.95 us  [swap(): lax.ppermute(field, ('gx', 'gy', 'gz'), pairs + [pair[::-1] for pair in p...]
  transfers between devices with their start and end apart: 2 -> 2, of which waited for: 2 -> 1; matrix products, arithmetic and copies ran while one was open for 0% -> 0% of each run, Pallas kernels for 0% -> 0%
where the time goes in v9:
time: 52.1 us; the launch traced here: 51.9 us
  blocking collectives  37.8 us (73%)
  Pallas kernels  5.62 us (11%)
  waiting for transfers between devices  4.95 us (10%)
  starting transfers between devices  2.47 us (5%)
  other arithmetic  0.93 us (2%)
    all_to_all x1, blocking collectives, whole_planes(): lax.all_to_all(parcels, ('gx', 'gy'), 0, 0, tiled=True)  15.8 us
    all_to_all x1, blocking collectives, whole_planes(): packed = lax.all_to_all(copies, ('gz', 'gx', 'gy'), 0, 0, tiled=True)  11.7 us
    all_to_all x1, blocking collectives, whole_planes(): lax.all_to_all(mine, ('gx', 'gy'), 0, 0, tiled=True)  10.2 us
    ppermute x2, waiting for transfers between devices, swap(): lax.ppermute(field, ('gx', 'gy', 'gz'), pairs + [pair[::-1] for pair in p...  4.95 us
    ppermute x2, starting transfers between devices, swap(): lax.ppermute(field, ('gx', 'gy', 'gz'), pairs + [pair[::-1] for pair in p...  2.47 us
    pallas_call x1, Pallas kernels, whole_planes(): pl.pallas_call(functools.partial(up_kernel, groups, by, share), out_shape...  2.09 us
    pallas_call x1, Pallas kernels, whole_planes(): pl.pallas_call(functools.partial(down_kernel, groups, by, share), out_sha...  1.96 us
  transfers between devices with their start and end apart: 2, of which 1 were waited for; matrix products, arithmetic and copies ran while one was open for 0% of the time, Pallas kernels for 0%

profile of v9, /device:TPU:0, one launch (start us, length us, event | category | flops | bytes accessed | tf_op | source)
XLA Modules:
  0.0 51.9 jit_solution(2980897479040553905)
XLA Ops:
  0.0 0.0 copy-start
  0.0 0.9 %multiply_multiply_fusion = (f32[16,8,128]{2,1,0:T(8,128)S(1)}, f32[16,8,128]{2,1,0:T(8,128)S(1)}) fusion(s32[16,8,128]{2,1,0:T(8,128)} %param.5, f32[16,8,128]{2,1,0:T(8,128)} %param.4), kind=kLoop, calls=%fused_computation | loop fusion | flops 65536 | bytes 262144 | tf_op jit(solution)/shard_map/mul | solution.py:633
  0.9 0.1 copy-done
  1.0 0.5 prepare.1
  1.5 15.8 %all_to_all.15.gathered = f32[8,48,128]{2,1,0:T(8,128)S(1)} all-to-all(f32[8,48,128]{2,1,0:T(8,128)S(1)} %prepare.1), channel_id=1, replica_groups=mesh['gx'=2,'gy'=4,'gz'=4] {'gx','gy'}, dimensions={0} | all-to-all | bytes 393216 | tf_op jit(solution)/shard_map/all_to_all | solution.py:645
  17.3 0.2 spread.1.own
  17.6 0.7 %collective-permute-start.1 = (f32[48,8,128]{2,1,0:T(8,128)S(1)}, f32[48,8,128]{2,1,0:T(8,128)S(1)}, u32[]{:S(2)}, u32[]{:S(2)}) collective-permute-start(f32[48,8,128]{2,1,0:T(8,128)S(1)} %spread.1.own), channel_id=1, source_target_pairs={{4,8},{12,28},{24,20},{16,17},{21,25},{29,13},{9,5},{1,2},{6,10},{... | collective-permute-start | bytes 589832 | tf_op jit(solution)/shard_map/ppermute | solution.py:653
  18.2 1.8 %collective-permute-start = (f32[48,8,128]{2,1,0:T(8,128)S(1)}, f32[48,8,128]{2,1,0:T(8,128)S(1)}, u32[]{:S(2)}, u32[]{:S(2)}) collective-permute-start(f32[48,8,128]{2,1,0:T(8,128)S(1)} %spread.1.own), channel_id=1, source_target_pairs={{0,4},{8,12},{28,24},{20,16},{17,21},{25,29},{13,9},{5,1},{2,6},{1... | collective-permute-start | bytes 589832 | tf_op jit(solution)/shard_map/ppermute | solution.py:653
  20.0 0.0 collective-permute-done.1.outer
  20.0 4.9 %collective-permute-done.inner = f32[48,8,128]{2,1,0:T(8,128)S(1)} collective-permute-done((f32[48,8,128]{2,1,0:T(8,128)S(1)}, f32[48,8,128]{2,1,0:T(8,128)S(1)}, u32[]{:S(2)}, u32[]{:S(2)}) %collective-permute-start) | collective-permute-done | bytes 196640 | tf_op jit(solution)/shard_map/ppermute | solution.py:653
  25.0 2.0 %down.1 = (f32[48,8,128]{2,1,0:T(8,128)S(1)}, f32[48,8,128]{2,1,0:T(8,128)S(1)}, f32[48,8,128]{2,1,0:T(8,128)S(1)}, f32[48,8,128]{2,1,0:T(8,128)S(1)}, f32[48,8,...) custom-call(f32[48,8,128]{2,1,0:T(8,128)S(1)} %spread.1.own, ...), custom_call_target="tpu_custom_call" | custom-call | tf_op jit(solution)/shard_map/down/pallas_call | solution.py:657
  27.0 11.7 %all_to_all.16.packed = f32[32,5,2,128]{3,2,1,0:T(2,128)S(1)} all-to-all(f32[32,5,2,128]{3,2,1,0:T(2,128)S(1)} %broadcast_in_dim.3), channel_id=1, replica_groups=mesh['gx'=2,'gy'=4,'gz'=4] {'gz','gx','gy'}, dimensions={0} | all-to-all | bytes 327680 | tf_op jit(solution)/shard_map/all_to_all | solution.py:665
  38.7 2.1 %up.1 = f32[8,16,128]{2,1,0:T(8,128)S(1)} custom-call(f32[32,5,2,128]{3,2,1,0:T(2,128)S(1)} %all_to_all.16.packed, f32[48,8,128]{2,1,0:T(8,128)S(1)} %get-tuple-element.25.xn1, f32[48,8,128]{2,1,0:T(8,128)S(1)} %get-tuple-element.26.xl1, f32[48,8,128]{2,1,0:T(8,128)S(1)} %get-tuple-element.27.yn1, f32[48,8,128]{2,1,0:T(8,128)S(1)} %get-tuple-element.28.yl1, ...), custom_call_target="tpu_custom_call" | custom-call | tf_op jit(solution)/shard_map/up/pallas_call | solution.py:667
  40.8 10.2 %all_to_all.17.blocks = f32[8,16,128]{2,1,0:T(8,128)S(1)} all-to-all(f32[8,16,128]{2,1,0:T(8,128)S(1)} %up.1), channel_id=1, replica_groups=mesh['gx'=2,'gy'=4,'gz'=4] {'gx','gy'}, dimensions={0} | all-to-all | bytes 131072 | tf_op jit(solution)/shard_map/all_to_all | solution.py:680
  51.1 0.8 %finish.1 = f32[16,8,128]{2,1,0:T(8,128)} custom-call(f32[8,16,128]{2,1,0:T(8,128)S(1)} %all_to_all.17.blocks), custom_call_target="tpu_custom_call" | custom-call | tf_op jit(solution)/shard_map/finish/pallas_call | solution.py:675
  (1 shorter events, 0.0 us)
Async XLA Ops:
  0.0 1.0 %copy-start = (bf16[32,16,256]{2,1,0:T(8,128)(2,1)S(1)}, bf16[32,16,256]{2,1,0:T(8,128)(2,1)}, u32[]{:S(2)}) copy-start(bf16[32,16,256]{2,1,0:T(8,128)(2,1)} %param.3) | copy-start | bytes 786436
  17.6 2.5 %collective-permute-start.1 = (f32[48,8,128]{2,1,0:T(8,128)S(1)}, f32[48,8,128]{2,1,0:T(8,128)S(1)}, u32[]{:S(2)}, u32[]{:S(2)}) collective-permute-start(f32[48,8,128]{2,1,0:T(8,128)S(1)} %spread.1.own), channel_id=1, source_target_pairs={{4,8},{12,28},{24,20},{16,17},{21,25},{29,13},{9,5},{1,2},{6,10},{... | collective-permute-start | bytes 589832 | tf_op jit(solution)/shard_map/ppermute | solution.py:653
  18.2 6.7 %collective-permute-start = (f32[48,8,128]{2,1,0:T(8,128)S(1)}, f32[48,8,128]{2,1,0:T(8,128)S(1)}, u32[]{:S(2)}, u32[]{:S(2)}) collective-permute-start(f32[48,8,128]{2,1,0:T(8,128)S(1)} %spread.1.own), channel_id=1, source_target_pairs={{0,4},{8,12},{28,24},{20,16},{17,21},{25,29},{13,9},{5,1},{2,6},{1... | collective-permute-start | bytes 589832 | tf_op jit(solution)/shard_map/ppermute | solution.py:653

commit v10 on v9

--- a/solution.py
+++ b/solution.py
@@ -332,31 +332,47 @@
     return group * nx * ny + row * ny + jnp.where(row % 2 == 1, ny - 1 - column, column)
 
 
-def prepare_kernel(share, res_ref, fluid_ref, pin_ref, out_ref):
-    bx, by, depth = fluid_ref.shape
+def prepare_kernel(
+    share, res_in, visc_in, pin_in, out_ref, res_ref, visc_ref, pin_ref, arrived
+):
+    copies = [
+        pltpu.make_async_copy(source, target, arrived.at[index])
+        for index, (source, target) in enumerate(
+            ((visc_in, visc_ref), (pin_in, pin_ref), (res_in, res_ref))
+        )
+    ]
+    for copy in copies:
+        copy.start()
+    bx, by, depth = visc_ref.shape
     cells = bx * by
     groups = bx // 4
+
+    def lane_of(x, y):
+        return (x % 4) * (groups * by) + (x // 4) * by + y
+
+    def send(index, field):
+        for rank in range(depth // share):
+            rows = slice(index * share, (index + 1) * share)
+            out_ref[own_peer_of(rank), rows] = field[rank * share : (rank + 1) * share]
+
+    cell = iota((cells, cells), 0)
+    lane = iota((cells, cells), 1)
+    chosen = where01(lane_of(cell // by, cell % by) == lane)
+    copies[0].wait()
+    fluid = 1.0 / visc_ref[...].reshape(cells, depth)
+    send(0, dot01(fluid.T, chosen))
+    copies[1].wait()
+    pin = 4.0 * pin_ref[...].reshape(cells, depth).astype(F32) * fluid
+    send(2, dot01(pin.T, chosen))
     pick = where01(iota((depth, 2 * depth), 1) // 2 == iota((depth, 2 * depth), 0))
+    fine = iota((4 * cells, cells), 0)
+    lane = iota((4 * cells, cells), 1)
+    chosen = where01(lane_of(fine // (4 * by), (fine % (2 * by)) // 2) == lane)
+    copies[2].wait()
     deep = lax.dot_general(
         pick, res_ref[...], (((1,), (1,)), ((), ())), preferred_element_type=F32
     )
-
-    def lane_of(x, y):
-        return (x % 4) * (groups * by) + (x // 4) * by + y
-
-    fine = iota((4 * cells, cells), 0)
-    lane = iota((4 * cells, cells), 1)
-    chosen = where01(lane_of(fine // (4 * by), (fine % (2 * by)) // 2) == lane)
-    rhs = dot01(deep, chosen)
-    cell = iota((cells, cells), 0)
-    lane = iota((cells, cells), 1)
-    chosen = where01(lane_of(cell // by, cell % by) == lane)
-    fluid = dot01(fluid_ref[...].reshape(cells, depth).T, chosen)
-    pin = dot01(pin_ref[...].reshape(cells, depth).T, chosen)
-    for rank in range(depth // share):
-        peer, begin = own_peer_of(rank), rank * share
-        for index, field in enumerate((fluid, rhs, pin)):
-            out_ref[peer, index * share : (index + 1) * share] = field[begin : begin + share]
+    send(1, dot01(deep, chosen))
 
 
 def spread_kernel(groups, by, gathered, own):
@@ -629,14 +645,20 @@
     def room(count):
         return pltpu.VMEM((count, ROWS, LANES), F32)
 
-    fluid = 1.0 / viscosity
-    pin = 4.0 * pinned.astype(F32) * fluid
+    residual = residual_q2.reshape(4 * bx * by, 2 * depth)
+    arguments = [
+        pltpu.with_memory_space_constraint(field, pltpu.HBM)
+        for field in (residual, viscosity, pinned)
+    ]
     parcels = pl.pallas_call(
         functools.partial(prepare_kernel, share),
+        in_specs=[pl.BlockSpec(memory_space=pltpu.HBM)] * 3,
         out_shape=blocks(peers, 3 * share),
+        scratch_shapes=[pltpu.VMEM(field.shape, field.dtype) for field in arguments]
+        + [pltpu.SemaphoreType.DMA((3,))],
         compiler_params=limit,
         name="prepare",
-    )(residual_q2.reshape(4 * bx * by, 2 * depth), fluid, pin)
+    )(*arguments)
     own = pl.pallas_call(
         functools.partial(spread_kernel, groups, by),
         out_shape=blocks(3 * share, ROWS),

time: 52.1 us -> 52.5 us (level)
  Pallas kernels: 5.62 us -> 7.03 us
  other arithmetic: 0.93 us -> 0 us
    pallas_call x1, Pallas kernels: 0.49 us -> 1.9 us  [whole_planes(): pl.pallas_call(functools.partial(prepare_kernel, share), in_specs=[pl.Blo...]
    mul x1 -> x0, other arithmetic: 0.93 us -> none  [whole_planes(): pin = 4.0 * pinned.astype(F32) * fluid]
where the time goes in v10:
time: 52.5 us; the launch traced here: 52.3 us
  blocking collectives  37.8 us (72%)
  Pallas kernels  7.03 us (13%)
  waiting for transfers between devices  4.96 us (9%)
  starting transfers between devices  2.47 us (5%)
    all_to_all x1, blocking collectives, whole_planes(): lax.all_to_all(parcels, ('gx', 'gy'), 0, 0, tiled=True)  15.8 us
    all_to_all x1, blocking collectives, whole_planes(): packed = lax.all_to_all(copies, ('gz', 'gx', 'gy'), 0, 0, tiled=True)  11.7 us
    all_to_all x1, blocking collectives, whole_planes(): lax.all_to_all(mine, ('gx', 'gy'), 0, 0, tiled=True)  10.2 us
    ppermute x2, waiting for transfers between devices, swap(): lax.ppermute(field, ('gx', 'gy', 'gz'), pairs + [pair[::-1] for pair in p...  4.96 us
    ppermute x2, starting transfers between devices, swap(): lax.ppermute(field, ('gx', 'gy', 'gz'), pairs + [pair[::-1] for pair in p...  2.47 us
    pallas_call x1, Pallas kernels, whole_planes(): pl.pallas_call(functools.partial(up_kernel, groups, by, share), out_shape...  2.09 us
    pallas_call x1, Pallas kernels, whole_planes(): pl.pallas_call(functools.partial(down_kernel, groups, by, share), out_sha...  1.96 us
    pallas_call x1, Pallas kernels, whole_planes(): pl.pallas_call(functools.partial(prepare_kernel, share), in_specs=[pl.Blo...  1.9 us
  transfers between devices with their start and end apart: 2, of which 1 were waited for; matrix products, arithmetic and copies ran while one was open for 0% of the time, Pallas kernels for 0%

profile of v10, /device:TPU:0, one launch (start us, length us, event | category | flops | bytes accessed | tf_op | source)
XLA Modules:
  0.0 52.3 jit_solution(17422219630187269466)
XLA Ops:
  0.0 1.9 %prepare.1 = f32[8,48,128]{2,1,0:T(8,128)S(1)} custom-call(bf16[512,256]{1,0:T(8,128)(2,1)} %bitcast.1, f32[16,8,128]{2,1,0:T(8,128)} %visc_in.1, s32[16,8,128]{2,1,0:T(8,128)} %pin_in.1), custom_call_target="tpu_custom_call" | custom-call | tf_op jit(solution)/shard_map/prepare/pallas_call | solution.py:653
  1.9 15.8 %all_to_all.15.gathered = f32[8,48,128]{2,1,0:T(8,128)S(1)} all-to-all(f32[8,48,128]{2,1,0:T(8,128)S(1)} %prepare.1), channel_id=1, replica_groups=mesh['gx'=2,'gy'=4,'gz'=4] {'gx','gy'}, dimensions={0} | all-to-all | bytes 393216 | tf_op jit(solution)/shard_map/all_to_all | solution.py:667
  17.7 0.2 spread.1.own
  18.0 0.7 %collective-permute-start.1 = (f32[48,8,128]{2,1,0:T(8,128)S(1)}, f32[48,8,128]{2,1,0:T(8,128)S(1)}, u32[]{:S(2)}, u32[]{:S(2)}) collective-permute-start(f32[48,8,128]{2,1,0:T(8,128)S(1)} %spread.1.own), channel_id=1, source_target_pairs={{4,8},{12,28},{24,20},{16,17},{21,25},{29,13},{9,5},{1,2},{6,10},{... | collective-permute-start | bytes 589832 | tf_op jit(solution)/shard_map/ppermute | solution.py:675
  18.6 1.8 %collective-permute-start = (f32[48,8,128]{2,1,0:T(8,128)S(1)}, f32[48,8,128]{2,1,0:T(8,128)S(1)}, u32[]{:S(2)}, u32[]{:S(2)}) collective-permute-start(f32[48,8,128]{2,1,0:T(8,128)S(1)} %spread.1.own), channel_id=1, source_target_pairs={{0,4},{8,12},{28,24},{20,16},{17,21},{25,29},{13,9},{5,1},{2,6},{1... | collective-permute-start | bytes 589832 | tf_op jit(solution)/shard_map/ppermute | solution.py:675
  20.4 0.0 collective-permute-done.1.outer
  20.4 5.0 %collective-permute-done.inner = f32[48,8,128]{2,1,0:T(8,128)S(1)} collective-permute-done((f32[48,8,128]{2,1,0:T(8,128)S(1)}, f32[48,8,128]{2,1,0:T(8,128)S(1)}, u32[]{:S(2)}, u32[]{:S(2)}) %collective-permute-start) | collective-permute-done | bytes 196640 | tf_op jit(solution)/shard_map/ppermute | solution.py:675
  25.4 2.0 %down.1 = (f32[48,8,128]{2,1,0:T(8,128)S(1)}, f32[48,8,128]{2,1,0:T(8,128)S(1)}, f32[48,8,128]{2,1,0:T(8,128)S(1)}, f32[48,8,128]{2,1,0:T(8,128)S(1)}, f32[48,8,...) custom-call(f32[48,8,128]{2,1,0:T(8,128)S(1)} %spread.1.own, ...), custom_call_target="tpu_custom_call" | custom-call | tf_op jit(solution)/shard_map/down/pallas_call | solution.py:679
  27.4 11.7 %all_to_all.16.packed = f32[32,5,2,128]{3,2,1,0:T(2,128)S(1)} all-to-all(f32[32,5,2,128]{3,2,1,0:T(2,128)S(1)} %broadcast_in_dim.3), channel_id=1, replica_groups=mesh['gx'=2,'gy'=4,'gz'=4] {'gz','gx','gy'}, dimensions={0} | all-to-all | bytes 327680 | tf_op jit(solution)/shard_map/all_to_all | solution.py:687
  39.1 2.1 %up.1 = f32[8,16,128]{2,1,0:T(8,128)S(1)} custom-call(f32[32,5,2,128]{3,2,1,0:T(2,128)S(1)} %all_to_all.16.packed, f32[48,8,128]{2,1,0:T(8,128)S(1)} %get-tuple-element.25.xn1, f32[48,8,128]{2,1,0:T(8,128)S(1)} %get-tuple-element.26.xl1, f32[48,8,128]{2,1,0:T(8,128)S(1)} %get-tuple-element.27.yn1, f32[48,8,128]{2,1,0:T(8,128)S(1)} %get-tuple-element.28.yl1, ...), custom_call_target="tpu_custom_call" | custom-call | tf_op jit(solution)/shard_map/up/pallas_call | solution.py:689
  41.2 10.2 %all_to_all.17.blocks = f32[8,16,128]{2,1,0:T(8,128)S(1)} all-to-all(f32[8,16,128]{2,1,0:T(8,128)S(1)} %up.1), channel_id=1, replica_groups=mesh['gx'=2,'gy'=4,'gz'=4] {'gx','gy'}, dimensions={0} | all-to-all | bytes 131072 | tf_op jit(solution)/shard_map/all_to_all | solution.py:702
  51.5 0.8 %finish.1 = f32[16,8,128]{2,1,0:T(8,128)} custom-call(f32[8,16,128]{2,1,0:T(8,128)S(1)} %all_to_all.17.blocks), custom_call_target="tpu_custom_call" | custom-call | tf_op jit(solution)/shard_map/finish/pallas_call | solution.py:697
  (1 shorter events, 0.0 us)
Async XLA Ops:
  18.0 2.5 %collective-permute-start.1 = (f32[48,8,128]{2,1,0:T(8,128)S(1)}, f32[48,8,128]{2,1,0:T(8,128)S(1)}, u32[]{:S(2)}, u32[]{:S(2)}) collective-permute-start(f32[48,8,128]{2,1,0:T(8,128)S(1)} %spread.1.own), channel_id=1, source_target_pairs={{4,8},{12,28},{24,20},{16,17},{21,25},{29,13},{9,5},{1,2},{6,10},{... | collective-permute-start | bytes 589832 | tf_op jit(solution)/shard_map/ppermute | solution.py:675
  18.6 6.8 %collective-permute-start = (f32[48,8,128]{2,1,0:T(8,128)S(1)}, f32[48,8,128]{2,1,0:T(8,128)S(1)}, u32[]{:S(2)}, u32[]{:S(2)}) collective-permute-start(f32[48,8,128]{2,1,0:T(8,128)S(1)} %spread.1.own), channel_id=1, source_target_pairs={{0,4},{8,12},{28,24},{20,16},{17,21},{25,29},{13,9},{5,1},{2,6},{1... | collective-permute-start | bytes 589832 | tf_op jit(solution)/shard_map/ppermute | solution.py:675

commit v11 on v9

--- a/solution.py
+++ b/solution.py
@@ -329,7 +329,8 @@
     group, rank = slab // (nx * ny), slab % (nx * ny)
     rank = jnp.where(group % 2 == 1, nx * ny - 1 - rank, rank)
     row, column = rank // ny, rank % ny
-    return group * nx * ny + row * ny + jnp.where(row % 2 == 1, ny - 1 - column, column)
+    peer = row * ny + jnp.where(row % 2 == 1, ny - 1 - column, column)
+    return peer * lax.axis_size("gz") + group
 
 
 def prepare_kernel(share, res_ref, fluid_ref, pin_ref, out_ref):
@@ -380,7 +381,7 @@
 
 def down_kernel(
     groups, by, depth,
-    own, inner, outer,
+    own, outer, inner,
     xn1, xl1, yn1, yl1, zn1, zl1, start1, diag1, corr1,
     xn2, xl2, yn2, yl2, zn2, zl2, start2, diag2, corr2,
     packed,
@@ -509,7 +510,7 @@
     shares = packed.shape[0]
     peers = SPLIT[0] * SPLIT[1]
     for slab in range(shares):
-        index = slab // peers * peers + peer_of(slab // peers, slab % peers)
+        index = peer_of(slab // peers, slab % peers) * (shares // peers) + slab // peers
         row = slab * count3
         first[row : row + 2] = packed[index, 0]
         first[row + 2 : row + 4] = packed[index, 1]
@@ -652,7 +653,7 @@
         pairs = [(device[i], device[i + 1]) for i in range(first, parts - 1, 2)]
         return lax.ppermute(field, ("gx", "gy", "gz"), pairs + [pair[::-1] for pair in pairs])
 
-    inner, outer = swap(own, 0), swap(own, 1)
+    outer, inner = swap(own, 1), swap(own, 0)
     saved = (blocks(planes, ROWS),) * 9 + (blocks(count2, ROWS),) * 9
     results = pl.pallas_call(
         functools.partial(down_kernel, groups, by, share),
@@ -660,9 +661,9 @@
         scratch_shapes=[room(planes)] * 4 + [room(count2)] * 5,
         compiler_params=limit,
         name="down",
-    )(own, inner, outer)
+    )(own, outer, inner)
     copies = jnp.broadcast_to(results[-1], (parts,) + results[-1].shape)
-    packed = lax.all_to_all(copies, ("gz", "gx", "gy"), 0, 0, tiled=True)
+    packed = lax.all_to_all(copies, ("gx", "gy", "gz"), 0, 0, tiled=True)
     depth3 = parts * share // 4
     mine = pl.pallas_call(
         functools.partial(up_kernel, groups, by, share),

time: 52.1 us -> 51.8 us (level)
  starting transfers between devices: 2.47 us -> 0.74 us
  blocking collectives: 37.8 us -> 39.1 us
    all_to_all x1, blocking collectives: 11.7 us -> 13.6 us  [whole_planes(): packed = lax.all_to_all(copies, ('gx', 'gy', 'gz'), 0, 0, tiled=True)]
    ppermute x2, starting transfers between devices: 2.47 us -> 0.74 us  [swap(): lax.ppermute(field, ('gx', 'gy', 'gz'), pairs + [pair[::-1] for pair in p...]
    all_to_all x1, blocking collectives: 10.2 us -> 9.7 us  [whole_planes(): lax.all_to_all(mine, ('gx', 'gy'), 0, 0, tiled=True)]
where the time goes in v11:
time: 51.8 us; the launch traced here: 51.6 us
  blocking collectives  39.1 us (75%)
  Pallas kernels  5.63 us (11%)
  waiting for transfers between devices  4.98 us (10%)
  other arithmetic  0.93 us (2%)
  starting transfers between devices  0.74 us (1%)
    all_to_all x1, blocking collectives, whole_planes(): lax.all_to_all(parcels, ('gx', 'gy'), 0, 0, tiled=True)  15.8 us
    all_to_all x1, blocking collectives, whole_planes(): packed = lax.all_to_all(copies, ('gx', 'gy', 'gz'), 0, 0, tiled=True)  13.6 us
    all_to_all x1, blocking collectives, whole_planes(): lax.all_to_all(mine, ('gx', 'gy'), 0, 0, tiled=True)  9.7 us
    ppermute x2, waiting for transfers between devices, swap(): lax.ppermute(field, ('gx', 'gy', 'gz'), pairs + [pair[::-1] for pair in p...  4.98 us
    pallas_call x1, Pallas kernels, whole_planes(): pl.pallas_call(functools.partial(up_kernel, groups, by, share), out_shape...  2.09 us
    pallas_call x1, Pallas kernels, whole_planes(): pl.pallas_call(functools.partial(down_kernel, groups, by, share), out_sha...  1.96 us
  transfers between devices with their start and end apart: 2, of which 1 were waited for; matrix products, arithmetic and copies ran while one was open for 0% of the time, Pallas kernels for 0%

profile of v11, /device:TPU:0, one launch (start us, length us, event | category | flops | bytes accessed | tf_op | source)
XLA Modules:
  0.0 51.6 jit_solution(11408115693363261385)
XLA Ops:
  0.0 0.0 copy-start
  0.0 0.9 %multiply_multiply_fusion = (f32[16,8,128]{2,1,0:T(8,128)S(1)}, f32[16,8,128]{2,1,0:T(8,128)S(1)}) fusion(s32[16,8,128]{2,1,0:T(8,128)} %param.5, f32[16,8,128]{2,1,0:T(8,128)} %param.4), kind=kLoop, calls=%fused_computation | loop fusion | flops 65536 | bytes 262144 | tf_op jit(solution)/shard_map/mul | solution.py:634
  0.9 0.1 copy-done
  1.0 0.5 prepare.1
  1.5 15.8 %all_to_all.15.gathered = f32[8,48,128]{2,1,0:T(8,128)S(1)} all-to-all(f32[8,48,128]{2,1,0:T(8,128)S(1)} %prepare.1), channel_id=1, replica_groups=mesh['gx'=2,'gy'=4,'gz'=4] {'gx','gy'}, dimensions={0} | all-to-all | bytes 393216 | tf_op jit(solution)/shard_map/all_to_all | solution.py:646
  17.3 0.2 spread.1.own
  17.6 0.1 collective-permute-start.1
  17.6 0.7 %collective-permute-start = (f32[48,8,128]{2,1,0:T(8,128)S(1)}, f32[48,8,128]{2,1,0:T(8,128)S(1)}, u32[]{:S(2)}, u32[]{:S(2)}) collective-permute-start(f32[48,8,128]{2,1,0:T(8,128)S(1)} %spread.1.own), channel_id=1, source_target_pairs={{4,8},{12,28},{24,20},{16,17},{21,25},{29,13},{9,5},{1,2},{6,10},{... | collective-permute-start | bytes 589832 | tf_op jit(solution)/shard_map/ppermute | solution.py:654
  18.3 5.0 %collective-permute-done.1.inner = f32[48,8,128]{2,1,0:T(8,128)S(1)} collective-permute-done((f32[48,8,128]{2,1,0:T(8,128)S(1)}, f32[48,8,128]{2,1,0:T(8,128)S(1)}, u32[]{:S(2)}, u32[]{:S(2)}) %collective-permute-start.1) | collective-permute-done | bytes 196640 | tf_op jit(solution)/shard_map/ppermute | solution.py:654
  23.3 0.0 collective-permute-done.outer
  23.3 2.0 %down.1 = (f32[48,8,128]{2,1,0:T(8,128)S(1)}, f32[48,8,128]{2,1,0:T(8,128)S(1)}, f32[48,8,128]{2,1,0:T(8,128)S(1)}, f32[48,8,128]{2,1,0:T(8,128)S(1)}, f32[48,8,...) custom-call(f32[48,8,128]{2,1,0:T(8,128)S(1)} %spread.1.own, ...), custom_call_target="tpu_custom_call" | custom-call | tf_op jit(solution)/shard_map/down/pallas_call | solution.py:658
  25.3 13.6 %all_to_all.16.packed = f32[32,5,2,128]{3,2,1,0:T(2,128)S(1)} all-to-all(f32[32,5,2,128]{3,2,1,0:T(2,128)S(1)} %broadcast_in_dim.3), channel_id=1, replica_groups=mesh['gx'=2,'gy'=4,'gz'=4] {'gx','gy','gz'}, dimensions={0} | all-to-all | bytes 327680 | tf_op jit(solution)/shard_map/all_to_all | solution.py:666
  39.0 2.1 %up.1 = f32[8,16,128]{2,1,0:T(8,128)S(1)} custom-call(f32[32,5,2,128]{3,2,1,0:T(2,128)S(1)} %all_to_all.16.packed, f32[48,8,128]{2,1,0:T(8,128)S(1)} %get-tuple-element.25.xn1, f32[48,8,128]{2,1,0:T(8,128)S(1)} %get-tuple-element.26.xl1, f32[48,8,128]{2,1,0:T(8,128)S(1)} %get-tuple-element.27.yn1, f32[48,8,128]{2,1,0:T(8,128)S(1)} %get-tuple-element.28.yl1, ...), custom_call_target="tpu_custom_call" | custom-call | tf_op jit(solution)/shard_map/up/pallas_call | solution.py:668
  41.1 9.7 %all_to_all.17.blocks = f32[8,16,128]{2,1,0:T(8,128)S(1)} all-to-all(f32[8,16,128]{2,1,0:T(8,128)S(1)} %up.1), channel_id=1, replica_groups=mesh['gx'=2,'gy'=4,'gz'=4] {'gx','gy'}, dimensions={0} | all-to-all | bytes 131072 | tf_op jit(solution)/shard_map/all_to_all | solution.py:681
  50.8 0.8 %finish.1 = f32[16,8,128]{2,1,0:T(8,128)} custom-call(f32[8,16,128]{2,1,0:T(8,128)S(1)} %all_to_all.17.blocks), custom_call_target="tpu_custom_call" | custom-call | tf_op jit(solution)/shard_map/finish/pallas_call | solution.py:676
  (1 shorter events, 0.0 us)
Async XLA Ops:
  0.0 1.0 %copy-start = (bf16[32,16,256]{2,1,0:T(8,128)(2,1)S(1)}, bf16[32,16,256]{2,1,0:T(8,128)(2,1)}, u32[]{:S(2)}) copy-start(bf16[32,16,256]{2,1,0:T(8,128)(2,1)} %param.3) | copy-start | bytes 786436
  17.6 5.7 %collective-permute-start.1 = (f32[48,8,128]{2,1,0:T(8,128)S(1)}, f32[48,8,128]{2,1,0:T(8,128)S(1)}, u32[]{:S(2)}, u32[]{:S(2)}) collective-permute-start(f32[48,8,128]{2,1,0:T(8,128)S(1)} %spread.1.own), channel_id=1, source_target_pairs={{0,4},{8,12},{28,24},{20,16},{17,21},{25,29},{13,9},{5,1},{2,6},{1... | collective-permute-start | bytes 589832 | tf_op jit(solution)/shard_map/ppermute | solution.py:654
  17.6 5.7 %collective-permute-start = (f32[48,8,128]{2,1,0:T(8,128)S(1)}, f32[48,8,128]{2,1,0:T(8,128)S(1)}, u32[]{:S(2)}, u32[]{:S(2)}) collective-permute-start(f32[48,8,128]{2,1,0:T(8,128)S(1)} %spread.1.own), channel_id=1, source_target_pairs={{4,8},{12,28},{24,20},{16,17},{21,25},{29,13},{9,5},{1,2},{6,10},{... | collective-permute-start | bytes 589832 | tf_op jit(solution)/shard_map/ppermute | solution.py:654

commit v12 on v11

--- a/solution.py
+++ b/solution.py
@@ -304,33 +304,50 @@
     return dot01(flat, chosen).reshape(field.shape)
 
 
-def peer_at(rank):
-    ny = SPLIT[1]
-    ix, place_on_row = rank // ny, rank % ny
-    return ix * ny + (ny - 1 - place_on_row if ix % 2 else place_on_row)
-
-
-def peer_of(group, rank):
-    return peer_at(SPLIT[0] * SPLIT[1] - 1 - rank if group % 2 else rank)
+def path_of(group):
+    nx, ny = SPLIT
+    row, column = 0, 0
+    for index in range(group + 1):
+        columns = list(range(ny)) if column == 0 else list(range(ny))[::-1]
+        if index % 2:
+            path = [(row, at) for at in columns] + [(1 - row, at) for at in columns[::-1]]
+        else:
+            path = []
+            for at in columns:
+                path += [(row, at), (1 - row, at)]
+                row = 1 - row
+        row, column = path[-1]
+    return [row * ny + column for row, column in path]
+
+
+def lookup(table, index):
+    found = table[0]
+    for at, value in enumerate(table[1:], 1):
+        found = jnp.where(index == at, value, found)
+    return found
 
 
 def own_peer_of(rank):
-    return jnp.where(lax.axis_index("gz") % 2 == 1, peer_of(1, rank), peer_of(0, rank))
-
-
-def slab_of(ix, iy, group):
+    return lookup([path_of(group)[rank] for group in range(lax.axis_size("gz"))], lax.axis_index("gz"))
+
+
+def slabs_of(groups):
+    peers = SPLIT[0] * SPLIT[1]
+    return [
+        group * peers + path_of(group).index(peer) for peer in range(peers) for group in range(groups)
+    ]
+
+
+def own_slab():
     nx, ny = SPLIT
-    rank = ix * ny + jnp.where(ix % 2 == 1, ny - 1 - iy, iy)
-    return group * nx * ny + jnp.where(group % 2 == 1, nx * ny - 1 - rank, rank)
-
-
-def device_of(slab):
-    nx, ny = SPLIT
-    group, rank = slab // (nx * ny), slab % (nx * ny)
-    rank = jnp.where(group % 2 == 1, nx * ny - 1 - rank, rank)
-    row, column = rank // ny, rank % ny
-    peer = row * ny + jnp.where(row % 2 == 1, ny - 1 - column, column)
-    return peer * lax.axis_size("gz") + group
+    groups = lax.axis_size("gz")
+    device = (lax.axis_index("gx") * ny + lax.axis_index("gy")) * groups + lax.axis_index("gz")
+    return lookup(slabs_of(groups), device)
+
+
+def devices_of(groups):
+    slabs = slabs_of(groups)
+    return [slabs.index(slab) for slab in range(len(slabs))]
 
 
 def prepare_kernel(share, res_ref, fluid_ref, pin_ref, out_ref):
@@ -388,7 +405,7 @@
     fluid1, rhs1, pin1, other1, fluid2, rhs2, pin2, other2, sums,
 ):
     planes = depth + 2 * HALO
-    part = slab_of(lax.axis_index("gx"), lax.axis_index("gy"), lax.axis_index("gz"))
+    part = own_slab()
     odd = part % 2 == 1
     for index, target in enumerate((fluid1, rhs1, pin1)):
         rows = slice(index * depth, (index + 1) * depth)
@@ -509,8 +526,8 @@
     count3 = depth // 4
     shares = packed.shape[0]
     peers = SPLIT[0] * SPLIT[1]
-    for slab in range(shares):
-        index = peer_of(slab // peers, slab % peers) * (shares // peers) + slab // peers
+    devices = devices_of(shares // peers)
+    for slab, index in enumerate(devices):
         row = slab * count3
         first[row : row + 2] = packed[index, 0]
         first[row + 2 : row + 4] = packed[index, 1]
@@ -532,17 +549,18 @@
     solved[NEAR + shares * count3 :] = jnp.zeros((2 * NEAR, LANES), F32)
 
     nx, ny = SPLIT
-    part = slab_of(lax.axis_index("gx"), lax.axis_index("gy"), lax.axis_index("gz"))
+    part = own_slab()
     count = count3 + 2 * NEAR
     tall = solved[pl.ds(part * count3, count + count3), :]
     fine, coarse = Level(0), Level(1)
-    cell = iota((LANES, ROWS * LANES), 0)
-    lane = iota((LANES, ROWS * LANES), 1)
-    same_y = cell % ROWS == (lane % coarse.ny) // 2
-    spread = where01((cell // ROWS == lane // LANES) & same_y)
-    wide = dot01(tall, spread)
+    cell = iota((LANES, LANES), 0)
+    lane = iota((LANES, LANES), 1)
+    spread = where01((cell < ROWS) & (cell == (lane % coarse.ny) // 2))
+    rows = tall.shape[0]
+    turned = [tall] + [pltpu.roll(tall, LANES - ROWS * row, 1) for row in range(1, ROWS)]
+    wide = dot01(jnp.concatenate(turned, axis=0), spread)
     for row in range(ROWS):
-        lifted[0:count, row, :] = wide[:count, row * LANES : (row + 1) * LANES]
+        lifted[0:rows, row, :] = wide[row * rows : (row + 1) * rows]
 
     fields1 = ((xn1, xl1, yn1, yl1, zn1, zl1), start1, diag1)
     fields2 = ((xn2, xl2, yn2, yl2, zn2, zl2), start2, diag2)
@@ -554,7 +572,7 @@
     row = iota((ROWS, LANES), 0)
 
     def unpacked(index, which):
-        pair = packed[device_of(jnp.clip(index, 0, shares - 1)), which]
+        pair = packed[lookup(devices, jnp.clip(index, 0, shares - 1)), which]
         total = None
         for shift in range(4):
             moved = pltpu.roll(pair, shift * (LANES // 4), 1)
@@ -647,7 +665,7 @@
     length = lax.axis_size("gz")
     parts = length * peers
 
-    device = [peer_of(i // peers, i % peers) * length + i // peers for i in range(parts)]
+    device = devices_of(length)
 
     def swap(field, first):
         pairs = [(device[i], device[i + 1]) for i in range(first, parts - 1, 2)]

time: 51.8 us -> 51.1 us (0.986)
  blocking collectives: 39.1 us -> 37.6 us
  starting transfers between devices: 0.74 us -> 1.29 us
    all_to_all x1, blocking collectives: 13.6 us -> 12.1 us  [whole_planes(): packed = lax.all_to_all(copies, ('gx', 'gy', 'gz'), 0, 0, tiled=True)]
    ppermute x2, starting transfers between devices: 0.74 us -> 1.29 us  [swap(): lax.ppermute(field, ('gx', 'gy', 'gz'), pairs + [pair[::-1] for pair in p...]
where the time goes in v12:
time: 51.1 us; the launch traced here: 50.9 us
  blocking collectives  37.6 us (74%)
  Pallas kernels  5.6 us (11%)
  waiting for transfers between devices  5.34 us (10%)
  starting transfers between devices  1.29 us (3%)
  other arithmetic  0.93 us (2%)
    all_to_all x1, blocking collectives, whole_planes(): lax.all_to_all(parcels, ('gx', 'gy'), 0, 0, tiled=True)  15.8 us
    all_to_all x1, blocking collectives, whole_planes(): packed = lax.all_to_all(copies, ('gx', 'gy', 'gz'), 0, 0, tiled=True)  12.1 us
    all_to_all x1, blocking collectives, whole_planes(): lax.all_to_all(mine, ('gx', 'gy'), 0, 0, tiled=True)  9.7 us
    ppermute x2, waiting for transfers between devices, swap(): lax.ppermute(field, ('gx', 'gy', 'gz'), pairs + [pair[::-1] for pair in p...  5.34 us
    pallas_call x1, Pallas kernels, whole_planes(): pl.pallas_call(functools.partial(up_kernel, groups, by, share), out_shape...  2.11 us
    pallas_call x1, Pallas kernels, whole_planes(): pl.pallas_call(functools.partial(down_kernel, groups, by, share), out_sha...  1.91 us
    ppermute x2, starting transfers between devices, swap(): lax.ppermute(field, ('gx', 'gy', 'gz'), pairs + [pair[::-1] for pair in p...  1.29 us
  transfers between devices with their start and end apart: 2, of which 1 were waited for; matrix products, arithmetic and copies ran while one was open for 0% of the time, Pallas kernels for 0%

profile of v12, /device:TPU:0, one launch (start us, length us, event | category | flops | bytes accessed | tf_op | source)
XLA Modules:
  0.0 50.9 jit_solution(4934766010807267501)
XLA Ops:
  0.0 0.0 copy-start
  0.0 0.9 %multiply_multiply_fusion = (f32[16,8,128]{2,1,0:T(8,128)S(1)}, f32[16,8,128]{2,1,0:T(8,128)S(1)}) fusion(s32[16,8,128]{2,1,0:T(8,128)} %param.5, f32[16,8,128]{2,1,0:T(8,128)} %param.4), kind=kLoop, calls=%fused_computation | loop fusion | flops 65536 | bytes 262144 | tf_op jit(solution)/shard_map/mul | solution.py:652
  0.9 0.1 copy-done
  1.0 0.5 prepare.1
  1.5 15.8 %all_to_all.15.gathered = f32[8,48,128]{2,1,0:T(8,128)S(1)} all-to-all(f32[8,48,128]{2,1,0:T(8,128)S(1)} %prepare.1), channel_id=1, replica_groups=mesh['gx'=2,'gy'=4,'gz'=4] {'gx','gy'}, dimensions={0} | all-to-all | bytes 393216 | tf_op jit(solution)/shard_map/all_to_all | solution.py:664
  17.3 0.2 spread.1.own
  17.6 0.6 %collective-permute-start.1 = (f32[48,8,128]{2,1,0:T(8,128)S(1)}, f32[48,8,128]{2,1,0:T(8,128)S(1)}, u32[]{:S(2)}, u32[]{:S(2)}) collective-permute-start(f32[48,8,128]{2,1,0:T(8,128)S(1)} %spread.1.own), channel_id=1, source_target_pairs={{0,16},{20,4},{8,24},{28,12},{13,9},{5,1},{17,21},{25,29},{30,14},... | collective-permute-start | bytes 589832 | tf_op jit(solution)/shard_map/ppermute | solution.py:672
  18.2 0.7 %collective-permute-start = (f32[48,8,128]{2,1,0:T(8,128)S(1)}, f32[48,8,128]{2,1,0:T(8,128)S(1)}, u32[]{:S(2)}, u32[]{:S(2)}) collective-permute-start(f32[48,8,128]{2,1,0:T(8,128)S(1)} %spread.1.own), channel_id=1, source_target_pairs={{16,20},{4,8},{24,28},{12,13},{9,5},{1,17},{21,25},{29,30},{14,10}... | collective-permute-start | bytes 589832 | tf_op jit(solution)/shard_map/ppermute | solution.py:672
  18.9 5.3 %collective-permute-done.1.inner = f32[48,8,128]{2,1,0:T(8,128)S(1)} collective-permute-done((f32[48,8,128]{2,1,0:T(8,128)S(1)}, f32[48,8,128]{2,1,0:T(8,128)S(1)}, u32[]{:S(2)}, u32[]{:S(2)}) %collective-permute-start.1) | collective-permute-done | bytes 196640 | tf_op jit(solution)/shard_map/ppermute | solution.py:672
  24.2 0.0 collective-permute-done.outer
  24.2 1.9 %down.1 = (f32[48,8,128]{2,1,0:T(8,128)S(1)}, f32[48,8,128]{2,1,0:T(8,128)S(1)}, f32[48,8,128]{2,1,0:T(8,128)S(1)}, f32[48,8,128]{2,1,0:T(8,128)S(1)}, f32[48,8,...) custom-call(f32[48,8,128]{2,1,0:T(8,128)S(1)} %spread.1.own, ...), custom_call_target="tpu_custom_call" | custom-call | tf_op jit(solution)/shard_map/down/pallas_call | solution.py:676
  26.2 12.1 %all_to_all.16.packed = f32[32,5,2,128]{3,2,1,0:T(2,128)S(1)} all-to-all(f32[32,5,2,128]{3,2,1,0:T(2,128)S(1)} %broadcast_in_dim.3), channel_id=1, replica_groups=mesh['gx'=2,'gy'=4,'gz'=4] {'gx','gy','gz'}, dimensions={0} | all-to-all | bytes 327680 | tf_op jit(solution)/shard_map/all_to_all | solution.py:684
  38.2 2.1 %up.1 = f32[8,16,128]{2,1,0:T(8,128)S(1)} custom-call(f32[32,5,2,128]{3,2,1,0:T(2,128)S(1)} %all_to_all.16.packed, f32[48,8,128]{2,1,0:T(8,128)S(1)} %get-tuple-element.25.xn1, f32[48,8,128]{2,1,0:T(8,128)S(1)} %get-tuple-element.26.xl1, f32[48,8,128]{2,1,0:T(8,128)S(1)} %get-tuple-element.27.yn1, f32[48,8,128]{2,1,0:T(8,128)S(1)} %get-tuple-element.28.yl1, ...), custom_call_target="tpu_custom_call" | custom-call | tf_op jit(solution)/shard_map/up/pallas_call | solution.py:686
  40.3 9.7 %all_to_all.17.blocks = f32[8,16,128]{2,1,0:T(8,128)S(1)} all-to-all(f32[8,16,128]{2,1,0:T(8,128)S(1)} %up.1), channel_id=1, replica_groups=mesh['gx'=2,'gy'=4,'gz'=4] {'gx','gy'}, dimensions={0} | all-to-all | bytes 131072 | tf_op jit(solution)/shard_map/all_to_all | solution.py:699
  50.0 0.8 %finish.1 = f32[16,8,128]{2,1,0:T(8,128)} custom-call(f32[8,16,128]{2,1,0:T(8,128)S(1)} %all_to_all.17.blocks), custom_call_target="tpu_custom_call" | custom-call | tf_op jit(solution)/shard_map/finish/pallas_call | solution.py:694
  (1 shorter events, 0.0 us)
Async XLA Ops:
  0.0 1.0 %copy-start = (bf16[32,16,256]{2,1,0:T(8,128)(2,1)S(1)}, bf16[32,16,256]{2,1,0:T(8,128)(2,1)}, u32[]{:S(2)}) copy-start(bf16[32,16,256]{2,1,0:T(8,128)(2,1)} %param.3) | copy-start | bytes 786436
  17.6 6.6 %collective-permute-start.1 = (f32[48,8,128]{2,1,0:T(8,128)S(1)}, f32[48,8,128]{2,1,0:T(8,128)S(1)}, u32[]{:S(2)}, u32[]{:S(2)}) collective-permute-start(f32[48,8,128]{2,1,0:T(8,128)S(1)} %spread.1.own), channel_id=1, source_target_pairs={{0,16},{20,4},{8,24},{28,12},{13,9},{5,1},{17,21},{25,29},{30,14},... | collective-permute-start | bytes 589832 | tf_op jit(solution)/shard_map/ppermute | solution.py:672
  18.2 6.0 %collective-permute-start = (f32[48,8,128]{2,1,0:T(8,128)S(1)}, f32[48,8,128]{2,1,0:T(8,128)S(1)}, u32[]{:S(2)}, u32[]{:S(2)}) collective-permute-start(f32[48,8,128]{2,1,0:T(8,128)S(1)} %spread.1.own), channel_id=1, source_target_pairs={{16,20},{4,8},{24,28},{12,13},{9,5},{1,17},{21,25},{29,30},{14,10}... | collective-permute-start | bytes 589832 | tf_op jit(solution)/shard_map/ppermute | solution.py:672

commit v13 on v12

--- a/solution.py
+++ b/solution.py
@@ -141,7 +141,7 @@
 SPLIT = (2, 4)
 ROWS = 8
 LANES = 128
-HALO = 16
+HALO = 10
 NEAR = 8
 PIECE = 8
 TINY = 1e-30
@@ -377,9 +377,16 @@
             out_ref[peer, index * share : (index + 1) * share] = field[begin : begin + share]
 
 
-def spread_kernel(groups, by, gathered, own):
+def spread_kernel(groups, by, gathered, own, inner, outer):
     for start in range(0, own.shape[0], ROWS):
         place(gathered, start, own, start, groups, by)
+    share = own.shape[0] // 3
+    odd = own_slab() % 2 == 1
+    top = share - HALO
+    for index in range(3):
+        rows = slice(index * HALO, (index + 1) * HALO)
+        inner[rows] = own[pl.ds(index * share + jnp.where(odd, 0, top), HALO)]
+        outer[rows] = own[pl.ds(index * share + jnp.where(odd, top, 0), HALO)]
 
 
 def place(gathered, row, target, plane, groups, by):
@@ -398,19 +405,19 @@
 
 def down_kernel(
     groups, by, depth,
-    own, outer, inner,
+    own, inner, outer,
     xn1, xl1, yn1, yl1, zn1, zl1, start1, diag1, corr1,
     xn2, xl2, yn2, yl2, zn2, zl2, start2, diag2, corr2,
-    packed,
+    packed, inner2, outer2,
     fluid1, rhs1, pin1, other1, fluid2, rhs2, pin2, other2, sums,
 ):
     planes = depth + 2 * HALO
     part = own_slab()
     odd = part % 2 == 1
     for index, target in enumerate((fluid1, rhs1, pin1)):
-        rows = slice(index * depth, (index + 1) * depth)
+        rows = slice(index * HALO, (index + 1) * HALO)
         target[0:HALO] = jnp.where(odd, inner[rows], outer[rows])
-        target[HALO : HALO + depth] = own[rows]
+        target[HALO : HALO + depth] = own[index * depth : (index + 1) * depth]
         target[HALO + depth :] = jnp.where(odd, outer[rows], inner[rows])
 
     fine, coarse = Level(0), Level(1)
@@ -420,19 +427,23 @@
     set_level(fine, 1, planes - 1, fluid1, pin1, rhs1, fields1)
     sweep(fine, 2, planes - 2, fields1, start1, other1)
     sweep(fine, 3, planes - 3, fields1, other1, corr1)
-    count2 = depth // 2 + 2 * NEAR
-    begin = HALO - 2 * NEAR
+    first2, last2 = NEAR - HALO // 2, NEAR + depth // 2 + HALO // 2
     for source, target, share in ((fluid1, fluid2, 8.0), (pin1, pin2, 4.0)):
-        whole = pair_sum(source[begin : begin + 2 * count2])
-        target[...] = in_lanes(whole, down1) * (1.0 / share)
-    low2, high2 = (begin + 4) // 2, count2 - (begin + 4) // 2
-    inner = high2 - low2
-    coarse_residual(fine, begin + 2 * low2, begin + 2 * high2, fields1, corr1, sums)
-    rhs2[low2:high2] = in_lanes(sums[0:inner], down1)
-    set_level(coarse, low2, high2, fluid2, pin2, rhs2, fields2)
+        target[first2:last2] = in_lanes(pair_sum(source[...]), down1) * (1.0 / share)
+    low2, high2 = first2 + 2, last2 - 2
+    coarse_residual(fine, 4, planes - 4, fields1, corr1, sums)
+    rhs2[low2:high2] = in_lanes(sums[0 : high2 - low2], down1)
+    set_level(coarse, low2 - 1, high2 + 1, fluid2, pin2, rhs2, fields2)
     sweep(coarse, low2 + 1, high2 - 1, fields2, start2, other2)
     sweep(coarse, low2 + 2, high2 - 2, fields2, other2, corr2)
-    coarse_residual(coarse, NEAR, NEAR + depth // 2, fields2, corr2, sums)
+    half = depth // 2
+    above, below = NEAR + half - 5, NEAR + 1
+    inner2[0:4] = corr2[pl.ds(jnp.where(odd, below, above), 4)]
+    outer2[0:4] = corr2[pl.ds(jnp.where(odd, above, below), 4)]
+    above, below = NEAR + half - 4, NEAR + 3
+    inner2[4] = start2[jnp.where(odd, below, above)]
+    outer2[4] = start2[jnp.where(odd, above, below)]
+    coarse_residual(coarse, NEAR, NEAR + half, fields2, corr2, sums)
     count3 = depth // 4
     rhs3 = in_lanes(sums[0:count3], down2)
     fluid3 = in_lanes(pair_sum(fluid2[NEAR : NEAR + 2 * count3]), down2) * 0.125
@@ -447,14 +458,6 @@
     packed[0] = first[0:2]
     packed[1] = first[2:4]
     packed[2] = jnp.where(lane[0:2] < ROWS, second[0:2], second[2:4])
-    lane = iota((1, LANES), 1) // (LANES // 4)
-    for index, plane in enumerate((NEAR + depth // 2 - 5, NEAR + 4)):
-        for half in range(2):
-            row = jnp.zeros((1, LANES), F32)
-            for quarter in range(4):
-                at = half * 4 + quarter
-                row = jnp.where(lane == quarter, corr2[plane, at : at + 1, :], row)
-            packed[3 + index, half : half + 1, :] = row
 
 
 def rolled(field, shift):
@@ -517,11 +520,11 @@
 
 def up_kernel(
     groups, by, depth,
-    packed,
+    packed, inner2, outer2,
     xn1, xl1, yn1, yl1, zn1, zl1, start1, diag1, corr1,
     xn2, xl2, yn2, yl2, zn2, zl2, start2, diag2, corr2,
     out_ref,
-    one1, two1, one2, two2, lifted, first, second, solved,
+    one1, two1, one2, two2, lifted, begun, first, second, solved,
 ):
     count3 = depth // 4
     shares = packed.shape[0]
@@ -563,28 +566,22 @@
         lifted[0:rows, row, :] = wide[row * rows : (row + 1) * rows]
 
     fields1 = ((xn1, xl1, yn1, yl1, zn1, zl1), start1, diag1)
-    fields2 = ((xn2, xl2, yn2, yl2, zn2, zl2), start2, diag2)
-    low, high = NEAR - 4, NEAR + depth // 2 + 4
-    parents = lifted[low // 2 + NEAR // 2 : high // 2 + NEAR // 2]
-    twice = jnp.broadcast_to(parents[:, None], (parents.shape[0], 2, ROWS, LANES))
+    fields2 = ((xn2, xl2, yn2, yl2, zn2, zl2), begun, diag2)
     reach = depth // 2 + NEAR
-    quarter = iota((ROWS, LANES), 1) // (LANES // 4)
-    row = iota((ROWS, LANES), 0)
-
-    def unpacked(index, which):
-        pair = packed[lookup(devices, jnp.clip(index, 0, shares - 1)), which]
-        total = None
-        for shift in range(4):
-            moved = pltpu.roll(pair, shift * (LANES // 4), 1)
-            wide = jnp.where(row < 4, moved[0:1, :], moved[1:2, :])
-            kept = jnp.where((quarter - shift) % 4 == row % 4, wide, 0.0)
-            total = kept if total is None else total + kept
-        return total
-
-    before, after = unpacked(part - 1, 3), unpacked(part + 1, 4)
-    one2[low - 1] = before + lifted[(low - 1) // 2 + NEAR // 2]
-    one2[low:high] = corr2[low:high] + twice.reshape(high - low, ROWS, LANES)
-    one2[high] = after + lifted[high // 2 + NEAR // 2]
+    odd = part % 2 == 1
+    below = jnp.where(odd, inner2[...], outer2[...])
+    above = jnp.where(odd, outer2[...], inner2[...])
+    for plane in range(NEAR - 5, reach + 5):
+        if plane < NEAR - 1:
+            corr = below[plane - (NEAR - 5)]
+        elif plane > reach:
+            corr = above[plane - (reach + 1)]
+        else:
+            corr = corr2[plane]
+        one2[plane] = corr + lifted[plane // 2 + NEAR // 2]
+    begun[NEAR - 4] = below[4]
+    begun[NEAR - 3 : reach + 3] = start2[NEAR - 3 : reach + 3]
+    begun[reach + 3] = above[4]
     sweep(coarse, NEAR - 4, reach + 4, fields2, one2, two2)
     sweep(coarse, NEAR - 3, reach + 3, fields2, two2, one2)
     sweep(coarse, NEAR - 2, reach + 2, fields2, one2, two2)
@@ -656,9 +653,9 @@
         compiler_params=limit,
         name="prepare",
     )(residual_q2.reshape(4 * bx * by, 2 * depth), fluid, pin)
-    own = pl.pallas_call(
+    own, inner, outer = pl.pallas_call(
         functools.partial(spread_kernel, groups, by),
-        out_shape=blocks(3 * share, ROWS),
+        out_shape=(blocks(3 * share, ROWS), blocks(3 * HALO, ROWS), blocks(3 * HALO, ROWS)),
         compiler_params=limit,
         name="spread",
     )(lax.all_to_all(parcels, ("gx", "gy"), 0, 0, tiled=True))
@@ -671,26 +668,28 @@
         pairs = [(device[i], device[i + 1]) for i in range(first, parts - 1, 2)]
         return lax.ppermute(field, ("gx", "gy", "gz"), pairs + [pair[::-1] for pair in pairs])
 
-    outer, inner = swap(own, 1), swap(own, 0)
+    outer, inner = swap(outer, 1), swap(inner, 0)
     saved = (blocks(planes, ROWS),) * 9 + (blocks(count2, ROWS),) * 9
     results = pl.pallas_call(
         functools.partial(down_kernel, groups, by, share),
-        out_shape=saved + (blocks(5, 2),),
+        out_shape=saved + (blocks(3, 2), blocks(5, ROWS), blocks(5, ROWS)),
         scratch_shapes=[room(planes)] * 4 + [room(count2)] * 5,
         compiler_params=limit,
         name="down",
-    )(own, outer, inner)
-    copies = jnp.broadcast_to(results[-1], (parts,) + results[-1].shape)
+    )(own, inner, outer)
+    saved, (parcel, inner, outer) = results[:-3], results[-3:]
+    outer, inner = swap(outer, 1), swap(inner, 0)
+    copies = jnp.broadcast_to(parcel, (parts,) + parcel.shape)
     packed = lax.all_to_all(copies, ("gx", "gy", "gz"), 0, 0, tiled=True)
     depth3 = parts * share // 4
     mine = pl.pallas_call(
         functools.partial(up_kernel, groups, by, share),
         out_shape=blocks(peers, share),
-        scratch_shapes=[room(planes), room(planes), room(count2), room(count2), room(count2)]
+        scratch_shapes=[room(planes)] * 2 + [room(count2)] * 4
         + [pltpu.VMEM((rows, LANES), F32) for rows in (depth3, depth3, depth3 + 3 * NEAR)],
         compiler_params=limit,
         name="up",
-    )(packed, *results[:-1])
+    )(packed, inner, outer, *saved)
     return pl.pallas_call(
         finish_kernel,
         out_shape=jax.ShapeDtypeStruct((bx, by, depth), F32),

time: 51.1 us -> 51.3 us (level)
  blocking collectives: 37.6 us -> 26.7 us
  starting transfers between devices: 1.29 us -> 8.23 us
  waiting for transfers between devices: 5.34 us -> 9.22 us
  local copies, waits for them, and re-layouts: 0.12 us -> 0.74 us
    all_to_all x1 -> x0, blocking collectives: 12.1 us -> none  [whole_planes(): packed = lax.all_to_all(copies, ('gx', 'gy', 'gz'), 0, 0, tiled=True)]
    all_to_all x0 -> x1, starting transfers between devices: none -> 4.46 us  [whole_planes(): packed = lax.all_to_all(copies, ('gx', 'gy', 'gz'), 0, 0, tiled=True)]
    all_to_all x0 -> x1, waiting for transfers between devices: none -> 4.09 us  [whole_planes(): packed = lax.all_to_all(copies, ('gx', 'gy', 'gz'), 0, 0, tiled=True)]
    ppermute x2 -> x4, starting transfers between devices: 1.29 us -> 3.77 us  [swap(): lax.ppermute(field, ('gx', 'gy', 'gz'), pairs + [pair[::-1] for pair in p...]
    all_to_all x1, blocking collectives: 9.7 us -> 10.9 us  [whole_planes(): lax.all_to_all(mine, ('gx', 'gy'), 0, 0, tiled=True)]
    broadcast_in_dim x1, local copies, waits for them, and re-layouts: 0.04 us -> 0.66 us  [whole_planes(): copies = jnp.broadcast_to(parcel, (parts,) + parcel.shape)]
    pallas_call x1, Pallas kernels: 1.91 us -> 1.38 us  [whole_planes(): pl.pallas_call(functools.partial(down_kernel, groups, by, share), out_sha...]
    ppermute x2 -> x4, waiting for transfers between devices: 5.34 us -> 5.13 us  [swap(): lax.ppermute(field, ('gx', 'gy', 'gz'), pairs + [pair[::-1] for pair in p...]
  transfers between devices with their start and end apart: 2 -> 5, of which waited for: 1 -> 3; matrix products, arithmetic and copies ran while one was open for 0% -> 0% of each run, Pallas kernels for 0% -> 0%
where the time goes in v13:
time: 51.3 us; the launch traced here: 51 us
  blocking collectives  26.7 us (52%)
  waiting for transfers between devices  9.22 us (18%)
  starting transfers between devices  8.23 us (16%)
  Pallas kernels  5.09 us (10%)
  other arithmetic  0.93 us (2%)
  local copies, waits for them, and re-layouts  0.74 us (1%)
    all_to_all x1, blocking collectives, whole_planes(): lax.all_to_all(parcels, ('gx', 'gy'), 0, 0, tiled=True)  15.8 us
    all_to_all x1, blocking collectives, whole_planes(): lax.all_to_all(mine, ('gx', 'gy'), 0, 0, tiled=True)  10.9 us
    ppermute x4, waiting for transfers between devices, swap(): lax.ppermute(field, ('gx', 'gy', 'gz'), pairs + [pair[::-1] for pair in p...  5.13 us
    all_to_all x1, starting transfers between devices, whole_planes(): packed = lax.all_to_all(copies, ('gx', 'gy', 'gz'), 0, 0, tiled=True)  4.46 us
    all_to_all x1, waiting for transfers between devices, whole_planes(): packed = lax.all_to_all(copies, ('gx', 'gy', 'gz'), 0, 0, tiled=True)  4.09 us
    ppermute x4, starting transfers between devices, swap(): lax.ppermute(field, ('gx', 'gy', 'gz'), pairs + [pair[::-1] for pair in p...  3.77 us
    pallas_call x1, Pallas kernels, whole_planes(): pl.pallas_call(functools.partial(up_kernel, groups, by, share), out_shape...  2.11 us
    pallas_call x1, Pallas kernels, whole_planes(): pl.pallas_call(functools.partial(down_kernel, groups, by, share), out_sha...  1.38 us
  transfers between devices with their start and end apart: 5, of which 3 were waited for; matrix products, arithmetic and copies ran while one was open for 0% of the time, Pallas kernels for 0%

profile of v13, /device:TPU:0, one launch (start us, length us, event | category | flops | bytes accessed | tf_op | source)
XLA Modules:
  0.0 51.0 jit_solution(1290419787420092269)
XLA Ops:
  0.0 0.0 copy-start
  0.0 0.9 %multiply_multiply_fusion = (f32[16,8,128]{2,1,0:T(8,128)S(1)}, f32[16,8,128]{2,1,0:T(8,128)S(1)}) fusion(s32[16,8,128]{2,1,0:T(8,128)} %param.5, f32[16,8,128]{2,1,0:T(8,128)} %param.4), kind=kLoop, calls=%fused_computation | loop fusion | flops 65536 | bytes 262144 | tf_op jit(solution)/shard_map/mul | solution.py:649
  0.9 0.1 copy-done
  1.0 0.5 prepare.1
  1.5 15.8 %all_to_all.15.gathered = f32[8,48,128]{2,1,0:T(8,128)S(1)} all-to-all(f32[8,48,128]{2,1,0:T(8,128)S(1)} %prepare.1), channel_id=1, replica_groups=mesh['gx'=2,'gy'=4,'gz'=4] {'gx','gy'}, dimensions={0} | all-to-all | bytes 393216 | tf_op jit(solution)/shard_map/all_to_all | solution.py:661
  17.3 0.3 spread.1
  17.6 0.6 %collective-permute-start = (f32[30,8,128]{2,1,0:T(8,128)S(1)}, f32[30,8,128]{2,1,0:T(8,128)S(1)}, u32[]{:S(2)}, u32[]{:S(2)}) collective-permute-start(f32[30,8,128]{2,1,0:T(8,128)S(1)} %get-tuple-element.30), channel_id=1, source_target_pairs={{0,16},{20,4},{8,24},{28,12},{13,9},{5,1},{17,21},{25,29},{30,14},... | collective-permute-start | bytes 368648 | tf_op jit(solution)/shard_map/ppermute | solution.py:669
  18.2 0.7 %collective-permute-start.1 = (f32[30,8,128]{2,1,0:T(8,128)S(1)}, f32[30,8,128]{2,1,0:T(8,128)S(1)}, u32[]{:S(2)}, u32[]{:S(2)}) collective-permute-start(f32[30,8,128]{2,1,0:T(8,128)S(1)} %get-tuple-element.31), channel_id=1, source_target_pairs={{16,20},{4,8},{24,28},{12,13},{9,5},{1,17},{21,25},{29,30},{14,10}... | collective-permute-start | bytes 368648 | tf_op jit(solution)/shard_map/ppermute | solution.py:669
  18.9 3.8 %collective-permute-done.inner = f32[30,8,128]{2,1,0:T(8,128)S(1)} collective-permute-done((f32[30,8,128]{2,1,0:T(8,128)S(1)}, f32[30,8,128]{2,1,0:T(8,128)S(1)}, u32[]{:S(2)}, u32[]{:S(2)}) %collective-permute-start) | collective-permute-done | bytes 122912 | tf_op jit(solution)/shard_map/ppermute | solution.py:669
  22.6 0.0 collective-permute-done.1.outer
  22.6 1.4 %down.1 = (f32[36,8,128]{2,1,0:T(8,128)S(1)}, f32[36,8,128]{2,1,0:T(8,128)S(1)}, f32[36,8,128]{2,1,0:T(8,128)S(1)}, f32[36,8,128]{2,1,0:T(8,128)S(1)}, f32[36,8,...) custom-call(f32[48,8,128]{2,1,0:T(8,128)S(1)} %get-tuple-element.29., ...), custom_call_target="tpu_custom_call" | custom-call | tf_op jit(solution)/shard_map/down/pallas_call | solution.py:673
  24.0 0.7 %broadcast_in_dim.3 = f32[32,3,2,128]{3,2,1,0:T(2,128)} broadcast(f32[3,2,128]{2,1,0:T(2,128)S(1)} %get-tuple-element.32), dimensions={1,2,3} | broadcast | bytes 101376 | tf_op jit(solution)/shard_map/broadcast_in_dim | solution.py:682
  24.7 4.5 %all-to-all-start.1 = ((f32[32,3,2,128]{3,2,1,0:T(2,128)}), f32[32,3,2,128]{3,2,1,0:T(2,128)S(1)}, u32[]{:S(2)}, u32[]{:S(2)}) async-start(f32[32,3,2,128]{3,2,1,0:T(2,128)} %broadcast_in_dim.3), calls=%async_computation.1 | async-start | bytes 196608 | tf_op jit(solution)/shard_map/all_to_all | solution.py:683
  29.2 1.8 %collective-permute-start.2 = (f32[5,8,128]{2,1,0:T(8,128)S(1)}, f32[5,8,128]{2,1,0:T(8,128)S(1)}, u32[]{:S(2)}, u32[]{:S(2)}) collective-permute-start(f32[5,8,128]{2,1,0:T(8,128)S(1)} %get-tuple-element.33), channel_id=1, source_target_pairs={{0,16},{20,4},{8,24},{28,12},{13,9},{5,1},{17,21},{25,29},{30,14},... | collective-permute-start | bytes 61448 | tf_op jit(solution)/shard_map/ppermute | solution.py:669
  31.0 0.7 %collective-permute-start.3 = (f32[5,8,128]{2,1,0:T(8,128)S(1)}, f32[5,8,128]{2,1,0:T(8,128)S(1)}, u32[]{:S(2)}, u32[]{:S(2)}) collective-permute-start(f32[5,8,128]{2,1,0:T(8,128)S(1)} %get-tuple-element.34), channel_id=1, source_target_pairs={{16,20},{4,8},{24,28},{12,13},{9,5},{1,17},{21,25},{29,30},{14,10}... | collective-permute-start | bytes 61448 | tf_op jit(solution)/shard_map/ppermute | solution.py:669
  31.7 1.4 %collective-permute-done.2.inner2 = f32[5,8,128]{2,1,0:T(8,128)S(1)} collective-permute-done((f32[5,8,128]{2,1,0:T(8,128)S(1)}, f32[5,8,128]{2,1,0:T(8,128)S(1)}, u32[]{:S(2)}, u32[]{:S(2)}) %collective-permute-start.2) | collective-permute-done | bytes 20512 | tf_op jit(solution)/shard_map/ppermute | solution.py:669
  33.0 0.0 collective-permute-done.3.outer2
  33.0 4.1 %all-to-all-done.1.packed = f32[32,3,2,128]{3,2,1,0:T(2,128)S(1)} async-done(((f32[32,3,2,128]{3,2,1,0:T(2,128)}), f32[32,3,2,128]{3,2,1,0:T(2,128)S(1)}, u32[]{:S(2)}, u32[]{:S(2)}) %all-to-all-start.1) | async-done | bytes 98336 | tf_op jit(solution)/shard_map/all_to_all | solution.py:683
  37.1 2.1 %up.1 = f32[8,16,128]{2,1,0:T(8,128)S(1)} custom-call(f32[32,3,2,128]{3,2,1,0:T(2,128)S(1)} %all-to-all-done.1.packed, f32[5,8,128]{2,1,0:T(8,128)S(1)} %collective-permute-done.2.inner2, f32[5,8,128]{2,1,0:T(8,128)S(1)} %collective-permute-done.3.outer2, f32[36,8,128]{2,1,0:T(8,128)S(1)} %get-tuple-element.35.xn1, f32[36,8,128]{2,1,0:T(8,128)S(1)} %get-tuple-element.36.xl1, ...), custom_call_target="tpu_custom_call" | custom-call | tf_op jit(solution)/shard_map/up/pallas_call | solution.py:685
  39.2 10.9 %all_to_all.16.blocks = f32[8,16,128]{2,1,0:T(8,128)S(1)} all-to-all(f32[8,16,128]{2,1,0:T(8,128)S(1)} %up.1), channel_id=1, replica_groups=mesh['gx'=2,'gy'=4,'gz'=4] {'gx','gy'}, dimensions={0} | all-to-all | bytes 131072 | tf_op jit(solution)/shard_map/all_to_all | solution.py:698
  50.2 0.8 %finish.1 = f32[16,8,128]{2,1,0:T(8,128)} custom-call(f32[8,16,128]{2,1,0:T(8,128)S(1)} %all_to_all.16.blocks), custom_call_target="tpu_custom_call" | custom-call | tf_op jit(solution)/shard_map/finish/pallas_call | solution.py:693
Async XLA Ops:
  0.0 1.0 %copy-start = (bf16[32,16,256]{2,1,0:T(8,128)(2,1)S(1)}, bf16[32,16,256]{2,1,0:T(8,128)(2,1)}, u32[]{:S(2)}) copy-start(bf16[32,16,256]{2,1,0:T(8,128)(2,1)} %param.3) | copy-start | bytes 786436
  17.6 5.1 %collective-permute-start = (f32[30,8,128]{2,1,0:T(8,128)S(1)}, f32[30,8,128]{2,1,0:T(8,128)S(1)}, u32[]{:S(2)}, u32[]{:S(2)}) collective-permute-start(f32[30,8,128]{2,1,0:T(8,128)S(1)} %get-tuple-element.30), channel_id=1, source_target_pairs={{0,16},{20,4},{8,24},{28,12},{13,9},{5,1},{17,21},{25,29},{30,14},... | collective-permute-start | bytes 368648 | tf_op jit(solution)/shard_map/ppermute | solution.py:669
  18.2 4.4 %collective-permute-start.1 = (f32[30,8,128]{2,1,0:T(8,128)S(1)}, f32[30,8,128]{2,1,0:T(8,128)S(1)}, u32[]{:S(2)}, u32[]{:S(2)}) collective-permute-start(f32[30,8,128]{2,1,0:T(8,128)S(1)} %get-tuple-element.31), channel_id=1, source_target_pairs={{16,20},{4,8},{24,28},{12,13},{9,5},{1,17},{21,25},{29,30},{14,10}... | collective-permute-start | bytes 368648 | tf_op jit(solution)/shard_map/ppermute | solution.py:669
  24.7 12.4 %all-to-all-start.1 = ((f32[32,3,2,128]{3,2,1,0:T(2,128)}), f32[32,3,2,128]{3,2,1,0:T(2,128)S(1)}, u32[]{:S(2)}, u32[]{:S(2)}) async-start(f32[32,3,2,128]{3,2,1,0:T(2,128)} %broadcast_in_dim.3), calls=%async_computation.1 | async-start | bytes 196608 | tf_op jit(solution)/shard_map/all_to_all | solution.py:683
  29.2 3.9 %collective-permute-start.2 = (f32[5,8,128]{2,1,0:T(8,128)S(1)}, f32[5,8,128]{2,1,0:T(8,128)S(1)}, u32[]{:S(2)}, u32[]{:S(2)}) collective-permute-start(f32[5,8,128]{2,1,0:T(8,128)S(1)} %get-tuple-element.33), channel_id=1, source_target_pairs={{0,16},{20,4},{8,24},{28,12},{13,9},{5,1},{17,21},{25,29},{30,14},... | collective-permute-start | bytes 61448 | tf_op jit(solution)/shard_map/ppermute | solution.py:669
  31.0 2.0 %collective-permute-start.3 = (f32[5,8,128]{2,1,0:T(8,128)S(1)}, f32[5,8,128]{2,1,0:T(8,128)S(1)}, u32[]{:S(2)}, u32[]{:S(2)}) collective-permute-start(f32[5,8,128]{2,1,0:T(8,128)S(1)} %get-tuple-element.34), channel_id=1, source_target_pairs={{16,20},{4,8},{24,28},{12,13},{9,5},{1,17},{21,25},{29,30},{14,10}... | collective-permute-start | bytes 61448 | tf_op jit(solution)/shard_map/ppermute | solution.py:669

commit v14 on v12

--- a/solution.py
+++ b/solution.py
@@ -262,12 +262,15 @@
     loop(low, high, PIECE, body)
 
 
-def sweep(level, low, high, fields, source, target):
+def swept(level, plane, count, fields, source, shift=0):
     scaled, start, _ = fields
-
+    mid, total = level.spread(source[pl.ds(plane - 1, count + 2)], scaled, plane - shift, count)
+    return (1.0 - OMEGA) * mid + (start[pl.ds(plane - shift, count)] + total)
+
+
+def sweep(level, low, high, fields, source, target, shift=0):
     def body(plane, count):
-        mid, total = level.spread(source[pl.ds(plane - 1, count + 2)], scaled, plane, count)
-        target[pl.ds(plane, count)] = (1.0 - OMEGA) * mid + (start[pl.ds(plane, count)] + total)
+        target[pl.ds(plane, count)] = swept(level, plane, count, fields, source, shift)
 
     loop(low, high, PIECE, body)
 
@@ -377,9 +380,15 @@
             out_ref[peer, index * share : (index + 1) * share] = field[begin : begin + share]
 
 
-def spread_kernel(groups, by, gathered, own):
+def spread_kernel(groups, by, gathered, own, straight):
     for start in range(0, own.shape[0], ROWS):
-        place(gathered, start, own, start, groups, by)
+        place(gathered, start, straight, start, groups, by)
+    share = own.shape[0] // 3
+    odd = own_slab() % 2 == 1
+    for index in range(3):
+        for plane in range(share):
+            at = jnp.where(odd, share - 1 - plane, plane)
+            own[index * share + plane] = straight[index * share + at]
 
 
 def place(gathered, row, target, plane, groups, by):
@@ -396,47 +405,72 @@
             target[pl.ds(plane, ROWS), ix * groups + part, :] = total
 
 
+def near_kernel(
+    depth,
+    own, inner,
+    saved1, saved2, fluid2, pin2, fluid3, pin3,
+    fluid1, rhs1, pin1, other1, rhs2, sums,
+):
+    for index, target in enumerate((fluid1, rhs1, pin1)):
+        target[0:depth] = own[index * depth : (index + 1) * depth]
+        for plane in range(HALO):
+            target[depth + plane] = inner[(index + 1) * depth - 1 - plane]
+    fine, coarse = Level(0), Level(1)
+    down1, down2 = lanes_down(0), lanes_down(1)
+    fields1, corr1 = (saved1[0:6], saved1[6], saved1[7]), saved1[8]
+    fields2 = (saved2[0:6], saved2[6], saved2[7])
+    planes = depth + HALO
+    set_level(fine, 1, planes - 1, fluid1, pin1, rhs1, fields1)
+    sweep(fine, 2, planes - 2, fields1, fields1[1], other1)
+    sweep(fine, 3, planes - 3, fields1, other1, corr1)
+    coarse_residual(fine, 4, planes - 4, fields1, corr1, sums)
+    count2 = planes // 2
+    for source, target, share in ((fluid1, fluid2, 8.0), (pin1, pin2, 4.0)):
+        target[NEAR : NEAR + count2] = in_lanes(pair_sum(source[...]), down1) * (1.0 / share)
+    low2, high2 = NEAR + 2, NEAR + count2 - 2
+    rhs2[low2:high2] = in_lanes(sums[0 : high2 - low2], down1)
+    set_level(coarse, low2, high2, fluid2, pin2, rhs2, fields2)
+    for source, target, scale in ((fluid2, fluid3, 0.125), (pin2, pin3, 0.25)):
+        target[...] = in_lanes(pair_sum(source[NEAR : NEAR + depth // 2]), down2) * scale
+
+
 def down_kernel(
-    groups, by, depth,
-    own, outer, inner,
-    xn1, xl1, yn1, yl1, zn1, zl1, start1, diag1, corr1,
-    xn2, xl2, yn2, yl2, zn2, zl2, start2, diag2, corr2,
+    depth,
+    own, outer, near2, near_fluid2, near_pin2, fluid3, pin3,
+    saved1, saved2,
     packed,
     fluid1, rhs1, pin1, other1, fluid2, rhs2, pin2, other2, sums,
 ):
-    planes = depth + 2 * HALO
-    part = own_slab()
-    odd = part % 2 == 1
+    planes = fluid1.shape[0]
     for index, target in enumerate((fluid1, rhs1, pin1)):
-        rows = slice(index * depth, (index + 1) * depth)
-        target[0:HALO] = jnp.where(odd, inner[rows], outer[rows])
-        target[HALO : HALO + depth] = own[rows]
-        target[HALO + depth :] = jnp.where(odd, outer[rows], inner[rows])
+        for plane in range(HALO):
+            target[plane] = outer[index * depth + HALO - 1 - plane]
+        target[HALO:planes] = own[index * depth : index * depth + planes - HALO]
 
     fine, coarse = Level(0), Level(1)
     down1, down2 = lanes_down(0), lanes_down(1)
-    fields1 = ((xn1, xl1, yn1, yl1, zn1, zl1), start1, diag1)
-    fields2 = ((xn2, xl2, yn2, yl2, zn2, zl2), start2, diag2)
+    fields1, corr1 = (saved1[0:6], saved1[6], saved1[7]), saved1[8]
+    fields2, corr2 = (saved2[0:6], saved2[6], saved2[7]), saved2[8]
     set_level(fine, 1, planes - 1, fluid1, pin1, rhs1, fields1)
-    sweep(fine, 2, planes - 2, fields1, start1, other1)
+    sweep(fine, 2, planes - 2, fields1, fields1[1], other1)
     sweep(fine, 3, planes - 3, fields1, other1, corr1)
     count2 = depth // 2 + 2 * NEAR
-    begin = HALO - 2 * NEAR
-    for source, target, share in ((fluid1, fluid2, 8.0), (pin1, pin2, 4.0)):
-        whole = pair_sum(source[begin : begin + 2 * count2])
-        target[...] = in_lanes(whole, down1) * (1.0 / share)
-    low2, high2 = (begin + 4) // 2, count2 - (begin + 4) // 2
-    inner = high2 - low2
-    coarse_residual(fine, begin + 2 * low2, begin + 2 * high2, fields1, corr1, sums)
-    rhs2[low2:high2] = in_lanes(sums[0:inner], down1)
-    set_level(coarse, low2, high2, fluid2, pin2, rhs2, fields2)
-    sweep(coarse, low2 + 1, high2 - 1, fields2, start2, other2)
+    low2, done, high2 = 2, NEAR + 2, count2 - 2
+    coarse_residual(fine, 2 * low2, 2 * done, fields1, corr1, sums)
+    for source, ready, target, share in (
+        (fluid1, near_fluid2, fluid2, 8.0), (pin1, near_pin2, pin2, 4.0)
+    ):
+        target[0:NEAR] = in_lanes(pair_sum(source[0:HALO]), down1) * (1.0 / share)
+        target[NEAR : done + 1] = ready[NEAR : done + 1]
+    rhs2[low2:done] = in_lanes(sums[0 : done - low2], down1)
+    set_level(coarse, low2, done, fluid2, pin2, rhs2, fields2)
+    for source, target in zip(near2, saved2[0:8]):
+        target[done:high2] = source[done:high2]
+    sweep(coarse, low2 + 1, high2 - 1, fields2, fields2[1], other2)
     sweep(coarse, low2 + 2, high2 - 2, fields2, other2, corr2)
     coarse_residual(coarse, NEAR, NEAR + depth // 2, fields2, corr2, sums)
     count3 = depth // 4
     rhs3 = in_lanes(sums[0:count3], down2)
-    fluid3 = in_lanes(pair_sum(fluid2[NEAR : NEAR + 2 * count3]), down2) * 0.125
-    pin3 = in_lanes(pair_sum(pin2[NEAR : NEAR + 2 * count3]), down2) * 0.25
     lane = iota((count3, LANES), 1) // ROWS
     first = jnp.zeros((count3, LANES), F32)
     second = jnp.zeros((count3, LANES), F32)
@@ -517,11 +551,9 @@
 
 def up_kernel(
     groups, by, depth,
-    packed,
-    xn1, xl1, yn1, yl1, zn1, zl1, start1, diag1, corr1,
-    xn2, xl2, yn2, yl2, zn2, zl2, start2, diag2, corr2,
+    packed, near1, far1, far2,
     out_ref,
-    one1, two1, one2, two2, lifted, first, second, solved,
+    one1, two1, one2, two2, lifted, first, second, solved, final,
 ):
     count3 = depth // 4
     shares = packed.shape[0]
@@ -529,11 +561,20 @@
     devices = devices_of(shares // peers)
     for slab, index in enumerate(devices):
         row = slab * count3
-        first[row : row + 2] = packed[index, 0]
-        first[row + 2 : row + 4] = packed[index, 1]
-        both = packed[index, 2]
-        second[row : row + 2] = both
-        second[row + 2 : row + 4] = pltpu.roll(both, LANES // 2, 1)
+        low, high, both = packed[index, 0], packed[index, 1], packed[index, 2]
+        rest = pltpu.roll(both, LANES // 2, 1)
+        if slab % 2:
+            for at, (level3, pin) in enumerate(((high, rest), (low, both))):
+                begin = row + 2 * at
+                first[begin : begin + 1] = level3[1:2]
+                first[begin + 1 : begin + 2] = level3[0:1]
+                second[begin : begin + 1] = pin[1:2]
+                second[begin + 1 : begin + 2] = pin[0:1]
+        else:
+            first[row : row + 2] = low
+            first[row + 2 : row + 4] = high
+            second[row : row + 2] = both
+            second[row + 2 : row + 4] = rest
     half = iota((shares * count3, LANES), 1) < LANES // 2
 
     def low_half(field):
@@ -562,11 +603,16 @@
     for row in range(ROWS):
         lifted[0:rows, row, :] = wide[row * rows : (row + 1) * rows]
 
-    fields1 = ((xn1, xl1, yn1, yl1, zn1, zl1), start1, diag1)
-    fields2 = ((xn2, xl2, yn2, yl2, zn2, zl2), start2, diag2)
+    odd = part % 2 == 1
+
+    def lifted_to(plane):
+        parent = plane // 2 + NEAR // 2
+        return lifted[jnp.where(odd, count - 1 - parent, parent)]
+
+    near_fields, near_corr1 = (near1[0:6], near1[6], near1[7]), near1[8]
+    far_fields, far_corr1 = (far1[0:6], far1[6], far1[7]), far1[8]
+    fields2, corr2 = (far2[0:6], far2[6], far2[7]), far2[8]
     low, high = NEAR - 4, NEAR + depth // 2 + 4
-    parents = lifted[low // 2 + NEAR // 2 : high // 2 + NEAR // 2]
-    twice = jnp.broadcast_to(parents[:, None], (parents.shape[0], 2, ROWS, LANES))
     reach = depth // 2 + NEAR
     quarter = iota((ROWS, LANES), 1) // (LANES // 4)
     row = iota((ROWS, LANES), 0)
@@ -581,10 +627,10 @@
             total = kept if total is None else total + kept
         return total
 
-    before, after = unpacked(part - 1, 3), unpacked(part + 1, 4)
-    one2[low - 1] = before + lifted[(low - 1) // 2 + NEAR // 2]
-    one2[low:high] = corr2[low:high] + twice.reshape(high - low, ROWS, LANES)
-    one2[high] = after + lifted[high // 2 + NEAR // 2]
+    one2[low - 1] = unpacked(jnp.where(odd, part + 1, part - 1), 4) + lifted_to(low - 1)
+    for plane in range(low, high):
+        one2[plane] = corr2[plane] + lifted_to(plane)
+    one2[high] = unpacked(jnp.where(odd, part - 1, part + 1), 3) + lifted_to(high)
     sweep(coarse, NEAR - 4, reach + 4, fields2, one2, two2)
     sweep(coarse, NEAR - 3, reach + 3, fields2, two2, one2)
     sweep(coarse, NEAR - 2, reach + 2, fields2, one2, two2)
@@ -597,18 +643,31 @@
     parents = lifted[0 : depth // 2 + 4]
     twice = jnp.broadcast_to(parents[:, None], (parents.shape[0], 2, ROWS, LANES))
     low, high = HALO - 4, HALO + depth + 4
-    one1[low:high] = corr1[low:high] + twice.reshape(high - low, ROWS, LANES)
+    turn = HALO + 3
+    for plane in range(low, high):
+        corr = far_corr1[plane] if plane < turn else near_corr1[plane - HALO]
+        one1[plane] = corr + lifted[(plane - low) // 2]
     reach = depth + HALO
-    sweep(fine, HALO - 2, reach + 2, fields1, one1, two1)
-    sweep(fine, HALO - 1, reach + 1, fields1, two1, one1)
-    sweep(fine, HALO, reach, fields1, one1, two1)
+    for more, source, target in ((2, one1, two1), (1, two1, one1)):
+        sweep(fine, HALO - more, turn, far_fields, source, target)
+        sweep(fine, turn, reach + more, near_fields, source, target, HALO)
+
+    def last(fields, shift):
+        def body(plane, count):
+            value = swept(fine, plane, count, fields, one1, shift)
+            value = value * fields[2][pl.ds(plane - shift, count)]
+            for index in range(count):
+                at = plane - HALO + index
+                final[jnp.where(odd, depth - 1 - at, at)] = value[index]
+
+        return body
+
+    loop(HALO, turn, PIECE, last(far_fields, 0))
+    loop(turn, reach, PIECE, last(near_fields, HALO))
 
     group = (iota((depth, LANES), 1) // by) % groups
     for ix in range(nx):
-        scaled = [
-            two1[HALO:reach, ix * groups + part, :] * diag1[HALO:reach, ix * groups + part, :]
-            for part in range(groups)
-        ]
+        scaled = [final[:, ix * groups + part, :] for part in range(groups)]
         for iy in range(ny):
             total = scaled[iy]
             for part in range(groups):
@@ -659,6 +718,7 @@
     own = pl.pallas_call(
         functools.partial(spread_kernel, groups, by),
         out_shape=blocks(3 * share, ROWS),
+        scratch_shapes=[room(3 * share)],
         compiler_params=limit,
         name="spread",
     )(lax.all_to_all(parcels, ("gx", "gy"), 0, 0, tiled=True))
@@ -672,25 +732,37 @@
         return lax.ppermute(field, ("gx", "gy", "gz"), pairs + [pair[::-1] for pair in pairs])
 
     outer, inner = swap(own, 1), swap(own, 0)
-    saved = (blocks(planes, ROWS),) * 9 + (blocks(count2, ROWS),) * 9
-    results = pl.pallas_call(
-        functools.partial(down_kernel, groups, by, share),
-        out_shape=saved + (blocks(5, 2),),
-        scratch_shapes=[room(planes)] * 4 + [room(count2)] * 5,
+    count3 = share // 4
+    near1, near2, far1, far2 = (
+        (blocks(count, ROWS),) * fields
+        for count, fields in ((share + HALO, 9), (count2, 8), (HALO + 8, 9), (count2, 9))
+    )
+    near1, near2, fluid2, pin2, fluid3, pin3 = pl.pallas_call(
+        functools.partial(near_kernel, share),
+        out_shape=(near1, near2) + (blocks(count2, ROWS),) * 2 + (blocks(count3, ROWS),) * 2,
+        scratch_shapes=[room(share + HALO)] * 4 + [room(count2)] * 2,
+        compiler_params=limit,
+        name="near",
+    )(own, inner)
+    far1, far2, parcel = pl.pallas_call(
+        functools.partial(down_kernel, share),
+        out_shape=(far1, far2, blocks(5, 2)),
+        scratch_shapes=[room(HALO + 8)] * 4 + [room(count2)] * 5,
         compiler_params=limit,
         name="down",
-    )(own, outer, inner)
-    copies = jnp.broadcast_to(results[-1], (parts,) + results[-1].shape)
+    )(own, outer, near2, fluid2, pin2, fluid3, pin3)
+    copies = jnp.broadcast_to(parcel, (parts,) + parcel.shape)
     packed = lax.all_to_all(copies, ("gx", "gy", "gz"), 0, 0, tiled=True)
-    depth3 = parts * share // 4
+    depth3 = parts * count3
     mine = pl.pallas_call(
         functools.partial(up_kernel, groups, by, share),
         out_shape=blocks(peers, share),
         scratch_shapes=[room(planes), room(planes), room(count2), room(count2), room(count2)]
-        + [pltpu.VMEM((rows, LANES), F32) for rows in (depth3, depth3, depth3 + 3 * NEAR)],
+        + [pltpu.VMEM((rows, LANES), F32) for rows in (depth3, depth3, depth3 + 3 * NEAR)]
+        + [room(share)],
         compiler_params=limit,
         name="up",
-    )(packed, *results[:-1])
+    )(packed, near1, far1, far2)
     return pl.pallas_call(
         finish_kernel,
         out_shape=jax.ShapeDtypeStruct((bx, by, depth), F32),

time: 51.1 us -> 50.4 us (0.986)
  blocking collectives: 37.6 us -> 36.6 us
    all_to_all x1, blocking collectives: 12.1 us -> 11.1 us  [whole_planes(): packed = lax.all_to_all(copies, ('gx', 'gy', 'gz'), 0, 0, tiled=True)]
    pallas_call x1 -> x2, Pallas kernels: 1.91 us -> 2.12 us  [the longest x1 1.19 us: whole_planes(): pl.pallas_call(functools.partial(down_kernel, share), out_shape=(far1, fa...]
  transfers between devices with their start and end apart: 2 -> 2, of which waited for: 1 -> 1; matrix products, arithmetic and copies ran while one was open for 0% -> 0% of each run, Pallas kernels for 0% -> 2%
where the time goes in v14:
time: 50.4 us; the launch traced here: 50.2 us
  blocking collectives  36.6 us (73%)
  Pallas kernels  5.85 us (12%)
  waiting for transfers between devices  5.34 us (11%)
  starting transfers between devices  1.29 us (3%)
  other arithmetic  0.93 us (2%)
    all_to_all x1, blocking collectives, whole_planes(): lax.all_to_all(parcels, ('gx', 'gy'), 0, 0, tiled=True)  15.8 us
    all_to_all x1, blocking collectives, whole_planes(): packed = lax.all_to_all(copies, ('gx', 'gy', 'gz'), 0, 0, tiled=True)  11.1 us
    all_to_all x1, blocking collectives, whole_planes(): lax.all_to_all(mine, ('gx', 'gy'), 0, 0, tiled=True)  9.7 us
    ppermute x2, waiting for transfers between devices, swap(): lax.ppermute(field, ('gx', 'gy', 'gz'), pairs + [pair[::-1] for pair in p...  5.34 us
    pallas_call x1, Pallas kernels, whole_planes(): pl.pallas_call(functools.partial(up_kernel, groups, by, share), out_shape...  2.14 us
    ppermute x2, starting transfers between devices, swap(): lax.ppermute(field, ('gx', 'gy', 'gz'), pairs + [pair[::-1] for pair in p...  1.29 us
    pallas_call x1, Pallas kernels, whole_planes(): pl.pallas_call(functools.partial(down_kernel, share), out_shape=(far1, fa...  1.19 us
  transfers between devices with their start and end apart: 2, of which 1 were waited for; matrix products, arithmetic and copies ran while one was open for 0% of the time, Pallas kernels for 2%

profile of v14, /device:TPU:0, one launch (start us, length us, event | category | flops | bytes accessed | tf_op | source)
XLA Modules:
  0.0 50.2 jit_solution(10623087813749573160)
XLA Ops:
  0.0 0.0 copy-start
  0.0 0.9 %multiply_multiply_fusion = (f32[16,8,128]{2,1,0:T(8,128)S(1)}, f32[16,8,128]{2,1,0:T(8,128)S(1)}) fusion(s32[16,8,128]{2,1,0:T(8,128)} %param.5, f32[16,8,128]{2,1,0:T(8,128)} %param.4), kind=kLoop, calls=%fused_computation | loop fusion | flops 65536 | bytes 262144 | tf_op jit(solution)/shard_map/mul | solution.py:711
  0.9 0.1 copy-done
  1.0 0.5 prepare.1
  1.5 15.8 %all_to_all.15.gathered = f32[8,48,128]{2,1,0:T(8,128)S(1)} all-to-all(f32[8,48,128]{2,1,0:T(8,128)S(1)} %prepare.1), channel_id=1, replica_groups=mesh['gx'=2,'gy'=4,'gz'=4] {'gx','gy'}, dimensions={0} | all-to-all | bytes 393216 | tf_op jit(solution)/shard_map/all_to_all | solution.py:724
  17.3 0.3 spread.1.own
  17.6 0.6 %collective-permute-start.1 = (f32[48,8,128]{2,1,0:T(8,128)S(1)}, f32[48,8,128]{2,1,0:T(8,128)S(1)}, u32[]{:S(2)}, u32[]{:S(2)}) collective-permute-start(f32[48,8,128]{2,1,0:T(8,128)S(1)} %spread.1.own), channel_id=1, source_target_pairs={{0,16},{20,4},{8,24},{28,12},{13,9},{5,1},{17,21},{25,29},{30,14},... | collective-permute-start | bytes 589832 | tf_op jit(solution)/shard_map/ppermute | solution.py:732
  18.2 0.7 %collective-permute-start = (f32[48,8,128]{2,1,0:T(8,128)S(1)}, f32[48,8,128]{2,1,0:T(8,128)S(1)}, u32[]{:S(2)}, u32[]{:S(2)}) collective-permute-start(f32[48,8,128]{2,1,0:T(8,128)S(1)} %spread.1.own), channel_id=1, source_target_pairs={{16,20},{4,8},{24,28},{12,13},{9,5},{1,17},{21,25},{29,30},{14,10}... | collective-permute-start | bytes 589832 | tf_op jit(solution)/shard_map/ppermute | solution.py:732
  18.9 5.3 %collective-permute-done.1.inner = f32[48,8,128]{2,1,0:T(8,128)S(1)} collective-permute-done((f32[48,8,128]{2,1,0:T(8,128)S(1)}, f32[48,8,128]{2,1,0:T(8,128)S(1)}, u32[]{:S(2)}, u32[]{:S(2)}) %collective-permute-start.1) | collective-permute-done | bytes 196640 | tf_op jit(solution)/shard_map/ppermute | solution.py:732
  24.2 0.9 %near.1 = (f32[32,8,128]{2,1,0:T(8,128)S(1)}, f32[32,8,128]{2,1,0:T(8,128)S(1)}, f32[32,8,128]{2,1,0:T(8,128)S(1)}, f32[32,8,128]{2,1,0:T(8,128)S(1)}, f32[32,8,...) custom-call(f32[48,8,128]{2,1,0:T(8,128)S(1)} %spread.1.own, ...), custom_call_target="tpu_custom_call" | custom-call | tf_op jit(solution)/shard_map/near/pallas_call | solution.py:740
  25.2 0.0 collective-permute-done.outer
  25.2 1.2 %down.1 = (f32[24,8,128]{2,1,0:T(8,128)S(1)}, f32[24,8,128]{2,1,0:T(8,128)S(1)}, f32[24,8,128]{2,1,0:T(8,128)S(1)}, f32[24,8,128]{2,1,0:T(8,128)S(1)}, f32[24,8,...) custom-call(f32[48,8,128]{2,1,0:T(8,128)S(1)} %spread.1.own, ...), custom_call_target="tpu_custom_call" | custom-call | tf_op jit(solution)/shard_map/down/pallas_call | solution.py:747
  26.4 11.1 %all_to_all.16.packed = f32[32,5,2,128]{3,2,1,0:T(2,128)S(1)} all-to-all(f32[32,5,2,128]{3,2,1,0:T(2,128)S(1)} %broadcast_in_dim.3), channel_id=1, replica_groups=mesh['gx'=2,'gy'=4,'gz'=4] {'gx','gy','gz'}, dimensions={0} | all-to-all | bytes 327680 | tf_op jit(solution)/shard_map/all_to_all | solution.py:755
  37.5 2.1 %up.1 = f32[8,16,128]{2,1,0:T(8,128)S(1)} custom-call(f32[32,5,2,128]{3,2,1,0:T(2,128)S(1)} %all_to_all.16.packed, f32[32,8,128]{2,1,0:T(8,128)S(1)} %get-tuple-element.58.near1_0_, f32[32,8,128]{2,1,0:T(8,128)S(1)} %get-tuple-element.59.near1_1_, f32[32,8,128]{2,1,0:T(8,128)S(1)} %get-tuple-element.60.near1_2_, ...), custom_call_target="tpu_custom_call" | custom-call | tf_op jit(solution)/shard_map/up/pallas_call | solution.py:757
  39.6 9.7 %all_to_all.17.blocks = f32[8,16,128]{2,1,0:T(8,128)S(1)} all-to-all(f32[8,16,128]{2,1,0:T(8,128)S(1)} %up.1), channel_id=1, replica_groups=mesh['gx'=2,'gy'=4,'gz'=4] {'gx','gy'}, dimensions={0} | all-to-all | bytes 131072 | tf_op jit(solution)/shard_map/all_to_all | solution.py:771
  49.4 0.8 %finish.1 = f32[16,8,128]{2,1,0:T(8,128)} custom-call(f32[8,16,128]{2,1,0:T(8,128)S(1)} %all_to_all.17.blocks), custom_call_target="tpu_custom_call" | custom-call | tf_op jit(solution)/shard_map/finish/pallas_call | solution.py:766
  (1 shorter events, 0.0 us)
Async XLA Ops:
  0.0 1.0 %copy-start = (bf16[32,16,256]{2,1,0:T(8,128)(2,1)S(1)}, bf16[32,16,256]{2,1,0:T(8,128)(2,1)}, u32[]{:S(2)}) copy-start(bf16[32,16,256]{2,1,0:T(8,128)(2,1)} %param.3) | copy-start | bytes 786436
  17.6 6.6 %collective-permute-start.1 = (f32[48,8,128]{2,1,0:T(8,128)S(1)}, f32[48,8,128]{2,1,0:T(8,128)S(1)}, u32[]{:S(2)}, u32[]{:S(2)}) collective-permute-start(f32[48,8,128]{2,1,0:T(8,128)S(1)} %spread.1.own), channel_id=1, source_target_pairs={{0,16},{20,4},{8,24},{28,12},{13,9},{5,1},{17,21},{25,29},{30,14},... | collective-permute-start | bytes 589832 | tf_op jit(solution)/shard_map/ppermute | solution.py:732
  18.2 6.9 %collective-permute-start = (f32[48,8,128]{2,1,0:T(8,128)S(1)}, f32[48,8,128]{2,1,0:T(8,128)S(1)}, u32[]{:S(2)}, u32[]{:S(2)}) collective-permute-start(f32[48,8,128]{2,1,0:T(8,128)S(1)} %spread.1.own), channel_id=1, source_target_pairs={{16,20},{4,8},{24,28},{12,13},{9,5},{1,17},{21,25},{29,30},{14,10}... | collective-permute-start | bytes 589832 | tf_op jit(solution)/shard_map/ppermute | solution.py:732

commit v15 on v14

--- a/solution.py
+++ b/solution.py
@@ -152,14 +152,14 @@
     return lax.broadcasted_iota(jnp.int32, shape, dim)
 
 
-def dot01(field, chosen, dims=(((1,), (0,)), ((), ()))):
+def dot01(field, chosen, parts=3):
     total = None
     rest = field
-    for part in range(3):
+    for part in range(parts):
         piece = rest.astype(jnp.bfloat16)
-        term = lax.dot_general(piece, chosen, dims, preferred_element_type=F32)
+        term = jnp.dot(piece, chosen, preferred_element_type=F32)
         total = term if total is None else total + term
-        if part < 2:
+        if part < parts - 1:
             rest = rest - piece.astype(F32)
     return total
 
@@ -302,9 +302,9 @@
     return where01((fine < ny * xs) & same_x & same_y)
 
 
-def in_lanes(field, chosen):
+def in_lanes(field, chosen, parts=3):
     flat = field.reshape(field.shape[0] * ROWS, LANES)
-    return dot01(flat, chosen).reshape(field.shape)
+    return dot01(flat, chosen, parts).reshape(field.shape)
 
 
 def path_of(group):
@@ -357,23 +357,20 @@
     bx, by, depth = fluid_ref.shape
     cells = bx * by
     groups = bx // 4
-    pick = where01(iota((depth, 2 * depth), 1) // 2 == iota((depth, 2 * depth), 0))
-    deep = lax.dot_general(
-        pick, res_ref[...], (((1,), (1,)), ((), ())), preferred_element_type=F32
+    order = [x for low in range(4) for x in range(low, bx, 4)]
+    fine = iota((cells, 4 * cells), 1)
+    x, y = fine // (4 * by), (fine % (2 * by)) // 2
+    chosen = where01((x % 4) * (groups * by) + (x // 4) * by + y == iota((cells, 4 * cells), 0))
+    wide = lax.dot_general(
+        chosen, res_ref[...], (((1,), (0,)), ((), ())), preferred_element_type=F32
     )
-
-    def lane_of(x, y):
-        return (x % 4) * (groups * by) + (x // 4) * by + y
-
-    fine = iota((4 * cells, cells), 0)
-    lane = iota((4 * cells, cells), 1)
-    chosen = where01(lane_of(fine // (4 * by), (fine % (2 * by)) // 2) == lane)
-    rhs = dot01(deep, chosen)
-    cell = iota((cells, cells), 0)
-    lane = iota((cells, cells), 1)
-    chosen = where01(lane_of(cell // by, cell % by) == lane)
-    fluid = dot01(fluid_ref[...].reshape(cells, depth).T, chosen)
-    pin = dot01(pin_ref[...].reshape(cells, depth).T, chosen)
+    rhs = dot10(where01(iota((depth, 2 * depth), 1) // 2 == iota((depth, 2 * depth), 0)), wide)
+
+    def turned(field_ref):
+        field = jnp.concatenate([field_ref[x : x + 1] for x in order], axis=0)
+        return field.reshape(cells, depth).T
+
+    fluid, pin = turned(fluid_ref), turned(pin_ref)
     for rank in range(depth // share):
         peer, begin = own_peer_of(rank), rank * share
         for index, field in enumerate((fluid, rhs, pin)):
@@ -491,18 +488,30 @@
             packed[3 + index, half : half + 1, :] = row
 
 
+def swapped(field):
+    return pltpu.roll(field, LANES // 2, 1)
+
+
 def rolled(field, shift):
     count = field.shape[0]
-    shift %= count
+    if abs(shift) == count:
+        return swapped(field)
     if shift % ROWS:
-        return pltpu.roll(field, shift, 0)
-    return jnp.concatenate([field[count - shift :], field[: count - shift]], axis=0)
+        moved = pltpu.roll(field, shift % count, 0)
+        row = iota(field.shape, 0)
+        crossed = row < shift if shift > 0 else row >= count + shift
+        return jnp.where(crossed, swapped(moved), moved)
+    cut = count - shift if shift > 0 else -shift
+    low, high = field[:cut], field[cut:]
+    return jnp.concatenate([swapped(high), low] if shift > 0 else [high, swapped(low)], axis=0)
 
 
 def columns(rhs, fluid, pin):
-    depth = fluid.shape[0]
-    z, lane = iota(fluid.shape, 0), iota(fluid.shape, 1)
+    count = fluid.shape[0]
+    depth = 2 * count
+    row, lane = iota(fluid.shape, 0), iota(fluid.shape, 1)
     y, x = lane % ROWS, (lane // ROWS) % ROWS
+    last = (row == count - 1) & (lane >= LANES // 2)
 
     def next_x(field):
         return pltpu.roll(field, LANES - ROWS, 1)
@@ -510,11 +519,15 @@
     def next_y(field):
         return pltpu.roll(field, LANES - 1, 1)
 
-    wz = jnp.where(z == depth - 1, 0.0, mean_of(fluid, rolled(fluid, -1), 4.0))
+    def total(field):
+        part = jnp.sum(field, axis=0, keepdims=True)
+        return part + swapped(part)
+
+    wz = jnp.where(last, 0.0, mean_of(fluid, rolled(fluid, -1), 4.0))
     wy = jnp.where(y == ROWS - 1, 0.0, mean_of(fluid, next_y(fluid), 4.0))
     wx = jnp.where(x == ROWS - 1, 0.0, mean_of(fluid, next_x(fluid), 4.0))
     across = (wx + pltpu.roll(wx, ROWS, 1)) + (wy + pltpu.roll(wy, 1, 1)) + pin
-    share = 1.0 / jnp.sum(across, axis=0, keepdims=True)
+    share = 1.0 / total(across)
 
     above, below, own = rolled(wz, 1), wz, across
     steps = []
@@ -531,7 +544,7 @@
     inverse = inverse_of(above + below + own)
 
     def solve(right):
-        mean = jnp.sum(right, axis=0, keepdims=True) * share
+        mean = total(right) * share
         for stride, up, down in steps:
             right = right + up * rolled(right, stride) + down * rolled(right, -stride)
         return right * inverse + mean
@@ -575,19 +588,18 @@
             first[row + 2 : row + 4] = high
             second[row : row + 2] = both
             second[row + 2 : row + 4] = rest
-    half = iota((shares * count3, LANES), 1) < LANES // 2
-
-    def low_half(field):
-        return jnp.where(half, field, pltpu.roll(field, LANES // 2, 1))
-
-    def high_half(field):
-        return jnp.where(half, pltpu.roll(field, LANES // 2, 1), field)
-
-    solved[NEAR : NEAR + shares * count3] = columns(
-        low_half(first[...]), high_half(first[...]), low_half(second[...])
+    count = shares * count3 // 2
+    low, high = first[:count], first[count:]
+    half = iota((count, LANES), 1) < LANES // 2
+    corr3 = columns(
+        jnp.where(half, low, swapped(high)),
+        jnp.where(half, swapped(low), high),
+        jnp.where(half, second[:count], swapped(second[count:])),
     )
     solved[0:NEAR] = jnp.zeros((NEAR, LANES), F32)
-    solved[NEAR + shares * count3 :] = jnp.zeros((2 * NEAR, LANES), F32)
+    solved[NEAR : NEAR + count] = corr3
+    solved[NEAR + count : NEAR + 2 * count] = swapped(corr3)
+    solved[NEAR + 2 * count :] = jnp.zeros((2 * NEAR, LANES), F32)
 
     nx, ny = SPLIT
     part = own_slab()
@@ -599,7 +611,7 @@
     spread = where01((cell < ROWS) & (cell == (lane % coarse.ny) // 2))
     rows = tall.shape[0]
     turned = [tall] + [pltpu.roll(tall, LANES - ROWS * row, 1) for row in range(1, ROWS)]
-    wide = dot01(jnp.concatenate(turned, axis=0), spread)
+    wide = dot01(jnp.concatenate(turned, axis=0), spread, 2)
     for row in range(ROWS):
         lifted[0:rows, row, :] = wide[row * rows : (row + 1) * rows]
 
@@ -639,7 +651,7 @@
     x_of = (fine_lane // fine.ny) // 2
     y_of = (fine_lane % fine.ny) // 2
     up = where01(coarse_lane == x_of * coarse.ny + y_of)
-    lifted[0 : depth // 2 + 4] = in_lanes(two2[NEAR - 2 : reach + 2], up)
+    lifted[0 : depth // 2 + 4] = in_lanes(two2[NEAR - 2 : reach + 2], up, 2)
     parents = lifted[0 : depth // 2 + 4]
     twice = jnp.broadcast_to(parents[:, None], (parents.shape[0], 2, ROWS, LANES))
     low, high = HALO - 4, HALO + depth + 4
@@ -679,14 +691,12 @@
 
 def finish_kernel(blocks, out_ref):
     bx, by, depth = out_ref.shape
-    cells = bx * by
-    cell = iota((cells, cells), 0)
-    lane = iota((cells, cells), 1)
-    x, y = cell // by, cell % by
-    chosen = where01((x % 4) * (bx // 4 * by) + (x // 4) * by + y == lane)
     peers = blocks.shape[0]
     ordered = jnp.concatenate([blocks[own_peer_of(rank)] for rank in range(peers)], axis=0)
-    out_ref[...] = dot10(chosen, ordered).reshape(out_ref.shape)
+    turned = ordered.T
+    for x in range(bx):
+        row = ((x % 4) * (bx // 4) + x // 4) * by
+        out_ref[x] = turned[row : row + by]
 
 
 def whole_planes(residual_q2, viscosity, pinned):

time: 50.4 us -> 50.7 us (level)
  no operation moved by 1% of the time
where the time goes in v15:
time: 50.7 us; the launch traced here: 50.5 us
  blocking collectives  36.6 us (72%)
  Pallas kernels  6.15 us (12%)
  waiting for transfers between devices  5.34 us (11%)
  starting transfers between devices  1.29 us (3%)
  other arithmetic  0.93 us (2%)
    all_to_all x1, blocking collectives, whole_planes(): lax.all_to_all(parcels, ('gx', 'gy'), 0, 0, tiled=True)  15.8 us
    all_to_all x1, blocking collectives, whole_planes(): packed = lax.all_to_all(copies, ('gx', 'gy', 'gz'), 0, 0, tiled=True)  11.1 us
    all_to_all x1, blocking collectives, whole_planes(): lax.all_to_all(mine, ('gx', 'gy'), 0, 0, tiled=True)  9.7 us
    ppermute x2, waiting for transfers between devices, swap(): lax.ppermute(field, ('gx', 'gy', 'gz'), pairs + [pair[::-1] for pair in p...  5.34 us
    pallas_call x1, Pallas kernels, whole_planes(): pl.pallas_call(functools.partial(up_kernel, groups, by, share), out_shape...  2.61 us
    ppermute x2, starting transfers between devices, swap(): lax.ppermute(field, ('gx', 'gy', 'gz'), pairs + [pair[::-1] for pair in p...  1.29 us
    pallas_call x1, Pallas kernels, whole_planes(): pl.pallas_call(functools.partial(down_kernel, share), out_shape=(far1, fa...  1.19 us
  transfers between devices with their start and end apart: 2, of which 1 were waited for; matrix products, arithmetic and copies ran while one was open for 0% of the time, Pallas kernels for 2%

profile of v15, /device:TPU:0, one launch (start us, length us, event | category | flops | bytes accessed | tf_op | source)
XLA Modules:
  0.0 50.5 jit_solution(14962548018020964746)
XLA Ops:
  0.0 0.0 copy-start
  0.0 0.9 %multiply_multiply_fusion = (f32[16,8,128]{2,1,0:T(8,128)S(1)}, f32[16,8,128]{2,1,0:T(8,128)S(1)}) fusion(s32[16,8,128]{2,1,0:T(8,128)} %param.5, f32[16,8,128]{2,1,0:T(8,128)} %param.4), kind=kLoop, calls=%fused_computation | loop fusion | flops 65536 | bytes 262144 | tf_op jit(solution)/shard_map/mul | solution.py:721
  0.9 0.1 copy-done
  1.0 0.4 prepare.1
  1.4 15.8 %all_to_all.15.gathered = f32[8,48,128]{2,1,0:T(8,128)S(1)} all-to-all(f32[8,48,128]{2,1,0:T(8,128)S(1)} %prepare.1), channel_id=1, replica_groups=mesh['gx'=2,'gy'=4,'gz'=4] {'gx','gy'}, dimensions={0} | all-to-all | bytes 393216 | tf_op jit(solution)/shard_map/all_to_all | solution.py:734
  17.2 0.3 spread.1.own
  17.5 0.6 %collective-permute-start.1 = (f32[48,8,128]{2,1,0:T(8,128)S(1)}, f32[48,8,128]{2,1,0:T(8,128)S(1)}, u32[]{:S(2)}, u32[]{:S(2)}) collective-permute-start(f32[48,8,128]{2,1,0:T(8,128)S(1)} %spread.1.own), channel_id=1, source_target_pairs={{0,16},{20,4},{8,24},{28,12},{13,9},{5,1},{17,21},{25,29},{30,14},... | collective-permute-start | bytes 589832 | tf_op jit(solution)/shard_map/ppermute | solution.py:742
  18.1 0.7 %collective-permute-start = (f32[48,8,128]{2,1,0:T(8,128)S(1)}, f32[48,8,128]{2,1,0:T(8,128)S(1)}, u32[]{:S(2)}, u32[]{:S(2)}) collective-permute-start(f32[48,8,128]{2,1,0:T(8,128)S(1)} %spread.1.own), channel_id=1, source_target_pairs={{16,20},{4,8},{24,28},{12,13},{9,5},{1,17},{21,25},{29,30},{14,10}... | collective-permute-start | bytes 589832 | tf_op jit(solution)/shard_map/ppermute | solution.py:742
  18.8 5.3 %collective-permute-done.1.inner = f32[48,8,128]{2,1,0:T(8,128)S(1)} collective-permute-done((f32[48,8,128]{2,1,0:T(8,128)S(1)}, f32[48,8,128]{2,1,0:T(8,128)S(1)}, u32[]{:S(2)}, u32[]{:S(2)}) %collective-permute-start.1) | collective-permute-done | bytes 196640 | tf_op jit(solution)/shard_map/ppermute | solution.py:742
  24.1 0.9 %near.1 = (f32[32,8,128]{2,1,0:T(8,128)S(1)}, f32[32,8,128]{2,1,0:T(8,128)S(1)}, f32[32,8,128]{2,1,0:T(8,128)S(1)}, f32[32,8,128]{2,1,0:T(8,128)S(1)}, f32[32,8,...) custom-call(f32[48,8,128]{2,1,0:T(8,128)S(1)} %spread.1.own, ...), custom_call_target="tpu_custom_call" | custom-call | tf_op jit(solution)/shard_map/near/pallas_call | solution.py:750
  25.1 0.0 collective-permute-done.outer
  25.1 1.2 %down.1 = (f32[24,8,128]{2,1,0:T(8,128)S(1)}, f32[24,8,128]{2,1,0:T(8,128)S(1)}, f32[24,8,128]{2,1,0:T(8,128)S(1)}, f32[24,8,128]{2,1,0:T(8,128)S(1)}, f32[24,8,...) custom-call(f32[48,8,128]{2,1,0:T(8,128)S(1)} %spread.1.own, ...), custom_call_target="tpu_custom_call" | custom-call | tf_op jit(solution)/shard_map/down/pallas_call | solution.py:757
  26.3 11.1 %all_to_all.16.packed = f32[32,5,2,128]{3,2,1,0:T(2,128)S(1)} all-to-all(f32[32,5,2,128]{3,2,1,0:T(2,128)S(1)} %broadcast_in_dim.3), channel_id=1, replica_groups=mesh['gx'=2,'gy'=4,'gz'=4] {'gx','gy','gz'}, dimensions={0} | all-to-all | bytes 327680 | tf_op jit(solution)/shard_map/all_to_all | solution.py:765
  37.4 2.6 %up.1 = f32[8,16,128]{2,1,0:T(8,128)S(1)} custom-call(f32[32,5,2,128]{3,2,1,0:T(2,128)S(1)} %all_to_all.16.packed, f32[32,8,128]{2,1,0:T(8,128)S(1)} %get-tuple-element.58.near1_0_, f32[32,8,128]{2,1,0:T(8,128)S(1)} %get-tuple-element.59.near1_1_, f32[32,8,128]{2,1,0:T(8,128)S(1)} %get-tuple-element.60.near1_2_, ...), custom_call_target="tpu_custom_call" | custom-call | tf_op jit(solution)/shard_map/up/pallas_call | solution.py:767
  40.1 9.7 %all_to_all.17.blocks = f32[8,16,128]{2,1,0:T(8,128)S(1)} all-to-all(f32[8,16,128]{2,1,0:T(8,128)S(1)} %up.1), channel_id=1, replica_groups=mesh['gx'=2,'gy'=4,'gz'=4] {'gx','gy'}, dimensions={0} | all-to-all | bytes 131072 | tf_op jit(solution)/shard_map/all_to_all | solution.py:781
  49.8 0.7 %finish.1 = f32[16,8,128]{2,1,0:T(8,128)} custom-call(f32[8,16,128]{2,1,0:T(8,128)S(1)} %all_to_all.17.blocks), custom_call_target="tpu_custom_call" | custom-call | tf_op jit(solution)/shard_map/finish/pallas_call | solution.py:776
  (1 shorter events, 0.0 us)
Async XLA Ops:
  0.0 1.0 %copy-start = (bf16[32,16,256]{2,1,0:T(8,128)(2,1)S(1)}, bf16[32,16,256]{2,1,0:T(8,128)(2,1)}, u32[]{:S(2)}) copy-start(bf16[32,16,256]{2,1,0:T(8,128)(2,1)} %param.3) | copy-start | bytes 786436
  17.5 6.6 %collective-permute-start.1 = (f32[48,8,128]{2,1,0:T(8,128)S(1)}, f32[48,8,128]{2,1,0:T(8,128)S(1)}, u32[]{:S(2)}, u32[]{:S(2)}) collective-permute-start(f32[48,8,128]{2,1,0:T(8,128)S(1)} %spread.1.own), channel_id=1, source_target_pairs={{0,16},{20,4},{8,24},{28,12},{13,9},{5,1},{17,21},{25,29},{30,14},... | collective-permute-start | bytes 589832 | tf_op jit(solution)/shard_map/ppermute | solution.py:742
  18.1 6.9 %collective-permute-start = (f32[48,8,128]{2,1,0:T(8,128)S(1)}, f32[48,8,128]{2,1,0:T(8,128)S(1)}, u32[]{:S(2)}, u32[]{:S(2)}) collective-permute-start(f32[48,8,128]{2,1,0:T(8,128)S(1)} %spread.1.own), channel_id=1, source_target_pairs={{16,20},{4,8},{24,28},{12,13},{9,5},{1,17},{21,25},{29,30},{14,10}... | collective-permute-start | bytes 589832 | tf_op jit(solution)/shard_map/ppermute | solution.py:742

commit v16 on v15

--- a/solution.py
+++ b/solution.py
@@ -488,30 +488,18 @@
             packed[3 + index, half : half + 1, :] = row
 
 
-def swapped(field):
-    return pltpu.roll(field, LANES // 2, 1)
-
-
 def rolled(field, shift):
     count = field.shape[0]
-    if abs(shift) == count:
-        return swapped(field)
+    shift %= count
     if shift % ROWS:
-        moved = pltpu.roll(field, shift % count, 0)
-        row = iota(field.shape, 0)
-        crossed = row < shift if shift > 0 else row >= count + shift
-        return jnp.where(crossed, swapped(moved), moved)
-    cut = count - shift if shift > 0 else -shift
-    low, high = field[:cut], field[cut:]
-    return jnp.concatenate([swapped(high), low] if shift > 0 else [high, swapped(low)], axis=0)
+        return pltpu.roll(field, shift, 0)
+    return jnp.concatenate([field[count - shift :], field[: count - shift]], axis=0)
 
 
 def columns(rhs, fluid, pin):
-    count = fluid.shape[0]
-    depth = 2 * count
-    row, lane = iota(fluid.shape, 0), iota(fluid.shape, 1)
+    depth = fluid.shape[0]
+    z, lane = iota(fluid.shape, 0), iota(fluid.shape, 1)
     y, x = lane % ROWS, (lane // ROWS) % ROWS
-    last = (row == count - 1) & (lane >= LANES // 2)
 
     def next_x(field):
         return pltpu.roll(field, LANES - ROWS, 1)
@@ -519,15 +507,11 @@
     def next_y(field):
         return pltpu.roll(field, LANES - 1, 1)
 
-    def total(field):
-        part = jnp.sum(field, axis=0, keepdims=True)
-        return part + swapped(part)
-
-    wz = jnp.where(last, 0.0, mean_of(fluid, rolled(fluid, -1), 4.0))
+    wz = jnp.where(z == depth - 1, 0.0, mean_of(fluid, rolled(fluid, -1), 4.0))
     wy = jnp.where(y == ROWS - 1, 0.0, mean_of(fluid, next_y(fluid), 4.0))
     wx = jnp.where(x == ROWS - 1, 0.0, mean_of(fluid, next_x(fluid), 4.0))
     across = (wx + pltpu.roll(wx, ROWS, 1)) + (wy + pltpu.roll(wy, 1, 1)) + pin
-    share = 1.0 / total(across)
+    share = 1.0 / jnp.sum(across, axis=0, keepdims=True)
 
     above, below, own = rolled(wz, 1), wz, across
     steps = []
@@ -544,7 +528,7 @@
     inverse = inverse_of(above + below + own)
 
     def solve(right):
-        mean = total(right) * share
+        mean = jnp.sum(right, axis=0, keepdims=True) * share
         for stride, up, down in steps:
             right = right + up * rolled(right, stride) + down * rolled(right, -stride)
         return right * inverse + mean
@@ -588,18 +572,19 @@
             first[row + 2 : row + 4] = high
             second[row : row + 2] = both
             second[row + 2 : row + 4] = rest
-    count = shares * count3 // 2
-    low, high = first[:count], first[count:]
-    half = iota((count, LANES), 1) < LANES // 2
-    corr3 = columns(
-        jnp.where(half, low, swapped(high)),
-        jnp.where(half, swapped(low), high),
-        jnp.where(half, second[:count], swapped(second[count:])),
+    half = iota((shares * count3, LANES), 1) < LANES // 2
+
+    def low_half(field):
+        return jnp.where(half, field, pltpu.roll(field, LANES // 2, 1))
+
+    def high_half(field):
+        return jnp.where(half, pltpu.roll(field, LANES // 2, 1), field)
+
+    solved[NEAR : NEAR + shares * count3] = columns(
+        low_half(first[...]), high_half(first[...]), low_half(second[...])
     )
     solved[0:NEAR] = jnp.zeros((NEAR, LANES), F32)
-    solved[NEAR : NEAR + count] = corr3
-    solved[NEAR + count : NEAR + 2 * count] = swapped(corr3)
-    solved[NEAR + 2 * count :] = jnp.zeros((2 * NEAR, LANES), F32)
+    solved[NEAR + shares * count3 :] = jnp.zeros((2 * NEAR, LANES), F32)
 
     nx, ny = SPLIT
     part = own_slab()

time: 50.7 us -> 50.2 us (level)
  Pallas kernels: 6.15 us -> 5.63 us
    pallas_call x1, Pallas kernels: 2.61 us -> 2.1 us  [whole_planes(): pl.pallas_call(functools.partial(up_kernel, groups, by, share), out_shape...]
where the time goes in v16:
time: 50.2 us; the launch traced here: 50 us
  blocking collectives  36.6 us (73%)
  Pallas kernels  5.63 us (11%)
  waiting for transfers between devices  5.34 us (11%)
  starting transfers between devices  1.29 us (3%)
  other arithmetic  0.93 us (2%)
    all_to_all x1, blocking collectives, whole_planes(): lax.all_to_all(parcels, ('gx', 'gy'), 0, 0, tiled=True)  15.8 us
    all_to_all x1, blocking collectives, whole_planes(): packed = lax.all_to_all(copies, ('gx', 'gy', 'gz'), 0, 0, tiled=True)  11.1 us
    all_to_all x1, blocking collectives, whole_planes(): lax.all_to_all(mine, ('gx', 'gy'), 0, 0, tiled=True)  9.7 us
    ppermute x2, waiting for transfers between devices, swap(): lax.ppermute(field, ('gx', 'gy', 'gz'), pairs + [pair[::-1] for pair in p...  5.34 us
    pallas_call x1, Pallas kernels, whole_planes(): pl.pallas_call(functools.partial(up_kernel, groups, by, share), out_shape...  2.1 us
    ppermute x2, starting transfers between devices, swap(): lax.ppermute(field, ('gx', 'gy', 'gz'), pairs + [pair[::-1] for pair in p...  1.29 us
    pallas_call x1, Pallas kernels, whole_planes(): pl.pallas_call(functools.partial(down_kernel, share), out_shape=(far1, fa...  1.19 us
  transfers between devices with their start and end apart: 2, of which 1 were waited for; matrix products, arithmetic and copies ran while one was open for 0% of the time, Pallas kernels for 2%

profile of v16, /device:TPU:0, one launch (start us, length us, event | category | flops | bytes accessed | tf_op | source)
XLA Modules:
  0.0 50.0 jit_solution(8110249368393522322)
XLA Ops:
  0.0 0.0 copy-start
  0.0 0.9 %multiply_multiply_fusion = (f32[16,8,128]{2,1,0:T(8,128)S(1)}, f32[16,8,128]{2,1,0:T(8,128)S(1)}) fusion(s32[16,8,128]{2,1,0:T(8,128)} %param.5, f32[16,8,128]{2,1,0:T(8,128)} %param.4), kind=kLoop, calls=%fused_computation | loop fusion | flops 65536 | bytes 262144 | tf_op jit(solution)/shard_map/mul | solution.py:706
  0.9 0.1 copy-done
  1.0 0.4 prepare.1
  1.4 15.8 %all_to_all.15.gathered = f32[8,48,128]{2,1,0:T(8,128)S(1)} all-to-all(f32[8,48,128]{2,1,0:T(8,128)S(1)} %prepare.1), channel_id=1, replica_groups=mesh['gx'=2,'gy'=4,'gz'=4] {'gx','gy'}, dimensions={0} | all-to-all | bytes 393216 | tf_op jit(solution)/shard_map/all_to_all | solution.py:719
  17.2 0.3 spread.1.own
  17.5 0.6 %collective-permute-start.1 = (f32[48,8,128]{2,1,0:T(8,128)S(1)}, f32[48,8,128]{2,1,0:T(8,128)S(1)}, u32[]{:S(2)}, u32[]{:S(2)}) collective-permute-start(f32[48,8,128]{2,1,0:T(8,128)S(1)} %spread.1.own), channel_id=1, source_target_pairs={{0,16},{20,4},{8,24},{28,12},{13,9},{5,1},{17,21},{25,29},{30,14},... | collective-permute-start | bytes 589832 | tf_op jit(solution)/shard_map/ppermute | solution.py:727
  18.1 0.7 %collective-permute-start = (f32[48,8,128]{2,1,0:T(8,128)S(1)}, f32[48,8,128]{2,1,0:T(8,128)S(1)}, u32[]{:S(2)}, u32[]{:S(2)}) collective-permute-start(f32[48,8,128]{2,1,0:T(8,128)S(1)} %spread.1.own), channel_id=1, source_target_pairs={{16,20},{4,8},{24,28},{12,13},{9,5},{1,17},{21,25},{29,30},{14,10}... | collective-permute-start | bytes 589832 | tf_op jit(solution)/shard_map/ppermute | solution.py:727
  18.8 5.3 %collective-permute-done.1.inner = f32[48,8,128]{2,1,0:T(8,128)S(1)} collective-permute-done((f32[48,8,128]{2,1,0:T(8,128)S(1)}, f32[48,8,128]{2,1,0:T(8,128)S(1)}, u32[]{:S(2)}, u32[]{:S(2)}) %collective-permute-start.1) | collective-permute-done | bytes 196640 | tf_op jit(solution)/shard_map/ppermute | solution.py:727
  24.1 0.9 %near.1 = (f32[32,8,128]{2,1,0:T(8,128)S(1)}, f32[32,8,128]{2,1,0:T(8,128)S(1)}, f32[32,8,128]{2,1,0:T(8,128)S(1)}, f32[32,8,128]{2,1,0:T(8,128)S(1)}, f32[32,8,...) custom-call(f32[48,8,128]{2,1,0:T(8,128)S(1)} %spread.1.own, ...), custom_call_target="tpu_custom_call" | custom-call | tf_op jit(solution)/shard_map/near/pallas_call | solution.py:735
  25.1 0.0 collective-permute-done.outer
  25.1 1.2 %down.1 = (f32[24,8,128]{2,1,0:T(8,128)S(1)}, f32[24,8,128]{2,1,0:T(8,128)S(1)}, f32[24,8,128]{2,1,0:T(8,128)S(1)}, f32[24,8,128]{2,1,0:T(8,128)S(1)}, f32[24,8,...) custom-call(f32[48,8,128]{2,1,0:T(8,128)S(1)} %spread.1.own, ...), custom_call_target="tpu_custom_call" | custom-call | tf_op jit(solution)/shard_map/down/pallas_call | solution.py:742
  26.3 11.1 %all_to_all.16.packed = f32[32,5,2,128]{3,2,1,0:T(2,128)S(1)} all-to-all(f32[32,5,2,128]{3,2,1,0:T(2,128)S(1)} %broadcast_in_dim.3), channel_id=1, replica_groups=mesh['gx'=2,'gy'=4,'gz'=4] {'gx','gy','gz'}, dimensions={0} | all-to-all | bytes 327680 | tf_op jit(solution)/shard_map/all_to_all | solution.py:750
  37.4 2.1 %up.1 = f32[8,16,128]{2,1,0:T(8,128)S(1)} custom-call(f32[32,5,2,128]{3,2,1,0:T(2,128)S(1)} %all_to_all.16.packed, f32[32,8,128]{2,1,0:T(8,128)S(1)} %get-tuple-element.58.near1_0_, f32[32,8,128]{2,1,0:T(8,128)S(1)} %get-tuple-element.59.near1_1_, f32[32,8,128]{2,1,0:T(8,128)S(1)} %get-tuple-element.60.near1_2_, ...), custom_call_target="tpu_custom_call" | custom-call | tf_op jit(solution)/shard_map/up/pallas_call | solution.py:752
  39.5 9.7 %all_to_all.17.blocks = f32[8,16,128]{2,1,0:T(8,128)S(1)} all-to-all(f32[8,16,128]{2,1,0:T(8,128)S(1)} %up.1), channel_id=1, replica_groups=mesh['gx'=2,'gy'=4,'gz'=4] {'gx','gy'}, dimensions={0} | all-to-all | bytes 131072 | tf_op jit(solution)/shard_map/all_to_all | solution.py:766
  49.2 0.7 %finish.1 = f32[16,8,128]{2,1,0:T(8,128)} custom-call(f32[8,16,128]{2,1,0:T(8,128)S(1)} %all_to_all.17.blocks), custom_call_target="tpu_custom_call" | custom-call | tf_op jit(solution)/shard_map/finish/pallas_call | solution.py:761
  (1 shorter events, 0.0 us)
Async XLA Ops:
  0.0 1.0 %copy-start = (bf16[32,16,256]{2,1,0:T(8,128)(2,1)S(1)}, bf16[32,16,256]{2,1,0:T(8,128)(2,1)}, u32[]{:S(2)}) copy-start(bf16[32,16,256]{2,1,0:T(8,128)(2,1)} %param.3) | copy-start | bytes 786436
  17.5 6.6 %collective-permute-start.1 = (f32[48,8,128]{2,1,0:T(8,128)S(1)}, f32[48,8,128]{2,1,0:T(8,128)S(1)}, u32[]{:S(2)}, u32[]{:S(2)}) collective-permute-start(f32[48,8,128]{2,1,0:T(8,128)S(1)} %spread.1.own), channel_id=1, source_target_pairs={{0,16},{20,4},{8,24},{28,12},{13,9},{5,1},{17,21},{25,29},{30,14},... | collective-permute-start | bytes 589832 | tf_op jit(solution)/shard_map/ppermute | solution.py:727
  18.1 6.9 %collective-permute-start = (f32[48,8,128]{2,1,0:T(8,128)S(1)}, f32[48,8,128]{2,1,0:T(8,128)S(1)}, u32[]{:S(2)}, u32[]{:S(2)}) collective-permute-start(f32[48,8,128]{2,1,0:T(8,128)S(1)} %spread.1.own), channel_id=1, source_target_pairs={{16,20},{4,8},{24,28},{12,13},{9,5},{1,17},{21,25},{29,30},{14,10}... | collective-permute-start | bytes 589832 | tf_op jit(solution)/shard_map/ppermute | solution.py:727

commit v17 on v16

--- a/solution.py
+++ b/solution.py
@@ -330,8 +330,21 @@
     return found
 
 
-def own_peer_of(rank):
-    return lookup([path_of(group)[rank] for group in range(lax.axis_size("gz"))], lax.axis_index("gz"))
+def slot_of(peer):
+    return SPLIT[0] * SPLIT[1] - 1 - peer
+
+
+def own_slot_of(rank):
+    groups = range(lax.axis_size("gz"))
+    return lookup([slot_of(path_of(group)[rank]) for group in groups], lax.axis_index("gz"))
+
+
+def exchange(field):
+    peers, groups = SPLIT[0] * SPLIT[1], lax.axis_size("gz")
+    order = sorted(range(peers), key=slot_of)
+    members = [[peer * groups + group for peer in order] for group in range(groups)]
+    axes = ("gx", "gy", "gz")
+    return lax.all_to_all(field, axes, 0, 0, axis_index_groups=members, tiled=True)
 
 
 def slabs_of(groups):
@@ -372,7 +385,7 @@
 
     fluid, pin = turned(fluid_ref), turned(pin_ref)
     for rank in range(depth // share):
-        peer, begin = own_peer_of(rank), rank * share
+        peer, begin = own_slot_of(rank), rank * share
         for index, field in enumerate((fluid, rhs, pin)):
             out_ref[peer, index * share : (index + 1) * share] = field[begin : begin + share]
 
@@ -392,7 +405,7 @@
     group = (iota((ROWS, LANES), 1) // by) % groups
     nx, ny = SPLIT
     for ix in range(nx):
-        found = [gathered[ix * ny + iy, pl.ds(row, ROWS), :] for iy in range(ny)]
+        found = [gathered[slot_of(ix * ny + iy), pl.ds(row, ROWS), :] for iy in range(ny)]
         for part in range(groups):
             total = found[part]
             for iy in range(ny):
@@ -671,13 +684,13 @@
                 if part != iy:
                     moved = pltpu.roll(scaled[part], (by * (part - iy)) % LANES, 1)
                     total = jnp.where(group == part, moved, total)
-            out_ref[ix * ny + iy] = total
+            out_ref[slot_of(ix * ny + iy)] = total
 
 
 def finish_kernel(blocks, out_ref):
     bx, by, depth = out_ref.shape
     peers = blocks.shape[0]
-    ordered = jnp.concatenate([blocks[own_peer_of(rank)] for rank in range(peers)], axis=0)
+    ordered = jnp.concatenate([blocks[own_slot_of(rank)] for rank in range(peers)], axis=0)
     turned = ordered.T
     for x in range(bx):
         row = ((x % 4) * (bx // 4) + x // 4) * by
@@ -716,7 +729,7 @@
         scratch_shapes=[room(3 * share)],
         compiler_params=limit,
         name="spread",
-    )(lax.all_to_all(parcels, ("gx", "gy"), 0, 0, tiled=True))
+    )(exchange(parcels))
     length = lax.axis_size("gz")
     parts = length * peers
 
@@ -763,7 +776,7 @@
         out_shape=jax.ShapeDtypeStruct((bx, by, depth), F32),
         compiler_params=limit,
         name="finish",
-    )(lax.all_to_all(mine, ("gx", "gy"), 0, 0, tiled=True))
+    )(exchange(mine))
 
 
 def one_tile_planes(mesh, viscosity):

time: 50.2 us -> 49.6 us (0.988)
  waiting for transfers between devices: 5.34 us -> 4.07 us
    all_to_all x1, blocking collectives: 11.1 us -> 15.5 us  [whole_planes(): packed = lax.all_to_all(copies, ('gx', 'gy', 'gz'), 0, 0, tiled=True)]
    all_to_all x2, blocking collectives: 25.5 us -> 21.5 us  [exchange(): lax.all_to_all(field, axes, 0, 0, axis_index_groups=members, tiled=True)]
    ppermute x2, waiting for transfers between devices: 5.34 us -> 4.07 us  [swap(): lax.ppermute(field, ('gx', 'gy', 'gz'), pairs + [pair[::-1] for pair in p...]
where the time goes in v17:
time: 49.6 us; the launch traced here: 49.4 us
  blocking collectives  36.9 us (74%)
  Pallas kernels  5.63 us (11%)
  waiting for transfers between devices  4.07 us (8%)
  starting transfers between devices  1.66 us (3%)
  other arithmetic  0.93 us (2%)
    all_to_all x2, blocking collectives, exchange(): lax.all_to_all(field, axes, 0, 0, axis_index_groups=members, tiled=True)  21.5 us
    all_to_all x1, blocking collectives, whole_planes(): packed = lax.all_to_all(copies, ('gx', 'gy', 'gz'), 0, 0, tiled=True)  15.5 us
    ppermute x2, waiting for transfers between devices, swap(): lax.ppermute(field, ('gx', 'gy', 'gz'), pairs + [pair[::-1] for pair in p...  4.07 us
    pallas_call x1, Pallas kernels, whole_planes(): pl.pallas_call(functools.partial(up_kernel, groups, by, share), out_shape...  2.1 us
    ppermute x2, starting transfers between devices, swap(): lax.ppermute(field, ('gx', 'gy', 'gz'), pairs + [pair[::-1] for pair in p...  1.66 us
    pallas_call x1, Pallas kernels, whole_planes(): pl.pallas_call(functools.partial(down_kernel, share), out_shape=(far1, fa...  1.19 us
  transfers between devices with their start and end apart: 2, of which 1 were waited for; matrix products, arithmetic and copies ran while one was open for 0% of the time, Pallas kernels for 2%

profile of v17, /device:TPU:0, one launch (start us, length us, event | category | flops | bytes accessed | tf_op | source)
XLA Modules:
  0.0 49.4 jit_solution(17628710123950749319)
XLA Ops:
  0.0 0.0 copy-start
  0.0 0.9 %multiply_multiply_fusion = (f32[16,8,128]{2,1,0:T(8,128)S(1)}, f32[16,8,128]{2,1,0:T(8,128)S(1)}) fusion(s32[16,8,128]{2,1,0:T(8,128)} %param.5, f32[16,8,128]{2,1,0:T(8,128)} %param.4), kind=kLoop, calls=%fused_computation | loop fusion | flops 65536 | bytes 262144 | tf_op jit(solution)/shard_map/mul | solution.py:719
  0.9 0.1 copy-done
  1.0 0.4 prepare.1
  1.4 12.8 %all_to_all.15.gathered = f32[8,48,128]{2,1,0:T(8,128)S(1)} all-to-all(f32[8,48,128]{2,1,0:T(8,128)S(1)} %prepare.1), channel_id=1, replica_groups={{28,24,20,16,12,8,4,0},{29,25,21,17,13,9,5,1},{30,26,22,18,14,10,6,2},{..., dimensions={0} | all-to-all | bytes 393216 | tf_op jit(solution)/shard_map/all_to_all | solution.py:347
  14.3 0.3 spread.1.own
  14.5 1.0 %collective-permute-start.1 = (f32[48,8,128]{2,1,0:T(8,128)S(1)}, f32[48,8,128]{2,1,0:T(8,128)S(1)}, u32[]{:S(2)}, u32[]{:S(2)}) collective-permute-start(f32[48,8,128]{2,1,0:T(8,128)S(1)} %spread.1.own), channel_id=1, source_target_pairs={{0,16},{20,4},{8,24},{28,12},{13,9},{5,1},{17,21},{25,29},{30,14},... | collective-permute-start | bytes 589832 | tf_op jit(solution)/shard_map/ppermute | solution.py:740
  15.5 0.7 %collective-permute-start = (f32[48,8,128]{2,1,0:T(8,128)S(1)}, f32[48,8,128]{2,1,0:T(8,128)S(1)}, u32[]{:S(2)}, u32[]{:S(2)}) collective-permute-start(f32[48,8,128]{2,1,0:T(8,128)S(1)} %spread.1.own), channel_id=1, source_target_pairs={{16,20},{4,8},{24,28},{12,13},{9,5},{1,17},{21,25},{29,30},{14,10}... | collective-permute-start | bytes 589832 | tf_op jit(solution)/shard_map/ppermute | solution.py:740
  16.2 4.1 %collective-permute-done.1.inner = f32[48,8,128]{2,1,0:T(8,128)S(1)} collective-permute-done((f32[48,8,128]{2,1,0:T(8,128)S(1)}, f32[48,8,128]{2,1,0:T(8,128)S(1)}, u32[]{:S(2)}, u32[]{:S(2)}) %collective-permute-start.1) | collective-permute-done | bytes 196640 | tf_op jit(solution)/shard_map/ppermute | solution.py:740
  20.3 0.9 %near.1 = (f32[32,8,128]{2,1,0:T(8,128)S(1)}, f32[32,8,128]{2,1,0:T(8,128)S(1)}, f32[32,8,128]{2,1,0:T(8,128)S(1)}, f32[32,8,128]{2,1,0:T(8,128)S(1)}, f32[32,8,...) custom-call(f32[48,8,128]{2,1,0:T(8,128)S(1)} %spread.1.own, ...), custom_call_target="tpu_custom_call" | custom-call | tf_op jit(solution)/shard_map/near/pallas_call | solution.py:748
  21.2 0.0 collective-permute-done.outer
  21.2 1.2 %down.1 = (f32[24,8,128]{2,1,0:T(8,128)S(1)}, f32[24,8,128]{2,1,0:T(8,128)S(1)}, f32[24,8,128]{2,1,0:T(8,128)S(1)}, f32[24,8,128]{2,1,0:T(8,128)S(1)}, f32[24,8,...) custom-call(f32[48,8,128]{2,1,0:T(8,128)S(1)} %spread.1.own, ...), custom_call_target="tpu_custom_call" | custom-call | tf_op jit(solution)/shard_map/down/pallas_call | solution.py:755
  22.4 15.5 %all_to_all.16.packed = f32[32,5,2,128]{3,2,1,0:T(2,128)S(1)} all-to-all(f32[32,5,2,128]{3,2,1,0:T(2,128)S(1)} %broadcast_in_dim.3), channel_id=1, replica_groups=mesh['gx'=2,'gy'=4,'gz'=4] {'gx','gy','gz'}, dimensions={0} | all-to-all | bytes 327680 | tf_op jit(solution)/shard_map/all_to_all | solution.py:763
  37.9 2.1 %up.1 = f32[8,16,128]{2,1,0:T(8,128)S(1)} custom-call(f32[32,5,2,128]{3,2,1,0:T(2,128)S(1)} %all_to_all.16.packed, f32[32,8,128]{2,1,0:T(8,128)S(1)} %get-tuple-element.58.near1_0_, f32[32,8,128]{2,1,0:T(8,128)S(1)} %get-tuple-element.59.near1_1_, f32[32,8,128]{2,1,0:T(8,128)S(1)} %get-tuple-element.60.near1_2_, ...), custom_call_target="tpu_custom_call" | custom-call | tf_op jit(solution)/shard_map/up/pallas_call | solution.py:765
  40.0 8.6 %all_to_all.17.blocks = f32[8,16,128]{2,1,0:T(8,128)S(1)} all-to-all(f32[8,16,128]{2,1,0:T(8,128)S(1)} %up.1), channel_id=1, replica_groups={{28,24,20,16,12,8,4,0},{29,25,21,17,13,9,5,1},{30,26,22,18,14,10,6,2},{..., dimensions={0} | all-to-all | bytes 131072 | tf_op jit(solution)/shard_map/all_to_all | solution.py:347
  48.7 0.7 %finish.1 = f32[16,8,128]{2,1,0:T(8,128)} custom-call(f32[8,16,128]{2,1,0:T(8,128)S(1)} %all_to_all.17.blocks), custom_call_target="tpu_custom_call" | custom-call | tf_op jit(solution)/shard_map/finish/pallas_call | solution.py:774
  (1 shorter events, 0.0 us)
Async XLA Ops:
  0.0 1.0 %copy-start = (bf16[32,16,256]{2,1,0:T(8,128)(2,1)S(1)}, bf16[32,16,256]{2,1,0:T(8,128)(2,1)}, u32[]{:S(2)}) copy-start(bf16[32,16,256]{2,1,0:T(8,128)(2,1)} %param.3) | copy-start | bytes 786436
  14.5 5.7 %collective-permute-start.1 = (f32[48,8,128]{2,1,0:T(8,128)S(1)}, f32[48,8,128]{2,1,0:T(8,128)S(1)}, u32[]{:S(2)}, u32[]{:S(2)}) collective-permute-start(f32[48,8,128]{2,1,0:T(8,128)S(1)} %spread.1.own), channel_id=1, source_target_pairs={{0,16},{20,4},{8,24},{28,12},{13,9},{5,1},{17,21},{25,29},{30,14},... | collective-permute-start | bytes 589832 | tf_op jit(solution)/shard_map/ppermute | solution.py:740
  15.5 5.7 %collective-permute-start = (f32[48,8,128]{2,1,0:T(8,128)S(1)}, f32[48,8,128]{2,1,0:T(8,128)S(1)}, u32[]{:S(2)}, u32[]{:S(2)}) collective-permute-start(f32[48,8,128]{2,1,0:T(8,128)S(1)} %spread.1.own), channel_id=1, source_target_pairs={{16,20},{4,8},{24,28},{12,13},{9,5},{1,17},{21,25},{29,30},{14,10}... | collective-permute-start | bytes 589832 | tf_op jit(solution)/shard_map/ppermute | solution.py:740

commit v18 on v17

--- a/solution.py
+++ b/solution.py
@@ -359,6 +359,22 @@
     groups = lax.axis_size("gz")
     device = (lax.axis_index("gx") * ny + lax.axis_index("gy")) * groups + lax.axis_index("gz")
     return lookup(slabs_of(groups), device)
+
+
+def slots_of(groups):
+    peers = SPLIT[0] * SPLIT[1]
+    return [
+        (groups - 1 - group) * peers + slot_of(peer)
+        for group in range(groups)
+        for peer in path_of(group)
+    ]
+
+
+def exchange_all(field):
+    groups = lax.axis_size("gz")
+    members = [device for _, device in sorted(zip(slots_of(groups), devices_of(groups)))]
+    axes = ("gx", "gy", "gz")
+    return lax.all_to_all(field, axes, 0, 0, axis_index_groups=[members], tiled=True)
 
 
 def devices_of(groups):
@@ -568,8 +584,8 @@
     count3 = depth // 4
     shares = packed.shape[0]
     peers = SPLIT[0] * SPLIT[1]
-    devices = devices_of(shares // peers)
-    for slab, index in enumerate(devices):
+    slots = slots_of(shares // peers)
+    for slab, index in enumerate(slots):
         row = slab * count3
         low, high, both = packed[index, 0], packed[index, 1], packed[index, 2]
         rest = pltpu.roll(both, LANES // 2, 1)
@@ -628,7 +644,7 @@
     row = iota((ROWS, LANES), 0)
 
     def unpacked(index, which):
-        pair = packed[lookup(devices, jnp.clip(index, 0, shares - 1)), which]
+        pair = packed[lookup(slots, jnp.clip(index, 0, shares - 1)), which]
         total = None
         for shift in range(4):
             moved = pltpu.roll(pair, shift * (LANES // 4), 1)
@@ -760,7 +776,7 @@
         name="down",
     )(own, outer, near2, fluid2, pin2, fluid3, pin3)
     copies = jnp.broadcast_to(parcel, (parts,) + parcel.shape)
-    packed = lax.all_to_all(copies, ("gx", "gy", "gz"), 0, 0, tiled=True)
+    packed = exchange_all(copies)
     depth3 = parts * count3
     mine = pl.pallas_call(
         functools.partial(up_kernel, groups, by, share),

time: 49.6 us -> 49.9 us (level)
  no operation moved by 1% of the time
where the time goes in v18:
time: 49.9 us; the launch traced here: 49.6 us
  blocking collectives  37.2 us (75%)
  Pallas kernels  5.63 us (11%)
  waiting for transfers between devices  4.07 us (8%)
  starting transfers between devices  1.66 us (3%)
  other arithmetic  0.93 us (2%)
    all_to_all x2, blocking collectives, exchange(): lax.all_to_all(field, axes, 0, 0, axis_index_groups=members, tiled=True)  21.5 us
    all_to_all x1, blocking collectives, exchange_all(): lax.all_to_all(field, axes, 0, 0, axis_index_groups=[members], tiled=True)  15.7 us
    ppermute x2, waiting for transfers between devices, swap(): lax.ppermute(field, ('gx', 'gy', 'gz'), pairs + [pair[::-1] for pair in p...  4.07 us
    pallas_call x1, Pallas kernels, whole_planes(): pl.pallas_call(functools.partial(up_kernel, groups, by, share), out_shape...  2.1 us
    ppermute x2, starting transfers between devices, swap(): lax.ppermute(field, ('gx', 'gy', 'gz'), pairs + [pair[::-1] for pair in p...  1.66 us
    pallas_call x1, Pallas kernels, whole_planes(): pl.pallas_call(functools.partial(down_kernel, share), out_shape=(far1, fa...  1.19 us
  transfers between devices with their start and end apart: 2, of which 1 were waited for; matrix products, arithmetic and copies ran while one was open for 0% of the time, Pallas kernels for 2%

profile of v18, /device:TPU:0, one launch (start us, length us, event | category | flops | bytes accessed | tf_op | source)
XLA Modules:
  0.0 49.6 jit_solution(3546820050783845958)
XLA Ops:
  0.0 0.0 copy-start
  0.0 0.9 %multiply_multiply_fusion = (f32[16,8,128]{2,1,0:T(8,128)S(1)}, f32[16,8,128]{2,1,0:T(8,128)S(1)}) fusion(s32[16,8,128]{2,1,0:T(8,128)} %param.5, f32[16,8,128]{2,1,0:T(8,128)} %param.4), kind=kLoop, calls=%fused_computation | loop fusion | flops 65536 | bytes 262144 | tf_op jit(solution)/shard_map/mul | solution.py:735
  0.9 0.1 copy-done
  1.0 0.4 prepare.1
  1.4 12.8 %all_to_all.15.gathered = f32[8,48,128]{2,1,0:T(8,128)S(1)} all-to-all(f32[8,48,128]{2,1,0:T(8,128)S(1)} %prepare.1), channel_id=1, replica_groups={{28,24,20,16,12,8,4,0},{29,25,21,17,13,9,5,1},{30,26,22,18,14,10,6,2},{..., dimensions={0} | all-to-all | bytes 393216 | tf_op jit(solution)/shard_map/all_to_all | solution.py:347
  14.3 0.3 spread.1.own
  14.5 1.0 %collective-permute-start.1 = (f32[48,8,128]{2,1,0:T(8,128)S(1)}, f32[48,8,128]{2,1,0:T(8,128)S(1)}, u32[]{:S(2)}, u32[]{:S(2)}) collective-permute-start(f32[48,8,128]{2,1,0:T(8,128)S(1)} %spread.1.own), channel_id=1, source_target_pairs={{0,16},{20,4},{8,24},{28,12},{13,9},{5,1},{17,21},{25,29},{30,14},... | collective-permute-start | bytes 589832 | tf_op jit(solution)/shard_map/ppermute | solution.py:756
  15.5 0.7 %collective-permute-start = (f32[48,8,128]{2,1,0:T(8,128)S(1)}, f32[48,8,128]{2,1,0:T(8,128)S(1)}, u32[]{:S(2)}, u32[]{:S(2)}) collective-permute-start(f32[48,8,128]{2,1,0:T(8,128)S(1)} %spread.1.own), channel_id=1, source_target_pairs={{16,20},{4,8},{24,28},{12,13},{9,5},{1,17},{21,25},{29,30},{14,10}... | collective-permute-start | bytes 589832 | tf_op jit(solution)/shard_map/ppermute | solution.py:756
  16.2 4.1 %collective-permute-done.1.inner = f32[48,8,128]{2,1,0:T(8,128)S(1)} collective-permute-done((f32[48,8,128]{2,1,0:T(8,128)S(1)}, f32[48,8,128]{2,1,0:T(8,128)S(1)}, u32[]{:S(2)}, u32[]{:S(2)}) %collective-permute-start.1) | collective-permute-done | bytes 196640 | tf_op jit(solution)/shard_map/ppermute | solution.py:756
  20.3 0.9 %near.1 = (f32[32,8,128]{2,1,0:T(8,128)S(1)}, f32[32,8,128]{2,1,0:T(8,128)S(1)}, f32[32,8,128]{2,1,0:T(8,128)S(1)}, f32[32,8,128]{2,1,0:T(8,128)S(1)}, f32[32,8,...) custom-call(f32[48,8,128]{2,1,0:T(8,128)S(1)} %spread.1.own, ...), custom_call_target="tpu_custom_call" | custom-call | tf_op jit(solution)/shard_map/near/pallas_call | solution.py:764
  21.2 0.0 collective-permute-done.outer
  21.2 1.2 %down.1 = (f32[24,8,128]{2,1,0:T(8,128)S(1)}, f32[24,8,128]{2,1,0:T(8,128)S(1)}, f32[24,8,128]{2,1,0:T(8,128)S(1)}, f32[24,8,128]{2,1,0:T(8,128)S(1)}, f32[24,8,...) custom-call(f32[48,8,128]{2,1,0:T(8,128)S(1)} %spread.1.own, ...), custom_call_target="tpu_custom_call" | custom-call | tf_op jit(solution)/shard_map/down/pallas_call | solution.py:771
  22.4 15.7 %all_to_all.16.packed = f32[32,5,2,128]{3,2,1,0:T(2,128)S(1)} all-to-all(f32[32,5,2,128]{3,2,1,0:T(2,128)S(1)} %broadcast_in_dim.3), channel_id=1, replica_groups={{31,27,23,19,15,11,7,3,30,26,22,18,14,10,6,2,29,25,21,17,13,9,5,1,28,24..., dimensions={0} | all-to-all | bytes 327680 | tf_op jit(solution)/shard_map/all_to_all | solution.py:377
  38.2 2.1 %up.1 = f32[8,16,128]{2,1,0:T(8,128)S(1)} custom-call(f32[32,5,2,128]{3,2,1,0:T(2,128)S(1)} %all_to_all.16.packed, f32[32,8,128]{2,1,0:T(8,128)S(1)} %get-tuple-element.58.near1_0_, f32[32,8,128]{2,1,0:T(8,128)S(1)} %get-tuple-element.59.near1_1_, f32[32,8,128]{2,1,0:T(8,128)S(1)} %get-tuple-element.60.near1_2_, ...), custom_call_target="tpu_custom_call" | custom-call | tf_op jit(solution)/shard_map/up/pallas_call | solution.py:781
  40.3 8.6 %all_to_all.17.blocks = f32[8,16,128]{2,1,0:T(8,128)S(1)} all-to-all(f32[8,16,128]{2,1,0:T(8,128)S(1)} %up.1), channel_id=1, replica_groups={{28,24,20,16,12,8,4,0},{29,25,21,17,13,9,5,1},{30,26,22,18,14,10,6,2},{..., dimensions={0} | all-to-all | bytes 131072 | tf_op jit(solution)/shard_map/all_to_all | solution.py:347
  48.9 0.7 %finish.1 = f32[16,8,128]{2,1,0:T(8,128)} custom-call(f32[8,16,128]{2,1,0:T(8,128)S(1)} %all_to_all.17.blocks), custom_call_target="tpu_custom_call" | custom-call | tf_op jit(solution)/shard_map/finish/pallas_call | solution.py:790
  (1 shorter events, 0.0 us)
Async XLA Ops:
  0.0 1.0 %copy-start = (bf16[32,16,256]{2,1,0:T(8,128)(2,1)S(1)}, bf16[32,16,256]{2,1,0:T(8,128)(2,1)}, u32[]{:S(2)}) copy-start(bf16[32,16,256]{2,1,0:T(8,128)(2,1)} %param.3) | copy-start | bytes 786436
  14.5 5.7 %collective-permute-start.1 = (f32[48,8,128]{2,1,0:T(8,128)S(1)}, f32[48,8,128]{2,1,0:T(8,128)S(1)}, u32[]{:S(2)}, u32[]{:S(2)}) collective-permute-start(f32[48,8,128]{2,1,0:T(8,128)S(1)} %spread.1.own), channel_id=1, source_target_pairs={{0,16},{20,4},{8,24},{28,12},{13,9},{5,1},{17,21},{25,29},{30,14},... | collective-permute-start | bytes 589832 | tf_op jit(solution)/shard_map/ppermute | solution.py:756
  15.5 5.7 %collective-permute-start = (f32[48,8,128]{2,1,0:T(8,128)S(1)}, f32[48,8,128]{2,1,0:T(8,128)S(1)}, u32[]{:S(2)}, u32[]{:S(2)}) collective-permute-start(f32[48,8,128]{2,1,0:T(8,128)S(1)} %spread.1.own), channel_id=1, source_target_pairs={{16,20},{4,8},{24,28},{12,13},{9,5},{1,17},{21,25},{29,30},{14,10}... | collective-permute-start | bytes 589832 | tf_op jit(solution)/shard_map/ppermute | solution.py:756

commit v19 on v17

--- a/solution.py
+++ b/solution.py
@@ -152,14 +152,14 @@
     return lax.broadcasted_iota(jnp.int32, shape, dim)
 
 
-def dot01(field, chosen, parts=3):
+def dot01(field, chosen):
     total = None
     rest = field
-    for part in range(parts):
+    for part in range(3):
         piece = rest.astype(jnp.bfloat16)
         term = jnp.dot(piece, chosen, preferred_element_type=F32)
         total = term if total is None else total + term
-        if part < parts - 1:
+        if part < 2:
             rest = rest - piece.astype(F32)
     return total
 
@@ -302,9 +302,9 @@
     return where01((fine < ny * xs) & same_x & same_y)
 
 
-def in_lanes(field, chosen, parts=3):
+def in_lanes(field, chosen):
     flat = field.reshape(field.shape[0] * ROWS, LANES)
-    return dot01(flat, chosen, parts).reshape(field.shape)
+    return dot01(flat, chosen).reshape(field.shape)
 
 
 def path_of(group):
@@ -390,7 +390,7 @@
             out_ref[peer, index * share : (index + 1) * share] = field[begin : begin + share]
 
 
-def spread_kernel(groups, by, gathered, own, straight):
+def spread_kernel(groups, by, gathered, own, inner, outer, straight):
     for start in range(0, own.shape[0], ROWS):
         place(gathered, start, straight, start, groups, by)
     share = own.shape[0] // 3
@@ -399,6 +399,13 @@
         for plane in range(share):
             at = jnp.where(odd, share - 1 - plane, plane)
             own[index * share + plane] = straight[index * share + at]
+    for target, drop in ((inner, 0), (outer, share - 1)):
+        row = 0
+        for index in range(3):
+            for plane in range(share):
+                if index == 0 or plane != drop:
+                    target[row] = own[index * share + plane]
+                    row += 1
 
 
 def place(gathered, row, target, plane, groups, by):
@@ -421,10 +428,15 @@
     saved1, saved2, fluid2, pin2, fluid3, pin3,
     fluid1, rhs1, pin1, other1, rhs2, sums,
 ):
+    row = 0
     for index, target in enumerate((fluid1, rhs1, pin1)):
         target[0:depth] = own[index * depth : (index + 1) * depth]
-        for plane in range(HALO):
-            target[depth + plane] = inner[(index + 1) * depth - 1 - plane]
+        count = HALO if index == 0 else HALO - 1
+        for plane in range(count):
+            target[depth + plane] = inner[row + count - 1 - plane]
+        if count < HALO:
+            target[depth + count] = jnp.zeros((ROWS, LANES), F32)
+        row += count
     fine, coarse = Level(0), Level(1)
     down1, down2 = lanes_down(0), lanes_down(1)
     fields1, corr1 = (saved1[0:6], saved1[6], saved1[7]), saved1[8]
@@ -452,9 +464,14 @@
     fluid1, rhs1, pin1, other1, fluid2, rhs2, pin2, other2, sums,
 ):
     planes = fluid1.shape[0]
+    row = 0
     for index, target in enumerate((fluid1, rhs1, pin1)):
-        for plane in range(HALO):
-            target[plane] = outer[index * depth + HALO - 1 - plane]
+        count = HALO if index == 0 else HALO - 1
+        if count < HALO:
+            target[0] = jnp.zeros((ROWS, LANES), F32)
+        for plane in range(count):
+            target[HALO - count + plane] = outer[row + count - 1 - plane]
+        row += count
         target[HALO:planes] = own[index * depth : index * depth + planes - HALO]
 
     fine, coarse = Level(0), Level(1)
@@ -488,6 +505,13 @@
         first = jnp.where(lane == row, rhs3[:, row, :], first)
         first = jnp.where(lane == ROWS + row, fluid3[:, row, :], first)
         second = jnp.where(lane % ROWS == row, pin3[:, row, :], second)
+    odd = own_slab() % 2 == 1
+
+    def ordered(field):
+        back = [field[row : row + 1] for row in reversed(range(count3))]
+        return jnp.where(odd, jnp.concatenate(back, axis=0), field)
+
+    first, second = ordered(first), ordered(second)
     packed[0] = first[0:2]
     packed[1] = first[2:4]
     packed[2] = jnp.where(lane[0:2] < ROWS, second[0:2], second[2:4])
@@ -528,7 +552,7 @@
 
     above, below, own = rolled(wz, 1), wz, across
     steps = []
-    stride = 1
+    stride, right = 1, rhs
     while stride < depth:
         inverse = inverse_of(above + below + own)
         up = above * rolled(inverse, stride)
@@ -536,17 +560,15 @@
         own = own + up * rolled(own, stride) + down * rolled(own, -stride)
         above = up * rolled(above, stride)
         below = down * rolled(below, -stride)
+        right = right + up * rolled(right, stride) + down * rolled(right, -stride)
         steps.append((stride, up, down))
         stride *= 2
     inverse = inverse_of(above + below + own)
 
-    def solve(right):
-        mean = jnp.sum(right, axis=0, keepdims=True) * share
-        for stride, up, down in steps:
-            right = right + up * rolled(right, stride) + down * rolled(right, -stride)
-        return right * inverse + mean
-
-    corr = solve(rhs)
+    def mean(right):
+        return jnp.sum(right, axis=0, keepdims=True) * share
+
+    corr = right * inverse + mean(rhs)
     flow_x = wx * (next_x(corr) - corr)
     flow_y = wy * (next_y(corr) - corr)
     flow_z = wz * (rolled(corr, -1) - corr)
@@ -556,7 +578,10 @@
         + (flow_y - pltpu.roll(flow_y, 1, 1))
         + (flow_z - rolled(flow_z, 1))
     )
-    return corr + solve(rest)
+    right = rest
+    for stride, up, down in steps:
+        right = right + up * rolled(right, stride) + down * rolled(right, -stride)
+    return (corr + mean(rest)) + right * inverse
 
 
 def up_kernel(
@@ -571,20 +596,11 @@
     devices = devices_of(shares // peers)
     for slab, index in enumerate(devices):
         row = slab * count3
-        low, high, both = packed[index, 0], packed[index, 1], packed[index, 2]
-        rest = pltpu.roll(both, LANES // 2, 1)
-        if slab % 2:
-            for at, (level3, pin) in enumerate(((high, rest), (low, both))):
-                begin = row + 2 * at
-                first[begin : begin + 1] = level3[1:2]
-                first[begin + 1 : begin + 2] = level3[0:1]
-                second[begin : begin + 1] = pin[1:2]
-                second[begin + 1 : begin + 2] = pin[0:1]
-        else:
-            first[row : row + 2] = low
-            first[row + 2 : row + 4] = high
-            second[row : row + 2] = both
-            second[row + 2 : row + 4] = rest
+        first[row : row + 2] = packed[index, 0]
+        first[row + 2 : row + 4] = packed[index, 1]
+        both = packed[index, 2]
+        second[row : row + 2] = both
+        second[row + 2 : row + 4] = pltpu.roll(both, LANES // 2, 1)
     half = iota((shares * count3, LANES), 1) < LANES // 2
 
     def low_half(field):
@@ -609,7 +625,7 @@
     spread = where01((cell < ROWS) & (cell == (lane % coarse.ny) // 2))
     rows = tall.shape[0]
     turned = [tall] + [pltpu.roll(tall, LANES - ROWS * row, 1) for row in range(1, ROWS)]
-    wide = dot01(jnp.concatenate(turned, axis=0), spread, 2)
+    wide = dot01(jnp.concatenate(turned, axis=0), spread)
     for row in range(ROWS):
         lifted[0:rows, row, :] = wide[row * rows : (row + 1) * rows]
 
@@ -649,7 +665,7 @@
     x_of = (fine_lane // fine.ny) // 2
     y_of = (fine_lane % fine.ny) // 2
     up = where01(coarse_lane == x_of * coarse.ny + y_of)
-    lifted[0 : depth // 2 + 4] = in_lanes(two2[NEAR - 2 : reach + 2], up, 2)
+    lifted[0 : depth // 2 + 4] = in_lanes(two2[NEAR - 2 : reach + 2], up)
     parents = lifted[0 : depth // 2 + 4]
     twice = jnp.broadcast_to(parents[:, None], (parents.shape[0], 2, ROWS, LANES))
     low, high = HALO - 4, HALO + depth + 4
@@ -723,9 +739,9 @@
         compiler_params=limit,
         name="prepare",
     )(residual_q2.reshape(4 * bx * by, 2 * depth), fluid, pin)
-    own = pl.pallas_call(
+    own, inner, outer = pl.pallas_call(
         functools.partial(spread_kernel, groups, by),
-        out_shape=blocks(3 * share, ROWS),
+        out_shape=(blocks(3 * share, ROWS),) + (blocks(3 * HALO - 2, ROWS),) * 2,
         scratch_shapes=[room(3 * share)],
         compiler_params=limit,
         name="spread",
@@ -739,7 +755,7 @@
         pairs = [(device[i], device[i + 1]) for i in range(first, parts - 1, 2)]
         return lax.ppermute(field, ("gx", "gy", "gz"), pairs + [pair[::-1] for pair in pairs])
 
-    outer, inner = swap(own, 1), swap(own, 0)
+    outer, inner = swap(outer, 1), swap(inner, 0)
     count3 = share // 4
     near1, near2, far1, far2 = (
         (blocks(count, ROWS),) * fields

time: 49.6 us -> 49.6 us (level)
  no operation moved by 1% of the time
where the time goes in v19:
time: 49.6 us; the launch traced here: 49.4 us
  blocking collectives  36.9 us (74%)
  Pallas kernels  5.71 us (12%)
  waiting for transfers between devices  3.98 us (8%)
  starting transfers between devices  1.66 us (3%)
  other arithmetic  0.93 us (2%)
    all_to_all x2, blocking collectives, exchange(): lax.all_to_all(field, axes, 0, 0, axis_index_groups=members, tiled=True)  21.5 us
    all_to_all x1, blocking collectives, whole_planes(): packed = lax.all_to_all(copies, ('gx', 'gy', 'gz'), 0, 0, tiled=True)  15.5 us
    ppermute x2, waiting for transfers between devices, swap(): lax.ppermute(field, ('gx', 'gy', 'gz'), pairs + [pair[::-1] for pair in p...  3.98 us
    pallas_call x1, Pallas kernels, whole_planes(): pl.pallas_call(functools.partial(up_kernel, groups, by, share), out_shape...  2.13 us
    ppermute x2, starting transfers between devices, swap(): lax.ppermute(field, ('gx', 'gy', 'gz'), pairs + [pair[::-1] for pair in p...  1.66 us
    pallas_call x1, Pallas kernels, whole_planes(): pl.pallas_call(functools.partial(down_kernel, share), out_shape=(far1, fa...  1.25 us
  transfers between devices with their start and end apart: 2, of which 1 were waited for; matrix products, arithmetic and copies ran while one was open for 0% of the time, Pallas kernels for 2%

profile of v19, /device:TPU:0, one launch (start us, length us, event | category | flops | bytes accessed | tf_op | source)
XLA Modules:
  0.0 49.4 jit_solution(3660826610041108973)
XLA Ops:
  0.0 0.0 copy-start
  0.0 0.9 %multiply_multiply_fusion = (f32[16,8,128]{2,1,0:T(8,128)S(1)}, f32[16,8,128]{2,1,0:T(8,128)S(1)}) fusion(s32[16,8,128]{2,1,0:T(8,128)} %param.5, f32[16,8,128]{2,1,0:T(8,128)} %param.4), kind=kLoop, calls=%fused_computation | loop fusion | flops 65536 | bytes 262144 | tf_op jit(solution)/shard_map/mul | solution.py:735
  0.9 0.1 copy-done
  1.0 0.4 prepare.1
  1.4 12.8 %all_to_all.15.gathered = f32[8,48,128]{2,1,0:T(8,128)S(1)} all-to-all(f32[8,48,128]{2,1,0:T(8,128)S(1)} %prepare.1), channel_id=1, replica_groups={{28,24,20,16,12,8,4,0},{29,25,21,17,13,9,5,1},{30,26,22,18,14,10,6,2},{..., dimensions={0} | all-to-all | bytes 393216 | tf_op jit(solution)/shard_map/all_to_all | solution.py:347
  14.3 0.3 spread.1
  14.5 1.0 %collective-permute-start.1 = (f32[46,8,128]{2,1,0:T(8,128)S(1)}, f32[46,8,128]{2,1,0:T(8,128)S(1)}, u32[]{:S(2)}, u32[]{:S(2)}) collective-permute-start(f32[46,8,128]{2,1,0:T(8,128)S(1)} %get-tuple-element.50), channel_id=1, source_target_pairs={{0,16},{20,4},{8,24},{28,12},{13,9},{5,1},{17,21},{25,29},{30,14},... | collective-permute-start | bytes 565256 | tf_op jit(solution)/shard_map/ppermute | solution.py:756
  15.5 0.7 %collective-permute-start = (f32[46,8,128]{2,1,0:T(8,128)S(1)}, f32[46,8,128]{2,1,0:T(8,128)S(1)}, u32[]{:S(2)}, u32[]{:S(2)}) collective-permute-start(f32[46,8,128]{2,1,0:T(8,128)S(1)} %get-tuple-element.49), channel_id=1, source_target_pairs={{16,20},{4,8},{24,28},{12,13},{9,5},{1,17},{21,25},{29,30},{14,10}... | collective-permute-start | bytes 565256 | tf_op jit(solution)/shard_map/ppermute | solution.py:756
  16.2 4.0 %collective-permute-done.1.inner = f32[46,8,128]{2,1,0:T(8,128)S(1)} collective-permute-done((f32[46,8,128]{2,1,0:T(8,128)S(1)}, f32[46,8,128]{2,1,0:T(8,128)S(1)}, u32[]{:S(2)}, u32[]{:S(2)}) %collective-permute-start.1) | collective-permute-done | bytes 188448 | tf_op jit(solution)/shard_map/ppermute | solution.py:756
  20.2 0.9 %near.1 = (f32[32,8,128]{2,1,0:T(8,128)S(1)}, f32[32,8,128]{2,1,0:T(8,128)S(1)}, f32[32,8,128]{2,1,0:T(8,128)S(1)}, f32[32,8,128]{2,1,0:T(8,128)S(1)}, f32[32,8,...) custom-call(f32[48,8,128]{2,1,0:T(8,128)S(1)} %get-tuple-element.48., ...), custom_call_target="tpu_custom_call" | custom-call | tf_op jit(solution)/shard_map/near/pallas_call | solution.py:764
  21.1 0.0 collective-permute-done.outer
  21.1 1.2 %down.1 = (f32[24,8,128]{2,1,0:T(8,128)S(1)}, f32[24,8,128]{2,1,0:T(8,128)S(1)}, f32[24,8,128]{2,1,0:T(8,128)S(1)}, f32[24,8,128]{2,1,0:T(8,128)S(1)}, f32[24,8,...) custom-call(f32[48,8,128]{2,1,0:T(8,128)S(1)} %get-tuple-element.48., ...), custom_call_target="tpu_custom_call" | custom-call | tf_op jit(solution)/shard_map/down/pallas_call | solution.py:771
  22.4 15.5 %all_to_all.16.packed = f32[32,5,2,128]{3,2,1,0:T(2,128)S(1)} all-to-all(f32[32,5,2,128]{3,2,1,0:T(2,128)S(1)} %broadcast_in_dim.3), channel_id=1, replica_groups=mesh['gx'=2,'gy'=4,'gz'=4] {'gx','gy','gz'}, dimensions={0} | all-to-all | bytes 327680 | tf_op jit(solution)/shard_map/all_to_all | solution.py:779
  37.9 2.1 %up.1 = f32[8,16,128]{2,1,0:T(8,128)S(1)} custom-call(f32[32,5,2,128]{3,2,1,0:T(2,128)S(1)} %all_to_all.16.packed, f32[32,8,128]{2,1,0:T(8,128)S(1)} %get-tuple-element.64.near1_0_, f32[32,8,128]{2,1,0:T(8,128)S(1)} %get-tuple-element.65.near1_1_, f32[32,8,128]{2,1,0:T(8,128)S(1)} %get-tuple-element.66.near1_2_, ...), custom_call_target="tpu_custom_call" | custom-call | tf_op jit(solution)/shard_map/up/pallas_call | solution.py:781
  40.0 8.6 %all_to_all.17.blocks = f32[8,16,128]{2,1,0:T(8,128)S(1)} all-to-all(f32[8,16,128]{2,1,0:T(8,128)S(1)} %up.1), channel_id=1, replica_groups={{28,24,20,16,12,8,4,0},{29,25,21,17,13,9,5,1},{30,26,22,18,14,10,6,2},{..., dimensions={0} | all-to-all | bytes 131072 | tf_op jit(solution)/shard_map/all_to_all | solution.py:347
  48.7 0.7 %finish.1 = f32[16,8,128]{2,1,0:T(8,128)} custom-call(f32[8,16,128]{2,1,0:T(8,128)S(1)} %all_to_all.17.blocks), custom_call_target="tpu_custom_call" | custom-call | tf_op jit(solution)/shard_map/finish/pallas_call | solution.py:790
  (1 shorter events, 0.0 us)
Async XLA Ops:
  0.0 1.0 %copy-start = (bf16[32,16,256]{2,1,0:T(8,128)(2,1)S(1)}, bf16[32,16,256]{2,1,0:T(8,128)(2,1)}, u32[]{:S(2)}) copy-start(bf16[32,16,256]{2,1,0:T(8,128)(2,1)} %param.3) | copy-start | bytes 786436
  14.5 5.6 %collective-permute-start.1 = (f32[46,8,128]{2,1,0:T(8,128)S(1)}, f32[46,8,128]{2,1,0:T(8,128)S(1)}, u32[]{:S(2)}, u32[]{:S(2)}) collective-permute-start(f32[46,8,128]{2,1,0:T(8,128)S(1)} %get-tuple-element.50), channel_id=1, source_target_pairs={{0,16},{20,4},{8,24},{28,12},{13,9},{5,1},{17,21},{25,29},{30,14},... | collective-permute-start | bytes 565256 | tf_op jit(solution)/shard_map/ppermute | solution.py:756
  15.5 5.6 %collective-permute-start = (f32[46,8,128]{2,1,0:T(8,128)S(1)}, f32[46,8,128]{2,1,0:T(8,128)S(1)}, u32[]{:S(2)}, u32[]{:S(2)}) collective-permute-start(f32[46,8,128]{2,1,0:T(8,128)S(1)} %get-tuple-element.49), channel_id=1, source_target_pairs={{16,20},{4,8},{24,28},{12,13},{9,5},{1,17},{21,25},{29,30},{14,10}... | collective-permute-start | bytes 565256 | tf_op jit(solution)/shard_map/ppermute | solution.py:756

commit v20 on v19

--- a/solution.py
+++ b/solution.py
@@ -312,7 +312,7 @@
     row, column = 0, 0
     for index in range(group + 1):
         columns = list(range(ny)) if column == 0 else list(range(ny))[::-1]
-        if index % 2:
+        if index % 2 == 0:
             path = [(row, at) for at in columns] + [(1 - row, at) for at in columns[::-1]]
         else:
             path = []

time: 49.6 us -> 49.8 us (level)
  starting transfers between devices: 1.66 us -> 2.25 us
    ppermute x2, starting transfers between devices: 1.66 us -> 2.25 us  [swap(): lax.ppermute(field, ('gx', 'gy', 'gz'), pairs + [pair[::-1] for pair in p...]
where the time goes in v20:
time: 49.8 us; the launch traced here: 49.5 us
  blocking collectives  36.5 us (73%)
  Pallas kernels  5.72 us (11%)
  waiting for transfers between devices  3.98 us (8%)
  starting transfers between devices  2.25 us (5%)
  other arithmetic  0.93 us (2%)
    all_to_all x2, blocking collectives, exchange(): lax.all_to_all(field, axes, 0, 0, axis_index_groups=members, tiled=True)  21.5 us
    all_to_all x1, blocking collectives, whole_planes(): packed = lax.all_to_all(copies, ('gx', 'gy', 'gz'), 0, 0, tiled=True)  15 us
    ppermute x2, waiting for transfers between devices, swap(): lax.ppermute(field, ('gx', 'gy', 'gz'), pairs + [pair[::-1] for pair in p...  3.98 us
    ppermute x2, starting transfers between devices, swap(): lax.ppermute(field, ('gx', 'gy', 'gz'), pairs + [pair[::-1] for pair in p...  2.25 us
    pallas_call x1, Pallas kernels, whole_planes(): pl.pallas_call(functools.partial(up_kernel, groups, by, share), out_shape...  2.13 us
    pallas_call x1, Pallas kernels, whole_planes(): pl.pallas_call(functools.partial(down_kernel, share), out_shape=(far1, fa...  1.25 us
  transfers between devices with their start and end apart: 2, of which 1 were waited for; matrix products, arithmetic and copies ran while one was open for 0% of the time, Pallas kernels for 2%

profile of v20, /device:TPU:0, one launch (start us, length us, event | category | flops | bytes accessed | tf_op | source)
XLA Modules:
  0.0 49.5 jit_solution(10784215990431582602)
XLA Ops:
  0.0 0.0 copy-start
  0.0 0.9 %multiply_multiply_fusion = (f32[16,8,128]{2,1,0:T(8,128)S(1)}, f32[16,8,128]{2,1,0:T(8,128)S(1)}) fusion(s32[16,8,128]{2,1,0:T(8,128)} %param.5, f32[16,8,128]{2,1,0:T(8,128)} %param.4), kind=kLoop, calls=%fused_computation | loop fusion | flops 65536 | bytes 262144 | tf_op jit(solution)/shard_map/mul | solution.py:735
  0.9 0.1 copy-done
  1.0 0.4 prepare.1
  1.4 12.8 %all_to_all.15.gathered = f32[8,48,128]{2,1,0:T(8,128)S(1)} all-to-all(f32[8,48,128]{2,1,0:T(8,128)S(1)} %prepare.1), channel_id=1, replica_groups={{28,24,20,16,12,8,4,0},{29,25,21,17,13,9,5,1},{30,26,22,18,14,10,6,2},{..., dimensions={0} | all-to-all | bytes 393216 | tf_op jit(solution)/shard_map/all_to_all | solution.py:347
  14.3 0.3 spread.1
  14.5 1.6 %collective-permute-start.1 = (f32[46,8,128]{2,1,0:T(8,128)S(1)}, f32[46,8,128]{2,1,0:T(8,128)S(1)}, u32[]{:S(2)}, u32[]{:S(2)}) collective-permute-start(f32[46,8,128]{2,1,0:T(8,128)S(1)} %get-tuple-element.50), channel_id=1, source_target_pairs={{0,4},{8,12},{28,24},{20,16},{17,1},{5,21},{25,9},{13,29},{30,26},... | collective-permute-start | bytes 565256 | tf_op jit(solution)/shard_map/ppermute | solution.py:756
  16.1 0.7 %collective-permute-start = (f32[46,8,128]{2,1,0:T(8,128)S(1)}, f32[46,8,128]{2,1,0:T(8,128)S(1)}, u32[]{:S(2)}, u32[]{:S(2)}) collective-permute-start(f32[46,8,128]{2,1,0:T(8,128)S(1)} %get-tuple-element.49), channel_id=1, source_target_pairs={{4,8},{12,28},{24,20},{16,17},{1,5},{21,25},{9,13},{29,30},{26,22}... | collective-permute-start | bytes 565256 | tf_op jit(solution)/shard_map/ppermute | solution.py:756
  16.8 4.0 %collective-permute-done.1.inner = f32[46,8,128]{2,1,0:T(8,128)S(1)} collective-permute-done((f32[46,8,128]{2,1,0:T(8,128)S(1)}, f32[46,8,128]{2,1,0:T(8,128)S(1)}, u32[]{:S(2)}, u32[]{:S(2)}) %collective-permute-start.1) | collective-permute-done | bytes 188448 | tf_op jit(solution)/shard_map/ppermute | solution.py:756
  20.8 0.9 %near.1 = (f32[32,8,128]{2,1,0:T(8,128)S(1)}, f32[32,8,128]{2,1,0:T(8,128)S(1)}, f32[32,8,128]{2,1,0:T(8,128)S(1)}, f32[32,8,128]{2,1,0:T(8,128)S(1)}, f32[32,8,...) custom-call(f32[48,8,128]{2,1,0:T(8,128)S(1)} %get-tuple-element.48., ...), custom_call_target="tpu_custom_call" | custom-call | tf_op jit(solution)/shard_map/near/pallas_call | solution.py:764
  21.7 0.0 collective-permute-done.outer
  21.7 1.2 %down.1 = (f32[24,8,128]{2,1,0:T(8,128)S(1)}, f32[24,8,128]{2,1,0:T(8,128)S(1)}, f32[24,8,128]{2,1,0:T(8,128)S(1)}, f32[24,8,128]{2,1,0:T(8,128)S(1)}, f32[24,8,...) custom-call(f32[48,8,128]{2,1,0:T(8,128)S(1)} %get-tuple-element.48., ...), custom_call_target="tpu_custom_call" | custom-call | tf_op jit(solution)/shard_map/down/pallas_call | solution.py:771
  23.0 15.0 %all_to_all.16.packed = f32[32,5,2,128]{3,2,1,0:T(2,128)S(1)} all-to-all(f32[32,5,2,128]{3,2,1,0:T(2,128)S(1)} %broadcast_in_dim.3), channel_id=1, replica_groups=mesh['gx'=2,'gy'=4,'gz'=4] {'gx','gy','gz'}, dimensions={0} | all-to-all | bytes 327680 | tf_op jit(solution)/shard_map/all_to_all | solution.py:779
  38.0 2.1 %up.1 = f32[8,16,128]{2,1,0:T(8,128)S(1)} custom-call(f32[32,5,2,128]{3,2,1,0:T(2,128)S(1)} %all_to_all.16.packed, f32[32,8,128]{2,1,0:T(8,128)S(1)} %get-tuple-element.64.near1_0_, f32[32,8,128]{2,1,0:T(8,128)S(1)} %get-tuple-element.65.near1_1_, f32[32,8,128]{2,1,0:T(8,128)S(1)} %get-tuple-element.66.near1_2_, ...), custom_call_target="tpu_custom_call" | custom-call | tf_op jit(solution)/shard_map/up/pallas_call | solution.py:781
  40.2 8.6 %all_to_all.17.blocks = f32[8,16,128]{2,1,0:T(8,128)S(1)} all-to-all(f32[8,16,128]{2,1,0:T(8,128)S(1)} %up.1), channel_id=1, replica_groups={{28,24,20,16,12,8,4,0},{29,25,21,17,13,9,5,1},{30,26,22,18,14,10,6,2},{..., dimensions={0} | all-to-all | bytes 131072 | tf_op jit(solution)/shard_map/all_to_all | solution.py:347
  48.8 0.7 %finish.1 = f32[16,8,128]{2,1,0:T(8,128)} custom-call(f32[8,16,128]{2,1,0:T(8,128)S(1)} %all_to_all.17.blocks), custom_call_target="tpu_custom_call" | custom-call | tf_op jit(solution)/shard_map/finish/pallas_call | solution.py:790
  (1 shorter events, 0.0 us)
Async XLA Ops:
  0.0 1.0 %copy-start = (bf16[32,16,256]{2,1,0:T(8,128)(2,1)S(1)}, bf16[32,16,256]{2,1,0:T(8,128)(2,1)}, u32[]{:S(2)}) copy-start(bf16[32,16,256]{2,1,0:T(8,128)(2,1)} %param.3) | copy-start | bytes 786436
  14.5 6.2 %collective-permute-start.1 = (f32[46,8,128]{2,1,0:T(8,128)S(1)}, f32[46,8,128]{2,1,0:T(8,128)S(1)}, u32[]{:S(2)}, u32[]{:S(2)}) collective-permute-start(f32[46,8,128]{2,1,0:T(8,128)S(1)} %get-tuple-element.50), channel_id=1, source_target_pairs={{0,4},{8,12},{28,24},{20,16},{17,1},{5,21},{25,9},{13,29},{30,26},... | collective-permute-start | bytes 565256 | tf_op jit(solution)/shard_map/ppermute | solution.py:756
  16.1 5.6 %collective-permute-start = (f32[46,8,128]{2,1,0:T(8,128)S(1)}, f32[46,8,128]{2,1,0:T(8,128)S(1)}, u32[]{:S(2)}, u32[]{:S(2)}) collective-permute-start(f32[46,8,128]{2,1,0:T(8,128)S(1)} %get-tuple-element.49), channel_id=1, source_target_pairs={{4,8},{12,28},{24,20},{16,17},{1,5},{21,25},{9,13},{29,30},{26,22}... | collective-permute-start | bytes 565256 | tf_op jit(solution)/shard_map/ppermute | solution.py:756

commit v21 on v19

--- a/solution.py
+++ b/solution.py
@@ -222,13 +222,22 @@
     def last_y(self, field):
         return pltpu.roll(field, 1, 2)
 
-    def spread(self, field, scaled, plane, count):
+    def spread(self, source, scaled, plane, shift, count):
+        field = source[pl.ds(plane - 1, count + 2)]
         mid = field[1:-1]
+        rows = source.reshape(source.shape[0] * ROWS, LANES)
+        ahead = rows[pl.ds(plane * ROWS + 1, count * ROWS)].reshape(mid.shape)
+        behind = rows[pl.ds(plane * ROWS - 1, count * ROWS)].reshape(mid.shape)
+        within = (iota(mid.shape, 2) // self.ny) % self.xs
         near = (
-            self.next_x(mid), self.last_x(mid), self.next_y(mid), self.last_y(mid),
-            field[2:], field[:-2],
+            pltpu.roll(jnp.where(within == 0, ahead, mid), LANES - self.ny, 2),
+            pltpu.roll(jnp.where(within == self.xs - 1, behind, mid), self.ny, 2),
+            self.next_y(mid),
+            self.last_y(mid),
+            field[2:],
+            field[:-2],
         )
-        terms = [weight[pl.ds(plane, count)] * value for weight, value in zip(scaled, near)]
+        terms = [weight[pl.ds(plane - shift, count)] * value for weight, value in zip(scaled, near)]
         return mid, ((terms[0] + terms[1]) + (terms[2] + terms[3])) + (terms[4] + terms[5])
 
 
@@ -264,7 +273,7 @@
 
 def swept(level, plane, count, fields, source, shift=0):
     scaled, start, _ = fields
-    mid, total = level.spread(source[pl.ds(plane - 1, count + 2)], scaled, plane - shift, count)
+    mid, total = level.spread(source, scaled, plane, shift, count)
     return (1.0 - OMEGA) * mid + (start[pl.ds(plane - shift, count)] + total)
 
 
@@ -284,7 +293,7 @@
     scaled, start, diag = fields
 
     def body(plane, count):
-        mid, total = level.spread(corr[pl.ds(plane - 1, count + 2)], scaled, plane, count)
+        mid, total = level.spread(corr, scaled, plane, 0, count)
         rest = (start[pl.ds(plane, count)] + total) - OMEGA * mid
         rest = rest * (diag[pl.ds(plane, count)] * (1.0 / OMEGA))
         target[pl.ds((plane - low) // 2, count // 2)] = pair_sum(rest)

time: 49.6 us -> 49.8 us (level)
  no operation moved by 1% of the time
where the time goes in v21:
time: 49.8 us; the launch traced here: 49.6 us
  blocking collectives  36.9 us (74%)
  Pallas kernels  5.94 us (12%)
  waiting for transfers between devices  3.98 us (8%)
  starting transfers between devices  1.66 us (3%)
  other arithmetic  0.93 us (2%)
    all_to_all x2, blocking collectives, exchange(): lax.all_to_all(field, axes, 0, 0, axis_index_groups=members, tiled=True)  21.5 us
    all_to_all x1, blocking collectives, whole_planes(): packed = lax.all_to_all(copies, ('gx', 'gy', 'gz'), 0, 0, tiled=True)  15.5 us
    ppermute x2, waiting for transfers between devices, swap(): lax.ppermute(field, ('gx', 'gy', 'gz'), pairs + [pair[::-1] for pair in p...  3.98 us
    pallas_call x1, Pallas kernels, whole_planes(): pl.pallas_call(functools.partial(up_kernel, groups, by, share), out_shape...  2.23 us
    ppermute x2, starting transfers between devices, swap(): lax.ppermute(field, ('gx', 'gy', 'gz'), pairs + [pair[::-1] for pair in p...  1.66 us
    pallas_call x1, Pallas kernels, whole_planes(): pl.pallas_call(functools.partial(down_kernel, share), out_shape=(far1, fa...  1.35 us
  transfers between devices with their start and end apart: 2, of which 1 were waited for; matrix products, arithmetic and copies ran while one was open for 0% of the time, Pallas kernels for 2%

profile of v21, /device:TPU:0, one launch (start us, length us, event | category | flops | bytes accessed | tf_op | source)
XLA Modules:
  0.0 49.6 jit_solution(13428190783315510338)
XLA Ops:
  0.0 0.0 copy-start
  0.0 0.9 %multiply_multiply_fusion = (f32[16,8,128]{2,1,0:T(8,128)S(1)}, f32[16,8,128]{2,1,0:T(8,128)S(1)}) fusion(s32[16,8,128]{2,1,0:T(8,128)} %param.5, f32[16,8,128]{2,1,0:T(8,128)} %param.4), kind=kLoop, calls=%fused_computation | loop fusion | flops 65536 | bytes 262144 | tf_op jit(solution)/shard_map/mul | solution.py:744
  0.9 0.1 copy-done
  1.0 0.4 prepare.1
  1.4 12.8 %all_to_all.15.gathered = f32[8,48,128]{2,1,0:T(8,128)S(1)} all-to-all(f32[8,48,128]{2,1,0:T(8,128)S(1)} %prepare.1), channel_id=1, replica_groups={{28,24,20,16,12,8,4,0},{29,25,21,17,13,9,5,1},{30,26,22,18,14,10,6,2},{..., dimensions={0} | all-to-all | bytes 393216 | tf_op jit(solution)/shard_map/all_to_all | solution.py:356
  14.3 0.3 spread.1
  14.5 1.0 %collective-permute-start.1 = (f32[46,8,128]{2,1,0:T(8,128)S(1)}, f32[46,8,128]{2,1,0:T(8,128)S(1)}, u32[]{:S(2)}, u32[]{:S(2)}) collective-permute-start(f32[46,8,128]{2,1,0:T(8,128)S(1)} %get-tuple-element.50), channel_id=1, source_target_pairs={{0,16},{20,4},{8,24},{28,12},{13,9},{5,1},{17,21},{25,29},{30,14},... | collective-permute-start | bytes 565256 | tf_op jit(solution)/shard_map/ppermute | solution.py:765
  15.5 0.7 %collective-permute-start = (f32[46,8,128]{2,1,0:T(8,128)S(1)}, f32[46,8,128]{2,1,0:T(8,128)S(1)}, u32[]{:S(2)}, u32[]{:S(2)}) collective-permute-start(f32[46,8,128]{2,1,0:T(8,128)S(1)} %get-tuple-element.49), channel_id=1, source_target_pairs={{16,20},{4,8},{24,28},{12,13},{9,5},{1,17},{21,25},{29,30},{14,10}... | collective-permute-start | bytes 565256 | tf_op jit(solution)/shard_map/ppermute | solution.py:765
  16.2 4.0 %collective-permute-done.1.inner = f32[46,8,128]{2,1,0:T(8,128)S(1)} collective-permute-done((f32[46,8,128]{2,1,0:T(8,128)S(1)}, f32[46,8,128]{2,1,0:T(8,128)S(1)}, u32[]{:S(2)}, u32[]{:S(2)}) %collective-permute-start.1) | collective-permute-done | bytes 188448 | tf_op jit(solution)/shard_map/ppermute | solution.py:765
  20.2 0.9 %near.1 = (f32[32,8,128]{2,1,0:T(8,128)S(1)}, f32[32,8,128]{2,1,0:T(8,128)S(1)}, f32[32,8,128]{2,1,0:T(8,128)S(1)}, f32[32,8,128]{2,1,0:T(8,128)S(1)}, f32[32,8,...) custom-call(f32[48,8,128]{2,1,0:T(8,128)S(1)} %get-tuple-element.48., ...), custom_call_target="tpu_custom_call" | custom-call | tf_op jit(solution)/shard_map/near/pallas_call | solution.py:773
  21.1 0.0 collective-permute-done.outer
  21.1 1.3 %down.1 = (f32[24,8,128]{2,1,0:T(8,128)S(1)}, f32[24,8,128]{2,1,0:T(8,128)S(1)}, f32[24,8,128]{2,1,0:T(8,128)S(1)}, f32[24,8,128]{2,1,0:T(8,128)S(1)}, f32[24,8,...) custom-call(f32[48,8,128]{2,1,0:T(8,128)S(1)} %get-tuple-element.48., ...), custom_call_target="tpu_custom_call" | custom-call | tf_op jit(solution)/shard_map/down/pallas_call | solution.py:780
  22.5 15.5 %all_to_all.16.packed = f32[32,5,2,128]{3,2,1,0:T(2,128)S(1)} all-to-all(f32[32,5,2,128]{3,2,1,0:T(2,128)S(1)} %broadcast_in_dim.3), channel_id=1, replica_groups=mesh['gx'=2,'gy'=4,'gz'=4] {'gx','gy','gz'}, dimensions={0} | all-to-all | bytes 327680 | tf_op jit(solution)/shard_map/all_to_all | solution.py:788
  38.0 2.2 %up.1 = f32[8,16,128]{2,1,0:T(8,128)S(1)} custom-call(f32[32,5,2,128]{3,2,1,0:T(2,128)S(1)} %all_to_all.16.packed, f32[32,8,128]{2,1,0:T(8,128)S(1)} %get-tuple-element.64.near1_0_, f32[32,8,128]{2,1,0:T(8,128)S(1)} %get-tuple-element.65.near1_1_, f32[32,8,128]{2,1,0:T(8,128)S(1)} %get-tuple-element.66.near1_2_, ...), custom_call_target="tpu_custom_call" | custom-call | tf_op jit(solution)/shard_map/up/pallas_call | solution.py:790
  40.2 8.6 %all_to_all.17.blocks = f32[8,16,128]{2,1,0:T(8,128)S(1)} all-to-all(f32[8,16,128]{2,1,0:T(8,128)S(1)} %up.1), channel_id=1, replica_groups={{28,24,20,16,12,8,4,0},{29,25,21,17,13,9,5,1},{30,26,22,18,14,10,6,2},{..., dimensions={0} | all-to-all | bytes 131072 | tf_op jit(solution)/shard_map/all_to_all | solution.py:356
  48.9 0.7 %finish.1 = f32[16,8,128]{2,1,0:T(8,128)} custom-call(f32[8,16,128]{2,1,0:T(8,128)S(1)} %all_to_all.17.blocks), custom_call_target="tpu_custom_call" | custom-call | tf_op jit(solution)/shard_map/finish/pallas_call | solution.py:799
  (1 shorter events, 0.0 us)
Async XLA Ops:
  0.0 1.0 %copy-start = (bf16[32,16,256]{2,1,0:T(8,128)(2,1)S(1)}, bf16[32,16,256]{2,1,0:T(8,128)(2,1)}, u32[]{:S(2)}) copy-start(bf16[32,16,256]{2,1,0:T(8,128)(2,1)} %param.3) | copy-start | bytes 786436
  14.5 5.6 %collective-permute-start.1 = (f32[46,8,128]{2,1,0:T(8,128)S(1)}, f32[46,8,128]{2,1,0:T(8,128)S(1)}, u32[]{:S(2)}, u32[]{:S(2)}) collective-permute-start(f32[46,8,128]{2,1,0:T(8,128)S(1)} %get-tuple-element.50), channel_id=1, source_target_pairs={{0,16},{20,4},{8,24},{28,12},{13,9},{5,1},{17,21},{25,29},{30,14},... | collective-permute-start | bytes 565256 | tf_op jit(solution)/shard_map/ppermute | solution.py:765
  15.5 5.6 %collective-permute-start = (f32[46,8,128]{2,1,0:T(8,128)S(1)}, f32[46,8,128]{2,1,0:T(8,128)S(1)}, u32[]{:S(2)}, u32[]{:S(2)}) collective-permute-start(f32[46,8,128]{2,1,0:T(8,128)S(1)} %get-tuple-element.49), channel_id=1, source_target_pairs={{16,20},{4,8},{24,28},{12,13},{9,5},{1,17},{21,25},{29,30},{14,10}... | collective-permute-start | bytes 565256 | tf_op jit(solution)/shard_map/ppermute | solution.py:765

commit v22 on v19

--- a/solution.py
+++ b/solution.py
@@ -143,7 +143,7 @@
 LANES = 128
 HALO = 16
 NEAR = 8
-PIECE = 8
+PIECE = 4
 TINY = 1e-30
 F32 = jnp.float32
 

time: 49.6 us -> 49.7 us (level)
  no operation moved by 1% of the time
where the time goes in v22:
time: 49.7 us; the launch traced here: 49.4 us
  blocking collectives  36.8 us (74%)
  Pallas kernels  5.86 us (12%)
  waiting for transfers between devices  3.98 us (8%)
  starting transfers between devices  1.66 us (3%)
  other arithmetic  0.93 us (2%)
    all_to_all x2, blocking collectives, exchange(): lax.all_to_all(field, axes, 0, 0, axis_index_groups=members, tiled=True)  21.5 us
    all_to_all x1, blocking collectives, whole_planes(): packed = lax.all_to_all(copies, ('gx', 'gy', 'gz'), 0, 0, tiled=True)  15.4 us
    ppermute x2, waiting for transfers between devices, swap(): lax.ppermute(field, ('gx', 'gy', 'gz'), pairs + [pair[::-1] for pair in p...  3.98 us
    pallas_call x1, Pallas kernels, whole_planes(): pl.pallas_call(functools.partial(up_kernel, groups, by, share), out_shape...  2.13 us
    ppermute x2, starting transfers between devices, swap(): lax.ppermute(field, ('gx', 'gy', 'gz'), pairs + [pair[::-1] for pair in p...  1.66 us
    pallas_call x1, Pallas kernels, whole_planes(): pl.pallas_call(functools.partial(down_kernel, share), out_shape=(far1, fa...  1.24 us
    pallas_call x1, Pallas kernels, whole_planes(): pl.pallas_call(functools.partial(near_kernel, share), out_shape=(near1, n...  1.07 us
  transfers between devices with their start and end apart: 2, of which 1 were waited for; matrix products, arithmetic and copies ran while one was open for 0% of the time, Pallas kernels for 2%

profile of v22, /device:TPU:0, one launch (start us, length us, event | category | flops | bytes accessed | tf_op | source)
XLA Modules:
  0.0 49.4 jit_solution(14184755647317380991)
XLA Ops:
  0.0 0.0 copy-start
  0.0 0.9 %multiply_multiply_fusion = (f32[16,8,128]{2,1,0:T(8,128)S(1)}, f32[16,8,128]{2,1,0:T(8,128)S(1)}) fusion(s32[16,8,128]{2,1,0:T(8,128)} %param.5, f32[16,8,128]{2,1,0:T(8,128)} %param.4), kind=kLoop, calls=%fused_computation | loop fusion | flops 65536 | bytes 262144 | tf_op jit(solution)/shard_map/mul | solution.py:735
  0.9 0.1 copy-done
  1.0 0.4 prepare.1
  1.4 12.8 %all_to_all.15.gathered = f32[8,48,128]{2,1,0:T(8,128)S(1)} all-to-all(f32[8,48,128]{2,1,0:T(8,128)S(1)} %prepare.1), channel_id=1, replica_groups={{28,24,20,16,12,8,4,0},{29,25,21,17,13,9,5,1},{30,26,22,18,14,10,6,2},{..., dimensions={0} | all-to-all | bytes 393216 | tf_op jit(solution)/shard_map/all_to_all | solution.py:347
  14.3 0.3 spread.1
  14.5 1.0 %collective-permute-start.1 = (f32[46,8,128]{2,1,0:T(8,128)S(1)}, f32[46,8,128]{2,1,0:T(8,128)S(1)}, u32[]{:S(2)}, u32[]{:S(2)}) collective-permute-start(f32[46,8,128]{2,1,0:T(8,128)S(1)} %get-tuple-element.50), channel_id=1, source_target_pairs={{0,16},{20,4},{8,24},{28,12},{13,9},{5,1},{17,21},{25,29},{30,14},... | collective-permute-start | bytes 565256 | tf_op jit(solution)/shard_map/ppermute | solution.py:756
  15.5 0.7 %collective-permute-start = (f32[46,8,128]{2,1,0:T(8,128)S(1)}, f32[46,8,128]{2,1,0:T(8,128)S(1)}, u32[]{:S(2)}, u32[]{:S(2)}) collective-permute-start(f32[46,8,128]{2,1,0:T(8,128)S(1)} %get-tuple-element.49), channel_id=1, source_target_pairs={{16,20},{4,8},{24,28},{12,13},{9,5},{1,17},{21,25},{29,30},{14,10}... | collective-permute-start | bytes 565256 | tf_op jit(solution)/shard_map/ppermute | solution.py:756
  16.2 4.0 %collective-permute-done.1.inner = f32[46,8,128]{2,1,0:T(8,128)S(1)} collective-permute-done((f32[46,8,128]{2,1,0:T(8,128)S(1)}, f32[46,8,128]{2,1,0:T(8,128)S(1)}, u32[]{:S(2)}, u32[]{:S(2)}) %collective-permute-start.1) | collective-permute-done | bytes 188448 | tf_op jit(solution)/shard_map/ppermute | solution.py:756
  20.2 1.1 %near.1 = (f32[32,8,128]{2,1,0:T(8,128)S(1)}, f32[32,8,128]{2,1,0:T(8,128)S(1)}, f32[32,8,128]{2,1,0:T(8,128)S(1)}, f32[32,8,128]{2,1,0:T(8,128)S(1)}, f32[32,8,...) custom-call(f32[48,8,128]{2,1,0:T(8,128)S(1)} %get-tuple-element.48., ...), custom_call_target="tpu_custom_call" | custom-call | tf_op jit(solution)/shard_map/near/pallas_call | solution.py:764
  21.3 0.0 collective-permute-done.outer
  21.3 1.2 %down.1 = (f32[24,8,128]{2,1,0:T(8,128)S(1)}, f32[24,8,128]{2,1,0:T(8,128)S(1)}, f32[24,8,128]{2,1,0:T(8,128)S(1)}, f32[24,8,128]{2,1,0:T(8,128)S(1)}, f32[24,8,...) custom-call(f32[48,8,128]{2,1,0:T(8,128)S(1)} %get-tuple-element.48., ...), custom_call_target="tpu_custom_call" | custom-call | tf_op jit(solution)/shard_map/down/pallas_call | solution.py:771
  22.6 15.4 %all_to_all.16.packed = f32[32,5,2,128]{3,2,1,0:T(2,128)S(1)} all-to-all(f32[32,5,2,128]{3,2,1,0:T(2,128)S(1)} %broadcast_in_dim.3), channel_id=1, replica_groups=mesh['gx'=2,'gy'=4,'gz'=4] {'gx','gy','gz'}, dimensions={0} | all-to-all | bytes 327680 | tf_op jit(solution)/shard_map/all_to_all | solution.py:779
  37.9 2.1 %up.1 = f32[8,16,128]{2,1,0:T(8,128)S(1)} custom-call(f32[32,5,2,128]{3,2,1,0:T(2,128)S(1)} %all_to_all.16.packed, f32[32,8,128]{2,1,0:T(8,128)S(1)} %get-tuple-element.64.near1_0_, f32[32,8,128]{2,1,0:T(8,128)S(1)} %get-tuple-element.65.near1_1_, f32[32,8,128]{2,1,0:T(8,128)S(1)} %get-tuple-element.66.near1_2_, ...), custom_call_target="tpu_custom_call" | custom-call | tf_op jit(solution)/shard_map/up/pallas_call | solution.py:781
  40.1 8.6 %all_to_all.17.blocks = f32[8,16,128]{2,1,0:T(8,128)S(1)} all-to-all(f32[8,16,128]{2,1,0:T(8,128)S(1)} %up.1), channel_id=1, replica_groups={{28,24,20,16,12,8,4,0},{29,25,21,17,13,9,5,1},{30,26,22,18,14,10,6,2},{..., dimensions={0} | all-to-all | bytes 131072 | tf_op jit(solution)/shard_map/all_to_all | solution.py:347
  48.7 0.7 %finish.1 = f32[16,8,128]{2,1,0:T(8,128)} custom-call(f32[8,16,128]{2,1,0:T(8,128)S(1)} %all_to_all.17.blocks), custom_call_target="tpu_custom_call" | custom-call | tf_op jit(solution)/shard_map/finish/pallas_call | solution.py:790
  (1 shorter events, 0.0 us)
Async XLA Ops:
  0.0 1.0 %copy-start = (bf16[32,16,256]{2,1,0:T(8,128)(2,1)S(1)}, bf16[32,16,256]{2,1,0:T(8,128)(2,1)}, u32[]{:S(2)}) copy-start(bf16[32,16,256]{2,1,0:T(8,128)(2,1)} %param.3) | copy-start | bytes 786436
  14.5 5.6 %collective-permute-start.1 = (f32[46,8,128]{2,1,0:T(8,128)S(1)}, f32[46,8,128]{2,1,0:T(8,128)S(1)}, u32[]{:S(2)}, u32[]{:S(2)}) collective-permute-start(f32[46,8,128]{2,1,0:T(8,128)S(1)} %get-tuple-element.50), channel_id=1, source_target_pairs={{0,16},{20,4},{8,24},{28,12},{13,9},{5,1},{17,21},{25,29},{30,14},... | collective-permute-start | bytes 565256 | tf_op jit(solution)/shard_map/ppermute | solution.py:756
  15.5 5.7 %collective-permute-start = (f32[46,8,128]{2,1,0:T(8,128)S(1)}, f32[46,8,128]{2,1,0:T(8,128)S(1)}, u32[]{:S(2)}, u32[]{:S(2)}) collective-permute-start(f32[46,8,128]{2,1,0:T(8,128)S(1)} %get-tuple-element.49), channel_id=1, source_target_pairs={{16,20},{4,8},{24,28},{12,13},{9,5},{1,17},{21,25},{29,30},{14,10}... | collective-permute-start | bytes 565256 | tf_op jit(solution)/shard_map/ppermute | solution.py:756

commit v23 on v19

--- a/solution.py
+++ b/solution.py
@@ -331,7 +331,8 @@
 
 
 def slot_of(peer):
-    return SPLIT[0] * SPLIT[1] - 1 - peer
+    nx, ny = SPLIT
+    return nx * ny - 1 - (peer % ny * nx + peer // ny)
 
 
 def own_slot_of(rank):

time: 49.6 us -> 49.3 us (level)
  waiting for transfers between devices: 3.98 us -> 6.14 us
  blocking collectives: 36.9 us -> 35.1 us
  starting transfers between devices: 1.66 us -> 1.04 us
    all_to_all x1, blocking collectives: 15.5 us -> 12.5 us  [whole_planes(): packed = lax.all_to_all(copies, ('gx', 'gy', 'gz'), 0, 0, tiled=True)]
    ppermute x2, waiting for transfers between devices: 3.98 us -> 6.14 us  [swap(): lax.ppermute(field, ('gx', 'gy', 'gz'), pairs + [pair[::-1] for pair in p...]
    all_to_all x2, blocking collectives: 21.5 us -> 22.6 us  [exchange(): lax.all_to_all(field, axes, 0, 0, axis_index_groups=members, tiled=True)]
    ppermute x2, starting transfers between devices: 1.66 us -> 1.04 us  [swap(): lax.ppermute(field, ('gx', 'gy', 'gz'), pairs + [pair[::-1] for pair in p...]
where the time goes in v23:
time: 49.3 us; the launch traced here: 49.1 us
  blocking collectives  35.1 us (71%)
  waiting for transfers between devices  6.14 us (12%)
  Pallas kernels  5.71 us (12%)
  starting transfers between devices  1.04 us (2%)
  other arithmetic  0.93 us (2%)
    all_to_all x2, blocking collectives, exchange(): lax.all_to_all(field, axes, 0, 0, axis_index_groups=members, tiled=True)  22.6 us
    all_to_all x1, blocking collectives, whole_planes(): packed = lax.all_to_all(copies, ('gx', 'gy', 'gz'), 0, 0, tiled=True)  12.5 us
    ppermute x2, waiting for transfers between devices, swap(): lax.ppermute(field, ('gx', 'gy', 'gz'), pairs + [pair[::-1] for pair in p...  6.14 us
    pallas_call x1, Pallas kernels, whole_planes(): pl.pallas_call(functools.partial(up_kernel, groups, by, share), out_shape...  2.13 us
    pallas_call x1, Pallas kernels, whole_planes(): pl.pallas_call(functools.partial(down_kernel, share), out_shape=(far1, fa...  1.25 us
    ppermute x2, starting transfers between devices, swap(): lax.ppermute(field, ('gx', 'gy', 'gz'), pairs + [pair[::-1] for pair in p...  1.04 us
  transfers between devices with their start and end apart: 2, of which 1 were waited for; matrix products, arithmetic and copies ran while one was open for 0% of the time, Pallas kernels for 2%

profile of v23, /device:TPU:0, one launch (start us, length us, event | category | flops | bytes accessed | tf_op | source)
XLA Modules:
  0.0 49.1 jit_solution(18125196402735124380)
XLA Ops:
  0.0 0.0 copy-start
  0.0 0.9 %multiply_multiply_fusion = (f32[16,8,128]{2,1,0:T(8,128)S(1)}, f32[16,8,128]{2,1,0:T(8,128)S(1)}) fusion(s32[16,8,128]{2,1,0:T(8,128)} %param.5, f32[16,8,128]{2,1,0:T(8,128)} %param.4), kind=kLoop, calls=%fused_computation | loop fusion | flops 65536 | bytes 262144 | tf_op jit(solution)/shard_map/mul | solution.py:736
  0.9 0.1 copy-done
  1.0 0.4 prepare.1
  1.4 13.8 %all_to_all.15.gathered = f32[8,48,128]{2,1,0:T(8,128)S(1)} all-to-all(f32[8,48,128]{2,1,0:T(8,128)S(1)} %prepare.1), channel_id=1, replica_groups={{28,12,24,8,20,4,16,0},{29,13,25,9,21,5,17,1},{30,14,26,10,22,6,18,2},{..., dimensions={0} | all-to-all | bytes 393216 | tf_op jit(solution)/shard_map/all_to_all | solution.py:348
  15.2 0.3 spread.1
  15.5 0.4 collective-permute-start.1
  15.9 0.7 %collective-permute-start = (f32[46,8,128]{2,1,0:T(8,128)S(1)}, f32[46,8,128]{2,1,0:T(8,128)S(1)}, u32[]{:S(2)}, u32[]{:S(2)}) collective-permute-start(f32[46,8,128]{2,1,0:T(8,128)S(1)} %get-tuple-element.49), channel_id=1, source_target_pairs={{16,20},{4,8},{24,28},{12,13},{9,5},{1,17},{21,25},{29,30},{14,10}... | collective-permute-start | bytes 565256 | tf_op jit(solution)/shard_map/ppermute | solution.py:757
  16.5 6.1 %collective-permute-done.1.inner = f32[46,8,128]{2,1,0:T(8,128)S(1)} collective-permute-done((f32[46,8,128]{2,1,0:T(8,128)S(1)}, f32[46,8,128]{2,1,0:T(8,128)S(1)}, u32[]{:S(2)}, u32[]{:S(2)}) %collective-permute-start.1) | collective-permute-done | bytes 188448 | tf_op jit(solution)/shard_map/ppermute | solution.py:757
  22.7 0.9 %near.1 = (f32[32,8,128]{2,1,0:T(8,128)S(1)}, f32[32,8,128]{2,1,0:T(8,128)S(1)}, f32[32,8,128]{2,1,0:T(8,128)S(1)}, f32[32,8,128]{2,1,0:T(8,128)S(1)}, f32[32,8,...) custom-call(f32[48,8,128]{2,1,0:T(8,128)S(1)} %get-tuple-element.48., ...), custom_call_target="tpu_custom_call" | custom-call | tf_op jit(solution)/shard_map/near/pallas_call | solution.py:765
  23.6 0.0 collective-permute-done.outer
  23.6 1.2 %down.1 = (f32[24,8,128]{2,1,0:T(8,128)S(1)}, f32[24,8,128]{2,1,0:T(8,128)S(1)}, f32[24,8,128]{2,1,0:T(8,128)S(1)}, f32[24,8,128]{2,1,0:T(8,128)S(1)}, f32[24,8,...) custom-call(f32[48,8,128]{2,1,0:T(8,128)S(1)} %get-tuple-element.48., ...), custom_call_target="tpu_custom_call" | custom-call | tf_op jit(solution)/shard_map/down/pallas_call | solution.py:772
  24.9 12.5 %all_to_all.16.packed = f32[32,5,2,128]{3,2,1,0:T(2,128)S(1)} all-to-all(f32[32,5,2,128]{3,2,1,0:T(2,128)S(1)} %broadcast_in_dim.3), channel_id=1, replica_groups=mesh['gx'=2,'gy'=4,'gz'=4] {'gx','gy','gz'}, dimensions={0} | all-to-all | bytes 327680 | tf_op jit(solution)/shard_map/all_to_all | solution.py:780
  37.4 2.1 %up.1 = f32[8,16,128]{2,1,0:T(8,128)S(1)} custom-call(f32[32,5,2,128]{3,2,1,0:T(2,128)S(1)} %all_to_all.16.packed, f32[32,8,128]{2,1,0:T(8,128)S(1)} %get-tuple-element.64.near1_0_, f32[32,8,128]{2,1,0:T(8,128)S(1)} %get-tuple-element.65.near1_1_, f32[32,8,128]{2,1,0:T(8,128)S(1)} %get-tuple-element.66.near1_2_, ...), custom_call_target="tpu_custom_call" | custom-call | tf_op jit(solution)/shard_map/up/pallas_call | solution.py:782
  39.5 8.8 %all_to_all.17.blocks = f32[8,16,128]{2,1,0:T(8,128)S(1)} all-to-all(f32[8,16,128]{2,1,0:T(8,128)S(1)} %up.1), channel_id=1, replica_groups={{28,12,24,8,20,4,16,0},{29,13,25,9,21,5,17,1},{30,14,26,10,22,6,18,2},{..., dimensions={0} | all-to-all | bytes 131072 | tf_op jit(solution)/shard_map/all_to_all | solution.py:348
  48.4 0.7 %finish.1 = f32[16,8,128]{2,1,0:T(8,128)} custom-call(f32[8,16,128]{2,1,0:T(8,128)S(1)} %all_to_all.17.blocks), custom_call_target="tpu_custom_call" | custom-call | tf_op jit(solution)/shard_map/finish/pallas_call | solution.py:791
  (1 shorter events, 0.0 us)
Async XLA Ops:
  0.0 1.0 %copy-start = (bf16[32,16,256]{2,1,0:T(8,128)(2,1)S(1)}, bf16[32,16,256]{2,1,0:T(8,128)(2,1)}, u32[]{:S(2)}) copy-start(bf16[32,16,256]{2,1,0:T(8,128)(2,1)} %param.3) | copy-start | bytes 786436
  15.5 7.2 %collective-permute-start.1 = (f32[46,8,128]{2,1,0:T(8,128)S(1)}, f32[46,8,128]{2,1,0:T(8,128)S(1)}, u32[]{:S(2)}, u32[]{:S(2)}) collective-permute-start(f32[46,8,128]{2,1,0:T(8,128)S(1)} %get-tuple-element.50), channel_id=1, source_target_pairs={{0,16},{20,4},{8,24},{28,12},{13,9},{5,1},{17,21},{25,29},{30,14},... | collective-permute-start | bytes 565256 | tf_op jit(solution)/shard_map/ppermute | solution.py:757
  15.9 7.7 %collective-permute-start = (f32[46,8,128]{2,1,0:T(8,128)S(1)}, f32[46,8,128]{2,1,0:T(8,128)S(1)}, u32[]{:S(2)}, u32[]{:S(2)}) collective-permute-start(f32[46,8,128]{2,1,0:T(8,128)S(1)} %get-tuple-element.49), channel_id=1, source_target_pairs={{16,20},{4,8},{24,28},{12,13},{9,5},{1,17},{21,25},{29,30},{14,10}... | collective-permute-start | bytes 565256 | tf_op jit(solution)/shard_map/ppermute | solution.py:757

commit v24 on v23

--- a/solution.py
+++ b/solution.py
@@ -360,6 +360,20 @@
     groups = lax.axis_size("gz")
     device = (lax.axis_index("gx") * ny + lax.axis_index("gy")) * groups + lax.axis_index("gz")
     return lookup(slabs_of(groups), device)
+
+
+def slots_of(groups):
+    peers = SPLIT[0] * SPLIT[1]
+    return [
+        slot_of(peer) * groups + groups - 1 - group for group in range(groups) for peer in path_of(group)
+    ]
+
+
+def exchange_all(field):
+    groups = lax.axis_size("gz")
+    members = [device for _, device in sorted(zip(slots_of(groups), devices_of(groups)))]
+    axes = ("gx", "gy", "gz")
+    return lax.all_to_all(field, axes, 0, 0, axis_index_groups=[members], tiled=True)
 
 
 def devices_of(groups):
@@ -594,8 +608,8 @@
     count3 = depth // 4
     shares = packed.shape[0]
     peers = SPLIT[0] * SPLIT[1]
-    devices = devices_of(shares // peers)
-    for slab, index in enumerate(devices):
+    slots = slots_of(shares // peers)
+    for slab, index in enumerate(slots):
         row = slab * count3
         first[row : row + 2] = packed[index, 0]
         first[row + 2 : row + 4] = packed[index, 1]
@@ -645,7 +659,7 @@
     row = iota((ROWS, LANES), 0)
 
     def unpacked(index, which):
-        pair = packed[lookup(devices, jnp.clip(index, 0, shares - 1)), which]
+        pair = packed[lookup(slots, jnp.clip(index, 0, shares - 1)), which]
         total = None
         for shift in range(4):
             moved = pltpu.roll(pair, shift * (LANES // 4), 1)
@@ -777,7 +791,7 @@
         name="down",
     )(own, outer, near2, fluid2, pin2, fluid3, pin3)
     copies = jnp.broadcast_to(parcel, (parts,) + parcel.shape)
-    packed = lax.all_to_all(copies, ("gx", "gy", "gz"), 0, 0, tiled=True)
+    packed = exchange_all(copies)
     depth3 = parts * count3
     mine = pl.pallas_call(
         functools.partial(up_kernel, groups, by, share),

time: 49.3 us -> 48.9 us (level)
  no operation moved by 1% of the time
where the time goes in v24:
time: 48.9 us; the launch traced here: 48.7 us
  blocking collectives  34.7 us (71%)
  waiting for transfers between devices  6.14 us (13%)
  Pallas kernels  5.71 us (12%)
  starting transfers between devices  1.04 us (2%)
  other arithmetic  0.93 us (2%)
    all_to_all x2, blocking collectives, exchange(): lax.all_to_all(field, axes, 0, 0, axis_index_groups=members, tiled=True)  22.6 us
    all_to_all x1, blocking collectives, exchange_all(): lax.all_to_all(field, axes, 0, 0, axis_index_groups=[members], tiled=True)  12.1 us
    ppermute x2, waiting for transfers between devices, swap(): lax.ppermute(field, ('gx', 'gy', 'gz'), pairs + [pair[::-1] for pair in p...  6.14 us
    pallas_call x1, Pallas kernels, whole_planes(): pl.pallas_call(functools.partial(up_kernel, groups, by, share), out_shape...  2.13 us
    pallas_call x1, Pallas kernels, whole_planes(): pl.pallas_call(functools.partial(down_kernel, share), out_shape=(far1, fa...  1.25 us
    ppermute x2, starting transfers between devices, swap(): lax.ppermute(field, ('gx', 'gy', 'gz'), pairs + [pair[::-1] for pair in p...  1.04 us
  transfers between devices with their start and end apart: 2, of which 1 were waited for; matrix products, arithmetic and copies ran while one was open for 0% of the time, Pallas kernels for 2%

profile of v24, /device:TPU:0, one launch (start us, length us, event | category | flops | bytes accessed | tf_op | source)
XLA Modules:
  0.0 48.7 jit_solution(16064112224931360293)
XLA Ops:
  0.0 0.0 copy-start
  0.0 0.9 %multiply_multiply_fusion = (f32[16,8,128]{2,1,0:T(8,128)S(1)}, f32[16,8,128]{2,1,0:T(8,128)S(1)}) fusion(s32[16,8,128]{2,1,0:T(8,128)} %param.5, f32[16,8,128]{2,1,0:T(8,128)} %param.4), kind=kLoop, calls=%fused_computation | loop fusion | flops 65536 | bytes 262144 | tf_op jit(solution)/shard_map/mul | solution.py:750
  0.9 0.1 copy-done
  1.0 0.4 prepare.1
  1.4 13.8 %all_to_all.15.gathered = f32[8,48,128]{2,1,0:T(8,128)S(1)} all-to-all(f32[8,48,128]{2,1,0:T(8,128)S(1)} %prepare.1), channel_id=1, replica_groups={{28,12,24,8,20,4,16,0},{29,13,25,9,21,5,17,1},{30,14,26,10,22,6,18,2},{..., dimensions={0} | all-to-all | bytes 393216 | tf_op jit(solution)/shard_map/all_to_all | solution.py:348
  15.2 0.3 spread.1
  15.5 0.4 collective-permute-start.1
  15.9 0.7 %collective-permute-start = (f32[46,8,128]{2,1,0:T(8,128)S(1)}, f32[46,8,128]{2,1,0:T(8,128)S(1)}, u32[]{:S(2)}, u32[]{:S(2)}) collective-permute-start(f32[46,8,128]{2,1,0:T(8,128)S(1)} %get-tuple-element.49), channel_id=1, source_target_pairs={{16,20},{4,8},{24,28},{12,13},{9,5},{1,17},{21,25},{29,30},{14,10}... | collective-permute-start | bytes 565256 | tf_op jit(solution)/shard_map/ppermute | solution.py:771
  16.5 6.1 %collective-permute-done.1.inner = f32[46,8,128]{2,1,0:T(8,128)S(1)} collective-permute-done((f32[46,8,128]{2,1,0:T(8,128)S(1)}, f32[46,8,128]{2,1,0:T(8,128)S(1)}, u32[]{:S(2)}, u32[]{:S(2)}) %collective-permute-start.1) | collective-permute-done | bytes 188448 | tf_op jit(solution)/shard_map/ppermute | solution.py:771
  22.7 0.9 %near.1 = (f32[32,8,128]{2,1,0:T(8,128)S(1)}, f32[32,8,128]{2,1,0:T(8,128)S(1)}, f32[32,8,128]{2,1,0:T(8,128)S(1)}, f32[32,8,128]{2,1,0:T(8,128)S(1)}, f32[32,8,...) custom-call(f32[48,8,128]{2,1,0:T(8,128)S(1)} %get-tuple-element.48., ...), custom_call_target="tpu_custom_call" | custom-call | tf_op jit(solution)/shard_map/near/pallas_call | solution.py:779
  23.6 0.0 collective-permute-done.outer
  23.6 1.2 %down.1 = (f32[24,8,128]{2,1,0:T(8,128)S(1)}, f32[24,8,128]{2,1,0:T(8,128)S(1)}, f32[24,8,128]{2,1,0:T(8,128)S(1)}, f32[24,8,128]{2,1,0:T(8,128)S(1)}, f32[24,8,...) custom-call(f32[48,8,128]{2,1,0:T(8,128)S(1)} %get-tuple-element.48., ...), custom_call_target="tpu_custom_call" | custom-call | tf_op jit(solution)/shard_map/down/pallas_call | solution.py:786
  24.9 12.1 %all_to_all.16.packed = f32[32,5,2,128]{3,2,1,0:T(2,128)S(1)} all-to-all(f32[32,5,2,128]{3,2,1,0:T(2,128)S(1)} %broadcast_in_dim.3), channel_id=1, replica_groups={{31,30,29,28,15,14,13,12,27,26,25,24,11,10,9,8,23,22,21,20,7,6,5,4,19,1..., dimensions={0} | all-to-all | bytes 327680 | tf_op jit(solution)/shard_map/all_to_all | solution.py:376
  37.0 2.1 %up.1 = f32[8,16,128]{2,1,0:T(8,128)S(1)} custom-call(f32[32,5,2,128]{3,2,1,0:T(2,128)S(1)} %all_to_all.16.packed, f32[32,8,128]{2,1,0:T(8,128)S(1)} %get-tuple-element.64.near1_0_, f32[32,8,128]{2,1,0:T(8,128)S(1)} %get-tuple-element.65.near1_1_, f32[32,8,128]{2,1,0:T(8,128)S(1)} %get-tuple-element.66.near1_2_, ...), custom_call_target="tpu_custom_call" | custom-call | tf_op jit(solution)/shard_map/up/pallas_call | solution.py:796
  39.1 8.8 %all_to_all.17.blocks = f32[8,16,128]{2,1,0:T(8,128)S(1)} all-to-all(f32[8,16,128]{2,1,0:T(8,128)S(1)} %up.1), channel_id=1, replica_groups={{28,12,24,8,20,4,16,0},{29,13,25,9,21,5,17,1},{30,14,26,10,22,6,18,2},{..., dimensions={0} | all-to-all | bytes 131072 | tf_op jit(solution)/shard_map/all_to_all | solution.py:348
  48.0 0.7 %finish.1 = f32[16,8,128]{2,1,0:T(8,128)} custom-call(f32[8,16,128]{2,1,0:T(8,128)S(1)} %all_to_all.17.blocks), custom_call_target="tpu_custom_call" | custom-call | tf_op jit(solution)/shard_map/finish/pallas_call | solution.py:805
  (1 shorter events, 0.0 us)
Async XLA Ops:
  0.0 1.0 %copy-start = (bf16[32,16,256]{2,1,0:T(8,128)(2,1)S(1)}, bf16[32,16,256]{2,1,0:T(8,128)(2,1)}, u32[]{:S(2)}) copy-start(bf16[32,16,256]{2,1,0:T(8,128)(2,1)} %param.3) | copy-start | bytes 786436
  15.5 7.2 %collective-permute-start.1 = (f32[46,8,128]{2,1,0:T(8,128)S(1)}, f32[46,8,128]{2,1,0:T(8,128)S(1)}, u32[]{:S(2)}, u32[]{:S(2)}) collective-permute-start(f32[46,8,128]{2,1,0:T(8,128)S(1)} %get-tuple-element.50), channel_id=1, source_target_pairs={{0,16},{20,4},{8,24},{28,12},{13,9},{5,1},{17,21},{25,29},{30,14},... | collective-permute-start | bytes 565256 | tf_op jit(solution)/shard_map/ppermute | solution.py:771
  15.9 7.7 %collective-permute-start = (f32[46,8,128]{2,1,0:T(8,128)S(1)}, f32[46,8,128]{2,1,0:T(8,128)S(1)}, u32[]{:S(2)}, u32[]{:S(2)}) collective-permute-start(f32[46,8,128]{2,1,0:T(8,128)S(1)} %get-tuple-element.49), channel_id=1, source_target_pairs={{16,20},{4,8},{24,28},{12,13},{9,5},{1,17},{21,25},{29,30},{14,10}... | collective-permute-start | bytes 565256 | tf_op jit(solution)/shard_map/ppermute | solution.py:771

commit v25 on v24

--- a/solution.py
+++ b/solution.py
@@ -152,6 +152,14 @@
     return lax.broadcasted_iota(jnp.int32, shape, dim)
 
 
+def quotient(index, count):
+    return index >> (count.bit_length() - 1)
+
+
+def remainder(index, count):
+    return index & (count - 1)
+
+
 def dot01(field, chosen):
     total = None
     rest = field
@@ -198,23 +206,27 @@
         self.xs = 4 >> level
         self.factor = float(2**level)
 
-    def masks(self, shape):
-        lane = iota(shape, 2)
-        row = iota(shape, 1)
-        within = (lane // self.ny) % self.xs
-        y = lane % self.ny
-        last_x = (row == ROWS - 1) & (within == self.xs - 1)
-        return within, y == self.ny - 1, last_x
+    def within(self, shape):
+        lane = iota((1,) + shape[1:], 2)
+        return jnp.broadcast_to(remainder(quotient(lane, self.ny), self.xs), shape)
+
+    def ends(self, shape):
+        one = (1,) + shape[1:]
+        lane = iota(one, 2)
+        last_x = (iota(one, 1) == ROWS - 1) & (remainder(quotient(lane, self.ny), self.xs) == self.xs - 1)
+        last_y = remainder(lane, self.ny) == self.ny - 1
+        code = jnp.where(last_y, 1, 0) + jnp.where(last_x, 2, 0)
+        code = jnp.broadcast_to(code, shape)
+        return (code & 1) == 1, code >= 2
 
     def next_x(self, field):
-        within = (iota(field.shape, 2) // self.ny) % self.xs
         moved = pltpu.roll(field, LANES - self.ny, 2)
-        return jnp.where(within == self.xs - 1, pltpu.roll(moved, ROWS - 1, 1), moved)
+        wrapped = self.within(field.shape) == self.xs - 1
+        return jnp.where(wrapped, pltpu.roll(moved, ROWS - 1, 1), moved)
 
     def last_x(self, field):
-        within = (iota(field.shape, 2) // self.ny) % self.xs
         moved = pltpu.roll(field, self.ny, 2)
-        return jnp.where(within == 0, pltpu.roll(moved, 1, 1), moved)
+        return jnp.where(self.within(field.shape) == 0, pltpu.roll(moved, 1, 1), moved)
 
     def next_y(self, field):
         return pltpu.roll(field, LANES - 1, 2)
@@ -242,7 +254,7 @@
     def body(plane, count):
         wide = fluid[pl.ds(plane - 1, count + 2)]
         mid = wide[1:-1]
-        within, end_y, end_x = level.masks(mid.shape)
+        end_y, end_x = level.ends(mid.shape)
         to_x = jnp.where(end_x, 0.0, mean_of(mid, level.next_x(mid), level.factor))
         to_y = jnp.where(end_y, 0.0, mean_of(mid, level.next_y(mid), level.factor))
         to_z = mean_of(wide[:-1], wide[1:], level.factor)
@@ -297,8 +309,9 @@
     coarse = iota((LANES, LANES), 1)
     ny, xs = PLANE[1] >> level, 4 >> level
     half = xs // 2
-    same_x = ((fine // ny) % xs) // 2 == (coarse // (ny // 2)) % half
-    same_y = (fine % ny) // 2 == coarse % (ny // 2)
+    fine_x, coarse_x = remainder(quotient(fine, ny), xs), quotient(coarse, ny // 2)
+    same_x = quotient(fine_x, 2) == remainder(coarse_x, half)
+    same_y = quotient(remainder(fine, ny), 2) == remainder(coarse, ny // 2)
     return where01((fine < ny * xs) & same_x & same_y)
 
 
@@ -387,12 +400,13 @@
     groups = bx // 4
     order = [x for low in range(4) for x in range(low, bx, 4)]
     fine = iota((cells, 4 * cells), 1)
-    x, y = fine // (4 * by), (fine % (2 * by)) // 2
-    chosen = where01((x % 4) * (groups * by) + (x // 4) * by + y == iota((cells, 4 * cells), 0))
+    x, y = quotient(fine, 4 * by), quotient(remainder(fine, 2 * by), 2)
+    lane = remainder(x, 4) * (groups * by) + quotient(x, 4) * by + y
+    chosen = where01(lane == iota((cells, 4 * cells), 0))
     wide = lax.dot_general(
         chosen, res_ref[...], (((1,), (0,)), ((), ())), preferred_element_type=F32
     )
-    rhs = dot10(where01(iota((depth, 2 * depth), 1) // 2 == iota((depth, 2 * depth), 0)), wide)
+    rhs = dot10(where01(quotient(iota((depth, 2 * depth), 1), 2) == iota((depth, 2 * depth), 0)), wide)
 
     def turned(field_ref):
         field = jnp.concatenate([field_ref[x : x + 1] for x in order], axis=0)
@@ -424,7 +438,7 @@
 
 
 def place(gathered, row, target, plane, groups, by):
-    group = (iota((ROWS, LANES), 1) // by) % groups
+    group = remainder(quotient(iota((ROWS, LANES), 1), by), groups)
     nx, ny = SPLIT
     for ix in range(nx):
         found = [gathered[slot_of(ix * ny + iy), pl.ds(row, ROWS), :] for iy in range(ny)]
@@ -513,13 +527,13 @@
     coarse_residual(coarse, NEAR, NEAR + depth // 2, fields2, corr2, sums)
     count3 = depth // 4
     rhs3 = in_lanes(sums[0:count3], down2)
-    lane = iota((count3, LANES), 1) // ROWS
+    lane = quotient(iota((count3, LANES), 1), ROWS)
     first = jnp.zeros((count3, LANES), F32)
     second = jnp.zeros((count3, LANES), F32)
     for row in range(ROWS):
         first = jnp.where(lane == row, rhs3[:, row, :], first)
         first = jnp.where(lane == ROWS + row, fluid3[:, row, :], first)
-        second = jnp.where(lane % ROWS == row, pin3[:, row, :], second)
+        second = jnp.where(remainder(lane, ROWS) == row, pin3[:, row, :], second)
     odd = own_slab() % 2 == 1
 
     def ordered(field):
@@ -530,7 +544,7 @@
     packed[0] = first[0:2]
     packed[1] = first[2:4]
     packed[2] = jnp.where(lane[0:2] < ROWS, second[0:2], second[2:4])
-    lane = iota((1, LANES), 1) // (LANES // 4)
+    lane = quotient(iota((1, LANES), 1), LANES // 4)
     for index, plane in enumerate((NEAR + depth // 2 - 5, NEAR + 4)):
         for half in range(2):
             row = jnp.zeros((1, LANES), F32)
@@ -551,7 +565,7 @@
 def columns(rhs, fluid, pin):
     depth = fluid.shape[0]
     z, lane = iota(fluid.shape, 0), iota(fluid.shape, 1)
-    y, x = lane % ROWS, (lane // ROWS) % ROWS
+    y, x = remainder(lane, ROWS), remainder(quotient(lane, ROWS), ROWS)
 
     def next_x(field):
         return pltpu.roll(field, LANES - ROWS, 1)
@@ -637,7 +651,7 @@
     fine, coarse = Level(0), Level(1)
     cell = iota((LANES, LANES), 0)
     lane = iota((LANES, LANES), 1)
-    spread = where01((cell < ROWS) & (cell == (lane % coarse.ny) // 2))
+    spread = where01((cell < ROWS) & (cell == quotient(remainder(lane, coarse.ny), 2)))
     rows = tall.shape[0]
     turned = [tall] + [pltpu.roll(tall, LANES - ROWS * row, 1) for row in range(1, ROWS)]
     wide = dot01(jnp.concatenate(turned, axis=0), spread)
@@ -655,7 +669,7 @@
     fields2, corr2 = (far2[0:6], far2[6], far2[7]), far2[8]
     low, high = NEAR - 4, NEAR + depth // 2 + 4
     reach = depth // 2 + NEAR
-    quarter = iota((ROWS, LANES), 1) // (LANES // 4)
+    quarter = quotient(iota((ROWS, LANES), 1), LANES // 4)
     row = iota((ROWS, LANES), 0)
 
     def unpacked(index, which):
@@ -664,7 +678,7 @@
         for shift in range(4):
             moved = pltpu.roll(pair, shift * (LANES // 4), 1)
             wide = jnp.where(row < 4, moved[0:1, :], moved[1:2, :])
-            kept = jnp.where((quarter - shift) % 4 == row % 4, wide, 0.0)
+            kept = jnp.where(remainder(quarter - shift, 4) == remainder(row, 4), wide, 0.0)
             total = kept if total is None else total + kept
         return total
 
@@ -677,8 +691,8 @@
     sweep(coarse, NEAR - 2, reach + 2, fields2, one2, two2)
 
     fine_lane, coarse_lane = iota((LANES, LANES), 1), iota((LANES, LANES), 0)
-    x_of = (fine_lane // fine.ny) // 2
-    y_of = (fine_lane % fine.ny) // 2
+    x_of = quotient(fine_lane, 2 * fine.ny)
+    y_of = quotient(remainder(fine_lane, fine.ny), 2)
     up = where01(coarse_lane == x_of * coarse.ny + y_of)
     lifted[0 : depth // 2 + 4] = in_lanes(two2[NEAR - 2 : reach + 2], up)
     parents = lifted[0 : depth // 2 + 4]
@@ -706,7 +720,7 @@
     loop(HALO, turn, PIECE, last(far_fields, 0))
     loop(turn, reach, PIECE, last(near_fields, HALO))
 
-    group = (iota((depth, LANES), 1) // by) % groups
+    group = remainder(quotient(iota((depth, LANES), 1), by), groups)
     for ix in range(nx):
         scaled = [final[:, ix * groups + part, :] for part in range(groups)]
         for iy in range(ny):

time: 48.9 us -> 48.9 us (level)
  no operation moved by 1% of the time
where the time goes in v25:
time: 48.9 us; the launch traced here: 48.7 us
  blocking collectives  34.7 us (71%)
  waiting for transfers between devices  6.14 us (13%)
  Pallas kernels  5.71 us (12%)
  starting transfers between devices  1.04 us (2%)
  other arithmetic  0.93 us (2%)
    all_to_all x2, blocking collectives, exchange(): lax.all_to_all(field, axes, 0, 0, axis_index_groups=members, tiled=True)  22.6 us
    all_to_all x1, blocking collectives, exchange_all(): lax.all_to_all(field, axes, 0, 0, axis_index_groups=[members], tiled=True)  12.1 us
    ppermute x2, waiting for transfers between devices, swap(): lax.ppermute(field, ('gx', 'gy', 'gz'), pairs + [pair[::-1] for pair in p...  6.14 us
    pallas_call x1, Pallas kernels, whole_planes(): pl.pallas_call(functools.partial(up_kernel, groups, by, share), out_shape...  2.13 us
    pallas_call x1, Pallas kernels, whole_planes(): pl.pallas_call(functools.partial(down_kernel, share), out_shape=(far1, fa...  1.25 us
    ppermute x2, starting transfers between devices, swap(): lax.ppermute(field, ('gx', 'gy', 'gz'), pairs + [pair[::-1] for pair in p...  1.04 us
  transfers between devices with their start and end apart: 2, of which 1 were waited for; matrix products, arithmetic and copies ran while one was open for 0% of the time, Pallas kernels for 2%

profile of v25, /device:TPU:0, one launch (start us, length us, event | category | flops | bytes accessed | tf_op | source)
XLA Modules:
  0.0 48.7 jit_solution(1438713531354069636)
XLA Ops:
  0.0 0.0 copy-start
  0.0 0.9 %multiply_multiply_fusion = (f32[16,8,128]{2,1,0:T(8,128)S(1)}, f32[16,8,128]{2,1,0:T(8,128)S(1)}) fusion(s32[16,8,128]{2,1,0:T(8,128)} %param.5, f32[16,8,128]{2,1,0:T(8,128)} %param.4), kind=kLoop, calls=%fused_computation | loop fusion | flops 65536 | bytes 262144 | tf_op jit(solution)/shard_map/mul | solution.py:764
  0.9 0.1 copy-done
  1.0 0.4 prepare.1
  1.4 13.8 %all_to_all.15.gathered = f32[8,48,128]{2,1,0:T(8,128)S(1)} all-to-all(f32[8,48,128]{2,1,0:T(8,128)S(1)} %prepare.1), channel_id=1, replica_groups={{28,12,24,8,20,4,16,0},{29,13,25,9,21,5,17,1},{30,14,26,10,22,6,18,2},{..., dimensions={0} | all-to-all | bytes 393216 | tf_op jit(solution)/shard_map/all_to_all | solution.py:361
  15.2 0.3 spread.1
  15.5 0.4 collective-permute-start.1
  15.9 0.7 %collective-permute-start = (f32[46,8,128]{2,1,0:T(8,128)S(1)}, f32[46,8,128]{2,1,0:T(8,128)S(1)}, u32[]{:S(2)}, u32[]{:S(2)}) collective-permute-start(f32[46,8,128]{2,1,0:T(8,128)S(1)} %get-tuple-element.49), channel_id=1, source_target_pairs={{16,20},{4,8},{24,28},{12,13},{9,5},{1,17},{21,25},{29,30},{14,10}... | collective-permute-start | bytes 565256 | tf_op jit(solution)/shard_map/ppermute | solution.py:785
  16.5 6.1 %collective-permute-done.1.inner = f32[46,8,128]{2,1,0:T(8,128)S(1)} collective-permute-done((f32[46,8,128]{2,1,0:T(8,128)S(1)}, f32[46,8,128]{2,1,0:T(8,128)S(1)}, u32[]{:S(2)}, u32[]{:S(2)}) %collective-permute-start.1) | collective-permute-done | bytes 188448 | tf_op jit(solution)/shard_map/ppermute | solution.py:785
  22.7 0.9 %near.1 = (f32[32,8,128]{2,1,0:T(8,128)S(1)}, f32[32,8,128]{2,1,0:T(8,128)S(1)}, f32[32,8,128]{2,1,0:T(8,128)S(1)}, f32[32,8,128]{2,1,0:T(8,128)S(1)}, f32[32,8,...) custom-call(f32[48,8,128]{2,1,0:T(8,128)S(1)} %get-tuple-element.48., ...), custom_call_target="tpu_custom_call" | custom-call | tf_op jit(solution)/shard_map/near/pallas_call | solution.py:793
  23.6 0.0 collective-permute-done.outer
  23.6 1.2 %down.1 = (f32[24,8,128]{2,1,0:T(8,128)S(1)}, f32[24,8,128]{2,1,0:T(8,128)S(1)}, f32[24,8,128]{2,1,0:T(8,128)S(1)}, f32[24,8,128]{2,1,0:T(8,128)S(1)}, f32[24,8,...) custom-call(f32[48,8,128]{2,1,0:T(8,128)S(1)} %get-tuple-element.48., ...), custom_call_target="tpu_custom_call" | custom-call | tf_op jit(solution)/shard_map/down/pallas_call | solution.py:800
  24.9 12.1 %all_to_all.16.packed = f32[32,5,2,128]{3,2,1,0:T(2,128)S(1)} all-to-all(f32[32,5,2,128]{3,2,1,0:T(2,128)S(1)} %broadcast_in_dim.3), channel_id=1, replica_groups={{31,30,29,28,15,14,13,12,27,26,25,24,11,10,9,8,23,22,21,20,7,6,5,4,19,1..., dimensions={0} | all-to-all | bytes 327680 | tf_op jit(solution)/shard_map/all_to_all | solution.py:389
  37.0 2.1 %up.1 = f32[8,16,128]{2,1,0:T(8,128)S(1)} custom-call(f32[32,5,2,128]{3,2,1,0:T(2,128)S(1)} %all_to_all.16.packed, f32[32,8,128]{2,1,0:T(8,128)S(1)} %get-tuple-element.64.near1_0_, f32[32,8,128]{2,1,0:T(8,128)S(1)} %get-tuple-element.65.near1_1_, f32[32,8,128]{2,1,0:T(8,128)S(1)} %get-tuple-element.66.near1_2_, ...), custom_call_target="tpu_custom_call" | custom-call | tf_op jit(solution)/shard_map/up/pallas_call | solution.py:810
  39.2 8.8 %all_to_all.17.blocks = f32[8,16,128]{2,1,0:T(8,128)S(1)} all-to-all(f32[8,16,128]{2,1,0:T(8,128)S(1)} %up.1), channel_id=1, replica_groups={{28,12,24,8,20,4,16,0},{29,13,25,9,21,5,17,1},{30,14,26,10,22,6,18,2},{..., dimensions={0} | all-to-all | bytes 131072 | tf_op jit(solution)/shard_map/all_to_all | solution.py:361
  48.0 0.7 %finish.1 = f32[16,8,128]{2,1,0:T(8,128)} custom-call(f32[8,16,128]{2,1,0:T(8,128)S(1)} %all_to_all.17.blocks), custom_call_target="tpu_custom_call" | custom-call | tf_op jit(solution)/shard_map/finish/pallas_call | solution.py:819
  (1 shorter events, 0.0 us)
Async XLA Ops:
  0.0 1.0 %copy-start = (bf16[32,16,256]{2,1,0:T(8,128)(2,1)S(1)}, bf16[32,16,256]{2,1,0:T(8,128)(2,1)}, u32[]{:S(2)}) copy-start(bf16[32,16,256]{2,1,0:T(8,128)(2,1)} %param.3) | copy-start | bytes 786436
  15.5 7.2 %collective-permute-start.1 = (f32[46,8,128]{2,1,0:T(8,128)S(1)}, f32[46,8,128]{2,1,0:T(8,128)S(1)}, u32[]{:S(2)}, u32[]{:S(2)}) collective-permute-start(f32[46,8,128]{2,1,0:T(8,128)S(1)} %get-tuple-element.50), channel_id=1, source_target_pairs={{0,16},{20,4},{8,24},{28,12},{13,9},{5,1},{17,21},{25,29},{30,14},... | collective-permute-start | bytes 565256 | tf_op jit(solution)/shard_map/ppermute | solution.py:785
  15.9 7.7 %collective-permute-start = (f32[46,8,128]{2,1,0:T(8,128)S(1)}, f32[46,8,128]{2,1,0:T(8,128)S(1)}, u32[]{:S(2)}, u32[]{:S(2)}) collective-permute-start(f32[46,8,128]{2,1,0:T(8,128)S(1)} %get-tuple-element.49), channel_id=1, source_target_pairs={{16,20},{4,8},{24,28},{12,13},{9,5},{1,17},{21,25},{29,30},{14,10}... | collective-permute-start | bytes 565256 | tf_op jit(solution)/shard_map/ppermute | solution.py:785

commit v26 on v25

--- a/solution.py
+++ b/solution.py
@@ -451,10 +451,15 @@
             target[pl.ds(plane, ROWS), ix * groups + part, :] = total
 
 
+def ordered(field):
+    back = [field[row : row + 1] for row in reversed(range(field.shape[0]))]
+    return jnp.where(own_slab() % 2 == 1, jnp.concatenate(back, axis=0), field)
+
+
 def near_kernel(
     depth,
     own, inner,
-    saved1, saved2, fluid2, pin2, fluid3, pin3,
+    saved1, saved2, fluid2, pin2, fluids, pins,
     fluid1, rhs1, pin1, other1, rhs2, sums,
 ):
     row = 0
@@ -481,13 +486,22 @@
     low2, high2 = NEAR + 2, NEAR + count2 - 2
     rhs2[low2:high2] = in_lanes(sums[0 : high2 - low2], down1)
     set_level(coarse, low2, high2, fluid2, pin2, rhs2, fields2)
-    for source, target, scale in ((fluid2, fluid3, 0.125), (pin2, pin3, 0.25)):
-        target[...] = in_lanes(pair_sum(source[NEAR : NEAR + depth // 2]), down2) * scale
+    fluid3 = in_lanes(pair_sum(fluid2[NEAR : NEAR + depth // 2]), down2) * 0.125
+    pin3 = in_lanes(pair_sum(pin2[NEAR : NEAR + depth // 2]), down2) * 0.25
+    lane = quotient(iota((depth // 4, LANES), 1), ROWS)
+    first = jnp.zeros((depth // 4, LANES), F32)
+    second = jnp.zeros((depth // 4, LANES), F32)
+    for row in range(ROWS):
+        first = jnp.where(lane == ROWS + row, fluid3[:, row, :], first)
+        second = jnp.where(remainder(lane, ROWS) == row, pin3[:, row, :], second)
+    second = ordered(second)
+    fluids[...] = ordered(first)
+    pins[...] = jnp.where(lane[0:2] < ROWS, second[0:2], second[2:4])
 
 
 def down_kernel(
     depth,
-    own, outer, near2, near_fluid2, near_pin2, fluid3, pin3,
+    own, outer, near2, near_fluid2, near_pin2, fluids, pins,
     saved1, saved2,
     packed,
     fluid1, rhs1, pin1, other1, fluid2, rhs2, pin2, other2, sums,
@@ -529,29 +543,27 @@
     rhs3 = in_lanes(sums[0:count3], down2)
     lane = quotient(iota((count3, LANES), 1), ROWS)
     first = jnp.zeros((count3, LANES), F32)
-    second = jnp.zeros((count3, LANES), F32)
     for row in range(ROWS):
         first = jnp.where(lane == row, rhs3[:, row, :], first)
-        first = jnp.where(lane == ROWS + row, fluid3[:, row, :], first)
-        second = jnp.where(remainder(lane, ROWS) == row, pin3[:, row, :], second)
-    odd = own_slab() % 2 == 1
-
-    def ordered(field):
-        back = [field[row : row + 1] for row in reversed(range(count3))]
-        return jnp.where(odd, jnp.concatenate(back, axis=0), field)
-
-    first, second = ordered(first), ordered(second)
-    packed[0] = first[0:2]
-    packed[1] = first[2:4]
-    packed[2] = jnp.where(lane[0:2] < ROWS, second[0:2], second[2:4])
+    first = jnp.where(lane < ROWS, ordered(first), fluids[...])
+    copies = packed.shape[0]
+
+    def put(index, part):
+        packed[:, index] = jnp.broadcast_to(part[None], (copies,) + part.shape)
+
+    put(0, first[0:2])
+    put(1, first[2:4])
+    put(2, pins[...])
     lane = quotient(iota((1, LANES), 1), LANES // 4)
     for index, plane in enumerate((NEAR + depth // 2 - 5, NEAR + 4)):
+        both = []
         for half in range(2):
             row = jnp.zeros((1, LANES), F32)
             for quarter in range(4):
                 at = half * 4 + quarter
                 row = jnp.where(lane == quarter, corr2[plane, at : at + 1, :], row)
-            packed[3 + index, half : half + 1, :] = row
+            both.append(row)
+        put(3 + index, jnp.concatenate(both, axis=0))
 
 
 def rolled(field, shift):
@@ -790,22 +802,21 @@
         (blocks(count, ROWS),) * fields
         for count, fields in ((share + HALO, 9), (count2, 8), (HALO + 8, 9), (count2, 9))
     )
-    near1, near2, fluid2, pin2, fluid3, pin3 = pl.pallas_call(
+    near1, near2, fluid2, pin2, fluids, pins = pl.pallas_call(
         functools.partial(near_kernel, share),
-        out_shape=(near1, near2) + (blocks(count2, ROWS),) * 2 + (blocks(count3, ROWS),) * 2,
+        out_shape=(near1, near2) + (blocks(count2, ROWS),) * 2 + (flat(count3), flat(2)),
         scratch_shapes=[room(share + HALO)] * 4 + [room(count2)] * 2,
         compiler_params=limit,
         name="near",
     )(own, inner)
     far1, far2, parcel = pl.pallas_call(
         functools.partial(down_kernel, share),
-        out_shape=(far1, far2, blocks(5, 2)),
+        out_shape=(far1, far2, jax.ShapeDtypeStruct((parts, 5, 2, LANES), F32)),
         scratch_shapes=[room(HALO + 8)] * 4 + [room(count2)] * 5,
         compiler_params=limit,
         name="down",
-    )(own, outer, near2, fluid2, pin2, fluid3, pin3)
-    copies = jnp.broadcast_to(parcel, (parts,) + parcel.shape)
-    packed = exchange_all(copies)
+    )(own, outer, near2, fluid2, pin2, fluids, pins)
+    packed = exchange_all(parcel)
     depth3 = parts * count3
     mine = pl.pallas_call(
         functools.partial(up_kernel, groups, by, share),

time: 48.9 us -> 48.8 us (level)
  no operation moved by 1% of the time
where the time goes in v26:
time: 48.8 us; the launch traced here: 48.6 us
  blocking collectives  34.7 us (71%)
  waiting for transfers between devices  6.14 us (13%)
  Pallas kernels  5.64 us (12%)
  starting transfers between devices  1.04 us (2%)
  other arithmetic  0.93 us (2%)
    all_to_all x2, blocking collectives, exchange(): lax.all_to_all(field, axes, 0, 0, axis_index_groups=members, tiled=True)  22.6 us
    all_to_all x1, blocking collectives, exchange_all(): lax.all_to_all(field, axes, 0, 0, axis_index_groups=[members], tiled=True)  12.1 us
    ppermute x2, waiting for transfers between devices, swap(): lax.ppermute(field, ('gx', 'gy', 'gz'), pairs + [pair[::-1] for pair in p...  6.14 us
    pallas_call x1, Pallas kernels, whole_planes(): pl.pallas_call(functools.partial(up_kernel, groups, by, share), out_shape...  2.13 us
    pallas_call x1, Pallas kernels, whole_planes(): pl.pallas_call(functools.partial(down_kernel, share), out_shape=(far1, fa...  1.19 us
    ppermute x2, starting transfers between devices, swap(): lax.ppermute(field, ('gx', 'gy', 'gz'), pairs + [pair[::-1] for pair in p...  1.04 us
  transfers between devices with their start and end apart: 2, of which 1 were waited for; matrix products, arithmetic and copies ran while one was open for 0% of the time, Pallas kernels for 2%

profile of v26, /device:TPU:0, one launch (start us, length us, event | category | flops | bytes accessed | tf_op | source)
XLA Modules:
  0.0 48.6 jit_solution(10333983994862096480)
XLA Ops:
  0.0 0.0 copy-start
  0.0 0.9 %multiply_multiply_fusion = (f32[16,8,128]{2,1,0:T(8,128)S(1)}, f32[16,8,128]{2,1,0:T(8,128)S(1)}) fusion(s32[16,8,128]{2,1,0:T(8,128)} %param.5, f32[16,8,128]{2,1,0:T(8,128)} %param.4), kind=kLoop, calls=%fused_computation | loop fusion | flops 65536 | bytes 262144 | tf_op jit(solution)/shard_map/mul | solution.py:776
  0.9 0.1 copy-done
  1.0 0.4 prepare.1
  1.4 13.8 %all_to_all.15.gathered = f32[8,48,128]{2,1,0:T(8,128)S(1)} all-to-all(f32[8,48,128]{2,1,0:T(8,128)S(1)} %prepare.1), channel_id=1, replica_groups={{28,12,24,8,20,4,16,0},{29,13,25,9,21,5,17,1},{30,14,26,10,22,6,18,2},{..., dimensions={0} | all-to-all | bytes 393216 | tf_op jit(solution)/shard_map/all_to_all | solution.py:361
  15.2 0.3 spread.1
  15.5 0.4 collective-permute-start.1
  15.9 0.7 %collective-permute-start = (f32[46,8,128]{2,1,0:T(8,128)S(1)}, f32[46,8,128]{2,1,0:T(8,128)S(1)}, u32[]{:S(2)}, u32[]{:S(2)}) collective-permute-start(f32[46,8,128]{2,1,0:T(8,128)S(1)} %get-tuple-element.49), channel_id=1, source_target_pairs={{16,20},{4,8},{24,28},{12,13},{9,5},{1,17},{21,25},{29,30},{14,10}... | collective-permute-start | bytes 565256 | tf_op jit(solution)/shard_map/ppermute | solution.py:797
  16.5 6.1 %collective-permute-done.1.inner = f32[46,8,128]{2,1,0:T(8,128)S(1)} collective-permute-done((f32[46,8,128]{2,1,0:T(8,128)S(1)}, f32[46,8,128]{2,1,0:T(8,128)S(1)}, u32[]{:S(2)}, u32[]{:S(2)}) %collective-permute-start.1) | collective-permute-done | bytes 188448 | tf_op jit(solution)/shard_map/ppermute | solution.py:797
  22.7 0.9 %near.1 = (f32[32,8,128]{2,1,0:T(8,128)S(1)}, f32[32,8,128]{2,1,0:T(8,128)S(1)}, f32[32,8,128]{2,1,0:T(8,128)S(1)}, f32[32,8,128]{2,1,0:T(8,128)S(1)}, f32[32,8,...) custom-call(f32[48,8,128]{2,1,0:T(8,128)S(1)} %get-tuple-element.48., ...), custom_call_target="tpu_custom_call" | custom-call | tf_op jit(solution)/shard_map/near/pallas_call | solution.py:805
  23.6 0.0 collective-permute-done.outer
  23.6 1.2 %down.1 = (f32[24,8,128]{2,1,0:T(8,128)S(1)}, f32[24,8,128]{2,1,0:T(8,128)S(1)}, f32[24,8,128]{2,1,0:T(8,128)S(1)}, f32[24,8,128]{2,1,0:T(8,128)S(1)}, f32[24,8,...) custom-call(f32[48,8,128]{2,1,0:T(8,128)S(1)} %get-tuple-element.48., ...), custom_call_target="tpu_custom_call" | custom-call | tf_op jit(solution)/shard_map/down/pallas_call | solution.py:812
  24.8 12.1 %all_to_all.16.packed = f32[32,5,2,128]{3,2,1,0:T(2,128)S(1)} all-to-all(f32[32,5,2,128]{3,2,1,0:T(2,128)S(1)} %get-tuple-element.63), channel_id=1, replica_groups={{31,30,29,28,15,14,13,12,27,26,25,24,11,10,9,8,23,22,21,20,7,6,5,4,19,1..., dimensions={0} | all-to-all | bytes 327680 | tf_op jit(solution)/shard_map/all_to_all | solution.py:389
  36.9 2.1 %up.1 = f32[8,16,128]{2,1,0:T(8,128)S(1)} custom-call(f32[32,5,2,128]{3,2,1,0:T(2,128)S(1)} %all_to_all.16.packed, f32[32,8,128]{2,1,0:T(8,128)S(1)} %get-tuple-element.64.near1_0_, f32[32,8,128]{2,1,0:T(8,128)S(1)} %get-tuple-element.65.near1_1_, f32[32,8,128]{2,1,0:T(8,128)S(1)} %get-tuple-element.66.near1_2_, ...), custom_call_target="tpu_custom_call" | custom-call | tf_op jit(solution)/shard_map/up/pallas_call | solution.py:821
  39.0 8.8 %all_to_all.17.blocks = f32[8,16,128]{2,1,0:T(8,128)S(1)} all-to-all(f32[8,16,128]{2,1,0:T(8,128)S(1)} %up.1), channel_id=1, replica_groups={{28,12,24,8,20,4,16,0},{29,13,25,9,21,5,17,1},{30,14,26,10,22,6,18,2},{..., dimensions={0} | all-to-all | bytes 131072 | tf_op jit(solution)/shard_map/all_to_all | solution.py:361
  47.8 0.7 %finish.1 = f32[16,8,128]{2,1,0:T(8,128)} custom-call(f32[8,16,128]{2,1,0:T(8,128)S(1)} %all_to_all.17.blocks), custom_call_target="tpu_custom_call" | custom-call | tf_op jit(solution)/shard_map/finish/pallas_call | solution.py:830
Async XLA Ops:
  0.0 1.0 %copy-start = (bf16[32,16,256]{2,1,0:T(8,128)(2,1)S(1)}, bf16[32,16,256]{2,1,0:T(8,128)(2,1)}, u32[]{:S(2)}) copy-start(bf16[32,16,256]{2,1,0:T(8,128)(2,1)} %param.3) | copy-start | bytes 786436
  15.5 7.2 %collective-permute-start.1 = (f32[46,8,128]{2,1,0:T(8,128)S(1)}, f32[46,8,128]{2,1,0:T(8,128)S(1)}, u32[]{:S(2)}, u32[]{:S(2)}) collective-permute-start(f32[46,8,128]{2,1,0:T(8,128)S(1)} %get-tuple-element.50), channel_id=1, source_target_pairs={{0,16},{20,4},{8,24},{28,12},{13,9},{5,1},{17,21},{25,29},{30,14},... | collective-permute-start | bytes 565256 | tf_op jit(solution)/shard_map/ppermute | solution.py:797
  15.9 7.7 %collective-permute-start = (f32[46,8,128]{2,1,0:T(8,128)S(1)}, f32[46,8,128]{2,1,0:T(8,128)S(1)}, u32[]{:S(2)}, u32[]{:S(2)}) collective-permute-start(f32[46,8,128]{2,1,0:T(8,128)S(1)} %get-tuple-element.49), channel_id=1, source_target_pairs={{16,20},{4,8},{24,28},{12,13},{9,5},{1,17},{21,25},{29,30},{14,10}... | collective-permute-start | bytes 565256 | tf_op jit(solution)/shard_map/ppermute | solution.py:797
